TPU v7x, 32 devices: a whole 2x2x4 slice. The times are simulated.
32 devices in a mesh: grp: 1, row: 16 (over z, y, core), col: 2 (over x).
Axes of the slice: x: 2, y: 2, z: 4, core: 2. Of those that a mesh axis runs over, the one named last changes fastest.
Arguments:
- pair: bfloat16 [256, 256, 128], P(('grp', 'row'), 'col'), may hold values from -6 to 6
- mask: int32 [256], P('grp'), may hold values 0 or 1
- gain_in: float32 [128], replicated, may hold values from 0.1 to 1.9
- bias_in: float32 [128], replicated, may hold values from -3 to 3
- proj_weight: bfloat16 [128, 512], replicated, may hold values from -0.5 to 0.5
- gate_weight: bfloat16 [128, 128], replicated, may hold values from -0.5 to 0.5
- product_norm_gain: float32 [128], replicated, may hold values from 0.1 to 1.9
- product_norm_bias: float32 [128], replicated, may hold values from -3 to 3
- out_weight: bfloat16 [128, 128], replicated, may hold values from -0.5 to 0.5
- cotangent: bfloat16 [256, 256, 128], P(('grp', 'row'), 'col'), may hold values from -6 to 6
Outputs:
- update: bfloat16 [256, 256, 128], P(('grp', 'row'), 'col')
- grad_pair: bfloat16 [256, 256, 128], P(('grp', 'row'), 'col')
All inputs are finite; a program needn't handle non-finite values.
Results may differ from a plain program's by a relative error of at most 0.0076.
Values may be sent and summed in bfloat16 or wider, within the bound.
No kernel may reach another device: no remote copies, remote signals or barrier semaphores. Data moves between devices by JAX's collectives and lax.ppermute only.
A program may use at most 64 MiB of HBM per device.

v0:
```python
import jax
import jax.numpy as jnp
from jax import lax
from jax.sharding import PartitionSpec as P

EPS = 1e-05


def layer_normalize(values, reduce_dimension):
    feature_average = jnp.mean(values, axis=reduce_dimension, keepdims=True)
    centred = values - feature_average
    var = jnp.mean(centred * centred, axis=reduce_dimension, keepdims=True)
    inverse_deviation = lax.rsqrt(var + EPS)
    return (centred * inverse_deviation, inverse_deviation)


def regroup_in(values, n_row, n_col):
    depth, total, cols = values.shape
    rows = total // (n_row * n_col)
    shaped = values.reshape(depth, n_row, n_col, rows, cols).transpose(0, 1, 3, 2, 4)
    return shaped.reshape(depth, n_row * rows, n_col * cols)


def regroup_out(values, n_row, n_col):
    depth, full_rows, full_cols = values.shape
    rows = full_rows // n_row
    cols = full_cols // n_col
    shaped = values.reshape(depth, n_row, rows, n_col, cols).transpose(0, 1, 3, 2, 4)
    return shaped.reshape(depth, n_row * n_col * rows, cols)


def body(
    pair,
    mask,
    gain_in,
    bias_in,
    proj_weight,
    gate_weight,
    product_norm_gain,
    product_norm_bias,
    out_weight,
    cotangent,
):
    rows, cols, width = pair.shape
    hidden = out_weight.shape[0]
    n_row = lax.axis_size("row")
    n_col = lax.axis_size("col")
    mask_f = mask.astype(jnp.float32)
    row_mask = lax.dynamic_slice_in_dim(mask_f, lax.axis_index("row") * rows, rows)
    col_mask = lax.dynamic_slice_in_dim(mask_f, lax.axis_index("col") * cols, cols)
    pair_mask = (row_mask[:, None] * col_mask[None, :])[None]
    zhat, inv_in = layer_normalize(pair.astype(jnp.float32), 2)
    zbar = (zhat * gain_in + bias_in).astype(jnp.bfloat16)
    proj = jnp.einsum("ikc,ch->hik", zbar, proj_weight, preferred_element_type=jnp.float32)
    pa, qa = (proj[:hidden], proj[hidden : 2 * hidden])
    pb, qb = (proj[2 * hidden : 3 * hidden], proj[3 * hidden :])
    sig_a = jax.nn.sigmoid(pa)
    sig_b = jax.nn.sigmoid(pb)
    left = (sig_a * qa * pair_mask).astype(jnp.bfloat16)
    right = (sig_b * qb * pair_mask).astype(jnp.bfloat16)
    gate = jax.nn.sigmoid(
        jnp.einsum("ikc,cd->ikd", zbar, gate_weight, preferred_element_type=jnp.float32)
    )
    left_ch, right_ch = (
        lax.all_to_all(left, ("row", "col"), split_axis=0, concat_axis=1, tiled=True),
        lax.all_to_all(right, ("row", "col"), split_axis=0, concat_axis=1, tiled=True),
    )
    left_ch = regroup_in(left_ch, n_row, n_col)
    right_ch = regroup_in(right_ch, n_row, n_col)
    product = jnp.einsum(
        "hik,hjk->hij", left_ch, right_ch, preferred_element_type=jnp.float32
    ).astype(jnp.bfloat16)
    product_piece = lax.all_to_all(
        regroup_out(product, n_row, n_col), ("row", "col"), split_axis=1, concat_axis=0, tiled=True
    )
    normalized_input, product_inverse_deviation = layer_normalize(
        product_piece.astype(jnp.float32), 0
    )
    scaled_normalized = (
        normalized_input * product_norm_gain[:, None, None] + product_norm_bias[:, None, None]
    ).astype(jnp.bfloat16)
    proj_out = jnp.einsum(
        "hik,hc->ikc", scaled_normalized, out_weight, preferred_element_type=jnp.float32
    )
    update = (gate * proj_out).astype(jnp.bfloat16)
    cot_f = cotangent.astype(jnp.float32)
    grad_u = (cot_f * gate).astype(jnp.bfloat16)
    grad_gate = (cot_f * proj_out * gate * (1.0 - gate)).astype(jnp.bfloat16)
    grad_y = jnp.einsum("ikc,hc->hik", grad_u, out_weight, preferred_element_type=jnp.float32)
    normalized_gradient = grad_y * product_norm_gain[:, None, None]
    input_gradient = (
        (
            normalized_gradient
            - jnp.mean(normalized_gradient, axis=0, keepdims=True)
            - normalized_input
            * jnp.mean(normalized_gradient * normalized_input, axis=0, keepdims=True)
        )
        * product_inverse_deviation
    ).astype(jnp.bfloat16)
    grad_ch = regroup_in(
        lax.all_to_all(input_gradient, ("row", "col"), split_axis=0, concat_axis=1, tiled=True),
        n_row,
        n_col,
    )
    grad_left = jnp.einsum(
        "hij,hjk->hik", grad_ch, right_ch, preferred_element_type=jnp.float32
    ).astype(jnp.bfloat16)
    grad_right = jnp.einsum(
        "hij,hik->hjk", grad_ch, left_ch, preferred_element_type=jnp.float32
    ).astype(jnp.bfloat16)
    gl_tile, gr_tile = (
        lax.all_to_all(
            regroup_out(grad_left, n_row, n_col),
            ("row", "col"),
            split_axis=1,
            concat_axis=0,
            tiled=True,
        ),
        lax.all_to_all(
            regroup_out(grad_right, n_row, n_col),
            ("row", "col"),
            split_axis=1,
            concat_axis=0,
            tiled=True,
        ),
    )
    gl_f = gl_tile.astype(jnp.float32) * pair_mask
    gr_f = gr_tile.astype(jnp.float32) * pair_mask
    dproj = jnp.concatenate(
        [
            gl_f * qa * sig_a * (1.0 - sig_a),
            gl_f * sig_a,
            gr_f * qb * sig_b * (1.0 - sig_b),
            gr_f * sig_b,
        ],
        axis=0,
    ).astype(jnp.bfloat16)
    grad_zbar = jnp.einsum("hik,ch->ikc", dproj, proj_weight, preferred_element_type=jnp.float32)
    grad_zbar = grad_zbar + jnp.einsum(
        "ikd,cd->ikc", grad_gate, gate_weight, preferred_element_type=jnp.float32
    )
    grad_zh = grad_zbar * gain_in
    grad_pair = (
        (
            grad_zh
            - jnp.mean(grad_zh, axis=2, keepdims=True)
            - zhat * jnp.mean(grad_zh * zhat, axis=2, keepdims=True)
        )
        * inv_in
    ).astype(jnp.bfloat16)
    return (update, grad_pair)


def solution(mesh):
    placed = (
        P(("grp", "row"), "col", None),
        P("grp"),
        P(),
        P(),
        P(),
        P(),
        P(),
        P(),
        P(),
        P(("grp", "row"), "col", None),
    )
    return jax.shard_map(
        body,
        mesh=mesh,
        in_specs=placed,
        out_specs=(P(("grp", "row"), "col", None), P(("grp", "row"), "col", None)),
        check_vma=False,
    )
```

profile of v0, /device:TPU:0, one launch (start us, length us, event | category | flops | bytes accessed | tf_op | source)
XLA Modules:
  0.0 142.0 jit_solution(11755292013165962137)
XLA Ops:
  0.7 0.7 convert_element_type.90
  1.5 1.3 copy.95
  3.2 1.5 %convolution_bitcast_fusion = f32[512,16,128]{0,2,1:T(8,128)S(1)} fusion(bf16[128,512]{1,0:T(8,128)(2,1)S(1)} %copy-done, bf16[16,128,128]{1,2,0:T(8,128)(2,1)S(1)} %copy.95, f32[128]{0:T(128)} %param.13, f32[128]{0:T(128)} %param.12, f32[16,128]{1,0:T(8,128)S(1)} %add_rsqrt_fusion.1, f32[16,128]{1,0:T(8,128)S(1)} %broadcast_multiply_fusion.6), kind=kOutput, calls=%fused_computation | convolution fusion | flops 270008320 | bytes 4867072 | tf_op jit(solution)/shard_map/ikc,ch->hik/dot_general | solution.py:54
  4.7 1.9 %copy-done.1 = f32[512,16,128]{0,2,1:T(8,128)} copy-done((f32[512,16,128]{0,2,1:T(8,128)}, f32[512,16,128]{0,2,1:T(8,128)S(1)}, u32[]{:S(2)}) %copy-start.1) | copy-done | bytes 4194328
  7.2 1.2 copy.100
  8.4 7.3 %all-to-all-start.1 = ((bf16[128,16,128]{2,1,0:T(8,128)(2,1)}), bf16[128,16,128]{2,1,0:T(8,128)(2,1)S(1)}, u32[]{:S(2)}, u32[]{:S(2)}) async-start(bf16[128,16,128]{2,1,0:T(8,128)(2,1)} %copy.100), calls=%async_computation.1 | async-start | bytes 1048576 | tf_op jit(solution)/shard_map/all_to_all | solution.py:66
  15.7 1.2 copy.98
  16.9 13.8 %all-to-all-done.1 = bf16[128,16,128]{2,1,0:T(8,128)(2,1)S(1)} async-done(((bf16[128,16,128]{2,1,0:T(8,128)(2,1)}), bf16[128,16,128]{2,1,0:T(8,128)(2,1)S(1)}, u32[]{:S(2)}, u32[]{:S(2)}) %all-to-all-start.1) | async-done | bytes 524320 | tf_op jit(solution)/shard_map/all_to_all | solution.py:66
  30.7 3.6 %all-to-all-start = ((bf16[128,16,128]{2,1,0:T(8,128)(2,1)}), bf16[128,16,128]{2,1,0:T(8,128)(2,1)S(1)}, u32[]{:S(2)}, u32[]{:S(2)}) async-start(bf16[128,16,128]{2,1,0:T(8,128)(2,1)} %copy.98), calls=%async_computation | async-start | bytes 1048576 | tf_op jit(solution)/shard_map/all_to_all | solution.py:65
  35.2 14.1 %all-to-all-done = bf16[128,16,128]{2,1,0:T(8,128)(2,1)S(1)} async-done(((bf16[128,16,128]{2,1,0:T(8,128)(2,1)}), bf16[128,16,128]{2,1,0:T(8,128)(2,1)S(1)}, u32[]{:S(2)}, u32[]{:S(2)}) %all-to-all-start) | async-done | bytes 524320 | tf_op jit(solution)/shard_map/all_to_all | solution.py:65
  51.3 18.4 %all_to_all.72 = bf16[4,512,128]{2,0,1:T(4,128)(2,1)S(1)} all-to-all(bf16[4,512,128]{2,0,1:T(4,128)(2,1)S(1)} %copy.103), channel_id=1, replica_groups=mesh['grp'=1,'row'=16,'col'=2] {'row','col'}, dimensions={1} | all-to-all | bytes 1048576 | tf_op jit(solution)/shard_map/all_to_all | solution.py:73
  71.4 1.4 multiply_convert_fusion.5
  74.5 18.4 %all_to_all.73 = bf16[128,16,128]{2,1,0:T(8,128)(2,1)S(1)} all-to-all(bf16[128,16,128]{2,1,0:T(8,128)(2,1)S(1)} %copy.107), channel_id=1, replica_groups=mesh['grp'=1,'row'=16,'col'=2] {'row','col'}, dimensions={0} | all-to-all | bytes 1048576 | tf_op jit(solution)/shard_map/all_to_all | solution.py:101
  94.3 1.2 copy.111
  95.5 3.8 %all-to-all-start.4 = ((bf16[4,512,128]{2,0,1:T(4,128)(2,1)}), bf16[4,512,128]{2,0,1:T(4,128)(2,1)S(1)}, u32[]{:S(2)}, u32[]{:S(2)}) async-start(bf16[4,512,128]{2,0,1:T(4,128)(2,1)} %copy.111), calls=%async_computation.4 | async-start | bytes 1048576 | tf_op jit(solution)/shard_map/all_to_all | solution.py:112
  99.9 1.2 copy.117
  101.1 13.0 %all-to-all-done.4 = bf16[4,512,128]{2,0,1:T(4,128)(2,1)S(1)} async-done(((bf16[4,512,128]{2,0,1:T(4,128)(2,1)}), bf16[4,512,128]{2,0,1:T(4,128)(2,1)S(1)}, u32[]{:S(2)}, u32[]{:S(2)}) %all-to-all-start.4) | async-done | bytes 524320 | tf_op jit(solution)/shard_map/all_to_all | solution.py:112
  114.2 3.6 %all-to-all-start.5 = ((bf16[4,512,128]{2,0,1:T(4,128)(2,1)}), bf16[4,512,128]{2,0,1:T(4,128)(2,1)S(1)}, u32[]{:S(2)}, u32[]{:S(2)}) async-start(bf16[4,512,128]{2,0,1:T(4,128)(2,1)} %copy.117), calls=%async_computation.5 | async-start | bytes 1048576 | tf_op jit(solution)/shard_map/all_to_all | solution.py:119
  118.5 14.3 %all-to-all-done.5 = bf16[4,512,128]{2,0,1:T(4,128)(2,1)S(1)} async-done(((bf16[4,512,128]{2,0,1:T(4,128)(2,1)}), bf16[4,512,128]{2,0,1:T(4,128)(2,1)S(1)}, u32[]{:S(2)}, u32[]{:S(2)}) %all-to-all-start.5) | async-done | bytes 524320 | tf_op jit(solution)/shard_map/all_to_all | solution.py:119
  133.0 1.1 copy.119
  134.1 1.6 %copy.120 = f32[128,16,128]{0,2,1:T(8,128)S(1)} copy(f32[128,16,128]{2,1,0:T(8,128)} %bitcast.89) | data formatting | bytes 2097152 | tf_op jit(solution)/shard_map/convert_element_type | solution.py:128
  135.7 2.8 %multiply_convert_fusion.3 = (bf16[128,16,128]{0,2,1:T(8,128)(2,1)S(1)}, bf16[128,16,128]{0,2,1:T(8,128)(2,1)S(1)}, bf16[128,16,128]{0,2,1:T(8,128)(2,1)S(1)}, bf16[128,16,128]{0,2,1:T(8,128)(2,1)S(1)}) fusion(f32[512,16,128]{0,2,1:T(8,128)} %copy-done.1, f32[128,16,128]{0,2,1:T(8,128)S(1)} %copy.114, f32[16,128]{1,0:T(8,128)S(1)} %broadcast_multiply_fusion, ...), kind=kLoop, calls=%fused_computation.54 | loop fusion | flops 5767168 | bytes 8396800 | tf_op jit(solution)/shard_map/convert.11
  138.5 1.0 fusion
  141.0 1.0 copy.122
  (72 shorter events, 11.4 us)
Async XLA Ops:
  0.6 2.6 %copy-start = (bf16[128,512]{1,0:T(8,128)(2,1)S(1)}, bf16[128,512]{1,0:T(8,128)(2,1)}, u32[]{:S(2)}) copy-start(bf16[128,512]{1,0:T(8,128)(2,1)} %param.14) | copy-start | bytes 393220
  4.7 1.9 %copy-start.1 = (f32[512,16,128]{0,2,1:T(8,128)}, f32[512,16,128]{0,2,1:T(8,128)S(1)}, u32[]{:S(2)}) copy-start(f32[512,16,128]{0,2,1:T(8,128)S(1)} %convolution_bitcast_fusion) | copy-start | bytes 12582916
  8.4 22.3 %all-to-all-start.1 = ((bf16[128,16,128]{2,1,0:T(8,128)(2,1)}), bf16[128,16,128]{2,1,0:T(8,128)(2,1)S(1)}, u32[]{:S(2)}, u32[]{:S(2)}) async-start(bf16[128,16,128]{2,1,0:T(8,128)(2,1)} %copy.100), calls=%async_computation.1 | async-start | bytes 1048576 | tf_op jit(solution)/shard_map/all_to_all | solution.py:66
  30.7 18.6 %all-to-all-start = ((bf16[128,16,128]{2,1,0:T(8,128)(2,1)}), bf16[128,16,128]{2,1,0:T(8,128)(2,1)S(1)}, u32[]{:S(2)}, u32[]{:S(2)}) async-start(bf16[128,16,128]{2,1,0:T(8,128)(2,1)} %copy.98), calls=%async_computation | async-start | bytes 1048576 | tf_op jit(solution)/shard_map/all_to_all | solution.py:65
  50.7 20.2 %copy-start.8 = (bf16[128,128]{1,0:T(8,128)(2,1)S(1)}, bf16[128,128]{1,0:T(8,128)(2,1)}, u32[]{:S(2)}) copy-start(bf16[128,128]{1,0:T(8,128)(2,1)} %param.18) | copy-start | bytes 98308
  50.7 20.2 %copy-start.11 = (f32[128]{0:T(128)S(1)}, f32[128]{0:T(128)}, u32[]{:S(2)}) copy-start(f32[128]{0:T(128)} %param.16) | copy-start | bytes 1540
  50.7 20.2 %copy-start.12 = (f32[128]{0:T(128)S(1)}, f32[128]{0:T(128)}, u32[]{:S(2)}) copy-start(f32[128]{0:T(128)} %param.17) | copy-start | bytes 1540
  51.2 20.1 %copy-start.9 = (bf16[128,128]{1,0:T(8,128)(2,1)S(1)}, bf16[128,128]{1,0:T(8,128)(2,1)}, u32[]{:S(2)}) copy-start(bf16[128,128]{1,0:T(8,128)(2,1)} %param.15) | copy-start | bytes 98308
  51.3 20.1 %copy-start.10 = (f32[128]{0:T(128)S(1)}, f32[128]{0:T(128)}, u32[]{:S(2)}) copy-start(f32[128]{0:T(128)} %param.12) | copy-start | bytes 1540
  51.3 20.1 %copy-start.13 = (f32[128]{0:T(128)S(1)}, f32[128]{0:T(128)}, u32[]{:S(2)}) copy-start(f32[128]{0:T(128)} %param.13) | copy-start | bytes 1540
  70.9 1.9 %copy-start.6 = (bf16[16,128,128]{2,1,0:T(8,128)(2,1)S(1)}, bf16[16,128,128]{2,1,0:T(8,128)(2,1)}, u32[]{:S(2)}) copy-start(bf16[16,128,128]{2,1,0:T(8,128)(2,1)} %param.19) | copy-start | bytes 1572868
  71.4 1.8 %copy-start.2 = (f32[16,128,128]{2,1,0:T(8,128)}, f32[16,128,128]{2,1,0:T(8,128)S(1)}, u32[]{:S(2)}) copy-start(f32[16,128,128]{2,1,0:T(8,128)S(1)} %fusion.35) | copy-start | bytes 3145732
  72.8 1.0 copy-start.4
  95.5 18.6 %all-to-all-start.4 = ((bf16[4,512,128]{2,0,1:T(4,128)(2,1)}), bf16[4,512,128]{2,0,1:T(4,128)(2,1)S(1)}, u32[]{:S(2)}, u32[]{:S(2)}) async-start(bf16[4,512,128]{2,0,1:T(4,128)(2,1)} %copy.111), calls=%async_computation.4 | async-start | bytes 1048576 | tf_op jit(solution)/shard_map/all_to_all | solution.py:112
  114.2 18.6 %all-to-all-start.5 = ((bf16[4,512,128]{2,0,1:T(4,128)(2,1)}), bf16[4,512,128]{2,0,1:T(4,128)(2,1)S(1)}, u32[]{:S(2)}, u32[]{:S(2)}) async-start(bf16[4,512,128]{2,0,1:T(4,128)(2,1)} %copy.117), calls=%async_computation.5 | async-start | bytes 1048576 | tf_op jit(solution)/shard_map/all_to_all | solution.py:119
  138.4 1.2 copy-start.3
  138.4 1.5 %copy-start.5 = (f32[16,128,128]{2,1,0:T(8,128)S(1)}, f32[16,128,128]{2,1,0:T(8,128)}, u32[]{:S(2)}) copy-start(f32[16,128,128]{2,1,0:T(8,128)} %copy-done.4) | copy-start | bytes 3145732
  138.5 1.7 %copy-start.7 = (bf16[16,128,128]{2,1,0:T(8,128)(2,1)S(1)}, bf16[16,128,128]{2,1,0:T(8,128)(2,1)}, u32[]{:S(2)}) copy-start(bf16[16,128,128]{2,1,0:T(8,128)(2,1)} %param.19) | copy-start | bytes 1572868
where the time goes:
time: 143 us; the launch traced here: 142 us
  waiting for transfers between devices  55.2 us (39%)
  blocking collectives  36.9 us (26%)
  local copies, waits for them, and re-layouts  18.6 us (13%)
  starting transfers between devices  18.3 us (13%)
  matrix products  6.24 us (4%)
  other arithmetic  5.7 us (4%)
    all_to_all x1, blocking collectives, body(): lax.all_to_all(input_gradient, ('row', 'col'), split_axis=0, concat_axis=...  18.4 us
    all_to_all x1, blocking collectives, body(): lax.all_to_all(regroup_out(product, n_row, n_col), ('row', 'col'), split_...  18.4 us
    all_to_all x1, waiting for transfers between devices, body(): lax.all_to_all(regroup_out(grad_right, n_row, n_col), ('row', 'col'), spl...  14.3 us
    all_to_all x1, waiting for transfers between devices, body(): lax.all_to_all(left, ('row', 'col'), split_axis=0, concat_axis=1, tiled=T...  14.1 us
    all_to_all x1, waiting for transfers between devices, body(): lax.all_to_all(right, ('row', 'col'), split_axis=0, concat_axis=1, tiled=...  13.8 us
    all_to_all x1, waiting for transfers between devices, body(): lax.all_to_all(regroup_out(grad_left, n_row, n_col), ('row', 'col'), spli...  13 us
    all_to_all x1, starting transfers between devices, body(): lax.all_to_all(right, ('row', 'col'), split_axis=0, concat_axis=1, tiled=...  7.3 us
    unnamed x30, local copies, waits for them, and re-layouts  5.52 us
  transfers between devices with their start and end apart: 4, of which 4 were waited for; matrix products, arithmetic and copies ran while one was open for 3% of the time, Pallas kernels for 0%

commit v1 on v0

--- a/solution.py
+++ b/solution.py
@@ -61,12 +61,19 @@
     gate = jax.nn.sigmoid(
         jnp.einsum("ikc,cd->ikd", zbar, gate_weight, preferred_element_type=jnp.float32)
     )
-    left_ch, right_ch = (
-        lax.all_to_all(left, ("row", "col"), split_axis=0, concat_axis=1, tiled=True),
-        lax.all_to_all(right, ("row", "col"), split_axis=0, concat_axis=1, tiled=True),
+    n_dev = n_row * n_col
+    share = hidden // n_dev
+    both = jnp.concatenate(
+        [
+            left.reshape(n_dev, share, rows, cols),
+            right.reshape(n_dev, share, rows, cols),
+        ],
+        axis=1,
     )
-    left_ch = regroup_in(left_ch, n_row, n_col)
-    right_ch = regroup_in(right_ch, n_row, n_col)
+    both = lax.all_to_all(both, ("row", "col"), split_axis=0, concat_axis=0, tiled=True)
+    both = both.reshape(n_row, n_col, 2 * share, rows, cols).transpose(2, 0, 3, 1, 4)
+    both = both.reshape(2 * share, n_row * rows, n_col * cols)
+    left_ch, right_ch = both[:share], both[share:]
     product = jnp.einsum(
         "hik,hjk->hij", left_ch, right_ch, preferred_element_type=jnp.float32
     ).astype(jnp.bfloat16)
@@ -108,22 +115,12 @@
     grad_right = jnp.einsum(
         "hij,hik->hjk", grad_ch, left_ch, preferred_element_type=jnp.float32
     ).astype(jnp.bfloat16)
-    gl_tile, gr_tile = (
-        lax.all_to_all(
-            regroup_out(grad_left, n_row, n_col),
-            ("row", "col"),
-            split_axis=1,
-            concat_axis=0,
-            tiled=True,
-        ),
-        lax.all_to_all(
-            regroup_out(grad_right, n_row, n_col),
-            ("row", "col"),
-            split_axis=1,
-            concat_axis=0,
-            tiled=True,
-        ),
-    )
+    grads = jnp.concatenate([grad_left, grad_right], axis=0)
+    grads = grads.reshape(2 * share, n_row, rows, n_col, cols).transpose(1, 3, 0, 2, 4)
+    grads = grads.reshape(n_dev, 2 * share, rows, cols)
+    grads = lax.all_to_all(grads, ("row", "col"), split_axis=0, concat_axis=0, tiled=True)
+    gl_tile = grads[:, :share].reshape(hidden, rows, cols)
+    gr_tile = grads[:, share:].reshape(hidden, rows, cols)
     gl_f = gl_tile.astype(jnp.float32) * pair_mask
     gr_f = gr_tile.astype(jnp.float32) * pair_mask
     dproj = jnp.concatenate(

time: 143 us -> 129 us (0.902)
  blocking collectives: 36.9 us -> 99.9 us
  waiting for transfers between devices: 55.2 us -> 0 us
  starting transfers between devices: 18.3 us -> 0 us
  local copies, waits for them, and re-layouts: 18.6 us -> 14.8 us
    all_to_all x0 -> x2, blocking collectives: none -> 63 us  [the longest x1 33.3 us: body(): lax.all_to_all(both, ('row', 'col'), split_axis=0, concat_axis=0, tiled=T...]
    all_to_all x4 -> x0, waiting for transfers between devices: 55.2 us -> none  [the longest x1 14.3 us: body(): lax.all_to_all(regroup_out(grad_right, n_row, n_col), ('row', 'col'), spl...]
    all_to_all x4 -> x0, starting transfers between devices: 18.3 us -> none  [the longest x1 7.3 us: body(): lax.all_to_all(right, ('row', 'col'), split_axis=0, concat_axis=1, tiled=...]
    reshape x3 -> x1, local copies, waits for them, and re-layouts: 2.82 us -> 0.41 us  [regroup_out(): return shaped.reshape(depth, n_row * n_col * rows, cols)]
    slice x0 -> x4, local copies, waits for them, and re-layouts: none -> 1.64 us  [the longest x3 1.43 us: body(): left_ch, right_ch = (both[:share], both[share:])]
  transfers between devices with their start and end apart: 4 -> 0, of which waited for: 4 -> 0; matrix products, arithmetic and copies ran while one was open for 3% -> 0% of each run, Pallas kernels for 0% -> 0%
where the time goes in v1:
time: 129 us
  blocking collectives  99.9 us (77%)
  local copies, waits for them, and re-layouts  14.8 us (11%)
  other arithmetic  6.94 us (5%)
  matrix products  6.25 us (5%)
    all_to_all x1, blocking collectives, body(): lax.all_to_all(both, ('row', 'col'), split_axis=0, concat_axis=0, tiled=T...  33.3 us
    all_to_all x1, blocking collectives, body(): lax.all_to_all(grads, ('row', 'col'), split_axis=0, concat_axis=0, tiled=...  29.7 us
    all_to_all x1, blocking collectives, body(): lax.all_to_all(regroup_out(product, n_row, n_col), ('row', 'col'), split_...  18.4 us
    all_to_all x1, blocking collectives, body(): lax.all_to_all(input_gradient, ('row', 'col'), split_axis=0, concat_axis=...  18.4 us
    unnamed x30, local copies, waits for them, and re-layouts  5.5 us
    another operation x1, other arithmetic  2.75 us

profile of v1, /device:TPU:0, one launch (start us, length us, event | category | flops | bytes accessed | tf_op | source)
XLA Modules:
  0.0 129.0 jit_solution(4723855238626847977)
XLA Ops:
  0.7 0.7 convert_element_type.78
  1.5 1.3 %copy.75 = bf16[16,128,128]{1,2,0:T(8,128)(2,1)S(1)} copy(bf16[16,128,128]{2,1,0:T(8,128)(2,1)} %param.10) | data formatting | bytes 1048576 | tf_op args[0]
  3.2 1.5 %convolution_bitcast_fusion = f32[512,16,128]{0,2,1:T(8,128)S(1)} fusion(bf16[128,512]{1,0:T(8,128)(2,1)S(1)} %copy-done, bf16[16,128,128]{1,2,0:T(8,128)(2,1)S(1)} %copy.75, f32[128]{0:T(128)} %param.13, f32[128]{0:T(128)} %param.12, f32[16,128]{1,0:T(8,128)S(1)} %add_rsqrt_fusion.1, f32[16,128]{1,0:T(8,128)S(1)} %broadcast_multiply_fusion.6), kind=kOutput, calls=%fused_computation | convolution fusion | flops 270008320 | bytes 4867072 | tf_op jit(solution)/shard_map/ikc,ch->hik/dot_general | solution.py:54
  4.7 1.9 %copy-done.1 = f32[512,16,128]{0,2,1:T(8,128)} copy-done((f32[512,16,128]{0,2,1:T(8,128)}, f32[512,16,128]{0,2,1:T(8,128)S(1)}, u32[]{:S(2)}) %copy-start.1) | copy-done | bytes 4194328
  6.6 0.6 multiply_convert_fusion.7
  7.2 0.4 copy.78
  7.7 0.4 copy.79
  8.2 33.3 %all_to_all.34 = bf16[32,8,16,128]{3,2,1,0:T(8,128)(2,1)S(1)} all-to-all(bf16[32,8,16,128]{3,2,1,0:T(8,128)(2,1)S(1)} %pad_maximum_fusion), channel_id=1, replica_groups=mesh['grp'=1,'row'=16,'col'=2] {'row','col'}, dimensions={0} | all-to-all | bytes 2097152 | tf_op jit(solution)/shard_map/all_to_all | solution.py:73
  41.5 1.6 %copy.104 = bf16[16,2,8,16,128]{4,1,3,0,2:T(2,128)(2,1)S(1)} copy(bf16[16,2,8,16,128]{4,3,2,1,0:T(8,128)(2,1)S(1)} %bitcast.71) | data formatting | bytes 2097152 | tf_op jit(solution)/shard_map/reshape | solution.py:74
  43.2 0.8 fusion.57
  45.7 18.4 %all_to_all.35 = bf16[4,512,128]{2,0,1:T(4,128)(2,1)S(1)} all-to-all(bf16[4,512,128]{2,0,1:T(4,128)(2,1)S(1)} %copy.82), channel_id=1, replica_groups=mesh['grp'=1,'row'=16,'col'=2] {'row','col'}, dimensions={1} | all-to-all | bytes 1048576 | tf_op jit(solution)/shard_map/all_to_all | solution.py:80
  64.6 0.7 copy.84
  65.3 0.4 fusion.35
  65.8 1.4 %multiply_convert_fusion.5 = (bf16[16,128,128]{2,1,0:T(8,128)(2,1)}, f32[16,128,128]{2,1,0:T(8,128)S(1)}) fusion(f32[16,128,128]{2,1,0:T(8,128)S(1)} %fusion.35, bf16[128,128]{1,0:T(8,128)(2,1)S(1)} %copy-done.9, bf16[16,128,128]{1,2,0:T(8,128)(2,1)S(1)} %copy.75, f32[128]{0:T(128)S(1)} %copy-done.13, f32[128]{0:T(128)S(1)} %copy-done.10, ...), kind=kOutput, calls=%fused_computation.58 | convolution fusion | flops 69992448 | bytes 3195904 | tf_op jit(solution)/shard_map/ikc,cd->ikd/dot_general | solution.py:62
  67.6 0.6 copy-done.4
  68.8 18.4 %all_to_all.36 = bf16[128,16,128]{2,1,0:T(8,128)(2,1)S(1)} all-to-all(bf16[128,16,128]{2,1,0:T(8,128)(2,1)S(1)} %copy.86), channel_id=1, replica_groups=mesh['grp'=1,'row'=16,'col'=2] {'row','col'}, dimensions={0} | all-to-all | bytes 1048576 | tf_op jit(solution)/shard_map/all_to_all | solution.py:108
  87.3 0.5 copy.88
  89.5 29.7 %all_to_all.37 = bf16[32,8,16,128]{3,2,1,0:T(8,128)(2,1)S(1)} all-to-all(bf16[32,8,16,128]{3,2,1,0:T(8,128)(2,1)S(1)} %bitcast.73), channel_id=1, replica_groups=mesh['grp'=1,'row'=16,'col'=2] {'row','col'}, dimensions={0} | all-to-all | bytes 2097152 | tf_op jit(solution)/shard_map/all_to_all | solution.py:121
  119.9 1.1 bitcast_convert_fusion
  121.0 1.6 %copy.92 = f32[128,16,128]{0,2,1:T(8,128)S(1)} copy(f32[128,16,128]{2,1,0:T(8,128)} %bitcast_convert_fusion) | data formatting | bytes 2097152 | tf_op jit(solution)/shard_map/convert_element_type | solution.py:125
  122.6 2.8 %multiply_convert_fusion.3 = (bf16[128,16,128]{0,2,1:T(8,128)(2,1)S(1)}, bf16[128,16,128]{0,2,1:T(8,128)(2,1)S(1)}, bf16[128,16,128]{0,2,1:T(8,128)(2,1)S(1)}, bf16[128,16,128]{0,2,1:T(8,128)(2,1)S(1)}) fusion(f32[512,16,128]{0,2,1:T(8,128)} %copy-done.1, f32[128,16,128]{0,2,1:T(8,128)S(1)} %copy.91, f32[16,128]{1,0:T(8,128)S(1)} %broadcast_multiply_fusion, ...), kind=kLoop, calls=%fused_computation.55 | loop fusion | flops 5767168 | bytes 8396800 | tf_op jit(solution)/shard_map/convert.7
  125.4 1.0 fusion
  127.0 0.6 fusion.54
  127.9 1.0 copy.94
  (61 shorter events, 7.1 us)
Async XLA Ops:
  0.6 2.6 %copy-start = (bf16[128,512]{1,0:T(8,128)(2,1)S(1)}, bf16[128,512]{1,0:T(8,128)(2,1)}, u32[]{:S(2)}) copy-start(bf16[128,512]{1,0:T(8,128)(2,1)} %param.14) | copy-start | bytes 393220
  4.7 1.9 %copy-start.1 = (f32[512,16,128]{0,2,1:T(8,128)}, f32[512,16,128]{0,2,1:T(8,128)S(1)}, u32[]{:S(2)}) copy-start(f32[512,16,128]{0,2,1:T(8,128)S(1)} %convolution_bitcast_fusion) | copy-start | bytes 12582916
  45.1 20.2 %copy-start.8 = (bf16[128,128]{1,0:T(8,128)(2,1)S(1)}, bf16[128,128]{1,0:T(8,128)(2,1)}, u32[]{:S(2)}) copy-start(bf16[128,128]{1,0:T(8,128)(2,1)} %param.18) | copy-start | bytes 98308
  45.1 20.2 %copy-start.11 = (f32[128]{0:T(128)S(1)}, f32[128]{0:T(128)}, u32[]{:S(2)}) copy-start(f32[128]{0:T(128)} %param.16) | copy-start | bytes 1540
  45.1 20.2 %copy-start.12 = (f32[128]{0:T(128)S(1)}, f32[128]{0:T(128)}, u32[]{:S(2)}) copy-start(f32[128]{0:T(128)} %param.17) | copy-start | bytes 1540
  45.6 20.1 %copy-start.9 = (bf16[128,128]{1,0:T(8,128)(2,1)S(1)}, bf16[128,128]{1,0:T(8,128)(2,1)}, u32[]{:S(2)}) copy-start(bf16[128,128]{1,0:T(8,128)(2,1)} %param.15) | copy-start | bytes 98308
  45.6 20.1 %copy-start.10 = (f32[128]{0:T(128)S(1)}, f32[128]{0:T(128)}, u32[]{:S(2)}) copy-start(f32[128]{0:T(128)} %param.12) | copy-start | bytes 1540
  45.6 20.1 %copy-start.13 = (f32[128]{0:T(128)S(1)}, f32[128]{0:T(128)}, u32[]{:S(2)}) copy-start(f32[128]{0:T(128)} %param.13) | copy-start | bytes 1540
  65.3 1.9 %copy-start.6 = (bf16[16,128,128]{2,1,0:T(8,128)(2,1)S(1)}, bf16[16,128,128]{2,1,0:T(8,128)(2,1)}, u32[]{:S(2)}) copy-start(bf16[16,128,128]{2,1,0:T(8,128)(2,1)} %param.19) | copy-start | bytes 1572868
  65.8 1.8 %copy-start.2 = (f32[16,128,128]{2,1,0:T(8,128)}, f32[16,128,128]{2,1,0:T(8,128)S(1)}, u32[]{:S(2)}) copy-start(f32[16,128,128]{2,1,0:T(8,128)S(1)} %fusion.35) | copy-start | bytes 3145732
  67.2 1.0 copy-start.4
  125.4 1.2 copy-start.3
  125.4 1.5 %copy-start.5 = (f32[16,128,128]{2,1,0:T(8,128)S(1)}, f32[16,128,128]{2,1,0:T(8,128)}, u32[]{:S(2)}) copy-start(f32[16,128,128]{2,1,0:T(8,128)} %copy-done.4) | copy-start | bytes 3145732
  125.4 1.7 %copy-start.7 = (bf16[16,128,128]{2,1,0:T(8,128)(2,1)S(1)}, bf16[16,128,128]{2,1,0:T(8,128)(2,1)}, u32[]{:S(2)}) copy-start(bf16[16,128,128]{2,1,0:T(8,128)(2,1)} %param.19) | copy-start | bytes 1572868

commit v2 on v1

v2 whole, which is shorter than its diff:
```python
import jax
import jax.numpy as jnp
from jax import lax
from jax.experimental import pallas as pl
from jax.experimental.pallas import tpu as pltpu
from jax.sharding import PartitionSpec as P

EPS = 1e-05
F32 = jnp.float32
BF16 = jnp.bfloat16
MIB = 1 << 20


def dot(a, b, over=((1,), (0,))):
    return lax.dot_general(a, b, (over, ((), ())), preferred_element_type=F32)


def eye(size):
    down = lax.broadcasted_iota(jnp.int32, (size, size), 0)
    across = lax.broadcasted_iota(jnp.int32, (size, size), 1)
    return (down == across).astype(BF16)


def turned(values):
    return dot(eye(values.shape[1]), values, ((1,), (1,)))


def down_lanes(vector, lanes):
    return jnp.broadcast_to(vector[None, :], (lanes, vector.shape[0])).T


def turned_weight(weight):
    c, m = weight.shape
    return jnp.concatenate(
        [turned(weight[:, at : at + c]) for at in range(0, m, c)], axis=0
    ).astype(BF16)


def normalized(values):
    mean = jnp.mean(values, axis=0, keepdims=True)
    centred = values - mean
    var = jnp.mean(centred * centred, axis=0, keepdims=True)
    inverse = lax.rsqrt(var + EPS)
    return centred * inverse, inverse


def masks_of(mask_s, mask_v, rows, cols):
    first_row = lax.axis_index("row") * rows
    first_col = pl.multiple_of(lax.axis_index("col") * cols, cols)
    col_mask = mask_v[:, pl.ds(first_col, cols)].astype(F32)
    return first_row, col_mask


def front_kernel(pair, mask_s, mask_v, gain, bias, proj_weight, out, gain_b, bias_b, left, right):
    rows, cols, width = pair.shape
    n_dev, share2 = out.shape[0], out.shape[1]
    share = share2 // 2
    hidden = n_dev * share
    first_row, col_mask = masks_of(mask_s, mask_v, rows, cols)
    gain_b[...] = down_lanes(gain[...], cols)
    bias_b[...] = down_lanes(bias[...], cols)
    weight = turned_weight(proj_weight[...])

    def row(i, carry):
        zhat, _ = normalized(turned(pair[i]))
        zbar = (zhat * gain_b[...] + bias_b[...]).astype(BF16)
        proj = dot(weight, zbar)
        pm = col_mask * mask_s[first_row + i].astype(F32)
        pa, qa = proj[:hidden], proj[hidden : 2 * hidden]
        pb, qb = proj[2 * hidden : 3 * hidden], proj[3 * hidden :]
        left[pl.ds(i, hidden, stride=rows), :] = jax.nn.sigmoid(pa) * qa * pm
        right[pl.ds(i, hidden, stride=rows), :] = jax.nn.sigmoid(pb) * qb * pm
        return carry

    lax.fori_loop(0, rows, row, 0, unroll=2)
    shape = (n_dev, share, rows, cols)
    out[:, :share] = left[...].reshape(shape).astype(BF16)
    out[:, share:] = right[...].reshape(shape).astype(BF16)


def side_kernel(
    pair, cot, mask_s, mask_v, gain, bias, proj_weight, gate_weight, norm_gain, out_weight,
    coef, zhat_out, inv_out, gate_out, dxh_out, gain_b, bias_b, norm_gain_b,
):
    rows, cols, width = pair.shape
    hidden = out_weight.shape[0]
    first_row, col_mask = masks_of(mask_s, mask_v, rows, cols)
    gain_b[...] = down_lanes(gain[...], cols)
    bias_b[...] = down_lanes(bias[...], cols)
    norm_gain_b[...] = down_lanes(norm_gain[...], cols)
    weight = turned_weight(proj_weight[...])
    gate_t = turned_weight(gate_weight[...])

    def row(i, carry):
        zhat, inverse = normalized(turned(pair[i]))
        zhat_out[i] = zhat
        inv_out[pl.ds(i, 1), :] = inverse
        zbar = (zhat * gain_b[...] + bias_b[...]).astype(BF16)
        proj = dot(weight, zbar)
        pm = col_mask * mask_s[first_row + i].astype(F32)
        pa, qa = proj[:hidden], proj[hidden : 2 * hidden]
        pb, qb = proj[2 * hidden : 3 * hidden], proj[3 * hidden :]
        sa, sb = jax.nn.sigmoid(pa), jax.nn.sigmoid(pb)
        coef[i, :hidden] = pm * qa * sa * (1.0 - sa)
        coef[i, hidden : 2 * hidden] = pm * sa
        coef[i, 2 * hidden : 3 * hidden] = pm * qb * sb * (1.0 - sb)
        coef[i, 3 * hidden :] = pm * sb
        gate = jax.nn.sigmoid(dot(turned(zbar).astype(BF16), gate_t, ((1,), (1,))))
        gate_out[i] = gate
        du = (cot[i].astype(F32) * gate).astype(BF16)
        dy = dot(out_weight[...], du, ((1,), (1,)))
        dxh_out[pl.ds(i, hidden, stride=rows), :] = dy * norm_gain_b[...]
        return carry

    lax.fori_loop(0, rows, row, 0)


def channel_matrix(ref, at):
    n_row, n_col, _, rows, cols = ref.shape
    return jnp.concatenate(
        [ref[:, c, at].reshape(n_row * rows, cols) for c in range(n_col)], axis=1
    )


def put_channel(ref, at, values):
    n_row, n_col, _, rows, cols = ref.shape
    values = values.astype(BF16)
    for c in range(n_col):
        ref[:, c, at] = values[:, c * cols : (c + 1) * cols].reshape(n_row, rows, cols)


def product_kernel(both, out):
    share = out.shape[2]
    for h in range(share):
        put_channel(
            out, h,
            dot(channel_matrix(both, h), channel_matrix(both, share + h), ((1,), (1,))),
        )


def middle_kernel(product, dxh, out, xhat):
    hidden = product.shape[0]
    values = product[...].astype(F32)
    mean = jnp.sum(values, axis=0) * (1.0 / hidden)
    centred = values - mean[None]
    var = jnp.sum(centred * centred, axis=0) * (1.0 / hidden)
    inverse = lax.rsqrt(var + EPS)
    xhat[...] = centred * inverse[None]
    m1 = jnp.sum(dxh[...], axis=0) * (1.0 / hidden)
    m2 = jnp.sum(dxh[...] * xhat[...], axis=0) * (1.0 / hidden)
    out[...] = ((dxh[...] - m1[None] - xhat[...] * m2[None]) * inverse[None]).astype(BF16)


def update_kernel(
    product, gate, cot, norm_gain, norm_bias, out_weight, gate_weight,
    update, dzg, spread, norm_gain_b, norm_bias_b,
):
    hidden, rows, cols = product.shape
    norm_gain_b[...] = down_lanes(norm_gain[...], cols)
    norm_bias_b[...] = down_lanes(norm_bias[...], cols)
    spread[...] = product[...].astype(F32).reshape(hidden * rows, cols)

    def row(i, carry):
        xhat, _ = normalized(spread[pl.ds(i, hidden, stride=rows), :])
        ybar = (xhat * norm_gain_b[...] + norm_bias_b[...]).astype(BF16)
        u = dot(turned(ybar).astype(BF16), out_weight[...])
        g = gate[i]
        update[i] = (g * u).astype(BF16)
        dgp = (cot[i].astype(F32) * u * g * (1.0 - g)).astype(BF16)
        dzg[i] = dot(gate_weight[...], dgp, ((1,), (1,)))
        return carry

    lax.fori_loop(0, rows, row, 0)


def grads_kernel(both, grad, out):
    share = grad.shape[2]
    for h in range(share):
        g = channel_matrix(grad, h)
        put_channel(out, h, dot(g, channel_matrix(both, share + h)))
        put_channel(out, share + h, dot(g, channel_matrix(both, h), ((0,), (0,))))


def back_kernel(grads, coef, zhat, inv, dzg, gain, proj_weight, out, gain_b, left, right):
    rows, cols, width = out.shape
    n_dev, share2 = grads.shape[0], grads.shape[1]
    share = share2 // 2
    hidden = n_dev * share
    gain_b[...] = down_lanes(gain[...], cols)
    left[...] = grads[:, :share].astype(F32).reshape(hidden * rows, cols)
    right[...] = grads[:, share:].astype(F32).reshape(hidden * rows, cols)

    def row(i, carry):
        gl = left[pl.ds(i, hidden, stride=rows), :]
        gr = right[pl.ds(i, hidden, stride=rows), :]
        dproj = jnp.concatenate(
            [
                (gl * coef[i, :hidden]).astype(BF16),
                (gl * coef[i, hidden : 2 * hidden]).astype(BF16),
                (gr * coef[i, 2 * hidden : 3 * hidden]).astype(BF16),
                (gr * coef[i, 3 * hidden :]).astype(BF16),
            ],
            axis=0,
        )
        dzh = (dot(proj_weight[...], dproj) + dzg[i]) * gain_b[...]
        z = zhat[i]
        m1 = jnp.mean(dzh, axis=0, keepdims=True)
        m2 = jnp.mean(dzh * z, axis=0, keepdims=True)
        grad = ((dzh - m1 - z * m2) * inv[pl.ds(i, 1), :]).astype(BF16)
        out[i] = turned(grad).astype(BF16)
        return carry

    lax.fori_loop(0, rows, row, 0, unroll=2)


VMEM = pl.BlockSpec(memory_space=pltpu.VMEM)
SMEM = pl.BlockSpec(memory_space=pltpu.SMEM)


def call(kernel, outs, scratch, args, smem=(), flops=0, moved=0, limit=32):
    return pl.pallas_call(
        kernel,
        out_shape=outs,
        in_specs=[SMEM if at in smem else VMEM for at in range(len(args))],
        out_specs=jax.tree.map(lambda _: VMEM, outs),
        scratch_shapes=[pltpu.VMEM(shape, dtype) for shape, dtype in scratch],
        compiler_params=pltpu.CompilerParams(vmem_limit_bytes=limit * MIB),
        cost_estimate=pl.CostEstimate(flops=flops, bytes_accessed=moved, transcendentals=0),
    )(*args)


def body(
    pair, mask, gain_in, bias_in, proj_weight, gate_weight,
    product_norm_gain, product_norm_bias, out_weight, cotangent,
):
    rows, cols, width = pair.shape
    hidden = out_weight.shape[0]
    n_row = lax.axis_size("row")
    n_col = lax.axis_size("col")
    n_dev = n_row * n_col
    share = hidden // n_dev
    cells = rows * cols
    mask_v = mask.reshape(1, -1)

    def shape(*dims, dtype=BF16):
        return jax.ShapeDtypeStruct(dims, dtype)

    def exchange(values):
        return lax.all_to_all(values, ("row", "col"), split_axis=0, concat_axis=0, tiled=True)

    square = ((width, cols), F32)
    plane = ((hidden * rows, cols), F32)
    send = call(
        front_kernel,
        shape(n_dev, 2 * share, rows, cols),
        [square, square, plane, plane],
        (pair, mask, mask_v, gain_in, bias_in, proj_weight),
        smem=(1,),
        flops=2 * cells * width * 5 * hidden,
        moved=6 * cells * width,
    )
    both = exchange(send).reshape(n_row, n_col, 2 * share, rows, cols)
    coef, zhat, inv, gate, dxh = call(
        side_kernel,
        (
            shape(rows, 4 * hidden, cols, dtype=F32),
            shape(rows, width, cols, dtype=F32),
            shape(rows, cols, dtype=F32),
            shape(rows, cols, width, dtype=F32),
            shape(hidden * rows, cols, dtype=F32),
        ),
        [square, square, square],
        (
            pair, cotangent, mask, mask_v, gain_in, bias_in, proj_weight, gate_weight,
            product_norm_gain, out_weight,
        ),
        smem=(2,),
        flops=2 * cells * width * 8 * hidden,
        moved=32 * cells * width,
    )
    product = call(
        product_kernel,
        shape(n_row, n_col, share, rows, cols),
        [],
        (both,),
        flops=2 * share * (n_row * rows) ** 3,
        moved=6 * cells * hidden,
    )
    product = exchange(product.reshape(n_dev, share, rows, cols)).reshape(hidden, rows, cols)
    grad = call(
        middle_kernel,
        shape(hidden, rows, cols),
        [((hidden, rows, cols), F32)],
        (product, dxh.reshape(hidden, rows, cols)),
        flops=20 * cells * hidden,
        moved=8 * cells * hidden,
    )
    grad = exchange(grad.reshape(n_dev, share, rows, cols))
    update, dzg = call(
        update_kernel,
        (shape(rows, cols, width), shape(rows, width, cols, dtype=F32)),
        [plane, square, square],
        (
            product, gate, cotangent, product_norm_gain, product_norm_bias, out_weight,
            gate_weight,
        ),
        flops=2 * cells * width * 3 * hidden,
        moved=14 * cells * hidden,
    )
    grads = call(
        grads_kernel,
        shape(n_row, n_col, 2 * share, rows, cols),
        [],
        (both, grad.reshape(n_row, n_col, share, rows, cols)),
        flops=4 * share * (n_row * rows) ** 3,
        moved=10 * cells * hidden,
    )
    grads = exchange(grads.reshape(n_dev, 2 * share, rows, cols))
    grad_pair = call(
        back_kernel,
        shape(rows, cols, width),
        [square, plane, plane],
        (grads, coef, zhat, inv, dzg, gain_in, proj_weight),
        flops=2 * cells * width * 5 * hidden,
        moved=30 * cells * width,
    )
    return (update, grad_pair)


def solution(mesh):
    placed = (
        P(("grp", "row"), "col", None),
        P("grp"),
        P(),
        P(),
        P(),
        P(),
        P(),
        P(),
        P(),
        P(("grp", "row"), "col", None),
    )
    return jax.shard_map(
        body,
        mesh=mesh,
        in_specs=placed,
        out_specs=(P(("grp", "row"), "col", None), P(("grp", "row"), "col", None)),
        check_vma=False,
    )
```

time: 129 us -> 128 us (level)
  blocking collectives: 99.9 us -> 54 us
  Pallas kernels: 0 us -> 34.7 us
  waiting for transfers between devices: 0 us -> 14 us
  starting transfers between devices: 0 us -> 7.25 us
  other arithmetic: 6.94 us -> 0 us
  matrix products: 6.25 us -> 0 us
  local copies, waits for them, and re-layouts: 14.8 us -> 16.9 us
    all_to_all x4 -> x2, blocking collectives: 99.9 us -> 54 us  [exchange(): lax.all_to_all(values, ('row', 'col'), split_axis=0, concat_axis=0, tiled...]
    pallas_call x0 -> x7, Pallas kernels: none -> 34.7 us  [call(): pl.pallas_call(kernel, out_shape=outs, in_specs=[SMEM if at in smem else...]
    all_to_all x0 -> x2, waiting for transfers between devices: none -> 14 us  [exchange(): lax.all_to_all(values, ('row', 'col'), split_axis=0, concat_axis=0, tiled...]
    unnamed x30 -> x48, local copies, waits for them, and re-layouts: 5.5 us -> 16.9 us
    all_to_all x0 -> x2, starting transfers between devices: none -> 7.25 us  [exchange(): lax.all_to_all(values, ('row', 'col'), split_axis=0, concat_axis=0, tiled...]
    dot_general x9 -> x0, matrix products: 6.25 us -> none  [the longest x1 1.5 us: body(): jnp.einsum('ikc,ch->hik', zbar, proj_weight, preferred_element_type=jnp.f...]
    convert_element_type x6 -> x0, local copies, waits for them, and re-layouts: 3.88 us -> none  [the longest x1 1.58 us: body(): gr_f = gr_tile.astype(jnp.float32) * pair_mask]
    convert_element_type x6 -> x0, other arithmetic: 3.19 us -> none  [the longest x1 1.11 us: body(): gr_f = gr_tile.astype(jnp.float32) * pair_mask]
  transfers between devices with their start and end apart: 0 -> 2, of which waited for: 0 -> 1; matrix products, arithmetic and copies ran while one was open for 0% -> 0% of each run, Pallas kernels for 0% -> 16%
where the time goes in v2:
time: 128 us
  blocking collectives  54 us (42%)
  Pallas kernels  34.7 us (27%)
  local copies, waits for them, and re-layouts  16.9 us (13%)
  waiting for transfers between devices  14 us (11%)
  starting transfers between devices  7.25 us (6%)
    all_to_all x2, blocking collectives, exchange(): lax.all_to_all(values, ('row', 'col'), split_axis=0, concat_axis=0, tiled...  54 us
    pallas_call x7, Pallas kernels, call(): pl.pallas_call(kernel, out_shape=outs, in_specs=[SMEM if at in smem else...  34.7 us
    unnamed x48, local copies, waits for them, and re-layouts  16.9 us
    all_to_all x2, waiting for transfers between devices, exchange(): lax.all_to_all(values, ('row', 'col'), split_axis=0, concat_axis=0, tiled...  14 us
    all_to_all x2, starting transfers between devices, exchange(): lax.all_to_all(values, ('row', 'col'), split_axis=0, concat_axis=0, tiled...  7.25 us
  transfers between devices with their start and end apart: 2, of which 1 were waited for; matrix products, arithmetic and copies ran while one was open for 0% of the time, Pallas kernels for 16%

profile of v2, /device:TPU:0, one launch (start us, length us, event | category | flops | bytes accessed | tf_op | source)
XLA Modules:
  0.0 127.6 jit_solution(13300971438461869927)
XLA Ops:
  0.7 0.9 copy-done.8
  1.6 1.0 copy-done.10
  4.6 4.8 %shard_map.113 = bf16[32,8,16,128]{3,2,1,0:T(8,128)(2,1)S(1)} custom-call(bf16[16,128,128]{2,1,0:T(8,128)(2,1)S(1)} %copy-done.10, s32[256]{0:T(256)S(1)} %copy-done.16, s32[1,256]{1,0:T(1,128)S(1)} %bitcast.15, f32[128]{0:T(128)S(1)} %copy-done.18, f32[128]{0:T(128)S(1)} %copy-done.20, bf16[128,512]{1,0:T(8,128)(2,1)S(1)} %copy-done.8), custom_call_target="tpu_custom_call" | custom-call | flops 335544320 | bytes 1572864 | tf_op jit(solution)/shard_map/pallas_call | solution.py:221
  9.4 33.3 %all_to_all.20 = bf16[32,8,16,128]{3,2,1,0:T(8,128)(2,1)S(1)} all-to-all(bf16[32,8,16,128]{3,2,1,0:T(8,128)(2,1)S(1)} %shard_map.113), channel_id=1, replica_groups=mesh['grp'=1,'row'=16,'col'=2] {'row','col'}, dimensions={0} | all-to-all | bytes 2097152 | tf_op jit(solution)/shard_map/all_to_all | solution.py:249
  42.8 1.1 shard_map.114
  43.9 3.6 %all-to-all-start.1 = ((bf16[32,4,16,128]{3,2,1,0:T(8,128)(2,1)}), bf16[32,4,16,128]{3,2,1,0:T(8,128)(2,1)S(1)}, u32[]{:S(2)}, u32[]{:S(2)}) async-start(bf16[32,4,16,128]{3,2,1,0:T(8,128)(2,1)} %bitcast.2), calls=%async_computation.1 | async-start | bytes 1048576 | tf_op jit(solution)/shard_map/all_to_all | solution.py:249
  47.6 1.0 copy-done.12
  48.7 11.6 %shard_map.115 = (f32[16,512,128]{2,1,0:T(8,128)S(1)}, f32[16,128,128]{2,1,0:T(8,128)S(1)}, f32[16,128]{1,0:T(8,128)S(1)}, f32[16,128,128]{2,1,0:T(8,128)S(1)}, f32[2048,128]{1,0:T(8,128)S(1)}) custom-call(bf16[16,128,128]{2,1,0:T(8,128)(2,1)S(1)} %copy-done.11, bf16[16,128,128]{2,1,0:T(8,128)(2,1)S(1)} %copy-done.12, s32[256]{0:T(256)S(1)} %copy-done.17, ...), custom_call_target="tpu_custom_call" | custom-call | flops 536870912 | bytes 8388608 | tf_op jit(solution)/shard_map/pallas_call | solution.py:221
  60.2 2.0 %copy-done = f32[16,512,128]{2,1,0:T(8,128)} copy-done((f32[16,512,128]{2,1,0:T(8,128)}, f32[16,512,128]{2,1,0:T(8,128)S(1)}, u32[]{:S(2)}) %copy-start) | copy-done | bytes 4194328
  62.2 1.0 copy-done.4
  63.2 1.0 copy-done.6
  64.2 1.2 copy-done.5
  65.4 0.7 shard_map.117
  66.1 20.6 %all_to_all.21 = bf16[32,4,16,128]{3,2,1,0:T(8,128)(2,1)S(1)} all-to-all(bf16[32,4,16,128]{3,2,1,0:T(8,128)(2,1)S(1)} %bitcast.13), channel_id=1, replica_groups=mesh['grp'=1,'row'=16,'col'=2] {'row','col'}, dimensions={0} | all-to-all | bytes 1048576 | tf_op jit(solution)/shard_map/all_to_all | solution.py:249
  86.8 1.5 %shard_map.118 = bf16[16,2,8,16,128]{4,3,2,1,0:T(8,128)(2,1)} custom-call(bf16[16,2,8,16,128]{4,3,2,1,0:T(8,128)(2,1)S(1)} %bitcast.9, bf16[16,2,4,16,128]{4,3,2,1,0:T(8,128)(2,1)S(1)} %bitcast.12), custom_call_target="tpu_custom_call" | custom-call | flops 268435456 | bytes 2621440 | tf_op jit(solution)/shard_map/pallas_call | solution.py:221
  88.2 3.6 %all-to-all-start.3 = ((bf16[32,8,16,128]{3,2,1,0:T(8,128)(2,1)}), bf16[32,8,16,128]{3,2,1,0:T(8,128)(2,1)S(1)}, u32[]{:S(2)}, u32[]{:S(2)}) async-start(bf16[32,8,16,128]{3,2,1,0:T(8,128)(2,1)} %bitcast.7), calls=%async_computation.3 | async-start | bytes 2097152 | tf_op jit(solution)/shard_map/all_to_all | solution.py:249
  91.9 1.2 copy-done.7
  93.1 1.0 copy-done.13
  94.1 8.9 %shard_map.116 = (bf16[16,128,128]{2,1,0:T(8,128)(2,1)}, f32[16,128,128]{2,1,0:T(8,128)S(1)}) custom-call(bf16[128,16,128]{2,1,0:T(8,128)(2,1)S(1)} %bitcast.11, f32[16,128,128]{2,1,0:T(8,128)S(1)} %copy-done.7, bf16[16,128,128]{2,1,0:T(8,128)(2,1)S(1)} %copy-done.13, f32[128]{0:T(128)S(1)} %copy-done.22, f32[128]{0:T(128)S(1)} %copy-done.23, ...), custom_call_target="tpu_custom_call" | custom-call | flops 201326592 | bytes 3670016 | tf_op jit(solution)/shard_map/pallas_call | solution.py:221
  103.1 1.0 copy-done.2
  104.1 14.0 %all-to-all-done.3.grads = bf16[32,8,16,128]{3,2,1,0:T(8,128)(2,1)S(1)} async-done(((bf16[32,8,16,128]{3,2,1,0:T(8,128)(2,1)}), bf16[32,8,16,128]{3,2,1,0:T(8,128)(2,1)S(1)}, u32[]{:S(2)}, u32[]{:S(2)}) %all-to-all-start.3) | async-done | bytes 1048608 | tf_op jit(solution)/shard_map/all_to_all | solution.py:249
  118.1 2.2 %copy-done.1 = f32[16,512,128]{2,1,0:T(8,128)S(1)} copy-done((f32[16,512,128]{2,1,0:T(8,128)S(1)}, f32[16,512,128]{2,1,0:T(8,128)}, u32[]{:S(2)}) %copy-start.1) | copy-done | bytes 4194328
  120.3 1.2 copy-done.3
  121.5 6.1 %shard_map.119 = bf16[16,128,128]{2,1,0:T(8,128)(2,1)} custom-call(bf16[32,8,16,128]{3,2,1,0:T(8,128)(2,1)S(1)} %all-to-all-done.3.grads, f32[16,512,128]{2,1,0:T(8,128)S(1)} %copy-done.1, f32[16,128,128]{2,1,0:T(8,128)S(1)} %get-tuple-element.13.zhat, f32[16,128]{1,0:T(8,128)S(1)} %get-tuple-element.14.inv, f32[16,128,128]{2,1,0:T(8,128)S(1)} %copy-done.3, ...), custom_call_target="tpu_custom_call" | custom-call | flops 335544320 | bytes 7864320 | tf_op jit(solution)/shard_map/pallas_call | solution.py:221
  (37 shorter events, 2.0 us)
Async XLA Ops:
  0.6 46.9 %copy-start.17 = (s32[256]{0:T(256)S(1)}, s32[256]{0:T(256)}, u32[]{:S(2)}) copy-start(s32[256]{0:T(256)} %mask_s.3) | copy-start | bytes 3076
  0.6 46.9 %copy-start.19 = (f32[128]{0:T(128)S(1)}, f32[128]{0:T(128)}, u32[]{:S(2)}) copy-start(f32[128]{0:T(128)} %gain.5) | copy-start | bytes 1540
  0.7 0.9 copy-start.8
  1.6 1.0 copy-start.10
  2.6 0.7 copy-start.16
  4.6 42.9 %copy-start.9 = (bf16[128,512]{1,0:T(8,128)(2,1)S(1)}, bf16[128,512]{1,0:T(8,128)(2,1)}, u32[]{:S(2)}) copy-start(bf16[128,512]{1,0:T(8,128)(2,1)} %proj_weight.5) | copy-start | bytes 393220
  4.6 43.0 %copy-start.11 = (bf16[16,128,128]{2,1,0:T(8,128)(2,1)S(1)}, bf16[16,128,128]{2,1,0:T(8,128)(2,1)}, u32[]{:S(2)}) copy-start(bf16[16,128,128]{2,1,0:T(8,128)(2,1)} %pair.3) | copy-start | bytes 1572868
  4.6 43.0 %copy-start.14 = (bf16[128,128]{1,0:T(8,128)(2,1)S(1)}, bf16[128,128]{1,0:T(8,128)(2,1)}, u32[]{:S(2)}) copy-start(bf16[128,128]{1,0:T(8,128)(2,1)} %gate_weight.3) | copy-start | bytes 98308
  4.6 43.0 %copy-start.15 = (bf16[128,128]{1,0:T(8,128)(2,1)S(1)}, bf16[128,128]{1,0:T(8,128)(2,1)}, u32[]{:S(2)}) copy-start(bf16[128,128]{1,0:T(8,128)(2,1)} %out_weight.3) | copy-start | bytes 98308
  4.6 43.0 %copy-start.21 = (f32[128]{0:T(128)S(1)}, f32[128]{0:T(128)}, u32[]{:S(2)}) copy-start(f32[128]{0:T(128)} %bias.3) | copy-start | bytes 1540
  4.6 43.0 %copy-start.22 = (f32[128]{0:T(128)S(1)}, f32[128]{0:T(128)}, u32[]{:S(2)}) copy-start(f32[128]{0:T(128)} %norm_gain.3) | copy-start | bytes 1540
  43.9 20.3 %all-to-all-start.1 = ((bf16[32,4,16,128]{3,2,1,0:T(8,128)(2,1)}), bf16[32,4,16,128]{3,2,1,0:T(8,128)(2,1)S(1)}, u32[]{:S(2)}, u32[]{:S(2)}) async-start(bf16[32,4,16,128]{3,2,1,0:T(8,128)(2,1)} %bitcast.2), calls=%async_computation.1 | async-start | bytes 1048576 | tf_op jit(solution)/shard_map/all_to_all | solution.py:249
  47.6 1.0 copy-start.12
  60.2 2.0 %copy-start = (f32[16,512,128]{2,1,0:T(8,128)}, f32[16,512,128]{2,1,0:T(8,128)S(1)}, u32[]{:S(2)}) copy-start(f32[16,512,128]{2,1,0:T(8,128)S(1)} %get-tuple-element.12.coef) | copy-start | bytes 12582916
  62.2 1.0 copy-start.4
  63.2 1.0 copy-start.6
  64.2 27.7 %copy-start.23 = (f32[128]{0:T(128)S(1)}, f32[128]{0:T(128)}, u32[]{:S(2)}) copy-start(f32[128]{0:T(128)} %norm_bias.1) | copy-start | bytes 1540
  64.2 1.2 copy-start.5
  88.2 29.9 %all-to-all-start.3 = ((bf16[32,8,16,128]{3,2,1,0:T(8,128)(2,1)}), bf16[32,8,16,128]{3,2,1,0:T(8,128)(2,1)S(1)}, u32[]{:S(2)}, u32[]{:S(2)}) async-start(bf16[32,8,16,128]{3,2,1,0:T(8,128)(2,1)} %bitcast.7), calls=%async_computation.3 | async-start | bytes 2097152 | tf_op jit(solution)/shard_map/all_to_all | solution.py:249
  91.9 1.2 copy-start.7
  93.1 1.0 copy-start.13
  103.1 1.0 copy-start.2
  118.1 2.2 %copy-start.1 = (f32[16,512,128]{2,1,0:T(8,128)S(1)}, f32[16,512,128]{2,1,0:T(8,128)}, u32[]{:S(2)}) copy-start(f32[16,512,128]{2,1,0:T(8,128)} %copy-done) | copy-start | bytes 12582916
  120.3 1.2 copy-start.3
  (2 other events, 1.3 us)

commit v3 on v2

v3 whole, which is shorter than its diff:
```python
import math

import jax
import jax.numpy as jnp
from jax import lax
from jax.experimental import pallas as pl
from jax.experimental.pallas import tpu as pltpu
from jax.sharding import PartitionSpec as P

EPS = 1e-05
F32 = jnp.float32
BF16 = jnp.bfloat16
MIB = 1 << 20


def dot(a, b, over=((1,), (0,))):
    return lax.dot_general(a, b, (over, ((), ())), preferred_element_type=F32)


def eye(size):
    down = lax.broadcasted_iota(jnp.int32, (size, size), 0)
    across = lax.broadcasted_iota(jnp.int32, (size, size), 1)
    return (down == across).astype(F32).astype(BF16)


def turned(values):
    return dot(eye(values.shape[1]), values, ((1,), (1,)))


def down_lanes(vector, lanes):
    return jnp.broadcast_to(vector, (lanes, vector.shape[1])).T


def turned_weight(weight):
    c, m = weight.shape
    return jnp.concatenate(
        [turned(weight[:, at : at + c]) for at in range(0, m, c)], axis=0
    ).astype(BF16)


def sigmoid(values):
    return 0.5 + 0.5 * jnp.tanh(0.5 * values)


def normalized(values):
    mean = jnp.mean(values, axis=0, keepdims=True)
    centred = values - mean
    var = jnp.mean(centred * centred, axis=0, keepdims=True)
    inverse = lax.rsqrt(var + EPS)
    return centred * inverse, inverse


def start(sems, copies):
    running = [
        pltpu.make_async_copy(source, target, sems.at[at])
        for at, (source, target) in enumerate(copies)
    ]
    for copy in running:
        copy.start()
    return running


def wait(copies):
    for copy in copies:
        copy.wait()


def groups_of(rows):
    size = math.gcd(rows, 4)
    return [(at, size) for at in range(0, rows, size)]


def side_by_side(ref, at, size):
    return jnp.concatenate([ref[at + r] for r in range(size)], axis=1)


def pair_mask(mask_s, mask_v, at, size, rows, cols):
    first_row = lax.axis_index("row") * rows + at
    first_col = pl.multiple_of(lax.axis_index("col") * cols, cols)
    col_mask = mask_v[:, pl.ds(first_col, cols)].astype(F32)
    return jnp.concatenate(
        [col_mask * mask_s[first_row + r].astype(F32) for r in range(size)], axis=1
    )


def front_kernel(
    pair_h, mask_h, mask_row_h, gain_h, bias_h, proj_h, out,
    pair, mask_s, mask_v, gain, bias, proj_weight, left, right, sems, row_sems,
):
    rows, cols, width = pair.shape
    n_dev, share2 = out.shape[0], out.shape[1]
    share = share2 // 2
    hidden = n_dev * share
    groups = groups_of(rows)
    small = start(
        sems,
        [(gain_h, gain), (bias_h, bias), (proj_h, proj_weight), (mask_h, mask_s), (mask_row_h, mask_v)],
    )
    blocks = start(
        row_sems,
        [(pair_h.at[pl.ds(at, size)], pair.at[pl.ds(at, size)]) for at, size in groups],
    )
    wait(small)
    gain_b = jnp.concatenate([down_lanes(gain[...], cols)] * groups[0][1], axis=1)
    bias_b = jnp.concatenate([down_lanes(bias[...], cols)] * groups[0][1], axis=1)
    weight = turned_weight(proj_weight[...])
    for (at, size), block in zip(groups, blocks):
        block.wait()
        zhat, _ = normalized(turned(pair[at : at + size].reshape(size * cols, width)))
        zbar = (zhat * gain_b + bias_b).astype(BF16)
        pm = pair_mask(mask_s, mask_v, at, size, rows, cols)
        for part, target in ((0, left), (2, right)):
            p = dot(weight[part * hidden : (part + 1) * hidden], zbar)
            q = dot(weight[(part + 1) * hidden : (part + 2) * hidden], zbar)
            values = sigmoid(p) * q * pm
            for r in range(size):
                target[pl.ds(at + r, hidden, stride=rows), :] = values[:, r * cols : (r + 1) * cols]
    shape = (n_dev, share, rows, cols)
    out[:, :share] = left[...].reshape(shape).astype(BF16)
    out[:, share:] = right[...].reshape(shape).astype(BF16)


def side_kernel(
    pair_h, cot_h, mask_h, mask_row_h, gain_h, bias_h, proj_h, gate_h, norm_gain_h, out_w_h,
    coef_h, zhat_h, inv_h, gate_out_h, dxh_h,
    pair, cot, mask_s, mask_v, gain, bias, proj_weight, gate_weight, norm_gain, out_weight,
    coef, zhat_out, inv_out, gate_out, dxh_out, in_sems, out_sems,
):
    rows, cols, width = pair.shape
    hidden = out_weight.shape[0]
    wait(
        start(
            in_sems,
            [
                (pair_h, pair), (cot_h, cot), (mask_h, mask_s), (mask_row_h, mask_v),
                (gain_h, gain), (bias_h, bias), (proj_h, proj_weight), (gate_h, gate_weight),
                (norm_gain_h, norm_gain), (out_w_h, out_weight),
            ],
        )
    )
    groups = groups_of(rows)
    gain_b = jnp.concatenate([down_lanes(gain[...], cols)] * groups[0][1], axis=1)
    bias_b = jnp.concatenate([down_lanes(bias[...], cols)] * groups[0][1], axis=1)
    norm_gain_b = jnp.concatenate([down_lanes(norm_gain[...], cols)] * groups[0][1], axis=1)
    weight = turned_weight(proj_weight[...])
    gate_t = turned_weight(gate_weight[...])
    for at, size in groups:
        zhat, inverse = normalized(turned(pair[at : at + size].reshape(size * cols, width)))
        zbar = (zhat * gain_b + bias_b).astype(BF16)
        pm = pair_mask(mask_s, mask_v, at, size, rows, cols)
        gate = sigmoid(dot(gate_t, zbar))
        cot_t = turned(cot[at : at + size].reshape(size * cols, width))
        dxh = dot(out_weight[...], (cot_t * gate).astype(BF16)) * norm_gain_b
        dxh = dxh - jnp.mean(dxh, axis=0, keepdims=True)
        for r in range(size):
            lanes = slice(r * cols, (r + 1) * cols)
            zhat_out[at + r] = zhat[:, lanes]
            inv_out[at + r : at + r + 1] = inverse[:, lanes]
            gate_out[at + r] = gate[:, lanes]
            dxh_out[pl.ds(at + r, hidden, stride=rows), :] = dxh[:, lanes]
        for part in (0, 2):
            s = sigmoid(dot(weight[part * hidden : (part + 1) * hidden], zbar))
            q = dot(weight[(part + 1) * hidden : (part + 2) * hidden], zbar)
            first = pm * q * s * (1.0 - s)
            second = pm * s
            for r in range(size):
                lanes = slice(r * cols, (r + 1) * cols)
                coef[at + r, part * hidden : (part + 1) * hidden] = first[:, lanes]
                coef[at + r, (part + 1) * hidden : (part + 2) * hidden] = second[:, lanes]
    wait(
        start(
            out_sems,
            [
                (coef, coef_h), (zhat_out, zhat_h), (inv_out, inv_h), (gate_out, gate_out_h),
                (dxh_out, dxh_h),
            ],
        )
    )


def channel_matrix(ref, at):
    n_row, n_col, _, rows, cols = ref.shape
    return jnp.concatenate(
        [ref[:, c, at].reshape(n_row * rows, cols) for c in range(n_col)], axis=1
    )


def put_channel(ref, at, values):
    n_row, n_col, _, rows, cols = ref.shape
    values = values.astype(BF16)
    for c in range(n_col):
        ref[:, c, at] = values[:, c * cols : (c + 1) * cols].reshape(n_row, rows, cols)


def product_kernel(both, after, out):
    share = out.shape[2]
    for h in range(share):
        put_channel(
            out, h,
            dot(channel_matrix(both, h), channel_matrix(both, share + h), ((1,), (1,))),
        )


def middle_kernel(product, dxh_h, out, dxh, xhat, sems):
    hidden = product.shape[0]
    (copy,) = start(sems, [(dxh_h, dxh)])
    values = product[...].astype(F32)
    mean = jnp.sum(values, axis=0) * (1.0 / hidden)
    centred = values - mean[None]
    var = jnp.sum(centred * centred, axis=0) * (1.0 / hidden)
    inverse = lax.rsqrt(var + EPS)
    xhat[...] = centred * inverse[None]
    copy.wait()
    m2 = jnp.sum(dxh[...] * xhat[...], axis=0) * (1.0 / hidden)
    out[...] = ((dxh[...] - xhat[...] * m2[None]) * inverse[None]).astype(BF16)


def update_kernel(
    product, gate_h, cot_h, norm_gain_h, norm_bias_h, out_w_h, gate_w_h, update_h, dzg_h,
    gate, cot, norm_gain, norm_bias, out_weight, gate_weight, update, dzg, spread,
    in_sems, out_sems,
):
    hidden, rows, cols = product.shape
    width = cot.shape[2]
    copies = start(
        in_sems,
        [
            (gate_h, gate), (cot_h, cot), (norm_gain_h, norm_gain), (norm_bias_h, norm_bias),
            (out_w_h, out_weight), (gate_w_h, gate_weight),
        ],
    )
    spread[...] = product[...].astype(F32).reshape(hidden * rows, cols)
    wait(copies)
    groups = groups_of(rows)
    norm_gain_b = jnp.concatenate([down_lanes(norm_gain[...], cols)] * groups[0][1], axis=1)
    norm_bias_b = jnp.concatenate([down_lanes(norm_bias[...], cols)] * groups[0][1], axis=1)
    out_t = turned_weight(out_weight[...])
    for at, size in groups:
        xhat, _ = normalized(
            jnp.concatenate(
                [spread[pl.ds(at + r, hidden, stride=rows), :] for r in range(size)], axis=1
            )
        )
        ybar = (xhat * norm_gain_b + norm_bias_b).astype(BF16)
        u = dot(out_t, ybar)
        g = side_by_side(gate, at, size)
        done = (g * u).astype(BF16)
        cot_t = turned(cot[at : at + size].reshape(size * cols, width))
        back = dot(gate_weight[...], (cot_t * u * g * (1.0 - g)).astype(BF16))
        for r in range(size):
            lanes = slice(r * cols, (r + 1) * cols)
            update[at + r] = turned(done[:, lanes]).astype(BF16)
            dzg[at + r] = back[:, lanes]
    wait(start(out_sems, [(update, update_h), (dzg, dzg_h)]))


def grads_kernel(both, grad, out):
    share = grad.shape[2]
    for h in range(share):
        g = channel_matrix(grad, h)
        put_channel(out, h, dot(g, channel_matrix(both, share + h)))
        put_channel(out, share + h, dot(g, channel_matrix(both, h), ((0,), (0,))))


def back_kernel(
    grads, coef_h, zhat_h, inv_h, dzg_h, gain_h, proj_h, out_h,
    coef, zhat, inv, dzg, gain, proj_weight, out, left, right,
    sems, coef_sems, zhat_sems, dzg_sems, out_sems,
):
    rows, cols, width = out.shape
    n_dev, share2 = grads.shape[0], grads.shape[1]
    share = share2 // 2
    hidden = n_dev * share
    groups = groups_of(rows)

    def blocks_of(source, target):
        return [(source.at[pl.ds(at, size)], target.at[pl.ds(at, size)]) for at, size in groups]

    small = start(sems, [(gain_h, gain), (proj_h, proj_weight), (inv_h, inv)])
    blocks = [
        start(coef_sems, blocks_of(coef_h, coef)),
        start(zhat_sems, blocks_of(zhat_h, zhat)),
        start(dzg_sems, blocks_of(dzg_h, dzg)),
    ]
    left[...] = grads[:, :share].astype(F32).reshape(hidden * rows, cols)
    right[...] = grads[:, share:].astype(F32).reshape(hidden * rows, cols)
    wait(small)
    gain_b = jnp.concatenate([down_lanes(gain[...], cols)] * groups[0][1], axis=1)
    leaving = []
    for n, (at, size) in enumerate(groups):
        wait([copies[n] for copies in blocks])
        columns = []
        for r in range(size):
            gl = left[pl.ds(at + r, hidden, stride=rows), :]
            gr = right[pl.ds(at + r, hidden, stride=rows), :]
            columns.append(
                jnp.concatenate(
                    [
                        (g * coef[at + r, part * hidden : (part + 1) * hidden]).astype(BF16)
                        for part, g in enumerate((gl, gl, gr, gr))
                    ],
                    axis=0,
                )
            )
        dproj = jnp.concatenate(columns, axis=1)
        dzh = (dot(proj_weight[...], dproj) + side_by_side(dzg, at, size)) * gain_b
        z = side_by_side(zhat, at, size)
        inverse = jnp.concatenate([inv[at + r : at + r + 1] for r in range(size)], axis=1)
        m1 = jnp.mean(dzh, axis=0, keepdims=True)
        m2 = jnp.mean(dzh * z, axis=0, keepdims=True)
        grad = ((dzh - m1 - z * m2) * inverse).astype(BF16)
        for r in range(size):
            out[at + r] = turned(grad[:, r * cols : (r + 1) * cols]).astype(BF16)
        copy = pltpu.make_async_copy(
            out.at[pl.ds(at, size)], out_h.at[pl.ds(at, size)], out_sems.at[n]
        )
        copy.start()
        leaving.append(copy)
    wait(leaving)


def call(kernel, outs, scratch, args, near=(), outs_near=False, flops=0, moved=0, limit=24):
    here = pl.BlockSpec(memory_space=pltpu.VMEM)
    far = pl.BlockSpec(memory_space=pltpu.HBM)
    return pl.pallas_call(
        kernel,
        out_shape=outs if outs_near else jax.tree.map(lambda out: pltpu.HBM(out.shape, out.dtype), outs),
        in_specs=[here if at in near else far for at in range(len(args))],
        out_specs=jax.tree.map(lambda _: here if outs_near else far, outs),
        scratch_shapes=scratch,
        compiler_params=pltpu.CompilerParams(vmem_limit_bytes=limit * MIB),
        cost_estimate=pl.CostEstimate(flops=flops, bytes_accessed=moved, transcendentals=0),
    )(
        *[
            arg if at in near else pltpu.with_memory_space_constraint(arg, pltpu.HBM)
            for at, arg in enumerate(args)
        ]
    )


def body(
    pair, mask, gain_in, bias_in, proj_weight, gate_weight,
    product_norm_gain, product_norm_bias, out_weight, cotangent,
):
    rows, cols, width = pair.shape
    hidden = out_weight.shape[0]
    n_row = lax.axis_size("row")
    n_col = lax.axis_size("col")
    n_dev = n_row * n_col
    share = hidden // n_dev
    cells = rows * cols
    n_groups = len(groups_of(rows))
    mask_row = mask.reshape(1, -1)
    gain_in, bias_in = gain_in.reshape(1, -1), bias_in.reshape(1, -1)
    norm_gain, norm_bias = product_norm_gain.reshape(1, -1), product_norm_bias.reshape(1, -1)

    def shape(*dims, dtype=BF16):
        return jax.ShapeDtypeStruct(dims, dtype)

    def vmem(*dims, dtype=BF16):
        return pltpu.VMEM(dims, dtype)

    def sems(count):
        return pltpu.SemaphoreType.DMA((count,))

    def exchange(values):
        return lax.all_to_all(values, ("row", "col"), split_axis=0, concat_axis=0, tiled=True)

    mask_s = pltpu.SMEM(mask.shape, jnp.int32)
    mask_v = vmem(*mask_row.shape, dtype=jnp.int32)
    vector = vmem(1, width, dtype=F32)
    plane = vmem(hidden * rows, cols, dtype=F32)
    block = vmem(rows, cols, width)
    wide = vmem(rows, width, cols, dtype=F32)
    square = vmem(width, hidden)
    send = call(
        front_kernel,
        shape(n_dev, 2 * share, rows, cols),
        [
            block, mask_s, mask_v, vector, vector, vmem(width, 4 * hidden), plane, plane,
            sems(5), sems(n_groups),
        ],
        (pair, mask, mask_row, gain_in, bias_in, proj_weight),
        outs_near=True,
        flops=2 * cells * width * 5 * hidden,
        moved=6 * cells * width,
    )
    both = exchange(send).reshape(n_row, n_col, 2 * share, rows, cols)
    coef, zhat, inv, gate, dxh = call(
        side_kernel,
        (
            shape(rows, 4 * hidden, cols, dtype=F32),
            shape(rows, width, cols, dtype=F32),
            shape(rows, cols, dtype=F32),
            shape(rows, width, cols, dtype=F32),
            shape(hidden * rows, cols, dtype=F32),
        ),
        [
            block, block, mask_s, mask_v, vector, vector, vmem(width, 4 * hidden), square, vector,
            square, vmem(rows, 4 * hidden, cols, dtype=F32), wide, vmem(rows, cols, dtype=F32),
            wide, plane, sems(10), sems(5),
        ],
        (
            pair, cotangent, mask, mask_row, gain_in, bias_in, proj_weight, gate_weight,
            norm_gain, out_weight,
        ),
        flops=2 * cells * width * 8 * hidden,
        moved=32 * cells * width,
    )
    product = call(
        product_kernel,
        shape(n_row, n_col, share, rows, cols),
        [],
        (both, inv),
        near=(0,),
        outs_near=True,
        flops=2 * share * (n_row * rows) ** 3,
        moved=6 * cells * hidden,
    )
    product = exchange(product.reshape(n_dev, share, rows, cols)).reshape(hidden, rows, cols)
    spread = vmem(hidden, rows, cols, dtype=F32)
    grad = call(
        middle_kernel,
        shape(hidden, rows, cols),
        [spread, spread, sems(1)],
        (product, dxh.reshape(hidden, rows, cols)),
        near=(0,),
        outs_near=True,
        flops=20 * cells * hidden,
        moved=8 * cells * hidden,
    )
    grad = exchange(grad.reshape(n_dev, share, rows, cols))
    update, dzg = call(
        update_kernel,
        (shape(rows, cols, width), shape(rows, width, cols, dtype=F32)),
        [wide, block, vector, vector, square, square, block, wide, plane, sems(6), sems(2)],
        (product, gate, cotangent, norm_gain, norm_bias, out_weight, gate_weight),
        near=(0,),
        flops=2 * cells * width * 3 * hidden,
        moved=14 * cells * hidden,
    )
    grads = call(
        grads_kernel,
        shape(n_row, n_col, 2 * share, rows, cols),
        [],
        (both, grad.reshape(n_row, n_col, share, rows, cols)),
        near=(0, 1),
        outs_near=True,
        flops=4 * share * (n_row * rows) ** 3,
        moved=10 * cells * hidden,
    )
    grads = exchange(grads.reshape(n_dev, 2 * share, rows, cols))
    grad_pair = call(
        back_kernel,
        shape(rows, cols, width),
        [
            vmem(rows, 4 * hidden, cols, dtype=F32), wide, vmem(rows, cols, dtype=F32), wide,
            vector, vmem(width, 4 * hidden), block, plane, plane,
            sems(3), sems(n_groups), sems(n_groups), sems(n_groups), sems(n_groups),
        ],
        (grads, coef, zhat, inv, dzg, gain_in, proj_weight),
        near=(0,),
        flops=2 * cells * width * 5 * hidden,
        moved=30 * cells * width,
    )
    return (update, grad_pair)


def solution(mesh):
    placed = (
        P(("grp", "row"), "col", None),
        P("grp"),
        P(),
        P(),
        P(),
        P(),
        P(),
        P(),
        P(),
        P(("grp", "row"), "col", None),
    )
    return jax.shard_map(
        body,
        mesh=mesh,
        in_specs=placed,
        out_specs=(P(("grp", "row"), "col", None), P(("grp", "row"), "col", None)),
        check_vma=False,
    )
```

time: 128 us -> 115 us (0.90)
  waiting for transfers between devices: 14 us -> 40.7 us
  blocking collectives: 54 us -> 36.9 us
  local copies, waits for them, and re-layouts: 16.9 us -> 0 us
  Pallas kernels: 34.7 us -> 25.5 us
  starting transfers between devices: 7.25 us -> 10.9 us
    all_to_all x2, waiting for transfers between devices: 14 us -> 40.7 us  [exchange(): lax.all_to_all(values, ('row', 'col'), split_axis=0, concat_axis=0, tiled...]
    all_to_all x2, blocking collectives: 54 us -> 36.9 us  [exchange(): lax.all_to_all(values, ('row', 'col'), split_axis=0, concat_axis=0, tiled...]
    unnamed x48 -> x0, local copies, waits for them, and re-layouts: 16.9 us -> none
    pallas_call x7, Pallas kernels: 34.7 us -> 25.5 us  [call(): pl.pallas_call(kernel, out_shape=outs if outs_near else jax.tree.map(lamb...]
    all_to_all x2, starting transfers between devices: 7.25 us -> 10.9 us  [exchange(): lax.all_to_all(values, ('row', 'col'), split_axis=0, concat_axis=0, tiled...]
  transfers between devices with their start and end apart: 2 -> 2, of which waited for: 1 -> 2; matrix products, arithmetic and copies ran while one was open for 0% -> 0% of each run, Pallas kernels for 16% -> 10%
where the time goes in v3:
time: 115 us
  waiting for transfers between devices  40.7 us (35%)
  blocking collectives  36.9 us (32%)
  Pallas kernels  25.5 us (22%)
  starting transfers between devices  10.9 us (9%)
    all_to_all x2, waiting for transfers between devices, exchange(): lax.all_to_all(values, ('row', 'col'), split_axis=0, concat_axis=0, tiled...  40.7 us
    all_to_all x2, blocking collectives, exchange(): lax.all_to_all(values, ('row', 'col'), split_axis=0, concat_axis=0, tiled...  36.9 us
    pallas_call x7, Pallas kernels, call(): pl.pallas_call(kernel, out_shape=outs if outs_near else jax.tree.map(lamb...  25.5 us
    all_to_all x2, starting transfers between devices, exchange(): lax.all_to_all(values, ('row', 'col'), split_axis=0, concat_axis=0, tiled...  10.9 us
  transfers between devices with their start and end apart: 2, of which 2 were waited for; matrix products, arithmetic and copies ran while one was open for 0% of the time, Pallas kernels for 10%

profile of v3, /device:TPU:0, one launch (start us, length us, event | category | flops | bytes accessed | tf_op | source)
XLA Modules:
  0.0 114.7 jit_solution(4831625447463895066)
XLA Ops:
  0.6 4.9 %shard_map.113 = bf16[32,8,16,128]{3,2,1,0:T(8,128)(2,1)} custom-call(bf16[16,128,128]{2,1,0:T(8,128)(2,1)} %pair_h.3, s32[256]{0:T(256)} %mask_h.3, s32[1,256]{1,0:T(1,128)} %bitcast.20, f32[1,128]{1,0:T(1,128)} %bitcast.22, f32[1,128]{1,0:T(1,128)} %bitcast.25, bf16[128,512]{1,0:T(8,128)(2,1)} %proj_h.5), custom_call_target="tpu_custom_call" | custom-call | flops 335544320 | bytes 1572864 | tf_op jit(solution)/shard_map/pallas_call | solution.py:325
  5.5 7.3 %all-to-all-start = ((bf16[32,8,16,128]{3,2,1,0:T(8,128)(2,1)}), bf16[32,8,16,128]{3,2,1,0:T(8,128)(2,1)S(1)}, u32[]{:S(2)}, u32[]{:S(2)}) async-start(bf16[32,8,16,128]{3,2,1,0:T(8,128)(2,1)} %shard_map.113), calls=%async_computation | async-start | bytes 2097152 | tf_op jit(solution)/shard_map/all_to_all | solution.py:367
  12.9 7.6 %shard_map.114 = (f32[16,512,128]{2,1,0:T(8,128)}, f32[16,128,128]{2,1,0:T(8,128)}, f32[16,128]{1,0:T(8,128)}, f32[16,128,128]{2,1,0:T(8,128)}, f32[2048,128]{1,0:T(8,128)}) custom-call(bf16[16,128,128]{2,1,0:T(8,128)(2,1)} %pair_h.3, bf16[16,128,128]{2,1,0:T(8,128)(2,1)} %cot_h.3, s32[256]{0:T(256)} %mask_h.3, s32[1,256]{1,0:T(1,128)} %bitcast.21, ...), custom_call_target="tpu_custom_call" | custom-call | flops 536870912 | bytes 8388608 | tf_op jit(solution)/shard_map/pallas_call | solution.py:325
  20.5 18.6 %all-to-all-done = bf16[32,8,16,128]{3,2,1,0:T(8,128)(2,1)S(1)} async-done(((bf16[32,8,16,128]{3,2,1,0:T(8,128)(2,1)}), bf16[32,8,16,128]{3,2,1,0:T(8,128)(2,1)S(1)}, u32[]{:S(2)}, u32[]{:S(2)}) %all-to-all-start) | async-done | bytes 1048608 | tf_op jit(solution)/shard_map/all_to_all | solution.py:367
  39.1 0.3 shard_map.115
  39.4 18.4 %all_to_all.20 = bf16[32,4,16,128]{3,2,1,0:T(8,128)(2,1)S(1)} all-to-all(bf16[32,4,16,128]{3,2,1,0:T(8,128)(2,1)S(1)} %bitcast.17), channel_id=1, replica_groups=mesh['grp'=1,'row'=16,'col'=2] {'row','col'}, dimensions={0} | all-to-all | bytes 1048576 | tf_op jit(solution)/shard_map/all_to_all | solution.py:367
  57.9 1.5 %shard_map.117 = bf16[128,16,128]{2,1,0:T(8,128)(2,1)S(1)} custom-call(bf16[128,16,128]{2,1,0:T(8,128)(2,1)S(1)} %bitcast.14, f32[128,16,128]{2,1,0:T(8,128)} %bitcast.19), custom_call_target="tpu_custom_call" | custom-call | flops 5242880 | bytes 2097152 | tf_op jit(solution)/shard_map/pallas_call | solution.py:325
  59.4 18.4 %all_to_all.21 = bf16[32,4,16,128]{3,2,1,0:T(8,128)(2,1)S(1)} all-to-all(bf16[32,4,16,128]{3,2,1,0:T(8,128)(2,1)S(1)} %bitcast.18), channel_id=1, replica_groups=mesh['grp'=1,'row'=16,'col'=2] {'row','col'}, dimensions={0} | all-to-all | bytes 1048576 | tf_op jit(solution)/shard_map/all_to_all | solution.py:367
  77.8 1.5 %shard_map.118 = bf16[16,2,8,16,128]{4,3,2,1,0:T(8,128)(2,1)} custom-call(bf16[16,2,8,16,128]{4,3,2,1,0:T(8,128)(2,1)S(1)} %bitcast.13, bf16[16,2,4,16,128]{4,3,2,1,0:T(8,128)(2,1)S(1)} %bitcast.16), custom_call_target="tpu_custom_call" | custom-call | flops 268435456 | bytes 2621440 | tf_op jit(solution)/shard_map/pallas_call | solution.py:325
  79.3 3.6 %all-to-all-start.3 = ((bf16[32,8,16,128]{3,2,1,0:T(8,128)(2,1)}), bf16[32,8,16,128]{3,2,1,0:T(8,128)(2,1)S(1)}, u32[]{:S(2)}, u32[]{:S(2)}) async-start(bf16[32,8,16,128]{3,2,1,0:T(8,128)(2,1)} %bitcast.11), calls=%async_computation.3 | async-start | bytes 2097152 | tf_op jit(solution)/shard_map/all_to_all | solution.py:367
  82.9 4.1 %shard_map.116 = (bf16[16,128,128]{2,1,0:T(8,128)(2,1)}, f32[16,128,128]{2,1,0:T(8,128)}) custom-call(bf16[128,16,128]{2,1,0:T(8,128)(2,1)S(1)} %bitcast.15, f32[16,128,128]{2,1,0:T(8,128)} %get-tuple-element.10.gate_h, bf16[16,128,128]{2,1,0:T(8,128)(2,1)} %cot_h.3, f32[1,128]{1,0:T(1,128)} %bitcast.28, f32[1,128]{1,0:T(1,128)} %bitcast.29, ...), custom_call_target="tpu_custom_call" | custom-call | flops 201326592 | bytes 3670016 | tf_op jit(solution)/shard_map/pallas_call | solution.py:325
  87.1 22.1 %all-to-all-done.3.grads = bf16[32,8,16,128]{3,2,1,0:T(8,128)(2,1)S(1)} async-done(((bf16[32,8,16,128]{3,2,1,0:T(8,128)(2,1)}), bf16[32,8,16,128]{3,2,1,0:T(8,128)(2,1)S(1)}, u32[]{:S(2)}, u32[]{:S(2)}) %all-to-all-start.3) | async-done | bytes 1048608 | tf_op jit(solution)/shard_map/all_to_all | solution.py:367
  109.2 5.6 %shard_map.119 = bf16[16,128,128]{2,1,0:T(8,128)(2,1)} custom-call(bf16[32,8,16,128]{3,2,1,0:T(8,128)(2,1)S(1)} %all-to-all-done.3.grads, f32[16,512,128]{2,1,0:T(8,128)} %get-tuple-element.13.coef_h, f32[16,128,128]{2,1,0:T(8,128)} %get-tuple-element.14.zhat_h, f32[16,128]{1,0:T(8,128)} %get-tuple-element.9.after.inv_h, ...), custom_call_target="tpu_custom_call" | custom-call | flops 335544320 | bytes 7864320 | tf_op jit(solution)/shard_map/pallas_call | solution.py:325
Async XLA Ops:
  5.5 33.5 %all-to-all-start = ((bf16[32,8,16,128]{3,2,1,0:T(8,128)(2,1)}), bf16[32,8,16,128]{3,2,1,0:T(8,128)(2,1)S(1)}, u32[]{:S(2)}, u32[]{:S(2)}) async-start(bf16[32,8,16,128]{3,2,1,0:T(8,128)(2,1)} %shard_map.113), calls=%async_computation | async-start | bytes 2097152 | tf_op jit(solution)/shard_map/all_to_all | solution.py:367
  79.3 29.9 %all-to-all-start.3 = ((bf16[32,8,16,128]{3,2,1,0:T(8,128)(2,1)}), bf16[32,8,16,128]{3,2,1,0:T(8,128)(2,1)S(1)}, u32[]{:S(2)}, u32[]{:S(2)}) async-start(bf16[32,8,16,128]{3,2,1,0:T(8,128)(2,1)} %bitcast.11), calls=%async_computation.3 | async-start | bytes 2097152 | tf_op jit(solution)/shard_map/all_to_all | solution.py:367

commit v4 on v3

--- a/solution.py
+++ b/solution.py
@@ -1,3 +1,4 @@
+import functools
 import math
 
 import jax
@@ -75,7 +76,7 @@
 
 
 def pair_mask(mask_s, mask_v, at, size, rows, cols):
-    first_row = lax.axis_index("row") * rows + at
+    first_row = (lax.axis_index("half") * lax.axis_size("row") + lax.axis_index("row")) * rows + at
     first_col = pl.multiple_of(lax.axis_index("col") * cols, cols)
     col_mask = mask_v[:, pl.ds(first_col, cols)].astype(F32)
     return jnp.concatenate(
@@ -83,14 +84,17 @@
     )
 
 
+def place():
+    return lax.axis_index("row") * lax.axis_size("col") + lax.axis_index("col")
+
+
 def front_kernel(
-    pair_h, mask_h, mask_row_h, gain_h, bias_h, proj_h, out,
-    pair, mask_s, mask_v, gain, bias, proj_weight, left, right, sems, row_sems,
+    part, n_out, pair_h, mask_h, mask_row_h, gain_h, bias_h, proj_h, *refs
 ):
+    outs = refs[:n_out]
+    pair, mask_s, mask_v, gain, bias, proj_weight, plane, sems, row_sems = refs[n_out:]
     rows, cols, width = pair.shape
-    n_dev, share2 = out.shape[0], out.shape[1]
-    share = share2 // 2
-    hidden = n_dev * share
+    hidden = plane.shape[0] // rows
     groups = groups_of(rows)
     small = start(
         sems,
@@ -103,21 +107,29 @@
     wait(small)
     gain_b = jnp.concatenate([down_lanes(gain[...], cols)] * groups[0][1], axis=1)
     bias_b = jnp.concatenate([down_lanes(bias[...], cols)] * groups[0][1], axis=1)
-    weight = turned_weight(proj_weight[...])
+    weight = turned_weight(proj_weight[:, part * hidden : (part + 2) * hidden])
     for (at, size), block in zip(groups, blocks):
         block.wait()
         zhat, _ = normalized(turned(pair[at : at + size].reshape(size * cols, width)))
         zbar = (zhat * gain_b + bias_b).astype(BF16)
         pm = pair_mask(mask_s, mask_v, at, size, rows, cols)
-        for part, target in ((0, left), (2, right)):
-            p = dot(weight[part * hidden : (part + 1) * hidden], zbar)
-            q = dot(weight[(part + 1) * hidden : (part + 2) * hidden], zbar)
-            values = sigmoid(p) * q * pm
-            for r in range(size):
-                target[pl.ds(at + r, hidden, stride=rows), :] = values[:, r * cols : (r + 1) * cols]
-    shape = (n_dev, share, rows, cols)
-    out[:, :share] = left[...].reshape(shape).astype(BF16)
-    out[:, share:] = right[...].reshape(shape).astype(BF16)
+        values = sigmoid(dot(weight[:hidden], zbar)) * dot(weight[hidden:], zbar) * pm
+        for r in range(size):
+            plane[pl.ds(at + r, hidden, stride=rows), :] = values[:, r * cols : (r + 1) * cols]
+    if n_out == 1:
+        values = plane[...].reshape(outs[0].shape[1:]).astype(BF16)
+        for half in range(outs[0].shape[0]):
+            outs[0][half] = values
+    else:
+        give_pieces(plane, outs)
+
+
+def give_pieces(plane, outs):
+    here = place()
+    length = plane.shape[0] // len(outs)
+    for m, out in enumerate(outs):
+        first = pl.multiple_of((here ^ m) * length, length)
+        out[...] = plane[pl.ds(first, length), :].reshape(out.shape).astype(BF16)
 
 
 def side_kernel(
@@ -165,8 +177,8 @@
             second = pm * s
             for r in range(size):
                 lanes = slice(r * cols, (r + 1) * cols)
-                coef[at + r, part * hidden : (part + 1) * hidden] = first[:, lanes]
-                coef[at + r, (part + 1) * hidden : (part + 2) * hidden] = second[:, lanes]
+                coef[at + r, part] = first[:, lanes]
+                coef[at + r, part + 1] = second[:, lanes]
     wait(
         start(
             out_sems,
@@ -179,26 +191,30 @@
 
 
 def channel_matrix(ref, at):
-    n_row, n_col, _, rows, cols = ref.shape
+    *_, n_col, _, rows, cols = ref.shape
+    lead = (slice(None),) * (len(ref.shape) - 4)
     return jnp.concatenate(
-        [ref[:, c, at].reshape(n_row * rows, cols) for c in range(n_col)], axis=1
+        [ref[(*lead, c, at)].reshape(-1, cols) for c in range(n_col)], axis=1
     )
 
 
 def put_channel(ref, at, values):
-    n_row, n_col, _, rows, cols = ref.shape
+    *shape, n_col, _, rows, cols = ref.shape
+    lead = (slice(None),) * len(shape)
     values = values.astype(BF16)
     for c in range(n_col):
-        ref[:, c, at] = values[:, c * cols : (c + 1) * cols].reshape(n_row, rows, cols)
-
-
-def product_kernel(both, after, out):
-    share = out.shape[2]
+        ref[(*lead, c, at)] = values[:, c * cols : (c + 1) * cols].reshape(*shape, rows, cols)
+
+
+def product_kernel(right, after, *refs):
+    pieces, (out, left) = refs[:-2], refs[-2:]
+    here = place()
+    n_col, share = left.shape[1:3]
+    for m, piece in enumerate(pieces):
+        source = here ^ m
+        left[source // n_col, source % n_col] = piece[...]
     for h in range(share):
-        put_channel(
-            out, h,
-            dot(channel_matrix(both, h), channel_matrix(both, share + h), ((1,), (1,))),
-        )
+        put_channel(out, h, dot(channel_matrix(left, h), channel_matrix(right, h), ((1,), (1,))))
 
 
 def middle_kernel(product, dxh_h, out, dxh, xhat, sems):
@@ -254,23 +270,77 @@
     wait(start(out_sems, [(update, update_h), (dzg, dzg_h)]))
 
 
-def grads_kernel(both, grad, out):
-    share = grad.shape[2]
+def grad_right_kernel(grad, left, out):
+    for h in range(out.shape[-3]):
+        put_channel(out, h, dot(channel_matrix(grad, h), channel_matrix(left, h), ((0,), (0,))))
+
+
+def grad_left_kernel(grad, right, *refs):
+    outs, ready = refs[:-1], refs[-1]
+    here = place()
+    n_col, share = ready.shape[1:3]
     for h in range(share):
-        g = channel_matrix(grad, h)
-        put_channel(out, h, dot(g, channel_matrix(both, share + h)))
-        put_channel(out, share + h, dot(g, channel_matrix(both, h), ((0,), (0,))))
+        put_channel(ready, h, dot(channel_matrix(grad, h), channel_matrix(right, h)))
+    for m, out in enumerate(outs):
+        target = here ^ m
+        out[...] = ready[target // n_col, target % n_col]
+
+
+def through_projection(plane, coef, weight, at, size, rows):
+    hidden = plane.shape[0] // rows
+    columns = []
+    for r in range(size):
+        g = plane[pl.ds(at + r, hidden, stride=rows), :]
+        columns.append(
+            jnp.concatenate(
+                [(g * coef[at + r, part]).astype(BF16) for part in range(2)], axis=0
+            )
+        )
+    return dot(weight, jnp.concatenate(columns, axis=1))
+
+
+def back_left_kernel(coef_h, dzg_h, proj_h, *refs):
+    pieces, out_h = refs[:-9], refs[-9]
+    coef, dzg, proj_weight, out, plane, sems, coef_sems, dzg_sems = refs[-8:]
+    rows, width, cols = out.shape
+    hidden = plane.shape[0] // rows
+    groups = groups_of(rows)
+    small = start(sems, [(proj_h, proj_weight)])
+    blocks = [
+        start(
+            coef_sems,
+            [
+                (coef_h.at[pl.ds(at, size), pl.ds(0, 2)], coef.at[pl.ds(at, size)])
+                for at, size in groups
+            ],
+        ),
+        start(
+            dzg_sems,
+            [(dzg_h.at[pl.ds(at, size)], dzg.at[pl.ds(at, size)]) for at, size in groups],
+        ),
+    ]
+    here = place()
+    length = plane.shape[0] // len(pieces)
+    for m, piece in enumerate(pieces):
+        first = pl.multiple_of((here ^ m) * length, length)
+        plane[pl.ds(first, length), :] = piece[...].astype(F32).reshape(length, cols)
+    wait(small)
+    weight = proj_weight[:, : 2 * hidden]
+    for n, (at, size) in enumerate(groups):
+        wait([copies[n] for copies in blocks])
+        back = through_projection(plane, coef, weight, at, size, rows)
+        for r in range(size):
+            out[at + r] = back[:, r * cols : (r + 1) * cols] + dzg[at + r]
+    wait(start(sems, [(out, out_h)]))
 
 
 def back_kernel(
     grads, coef_h, zhat_h, inv_h, dzg_h, gain_h, proj_h, out_h,
-    coef, zhat, inv, dzg, gain, proj_weight, out, left, right,
+    coef, zhat, inv, dzg, gain, proj_weight, out, plane,
     sems, coef_sems, zhat_sems, dzg_sems, out_sems,
 ):
     rows, cols, width = out.shape
-    n_dev, share2 = grads.shape[0], grads.shape[1]
-    share = share2 // 2
-    hidden = n_dev * share
+    hidden = plane.shape[0] // rows
     groups = groups_of(rows)
 
     def blocks_of(source, target):
@@ -278,32 +348,28 @@
 
     small = start(sems, [(gain_h, gain), (proj_h, proj_weight), (inv_h, inv)])
     blocks = [
-        start(coef_sems, blocks_of(coef_h, coef)),
+        start(
+            coef_sems,
+            [
+                (coef_h.at[pl.ds(at, size), pl.ds(2, 2)], coef.at[pl.ds(at, size)])
+                for at, size in groups
+            ],
+        ),
         start(zhat_sems, blocks_of(zhat_h, zhat)),
         start(dzg_sems, blocks_of(dzg_h, dzg)),
     ]
-    left[...] = grads[:, :share].astype(F32).reshape(hidden * rows, cols)
-    right[...] = grads[:, share:].astype(F32).reshape(hidden * rows, cols)
+    total = grads[0].astype(F32)
+    for half in range(1, grads.shape[0]):
+        total = total + grads[half].astype(F32)
+    plane[...] = total.reshape(plane.shape)
     wait(small)
     gain_b = jnp.concatenate([down_lanes(gain[...], cols)] * groups[0][1], axis=1)
+    weight = proj_weight[:, 2 * hidden :]
     leaving = []
     for n, (at, size) in enumerate(groups):
         wait([copies[n] for copies in blocks])
-        columns = []
-        for r in range(size):
-            gl = left[pl.ds(at + r, hidden, stride=rows), :]
-            gr = right[pl.ds(at + r, hidden, stride=rows), :]
-            columns.append(
-                jnp.concatenate(
-                    [
-                        (g * coef[at + r, part * hidden : (part + 1) * hidden]).astype(BF16)
-                        for part, g in enumerate((gl, gl, gr, gr))
-                    ],
-                    axis=0,
-                )
-            )
-        dproj = jnp.concatenate(columns, axis=1)
-        dzh = (dot(proj_weight[...], dproj) + side_by_side(dzg, at, size)) * gain_b
+        back = through_projection(plane, coef, weight, at, size, rows)
+        dzh = (back + side_by_side(dzg, at, size)) * gain_b
         z = side_by_side(zhat, at, size)
         inverse = jnp.concatenate([inv[at + r : at + r + 1] for r in range(size)], axis=1)
         m1 = jnp.mean(dzh, axis=0, keepdims=True)
@@ -344,10 +410,11 @@
 ):
     rows, cols, width = pair.shape
     hidden = out_weight.shape[0]
+    n_half = lax.axis_size("half")
     n_row = lax.axis_size("row")
     n_col = lax.axis_size("col")
-    n_dev = n_row * n_col
-    share = hidden // n_dev
+    n_place = n_row * n_col
+    share = hidden // n_place
     cells = rows * cols
     n_groups = len(groups_of(rows))
     mask_row = mask.reshape(1, -1)
@@ -365,6 +432,18 @@
 
     def exchange(values):
         return lax.all_to_all(values, ("row", "col"), split_axis=0, concat_axis=0, tiled=True)
+
+    def exchange_all(values):
+        flat = values.reshape(n_half * n_place, share, rows, cols)
+        return lax.all_to_all(
+            flat, ("half", "row", "col"), split_axis=0, concat_axis=0, tiled=True
+        )
+
+    def exchange_pieces(pieces):
+        return pieces[:1] + tuple(
+            lax.ppermute(piece, ("row", "col"), [(at, at ^ m) for at in range(n_place)])
+            for m, piece in enumerate(pieces[1:], 1)
+        )
 
     mask_s = pltpu.SMEM(mask.shape, jnp.int32)
     mask_v = vmem(*mask_row.shape, dtype=jnp.int32)
@@ -373,31 +452,36 @@
     block = vmem(rows, cols, width)
     wide = vmem(rows, width, cols, dtype=F32)
     square = vmem(width, hidden)
-    send = call(
-        front_kernel,
-        shape(n_dev, 2 * share, rows, cols),
-        [
-            block, mask_s, mask_v, vector, vector, vmem(width, 4 * hidden), plane, plane,
-            sems(5), sems(n_groups),
-        ],
-        (pair, mask, mask_row, gain_in, bias_in, proj_weight),
-        outs_near=True,
-        flops=2 * cells * width * 5 * hidden,
-        moved=6 * cells * width,
-    )
-    both = exchange(send).reshape(n_row, n_col, 2 * share, rows, cols)
+    proj_v = vmem(width, 4 * hidden)
+    coef_v = vmem(rows, 2, hidden, cols, dtype=F32)
+    pieces_shape = (shape(share, rows, cols),) * n_place
+
+    def front(part, outs):
+        return call(
+            functools.partial(front_kernel, part, len(outs)),
+            outs,
+            [block, mask_s, mask_v, vector, vector, proj_v, plane, sems(5), sems(n_groups)],
+            (pair, mask, mask_row, gain_in, bias_in, proj_weight),
+            outs_near=True,
+            flops=2 * cells * width * 3 * hidden,
+            moved=5 * cells * width,
+        )
+
+    (right,) = front(2, (shape(n_half, n_place, share, rows, cols),))
+    right = exchange_all(right).reshape(n_half, n_row, n_col, share, rows, cols)
+    left = exchange_pieces(tuple(front(0, pieces_shape)))
     coef, zhat, inv, gate, dxh = call(
         side_kernel,
         (
-            shape(rows, 4 * hidden, cols, dtype=F32),
+            shape(rows, 4, hidden, cols, dtype=F32),
             shape(rows, width, cols, dtype=F32),
             shape(rows, cols, dtype=F32),
             shape(rows, width, cols, dtype=F32),
             shape(hidden * rows, cols, dtype=F32),
         ),
         [
-            block, block, mask_s, mask_v, vector, vector, vmem(width, 4 * hidden), square, vector,
-            square, vmem(rows, 4 * hidden, cols, dtype=F32), wide, vmem(rows, cols, dtype=F32),
+            block, block, mask_s, mask_v, vector, vector, proj_v, square, vector,
+            square, vmem(rows, 4, hidden, cols, dtype=F32), wide, vmem(rows, cols, dtype=F32),
             wide, plane, sems(10), sems(5),
         ],
         (
@@ -407,17 +491,17 @@
         flops=2 * cells * width * 8 * hidden,
         moved=32 * cells * width,
     )
-    product = call(
+    product, left = call(
         product_kernel,
-        shape(n_row, n_col, share, rows, cols),
+        (shape(n_row, n_col, share, rows, cols), shape(n_row, n_col, share, rows, cols)),
         [],
-        (both, inv),
-        near=(0,),
+        (right, inv, *left),
+        near=(0, *range(2, 2 + n_place)),
         outs_near=True,
-        flops=2 * share * (n_row * rows) ** 3,
-        moved=6 * cells * hidden,
-    )
-    product = exchange(product.reshape(n_dev, share, rows, cols)).reshape(hidden, rows, cols)
+        flops=2 * share * n_half * (n_row * rows) ** 2 * n_col * cols,
+        moved=8 * cells * hidden,
+    )
+    product = exchange(product.reshape(n_place, share, rows, cols)).reshape(hidden, rows, cols)
     spread = vmem(hidden, rows, cols, dtype=F32)
     grad = call(
         middle_kernel,
@@ -429,7 +513,8 @@
         flops=20 * cells * hidden,
         moved=8 * cells * hidden,
     )
-    grad = exchange(grad.reshape(n_dev, share, rows, cols))
+    grad = exchange(grad.reshape(n_place, share, rows, cols))
+    grad = grad.reshape(n_row, n_col, share, rows, cols)
     update, dzg = call(
         update_kernel,
         (shape(rows, cols, width), shape(rows, width, cols, dtype=F32)),
@@ -439,50 +524,63 @@
         flops=2 * cells * width * 3 * hidden,
         moved=14 * cells * hidden,
     )
-    grads = call(
-        grads_kernel,
-        shape(n_row, n_col, 2 * share, rows, cols),
+    grad_right = call(
+        grad_right_kernel,
+        shape(n_half, n_row, n_col, share, rows, cols),
         [],
-        (both, grad.reshape(n_row, n_col, share, rows, cols)),
+        (grad, left),
         near=(0, 1),
         outs_near=True,
-        flops=4 * share * (n_row * rows) ** 3,
-        moved=10 * cells * hidden,
-    )
-    grads = exchange(grads.reshape(n_dev, 2 * share, rows, cols))
+        flops=2 * share * n_half * (n_row * rows) ** 2 * n_col * cols,
+        moved=8 * cells * hidden,
+    )
+    grad_right = exchange_all(grad_right).reshape(n_half, n_place, share, rows, cols)
+    grad_left = call(
+        grad_left_kernel,
+        pieces_shape,
+        [vmem(n_row, n_col, share, rows, cols)],
+        (grad, right),
+        near=(0, 1),
+        outs_near=True,
+        flops=2 * share * n_half * (n_row * rows) ** 2 * n_col * cols,
+        moved=8 * cells * hidden,
+    )
+    grad_left = exchange_pieces(tuple(grad_left))
+    dzg = call(
+        back_left_kernel,
+        shape(rows, width, cols, dtype=F32),
+        [coef_v, wide, proj_v, wide, plane, sems(1), sems(n_groups), sems(n_groups)],
+        (coef, dzg, proj_weight, *grad_left),
+        near=tuple(range(3, 3 + n_place)),
+        flops=2 * cells * width * 2 * hidden,
+        moved=18 * cells * width,
+    )
     grad_pair = call(
         back_kernel,
         shape(rows, cols, width),
         [
-            vmem(rows, 4 * hidden, cols, dtype=F32), wide, vmem(rows, cols, dtype=F32), wide,
-            vector, vmem(width, 4 * hidden), block, plane, plane,
+            coef_v, wide, vmem(rows, cols, dtype=F32), wide, vector, proj_v, block, plane,
             sems(3), sems(n_groups), sems(n_groups), sems(n_groups), sems(n_groups),
         ],
-        (grads, coef, zhat, inv, dzg, gain_in, proj_weight),
+        (grad_right, coef, zhat, inv, dzg, gain_in, proj_weight),
         near=(0,),
-        flops=2 * cells * width * 5 * hidden,
-        moved=30 * cells * width,
+        flops=2 * cells * width * 3 * hidden,
+        moved=22 * cells * width,
     )
     return (update, grad_pair)
 
 
 def solution(mesh):
-    placed = (
-        P(("grp", "row"), "col", None),
-        P("grp"),
-        P(),
-        P(),
-        P(),
-        P(),
-        P(),
-        P(),
-        P(),
-        P(("grp", "row"), "col", None),
-    )
+    n_grp, n_row, n_col = (mesh.shape[name] for name in ("grp", "row", "col"))
+    n_half = math.gcd(n_row, 2)
+    split = jax.sharding.Mesh(
+        mesh.devices.reshape(n_grp, n_half, n_row // n_half, n_col), ("grp", "half", "row", "col")
+    )
+    cells = P(("grp", "half", "row"), "col", None)
     return jax.shard_map(
         body,
-        mesh=mesh,
-        in_specs=placed,
-        out_specs=(P(("grp", "row"), "col", None), P(("grp", "row"), "col", None)),
+        mesh=split,
+        in_specs=(cells, P("grp"), P(), P(), P(), P(), P(), P(), P(), cells),
+        out_specs=(cells, cells),
         check_vma=False,
     )

time: 115 us -> 122 us (1.061)
  starting transfers between devices: 10.9 us -> 51.5 us
  waiting for transfers between devices: 40.7 us -> 11.8 us
  blocking collectives: 36.9 us -> 25.3 us
  Pallas kernels: 25.5 us -> 31 us
    all_to_all x2, waiting for transfers between devices: 40.7 us -> 0.01 us  [exchange_all(): lax.all_to_all(flat, ('half', 'row', 'col'), split_axis=0, concat_axis=0,...]
    ppermute x0 -> x30, starting transfers between devices: none -> 39.4 us  [exchange_pieces(): lax.ppermute(piece, ('row', 'col'), [(at, at ^ m) for at in range(n_place)])]
    ppermute x0 -> x30, waiting for transfers between devices: none -> 11.8 us  [exchange_pieces(): lax.ppermute(piece, ('row', 'col'), [(at, at ^ m) for at in range(n_place)])]
    all_to_all x2, blocking collectives: 36.9 us -> 25.3 us  [exchange(): lax.all_to_all(values, ('row', 'col'), split_axis=0, concat_axis=0, tiled...]
    pallas_call x7 -> x10, Pallas kernels: 25.5 us -> 31 us  [call(): pl.pallas_call(kernel, out_shape=outs if outs_near else jax.tree.map(lamb...]
  transfers between devices with their start and end apart: 2 -> 32, of which waited for: 2 -> 4; matrix products, arithmetic and copies ran while one was open for 0% -> 0% of each run, Pallas kernels for 10% -> 16%
where the time goes in v4:
time: 122 us
  starting transfers between devices  51.5 us (42%)
  Pallas kernels  31 us (25%)
  blocking collectives  25.3 us (21%)
  waiting for transfers between devices  11.8 us (10%)
    ppermute x30, starting transfers between devices, exchange_pieces(): lax.ppermute(piece, ('row', 'col'), [(at, at ^ m) for at in range(n_place)])  39.4 us
    pallas_call x10, Pallas kernels, call(): pl.pallas_call(kernel, out_shape=outs if outs_near else jax.tree.map(lamb...  31 us
    all_to_all x2, blocking collectives, exchange(): lax.all_to_all(values, ('row', 'col'), split_axis=0, concat_axis=0, tiled...  25.3 us
    all_to_all x2, starting transfers between devices, exchange_all(): lax.all_to_all(flat, ('half', 'row', 'col'), split_axis=0, concat_axis=0,...  12 us
    ppermute x30, waiting for transfers between devices, exchange_pieces(): lax.ppermute(piece, ('row', 'col'), [(at, at ^ m) for at in range(n_place)])  11.8 us
  transfers between devices with their start and end apart: 32, of which 4 were waited for; matrix products, arithmetic and copies ran while one was open for 0% of the time, Pallas kernels for 16%

profile of v4, /device:TPU:0, one launch (start us, length us, event | category | flops | bytes accessed | tf_op | source)
XLA Modules:
  0.0 121.5 jit_solution(2708162485008203266)
XLA Ops:
  0.6 4.4 %shard_map.113 = bf16[2,16,8,16,128]{4,3,2,1,0:T(8,128)(2,1)} custom-call(bf16[16,128,128]{2,1,0:T(8,128)(2,1)} %pair_h.5, s32[256]{0:T(256)} %mask_h.5, s32[1,256]{1,0:T(1,128)} %bitcast.25, f32[1,128]{1,0:T(1,128)} %bitcast.28, f32[1,128]{1,0:T(1,128)} %bitcast.32, bf16[128,512]{1,0:T(8,128)(2,1)} %proj_h.9), custom_call_target="tpu_custom_call" | custom-call | flops 201326592 | bytes 1310720 | tf_op jit(solution)/shard_map/pallas_call | solution.py:391
  5.0 7.3 %all-to-all-start = ((bf16[32,8,16,128]{3,2,1,0:T(8,128)(2,1)}), bf16[32,8,16,128]{3,2,1,0:T(8,128)(2,1)S(1)}, u32[]{:S(2)}, u32[]{:S(2)}) async-start(bf16[32,8,16,128]{3,2,1,0:T(8,128)(2,1)} %bitcast.3), calls=%async_computation | async-start | bytes 2097152 | tf_op jit(solution)/shard_map/all_to_all | solution.py:438
  12.3 3.4 %shard_map.115 = (bf16[8,16,128]{2,1,0:T(8,128)(2,1)S(1)}, bf16[8,16,128]{2,1,0:T(8,128)(2,1)S(1)}, bf16[8,16,128]{2,1,0:T(8,128)(2,1)S(1)}, bf16[8,16,128]{2,1,...) custom-call(bf16[16,128,128]{2,1,0:T(8,128)(2,1)} %pair_h.5, ...), custom_call_target="tpu_custom_call" | custom-call | flops 201326592 | bytes 1310720 | tf_op jit(solution)/shard_map/pallas_call | solution.py:391
  15.7 1.8 %collective-permute-start = (bf16[8,16,128]{2,1,0:T(8,128)(2,1)S(1)}, bf16[8,16,128]{2,1,0:T(8,128)(2,1)S(1)}, u32[]{:S(2)}, u32[]{:S(2)}) collective-permute-start(bf16[8,16,128]{2,1,0:T(8,128)(2,1)S(1)} %get-tuple-element.45), channel_id=1, source_target_pairs={{0,1},{1,0},{2,3},{3,2},{4,5},{5,4},{6,7},{7,6},{8,9},{9,8},{10,11... | collective-permute-start | bytes 98312 | tf_op jit(solution)/shard_map/ppermute | solution.py:444
  20.6 2.4 %collective-permute-start.12 = (bf16[8,16,128]{2,1,0:T(8,128)(2,1)S(1)}, bf16[8,16,128]{2,1,0:T(8,128)(2,1)S(1)}, u32[]{:S(2)}, u32[]{:S(2)}) collective-permute-start(bf16[8,16,128]{2,1,0:T(8,128)(2,1)S(1)} %get-tuple-element.57), channel_id=1, source_target_pairs={{0,13},{1,12},{2,15},{3,14},{4,9},{5,8},{6,11},{7,10},{8,5},{9,4},... | collective-permute-start | bytes 98312 | tf_op jit(solution)/shard_map/ppermute | solution.py:444
  23.5 2.1 %collective-permute-start.14 = (bf16[8,16,128]{2,1,0:T(8,128)(2,1)S(1)}, bf16[8,16,128]{2,1,0:T(8,128)(2,1)S(1)}, u32[]{:S(2)}, u32[]{:S(2)}) collective-permute-start(bf16[8,16,128]{2,1,0:T(8,128)(2,1)S(1)} %get-tuple-element.59), channel_id=1, source_target_pairs={{0,15},{1,14},{2,13},{3,12},{4,11},{5,10},{6,9},{7,8},{8,7},{9,6},... | collective-permute-start | bytes 98312 | tf_op jit(solution)/shard_map/ppermute | solution.py:444
  25.6 5.4 %collective-permute-done.10.refs_11_ = bf16[8,16,128]{2,1,0:T(8,128)(2,1)S(1)} collective-permute-done((bf16[8,16,128]{2,1,0:T(8,128)(2,1)S(1)}, bf16[8,16,128]{2,1,0:T(8,128)(2,1)S(1)}, u32[]{:S(2)}, u32[]{:S(2)}) %collective-permute-start.10) | collective-permute-done | bytes 32800 | tf_op jit(solution)/shard_map/ppermute | solution.py:444
  31.7 1.8 %collective-permute-start.3 = (bf16[8,16,128]{2,1,0:T(8,128)(2,1)S(1)}, bf16[8,16,128]{2,1,0:T(8,128)(2,1)S(1)}, u32[]{:S(2)}, u32[]{:S(2)}) collective-permute-start(bf16[8,16,128]{2,1,0:T(8,128)(2,1)S(1)} %get-tuple-element.48), channel_id=1, source_target_pairs={{0,4},{1,5},{2,6},{3,7},{4,0},{5,1},{6,2},{7,3},{8,12},{9,13},{10,... | collective-permute-start | bytes 98312 | tf_op jit(solution)/shard_map/ppermute | solution.py:444
  33.5 1.6 %collective-permute-start.4 = (bf16[8,16,128]{2,1,0:T(8,128)(2,1)S(1)}, bf16[8,16,128]{2,1,0:T(8,128)(2,1)S(1)}, u32[]{:S(2)}, u32[]{:S(2)}) collective-permute-start(bf16[8,16,128]{2,1,0:T(8,128)(2,1)S(1)} %get-tuple-element.49), channel_id=1, source_target_pairs={{0,5},{1,4},{2,7},{3,6},{4,1},{5,0},{6,3},{7,2},{8,13},{9,12},{10,... | collective-permute-start | bytes 98312 | tf_op jit(solution)/shard_map/ppermute | solution.py:444
  36.9 4.1 %collective-permute-start.7 = (bf16[8,16,128]{2,1,0:T(8,128)(2,1)S(1)}, bf16[8,16,128]{2,1,0:T(8,128)(2,1)S(1)}, u32[]{:S(2)}, u32[]{:S(2)}) collective-permute-start(bf16[8,16,128]{2,1,0:T(8,128)(2,1)S(1)} %get-tuple-element.52), channel_id=1, source_target_pairs={{0,8},{1,9},{2,10},{3,11},{4,12},{5,13},{6,14},{7,15},{8,0},{9,1},... | collective-permute-start | bytes 98312 | tf_op jit(solution)/shard_map/ppermute | solution.py:444
  41.6 7.6 %shard_map.114 = (f32[16,4,128,128]{3,2,1,0:T(8,128)}, f32[16,128,128]{2,1,0:T(8,128)}, f32[16,128]{1,0:T(8,128)}, f32[16,128,128]{2,1,0:T(8,128)}, f32[2048,128]{1,0:T(8,128)}) custom-call(bf16[16,128,128]{2,1,0:T(8,128)(2,1)} %pair_h.5, bf16[16,128,128]{2,1,0:T(8,128)(2,1)} %cot_h.3, s32[256]{0:T(256)} %mask_h.5, s32[1,256]{1,0:T(1,128)} %bitcast.27, ...), custom_call_target="tpu_custom_call" | custom-call | flops 536870912 | bytes 8388608 | tf_op jit(solution)/shard_map/pallas_call | solution.py:391
  49.9 13.3 %all_to_all.20 = bf16[16,8,16,128]{3,2,1,0:T(8,128)(2,1)S(1)} all-to-all(bf16[16,8,16,128]{3,2,1,0:T(8,128)(2,1)S(1)} %bitcast.23), channel_id=1, replica_groups=mesh['grp'=1,'half'=2,'row'=8,'col'=2] {'row','col'}, dimensions={0} | all-to-all | bytes 1048576 | tf_op jit(solution)/shard_map/all_to_all | solution.py:434
  64.7 12.0 %all_to_all.21 = bf16[16,8,16,128]{3,2,1,0:T(8,128)(2,1)S(1)} all-to-all(bf16[16,8,16,128]{3,2,1,0:T(8,128)(2,1)S(1)} %bitcast.22), channel_id=1, replica_groups=mesh['grp'=1,'half'=2,'row'=8,'col'=2] {'row','col'}, dimensions={0} | all-to-all | bytes 1048576 | tf_op jit(solution)/shard_map/all_to_all | solution.py:434
  78.1 4.7 %all-to-all-start.3 = ((bf16[32,8,16,128]{3,2,1,0:T(8,128)(2,1)}), bf16[32,8,16,128]{3,2,1,0:T(8,128)(2,1)S(1)}, u32[]{:S(2)}, u32[]{:S(2)}) async-start(bf16[32,8,16,128]{3,2,1,0:T(8,128)(2,1)} %bitcast.21), calls=%async_computation.3 | async-start | bytes 2097152 | tf_op jit(solution)/shard_map/all_to_all | solution.py:438
  83.2 1.7 %collective-permute-start.15 = (bf16[8,16,128]{2,1,0:T(8,128)(2,1)S(1)}, bf16[8,16,128]{2,1,0:T(8,128)(2,1)S(1)}, u32[]{:S(2)}, u32[]{:S(2)}) collective-permute-start(bf16[8,16,128]{2,1,0:T(8,128)(2,1)S(1)} %get-tuple-element.69), channel_id=1, source_target_pairs={{0,1},{1,0},{2,3},{3,2},{4,5},{5,4},{6,7},{7,6},{8,9},{9,8},{10,11... | collective-permute-start | bytes 98312 | tf_op jit(solution)/shard_map/ppermute | solution.py:444
  88.5 5.2 %collective-permute-done.15.refs_1_ = bf16[8,16,128]{2,1,0:T(8,128)(2,1)S(1)} collective-permute-done((bf16[8,16,128]{2,1,0:T(8,128)(2,1)S(1)}, bf16[8,16,128]{2,1,0:T(8,128)(2,1)S(1)}, u32[]{:S(2)}, u32[]{:S(2)}) %collective-permute-start.15) | collective-permute-done | bytes 32800 | tf_op jit(solution)/shard_map/ppermute | solution.py:444
  93.8 1.7 %collective-permute-start.21 = (bf16[8,16,128]{2,1,0:T(8,128)(2,1)S(1)}, bf16[8,16,128]{2,1,0:T(8,128)(2,1)S(1)}, u32[]{:S(2)}, u32[]{:S(2)}) collective-permute-start(bf16[8,16,128]{2,1,0:T(8,128)(2,1)S(1)} %get-tuple-element.75), channel_id=1, source_target_pairs={{0,7},{1,6},{2,5},{3,4},{4,3},{5,2},{6,1},{7,0},{8,15},{9,14},{10,... | collective-permute-start | bytes 98312 | tf_op jit(solution)/shard_map/ppermute | solution.py:444
  96.0 2.4 %collective-permute-start.23 = (bf16[8,16,128]{2,1,0:T(8,128)(2,1)S(1)}, bf16[8,16,128]{2,1,0:T(8,128)(2,1)S(1)}, u32[]{:S(2)}, u32[]{:S(2)}) collective-permute-start(bf16[8,16,128]{2,1,0:T(8,128)(2,1)S(1)} %get-tuple-element.77), channel_id=1, source_target_pairs={{0,9},{1,8},{2,11},{3,10},{4,13},{5,12},{6,15},{7,14},{8,1},{9,0},... | collective-permute-start | bytes 98312 | tf_op jit(solution)/shard_map/ppermute | solution.py:444
  98.5 1.7 %collective-permute-start.25 = (bf16[8,16,128]{2,1,0:T(8,128)(2,1)S(1)}, bf16[8,16,128]{2,1,0:T(8,128)(2,1)S(1)}, u32[]{:S(2)}, u32[]{:S(2)}) collective-permute-start(bf16[8,16,128]{2,1,0:T(8,128)(2,1)S(1)} %get-tuple-element.79), channel_id=1, source_target_pairs={{0,11},{1,10},{2,9},{3,8},{4,15},{5,14},{6,13},{7,12},{8,3},{9,2},... | collective-permute-start | bytes 98312 | tf_op jit(solution)/shard_map/ppermute | solution.py:444
  101.5 4.5 %collective-permute-start.27 = (bf16[8,16,128]{2,1,0:T(8,128)(2,1)S(1)}, bf16[8,16,128]{2,1,0:T(8,128)(2,1)S(1)}, u32[]{:S(2)}, u32[]{:S(2)}) collective-permute-start(bf16[8,16,128]{2,1,0:T(8,128)(2,1)S(1)} %get-tuple-element.81), channel_id=1, source_target_pairs={{0,13},{1,12},{2,15},{3,14},{4,9},{5,8},{6,11},{7,10},{8,5},{9,4},... | collective-permute-start | bytes 98312 | tf_op jit(solution)/shard_map/ppermute | solution.py:444
  106.0 2.6 %collective-permute-start.29 = (bf16[8,16,128]{2,1,0:T(8,128)(2,1)S(1)}, bf16[8,16,128]{2,1,0:T(8,128)(2,1)S(1)}, u32[]{:S(2)}, u32[]{:S(2)}) collective-permute-start(bf16[8,16,128]{2,1,0:T(8,128)(2,1)S(1)} %get-tuple-element.83), channel_id=1, source_target_pairs={{0,15},{1,14},{2,13},{3,12},{4,11},{5,10},{6,9},{7,8},{8,7},{9,6},... | collective-permute-start | bytes 98312 | tf_op jit(solution)/shard_map/ppermute | solution.py:444
  108.6 4.2 %shard_map.117 = (bf16[16,128,128]{2,1,0:T(8,128)(2,1)}, f32[16,128,128]{2,1,0:T(8,128)}) custom-call(bf16[128,16,128]{2,1,0:T(8,128)(2,1)S(1)} %bitcast.19, f32[16,128,128]{2,1,0:T(8,128)} %get-tuple-element.61.gate_h, bf16[16,128,128]{2,1,0:T(8,128)(2,1)} %cot_h.3, f32[1,128]{1,0:T(1,128)} %bitcast.36, f32[1,128]{1,0:T(1,128)} %bitcast.37, ...), custom_call_target="tpu_custom_call" | custom-call | flops 201326592 | bytes 3670016 | tf_op jit(solution)/shard_map/pallas_call | solution.py:391
  112.9 3.8 %shard_map.121.dzg_h = f32[16,128,128]{2,1,0:T(8,128)} custom-call(f32[16,4,128,128]{3,2,1,0:T(8,128)} %get-tuple-element.65.coef_h, f32[16,128,128]{2,1,0:T(8,128)} %get-tuple-element.67.dzg_h, bf16[128,512]{1,0:T(8,128)(2,1)} %proj_h.9, bf16[8,16,128]{2,1,0:T(8,128)(2,1)S(1)} %get-tuple-element.68.refs_0_, ...), custom_call_target="tpu_custom_call" | custom-call | flops 134217728 | bytes 4718592 | tf_op jit(solution)/shard_map/pallas_call | solution.py:391
  116.7 4.6 %shard_map.122 = bf16[16,128,128]{2,1,0:T(8,128)(2,1)} custom-call(bf16[2,16,8,16,128]{4,3,2,1,0:T(8,128)(2,1)S(1)} %bitcast.20, f32[16,4,128,128]{3,2,1,0:T(8,128)} %get-tuple-element.65.coef_h, f32[16,128,128]{2,1,0:T(8,128)} %get-tuple-element.66.zhat_h, f32[16,128]{1,0:T(8,128)} %get-tuple-element.43.after.inv_h, f32[16,128,128]{2,1,0:T(8,128)} %shard_map.121.dzg_h, ...), custom_call_target="tpu_custom_call" | custom-call | flops 201326592 | bytes 5767168 | tf_op jit(solution)/shard_map/pallas_call | solution.py:391
  (54 shorter events, 16.1 us)
Async XLA Ops:
  5.0 44.3 %all-to-all-start = ((bf16[32,8,16,128]{3,2,1,0:T(8,128)(2,1)}), bf16[32,8,16,128]{3,2,1,0:T(8,128)(2,1)S(1)}, u32[]{:S(2)}, u32[]{:S(2)}) async-start(bf16[32,8,16,128]{3,2,1,0:T(8,128)(2,1)} %bitcast.3), calls=%async_computation | async-start | bytes 2097152 | tf_op jit(solution)/shard_map/all_to_all | solution.py:438
  17.6 13.4 %collective-permute-start.10 = (bf16[8,16,128]{2,1,0:T(8,128)(2,1)S(1)}, bf16[8,16,128]{2,1,0:T(8,128)(2,1)S(1)}, u32[]{:S(2)}, u32[]{:S(2)}) collective-permute-start(bf16[8,16,128]{2,1,0:T(8,128)(2,1)S(1)} %get-tuple-element.55), channel_id=1, source_target_pairs={{0,11},{1,10},{2,9},{3,8},{4,15},{5,14},{6,13},{7,12},{8,3},{9,2},... | collective-permute-start | bytes 98312 | tf_op jit(solution)/shard_map/ppermute | solution.py:444
  19.2 12.6 %collective-permute-start.11 = (bf16[8,16,128]{2,1,0:T(8,128)(2,1)S(1)}, bf16[8,16,128]{2,1,0:T(8,128)(2,1)S(1)}, u32[]{:S(2)}, u32[]{:S(2)}) collective-permute-start(bf16[8,16,128]{2,1,0:T(8,128)(2,1)S(1)} %get-tuple-element.56), channel_id=1, source_target_pairs={{0,12},{1,13},{2,14},{3,15},{4,8},{5,9},{6,10},{7,11},{8,4},{9,5},... | collective-permute-start | bytes 98312 | tf_op jit(solution)/shard_map/ppermute | solution.py:444
  20.6 12.9 %collective-permute-start.12 = (bf16[8,16,128]{2,1,0:T(8,128)(2,1)S(1)}, bf16[8,16,128]{2,1,0:T(8,128)(2,1)S(1)}, u32[]{:S(2)}, u32[]{:S(2)}) collective-permute-start(bf16[8,16,128]{2,1,0:T(8,128)(2,1)S(1)} %get-tuple-element.57), channel_id=1, source_target_pairs={{0,13},{1,12},{2,15},{3,14},{4,9},{5,8},{6,11},{7,10},{8,5},{9,4},... | collective-permute-start | bytes 98312 | tf_op jit(solution)/shard_map/ppermute | solution.py:444
  23.0 12.2 %collective-permute-start.13 = (bf16[8,16,128]{2,1,0:T(8,128)(2,1)S(1)}, bf16[8,16,128]{2,1,0:T(8,128)(2,1)S(1)}, u32[]{:S(2)}, u32[]{:S(2)}) collective-permute-start(bf16[8,16,128]{2,1,0:T(8,128)(2,1)S(1)} %get-tuple-element.58), channel_id=1, source_target_pairs={{0,14},{1,15},{2,12},{3,13},{4,10},{5,11},{6,8},{7,9},{8,6},{9,7},... | collective-permute-start | bytes 98312 | tf_op jit(solution)/shard_map/ppermute | solution.py:444
  23.5 12.0 %collective-permute-start.14 = (bf16[8,16,128]{2,1,0:T(8,128)(2,1)S(1)}, bf16[8,16,128]{2,1,0:T(8,128)(2,1)S(1)}, u32[]{:S(2)}, u32[]{:S(2)}) collective-permute-start(bf16[8,16,128]{2,1,0:T(8,128)(2,1)S(1)} %get-tuple-element.59), channel_id=1, source_target_pairs={{0,15},{1,14},{2,13},{3,12},{4,11},{5,10},{6,9},{7,8},{8,7},{9,6},... | collective-permute-start | bytes 98312 | tf_op jit(solution)/shard_map/ppermute | solution.py:444
  31.7 9.2 %collective-permute-start.3 = (bf16[8,16,128]{2,1,0:T(8,128)(2,1)S(1)}, bf16[8,16,128]{2,1,0:T(8,128)(2,1)S(1)}, u32[]{:S(2)}, u32[]{:S(2)}) collective-permute-start(bf16[8,16,128]{2,1,0:T(8,128)(2,1)S(1)} %get-tuple-element.48), channel_id=1, source_target_pairs={{0,4},{1,5},{2,6},{3,7},{4,0},{5,1},{6,2},{7,3},{8,12},{9,13},{10,... | collective-permute-start | bytes 98312 | tf_op jit(solution)/shard_map/ppermute | solution.py:444
  33.5 7.7 %collective-permute-start.4 = (bf16[8,16,128]{2,1,0:T(8,128)(2,1)S(1)}, bf16[8,16,128]{2,1,0:T(8,128)(2,1)S(1)}, u32[]{:S(2)}, u32[]{:S(2)}) collective-permute-start(bf16[8,16,128]{2,1,0:T(8,128)(2,1)S(1)} %get-tuple-element.49), channel_id=1, source_target_pairs={{0,5},{1,4},{2,7},{3,6},{4,1},{5,0},{6,3},{7,2},{8,13},{9,12},{10,... | collective-permute-start | bytes 98312 | tf_op jit(solution)/shard_map/ppermute | solution.py:444
  35.1 14.1 %collective-permute-start.5 = (bf16[8,16,128]{2,1,0:T(8,128)(2,1)S(1)}, bf16[8,16,128]{2,1,0:T(8,128)(2,1)S(1)}, u32[]{:S(2)}, u32[]{:S(2)}) collective-permute-start(bf16[8,16,128]{2,1,0:T(8,128)(2,1)S(1)} %get-tuple-element.50), channel_id=1, source_target_pairs={{0,6},{1,7},{2,4},{3,5},{4,2},{5,3},{6,0},{7,1},{8,14},{9,15},{10,... | collective-permute-start | bytes 98312 | tf_op jit(solution)/shard_map/ppermute | solution.py:444
  35.5 13.8 %collective-permute-start.6 = (bf16[8,16,128]{2,1,0:T(8,128)(2,1)S(1)}, bf16[8,16,128]{2,1,0:T(8,128)(2,1)S(1)}, u32[]{:S(2)}, u32[]{:S(2)}) collective-permute-start(bf16[8,16,128]{2,1,0:T(8,128)(2,1)S(1)} %get-tuple-element.51), channel_id=1, source_target_pairs={{0,7},{1,6},{2,5},{3,4},{4,3},{5,2},{6,1},{7,0},{8,15},{9,14},{10,... | collective-permute-start | bytes 98312 | tf_op jit(solution)/shard_map/ppermute | solution.py:444
  36.9 12.4 %collective-permute-start.7 = (bf16[8,16,128]{2,1,0:T(8,128)(2,1)S(1)}, bf16[8,16,128]{2,1,0:T(8,128)(2,1)S(1)}, u32[]{:S(2)}, u32[]{:S(2)}) collective-permute-start(bf16[8,16,128]{2,1,0:T(8,128)(2,1)S(1)} %get-tuple-element.52), channel_id=1, source_target_pairs={{0,8},{1,9},{2,10},{3,11},{4,12},{5,13},{6,14},{7,15},{8,0},{9,1},... | collective-permute-start | bytes 98312 | tf_op jit(solution)/shard_map/ppermute | solution.py:444
  40.9 8.4 %collective-permute-start.8 = (bf16[8,16,128]{2,1,0:T(8,128)(2,1)S(1)}, bf16[8,16,128]{2,1,0:T(8,128)(2,1)S(1)}, u32[]{:S(2)}, u32[]{:S(2)}) collective-permute-start(bf16[8,16,128]{2,1,0:T(8,128)(2,1)S(1)} %get-tuple-element.53), channel_id=1, source_target_pairs={{0,9},{1,8},{2,11},{3,10},{4,13},{5,12},{6,15},{7,14},{8,1},{9,0},... | collective-permute-start | bytes 98312 | tf_op jit(solution)/shard_map/ppermute | solution.py:444
  41.2 8.1 %collective-permute-start.9 = (bf16[8,16,128]{2,1,0:T(8,128)(2,1)S(1)}, bf16[8,16,128]{2,1,0:T(8,128)(2,1)S(1)}, u32[]{:S(2)}, u32[]{:S(2)}) collective-permute-start(bf16[8,16,128]{2,1,0:T(8,128)(2,1)S(1)} %get-tuple-element.54), channel_id=1, source_target_pairs={{0,10},{1,11},{2,8},{3,9},{4,14},{5,15},{6,12},{7,13},{8,2},{9,3},... | collective-permute-start | bytes 98312 | tf_op jit(solution)/shard_map/ppermute | solution.py:444
  78.1 38.6 %all-to-all-start.3 = ((bf16[32,8,16,128]{3,2,1,0:T(8,128)(2,1)}), bf16[32,8,16,128]{3,2,1,0:T(8,128)(2,1)S(1)}, u32[]{:S(2)}, u32[]{:S(2)}) async-start(bf16[32,8,16,128]{3,2,1,0:T(8,128)(2,1)} %bitcast.21), calls=%async_computation.3 | async-start | bytes 2097152 | tf_op jit(solution)/shard_map/all_to_all | solution.py:438
  83.2 10.5 %collective-permute-start.15 = (bf16[8,16,128]{2,1,0:T(8,128)(2,1)S(1)}, bf16[8,16,128]{2,1,0:T(8,128)(2,1)S(1)}, u32[]{:S(2)}, u32[]{:S(2)}) collective-permute-start(bf16[8,16,128]{2,1,0:T(8,128)(2,1)S(1)} %get-tuple-element.69), channel_id=1, source_target_pairs={{0,1},{1,0},{2,3},{3,2},{4,5},{5,4},{6,7},{7,6},{8,9},{9,8},{10,11... | collective-permute-start | bytes 98312 | tf_op jit(solution)/shard_map/ppermute | solution.py:444
  84.9 8.8 %collective-permute-start.16 = (bf16[8,16,128]{2,1,0:T(8,128)(2,1)S(1)}, bf16[8,16,128]{2,1,0:T(8,128)(2,1)S(1)}, u32[]{:S(2)}, u32[]{:S(2)}) collective-permute-start(bf16[8,16,128]{2,1,0:T(8,128)(2,1)S(1)} %get-tuple-element.70), channel_id=1, source_target_pairs={{0,2},{1,3},{2,0},{3,1},{4,6},{5,7},{6,4},{7,5},{8,10},{9,11},{10,... | collective-permute-start | bytes 98312 | tf_op jit(solution)/shard_map/ppermute | solution.py:444
  84.9 10.5 %collective-permute-start.17 = (bf16[8,16,128]{2,1,0:T(8,128)(2,1)S(1)}, bf16[8,16,128]{2,1,0:T(8,128)(2,1)S(1)}, u32[]{:S(2)}, u32[]{:S(2)}) collective-permute-start(bf16[8,16,128]{2,1,0:T(8,128)(2,1)S(1)} %get-tuple-element.71), channel_id=1, source_target_pairs={{0,3},{1,2},{2,1},{3,0},{4,7},{5,6},{6,5},{7,4},{8,11},{9,10},{10,... | collective-permute-start | bytes 98312 | tf_op jit(solution)/shard_map/ppermute | solution.py:444
  85.5 10.6 %collective-permute-start.18 = (bf16[8,16,128]{2,1,0:T(8,128)(2,1)S(1)}, bf16[8,16,128]{2,1,0:T(8,128)(2,1)S(1)}, u32[]{:S(2)}, u32[]{:S(2)}) collective-permute-start(bf16[8,16,128]{2,1,0:T(8,128)(2,1)S(1)} %get-tuple-element.72), channel_id=1, source_target_pairs={{0,4},{1,5},{2,6},{3,7},{4,0},{5,1},{6,2},{7,3},{8,12},{9,13},{10,... | collective-permute-start | bytes 98312 | tf_op jit(solution)/shard_map/ppermute | solution.py:444
  87.1 11.4 %collective-permute-start.19 = (bf16[8,16,128]{2,1,0:T(8,128)(2,1)S(1)}, bf16[8,16,128]{2,1,0:T(8,128)(2,1)S(1)}, u32[]{:S(2)}, u32[]{:S(2)}) collective-permute-start(bf16[8,16,128]{2,1,0:T(8,128)(2,1)S(1)} %get-tuple-element.73), channel_id=1, source_target_pairs={{0,5},{1,4},{2,7},{3,6},{4,1},{5,0},{6,3},{7,2},{8,13},{9,12},{10,... | collective-permute-start | bytes 98312 | tf_op jit(solution)/shard_map/ppermute | solution.py:444
  96.0 10.0 %collective-permute-start.23 = (bf16[8,16,128]{2,1,0:T(8,128)(2,1)S(1)}, bf16[8,16,128]{2,1,0:T(8,128)(2,1)S(1)}, u32[]{:S(2)}, u32[]{:S(2)}) collective-permute-start(bf16[8,16,128]{2,1,0:T(8,128)(2,1)S(1)} %get-tuple-element.77), channel_id=1, source_target_pairs={{0,9},{1,8},{2,11},{3,10},{4,13},{5,12},{6,15},{7,14},{8,1},{9,0},... | collective-permute-start | bytes 98312 | tf_op jit(solution)/shard_map/ppermute | solution.py:444
  98.4 7.6 %collective-permute-start.24 = (bf16[8,16,128]{2,1,0:T(8,128)(2,1)S(1)}, bf16[8,16,128]{2,1,0:T(8,128)(2,1)S(1)}, u32[]{:S(2)}, u32[]{:S(2)}) collective-permute-start(bf16[8,16,128]{2,1,0:T(8,128)(2,1)S(1)} %get-tuple-element.78), channel_id=1, source_target_pairs={{0,10},{1,11},{2,8},{3,9},{4,14},{5,15},{6,12},{7,13},{8,2},{9,3},... | collective-permute-start | bytes 98312 | tf_op jit(solution)/shard_map/ppermute | solution.py:444
  98.5 14.4 %collective-permute-start.25 = (bf16[8,16,128]{2,1,0:T(8,128)(2,1)S(1)}, bf16[8,16,128]{2,1,0:T(8,128)(2,1)S(1)}, u32[]{:S(2)}, u32[]{:S(2)}) collective-permute-start(bf16[8,16,128]{2,1,0:T(8,128)(2,1)S(1)} %get-tuple-element.79), channel_id=1, source_target_pairs={{0,11},{1,10},{2,9},{3,8},{4,15},{5,14},{6,13},{7,12},{8,3},{9,2},... | collective-permute-start | bytes 98312 | tf_op jit(solution)/shard_map/ppermute | solution.py:444
  100.1 12.8 %collective-permute-start.26 = (bf16[8,16,128]{2,1,0:T(8,128)(2,1)S(1)}, bf16[8,16,128]{2,1,0:T(8,128)(2,1)S(1)}, u32[]{:S(2)}, u32[]{:S(2)}) collective-permute-start(bf16[8,16,128]{2,1,0:T(8,128)(2,1)S(1)} %get-tuple-element.80), channel_id=1, source_target_pairs={{0,12},{1,13},{2,14},{3,15},{4,8},{5,9},{6,10},{7,11},{8,4},{9,5},... | collective-permute-start | bytes 98312 | tf_op jit(solution)/shard_map/ppermute | solution.py:444
  101.5 11.4 %collective-permute-start.27 = (bf16[8,16,128]{2,1,0:T(8,128)(2,1)S(1)}, bf16[8,16,128]{2,1,0:T(8,128)(2,1)S(1)}, u32[]{:S(2)}, u32[]{:S(2)}) collective-permute-start(bf16[8,16,128]{2,1,0:T(8,128)(2,1)S(1)} %get-tuple-element.81), channel_id=1, source_target_pairs={{0,13},{1,12},{2,15},{3,14},{4,9},{5,8},{6,11},{7,10},{8,5},{9,4},... | collective-permute-start | bytes 98312 | tf_op jit(solution)/shard_map/ppermute | solution.py:444
  (9 other events, 50.8 us)

commit v5 on v4

--- a/solution.py
+++ b/solution.py
@@ -76,7 +76,10 @@
 
 
 def pair_mask(mask_s, mask_v, at, size, rows, cols):
-    first_row = (lax.axis_index("half") * lax.axis_size("row") + lax.axis_index("row")) * rows + at
+    here = lax.axis_index("half")
+    for name in ("row", "core"):
+        here = here * lax.axis_size(name) + lax.axis_index(name)
+    first_row = here * rows + at
     first_col = pl.multiple_of(lax.axis_index("col") * cols, cols)
     col_mask = mask_v[:, pl.ds(first_col, cols)].astype(F32)
     return jnp.concatenate(
@@ -84,8 +87,18 @@
     )
 
 
-def place():
-    return lax.axis_index("row") * lax.axis_size("col") + lax.axis_index("col")
+def sources(n_row, n_quad):
+    row = lax.axis_index("row")
+    quad = lax.axis_index("core") * lax.axis_size("col") + lax.axis_index("col")
+    return [(m, n, (row ^ n) * n_quad + (quad ^ m)) for m in range(n_quad) for n in range(n_row)]
+
+
+def received(refs, n_row):
+    n_quad = len(refs) - n_row + 1
+    return [
+        (number, refs[m][0] if n == 0 else refs[n_quad + n - 1][m])
+        for m, n, number in sources(n_row, n_quad)
+    ]
 
 
 def front_kernel(
@@ -125,18 +138,19 @@
 
 
 def give_pieces(plane, outs):
-    here = place()
-    length = plane.shape[0] // len(outs)
-    for m, out in enumerate(outs):
-        first = pl.multiple_of((here ^ m) * length, length)
-        out[...] = plane[pl.ds(first, length), :].reshape(out.shape).astype(BF16)
+    n_row = outs[0].shape[0]
+    length = plane.shape[0] // (len(outs) * n_row)
+    for m, n, number in sources(n_row, len(outs)):
+        first = pl.multiple_of(number * length, length)
+        values = plane[pl.ds(first, length), :]
+        outs[m][n] = values.reshape(outs[m].shape[1:]).astype(BF16)
 
 
 def side_kernel(
-    pair_h, cot_h, mask_h, mask_row_h, gain_h, bias_h, proj_h, gate_h, norm_gain_h, out_w_h,
-    coef_h, zhat_h, inv_h, gate_out_h, dxh_h,
-    pair, cot, mask_s, mask_v, gain, bias, proj_weight, gate_weight, norm_gain, out_weight,
-    coef, zhat_out, inv_out, gate_out, dxh_out, in_sems, out_sems,
+    pair_h, cot_h, gain_h, bias_h, gate_h, norm_gain_h, out_w_h,
+    zhat_h, inv_h, gate_out_h, dxh_h,
+    pair, cot, gain, bias, gate_weight, norm_gain, out_weight,
+    zhat_out, inv_out, gate_out, dxh_out, in_sems, out_sems,
 ):
     rows, cols, width = pair.shape
     hidden = out_weight.shape[0]
@@ -144,9 +158,8 @@
         start(
             in_sems,
             [
-                (pair_h, pair), (cot_h, cot), (mask_h, mask_s), (mask_row_h, mask_v),
-                (gain_h, gain), (bias_h, bias), (proj_h, proj_weight), (gate_h, gate_weight),
-                (norm_gain_h, norm_gain), (out_w_h, out_weight),
+                (pair_h, pair), (cot_h, cot), (gain_h, gain), (bias_h, bias),
+                (gate_h, gate_weight), (norm_gain_h, norm_gain), (out_w_h, out_weight),
             ],
         )
     )
@@ -154,12 +167,10 @@
     gain_b = jnp.concatenate([down_lanes(gain[...], cols)] * groups[0][1], axis=1)
     bias_b = jnp.concatenate([down_lanes(bias[...], cols)] * groups[0][1], axis=1)
     norm_gain_b = jnp.concatenate([down_lanes(norm_gain[...], cols)] * groups[0][1], axis=1)
-    weight = turned_weight(proj_weight[...])
     gate_t = turned_weight(gate_weight[...])
     for at, size in groups:
         zhat, inverse = normalized(turned(pair[at : at + size].reshape(size * cols, width)))
         zbar = (zhat * gain_b + bias_b).astype(BF16)
-        pm = pair_mask(mask_s, mask_v, at, size, rows, cols)
         gate = sigmoid(dot(gate_t, zbar))
         cot_t = turned(cot[at : at + size].reshape(size * cols, width))
         dxh = dot(out_weight[...], (cot_t * gate).astype(BF16)) * norm_gain_b
@@ -170,24 +181,52 @@
             inv_out[at + r : at + r + 1] = inverse[:, lanes]
             gate_out[at + r] = gate[:, lanes]
             dxh_out[pl.ds(at + r, hidden, stride=rows), :] = dxh[:, lanes]
+    wait(
+        start(
+            out_sems,
+            [(zhat_out, zhat_h), (inv_out, inv_h), (gate_out, gate_out_h), (dxh_out, dxh_h)],
+        )
+    )
+
+
+def factors_kernel(
+    zhat_h, mask_h, mask_row_h, gain_h, bias_h, proj_h, after, coef_h,
+    zhat, mask_s, mask_v, gain, bias, proj_weight, coef, in_sems, out_sems,
+):
+    rows, width, cols = zhat.shape
+    hidden = coef.shape[2]
+    wait(
+        start(
+            in_sems,
+            [
+                (zhat_h, zhat), (mask_h, mask_s), (mask_row_h, mask_v), (gain_h, gain),
+                (bias_h, bias), (proj_h, proj_weight),
+            ],
+        )
+    )
+    groups = groups_of(rows)
+    gain_b = jnp.concatenate([down_lanes(gain[...], cols)] * groups[0][1], axis=1)
+    bias_b = jnp.concatenate([down_lanes(bias[...], cols)] * groups[0][1], axis=1)
+    weight = turned_weight(proj_weight[...])
+    leaving = []
+    for n, (at, size) in enumerate(groups):
+        zbar = (side_by_side(zhat, at, size) * gain_b + bias_b).astype(BF16)
+        pm = pair_mask(mask_s, mask_v, at, size, rows, cols)
         for part in (0, 2):
             s = sigmoid(dot(weight[part * hidden : (part + 1) * hidden], zbar))
             q = dot(weight[(part + 1) * hidden : (part + 2) * hidden], zbar)
-            first = pm * q * s * (1.0 - s)
             second = pm * s
+            first = second * q * (1.0 - s)
             for r in range(size):
                 lanes = slice(r * cols, (r + 1) * cols)
                 coef[at + r, part] = first[:, lanes]
                 coef[at + r, part + 1] = second[:, lanes]
-    wait(
-        start(
-            out_sems,
-            [
-                (coef, coef_h), (zhat_out, zhat_h), (inv_out, inv_h), (gate_out, gate_out_h),
-                (dxh_out, dxh_h),
-            ],
-        )
-    )
+        copy = pltpu.make_async_copy(
+            coef.at[pl.ds(at, size)], coef_h.at[pl.ds(at, size)], out_sems.at[n]
+        )
+        copy.start()
+        leaving.append(copy)
+    wait(leaving)
 
 
 def channel_matrix(ref, at):
@@ -206,18 +245,16 @@
         ref[(*lead, c, at)] = values[:, c * cols : (c + 1) * cols].reshape(*shape, rows, cols)
 
 
-def product_kernel(right, after, *refs):
+def product_kernel(n_row, right, after, *refs):
     pieces, (out, left) = refs[:-2], refs[-2:]
-    here = place()
     n_col, share = left.shape[1:3]
-    for m, piece in enumerate(pieces):
-        source = here ^ m
-        left[source // n_col, source % n_col] = piece[...]
+    for number, piece in received(pieces, n_row):
+        left[number // n_col, number % n_col] = piece
     for h in range(share):
         put_channel(out, h, dot(channel_matrix(left, h), channel_matrix(right, h), ((1,), (1,))))
 
 
-def middle_kernel(product, dxh_h, out, dxh, xhat, sems):
+def middle_kernel(product, dxh_h, after, out, dxh, xhat, sems):
     hidden = product.shape[0]
     (copy,) = start(sems, [(dxh_h, dxh)])
     values = product[...].astype(F32)
@@ -232,7 +269,7 @@
 
 
 def update_kernel(
-    product, gate_h, cot_h, norm_gain_h, norm_bias_h, out_w_h, gate_w_h, update_h, dzg_h,
+    product, gate_h, cot_h, norm_gain_h, norm_bias_h, out_w_h, gate_w_h, after, update_h, dzg_h,
     gate, cot, norm_gain, norm_bias, out_weight, gate_weight, update, dzg, spread,
     in_sems, out_sems,
 ):
@@ -270,20 +307,18 @@
     wait(start(out_sems, [(update, update_h), (dzg, dzg_h)]))
 
 
-def grad_right_kernel(grad, left, out):
+def grad_right_kernel(grad, left, after, out):
     for h in range(out.shape[-3]):
         put_channel(out, h, dot(channel_matrix(grad, h), channel_matrix(left, h), ((0,), (0,))))
 
 
 def grad_left_kernel(grad, right, *refs):
     outs, ready = refs[:-1], refs[-1]
-    here = place()
     n_col, share = ready.shape[1:3]
     for h in range(share):
         put_channel(ready, h, dot(channel_matrix(grad, h), channel_matrix(right, h)))
-    for m, out in enumerate(outs):
-        target = here ^ m
-        out[...] = ready[target // n_col, target % n_col]
+    for m, n, number in sources(outs[0].shape[0], len(outs)):
+        outs[m][n] = ready[number // n_col, number % n_col]
 
 
 def through_projection(plane, coef, weight, at, size, rows):
@@ -299,7 +334,7 @@
     return dot(weight, jnp.concatenate(columns, axis=1))
 
 
-def back_left_kernel(coef_h, dzg_h, proj_h, *refs):
+def back_left_kernel(n_row, coef_h, dzg_h, proj_h, *refs):
     pieces, out_h = refs[:-9], refs[-9]
     coef, dzg, proj_weight, out, plane, sems, coef_sems, dzg_sems = refs[-8:]
     rows, width, cols = out.shape
@@ -319,11 +354,11 @@
             [(dzg_h.at[pl.ds(at, size)], dzg.at[pl.ds(at, size)]) for at, size in groups],
         ),
     ]
-    here = place()
-    length = plane.shape[0] // len(pieces)
-    for m, piece in enumerate(pieces):
-        first = pl.multiple_of((here ^ m) * length, length)
-        plane[pl.ds(first, length), :] = piece[...].astype(F32).reshape(length, cols)
+    arrived = received(pieces, n_row)
+    length = plane.shape[0] // len(arrived)
+    for number, piece in arrived:
+        first = pl.multiple_of(number * length, length)
+        plane[pl.ds(first, length), :] = piece.astype(F32).reshape(length, cols)
     wait(small)
     weight = proj_weight[:, : 2 * hidden]
     for n, (at, size) in enumerate(groups):
@@ -385,21 +420,22 @@
     wait(leaving)
 
 
-def call(kernel, outs, scratch, args, near=(), outs_near=False, flops=0, moved=0, limit=24):
-    here = pl.BlockSpec(memory_space=pltpu.VMEM)
-    far = pl.BlockSpec(memory_space=pltpu.HBM)
+def call(kernel, outs, scratch, args, near=(), order=(), outs_near=False, flops=0, moved=0):
+    here, far = (pl.BlockSpec(memory_space=space) for space in (pltpu.VMEM, pltpu.HBM))
+    anywhere = pl.BlockSpec(memory_space=pl.ANY)
+    specs = [here if at in near else anywhere if at in order else far for at in range(len(args))]
     return pl.pallas_call(
         kernel,
-        out_shape=outs if outs_near else jax.tree.map(lambda out: pltpu.HBM(out.shape, out.dtype), outs),
-        in_specs=[here if at in near else far for at in range(len(args))],
+        out_shape=outs if outs_near else jax.tree.map(lambda o: pltpu.HBM(o.shape, o.dtype), outs),
+        in_specs=specs,
         out_specs=jax.tree.map(lambda _: here if outs_near else far, outs),
         scratch_shapes=scratch,
-        compiler_params=pltpu.CompilerParams(vmem_limit_bytes=limit * MIB),
+        compiler_params=pltpu.CompilerParams(vmem_limit_bytes=24 * MIB),
         cost_estimate=pl.CostEstimate(flops=flops, bytes_accessed=moved, transcendentals=0),
     )(
         *[
-            arg if at in near else pltpu.with_memory_space_constraint(arg, pltpu.HBM)
-            for at, arg in enumerate(args)
+            pltpu.with_memory_space_constraint(arg, pltpu.HBM) if spec is far else arg
+            for arg, spec in zip(args, specs)
         ]
     )
 
@@ -412,8 +448,12 @@
     hidden = out_weight.shape[0]
     n_half = lax.axis_size("half")
     n_row = lax.axis_size("row")
+    n_core = lax.axis_size("core")
     n_col = lax.axis_size("col")
-    n_place = n_row * n_col
+    n_quad = n_core * n_col
+    n_line = n_row * n_core
+    n_place = n_line * n_col
+    within = ("row", "core", "col")
     share = hidden // n_place
     cells = rows * cols
     n_groups = len(groups_of(rows))
@@ -431,19 +471,25 @@
         return pltpu.SemaphoreType.DMA((count,))
 
     def exchange(values):
-        return lax.all_to_all(values, ("row", "col"), split_axis=0, concat_axis=0, tiled=True)
+        return lax.all_to_all(values, within, split_axis=0, concat_axis=0, tiled=True)
 
     def exchange_all(values):
         flat = values.reshape(n_half * n_place, share, rows, cols)
         return lax.all_to_all(
-            flat, ("half", "row", "col"), split_axis=0, concat_axis=0, tiled=True
-        )
+            flat, ("half", *within), split_axis=0, concat_axis=0, tiled=True
+        )
+
+    def permute(values, axes, size, distance):
+        return lax.ppermute(values, axes, [(at, at ^ distance) for at in range(size)])
 
     def exchange_pieces(pieces):
-        return pieces[:1] + tuple(
-            lax.ppermute(piece, ("row", "col"), [(at, at ^ m) for at in range(n_place)])
-            for m, piece in enumerate(pieces[1:], 1)
-        )
+        first = [pieces[0]]
+        first += [permute(pieces[m], ("core", "col"), n_quad, m) for m in range(1, n_quad)]
+        second = [
+            permute(jnp.stack([piece[n] for piece in first]), ("row",), n_row, n)
+            for n in range(1, n_row)
+        ]
+        return tuple(first + second)
 
     mask_s = pltpu.SMEM(mask.shape, jnp.int32)
     mask_v = vmem(*mask_row.shape, dtype=jnp.int32)
@@ -454,7 +500,8 @@
     square = vmem(width, hidden)
     proj_v = vmem(width, 4 * hidden)
     coef_v = vmem(rows, 2, hidden, cols, dtype=F32)
-    pieces_shape = (shape(share, rows, cols),) * n_place
+    pieces_shape = (shape(n_row, share, rows, cols),) * n_quad
+    n_pieces = n_quad + n_row - 1
 
     def front(part, outs):
         return call(
@@ -468,38 +515,45 @@
         )
 
     (right,) = front(2, (shape(n_half, n_place, share, rows, cols),))
-    right = exchange_all(right).reshape(n_half, n_row, n_col, share, rows, cols)
+    right = exchange_all(right).reshape(n_half, n_line, n_col, share, rows, cols)
     left = exchange_pieces(tuple(front(0, pieces_shape)))
-    coef, zhat, inv, gate, dxh = call(
+    zhat, inv, gate, dxh = call(
         side_kernel,
         (
-            shape(rows, 4, hidden, cols, dtype=F32),
             shape(rows, width, cols, dtype=F32),
             shape(rows, cols, dtype=F32),
             shape(rows, width, cols, dtype=F32),
             shape(hidden * rows, cols, dtype=F32),
         ),
         [
-            block, block, mask_s, mask_v, vector, vector, proj_v, square, vector,
-            square, vmem(rows, 4, hidden, cols, dtype=F32), wide, vmem(rows, cols, dtype=F32),
-            wide, plane, sems(10), sems(5),
+            block, block, vector, vector, square, vector, square,
+            wide, vmem(rows, cols, dtype=F32), wide, plane, sems(7), sems(4),
         ],
-        (
-            pair, cotangent, mask, mask_row, gain_in, bias_in, proj_weight, gate_weight,
-            norm_gain, out_weight,
-        ),
-        flops=2 * cells * width * 8 * hidden,
-        moved=32 * cells * width,
+        (pair, cotangent, gain_in, bias_in, gate_weight, norm_gain, out_weight),
+        flops=2 * cells * width * 4 * hidden,
+        moved=16 * cells * width,
     )
     product, left = call(
-        product_kernel,
-        (shape(n_row, n_col, share, rows, cols), shape(n_row, n_col, share, rows, cols)),
+        functools.partial(product_kernel, n_row),
+        (shape(n_line, n_col, share, rows, cols), shape(n_line, n_col, share, rows, cols)),
         [],
         (right, inv, *left),
-        near=(0, *range(2, 2 + n_place)),
+        near=(0, *range(2, 2 + n_pieces)),
         outs_near=True,
-        flops=2 * share * n_half * (n_row * rows) ** 2 * n_col * cols,
+        flops=2 * share * n_half * (n_line * rows) ** 2 * n_col * cols,
         moved=8 * cells * hidden,
+    )
+    coef = call(
+        factors_kernel,
+        shape(rows, 4, hidden, cols, dtype=F32),
+        [
+            wide, mask_s, mask_v, vector, vector, proj_v, vmem(rows, 4, hidden, cols, dtype=F32),
+            sems(6), sems(n_groups),
+        ],
+        (zhat, mask, mask_row, gain_in, bias_in, proj_weight, product),
+        order=(6,),
+        flops=2 * cells * width * 5 * hidden,
+        moved=20 * cells * width,
     )
     product = exchange(product.reshape(n_place, share, rows, cols)).reshape(hidden, rows, cols)
     spread = vmem(hidden, rows, cols, dtype=F32)
@@ -507,51 +561,53 @@
         middle_kernel,
         shape(hidden, rows, cols),
         [spread, spread, sems(1)],
-        (product, dxh.reshape(hidden, rows, cols)),
+        (product, dxh.reshape(hidden, rows, cols), coef),
         near=(0,),
         outs_near=True,
         flops=20 * cells * hidden,
         moved=8 * cells * hidden,
     )
+    sent = grad
     grad = exchange(grad.reshape(n_place, share, rows, cols))
-    grad = grad.reshape(n_row, n_col, share, rows, cols)
+    grad = grad.reshape(n_line, n_col, share, rows, cols)
     update, dzg = call(
         update_kernel,
         (shape(rows, cols, width), shape(rows, width, cols, dtype=F32)),
         [wide, block, vector, vector, square, square, block, wide, plane, sems(6), sems(2)],
-        (product, gate, cotangent, norm_gain, norm_bias, out_weight, gate_weight),
+        (product, gate, cotangent, norm_gain, norm_bias, out_weight, gate_weight, sent),
         near=(0,),
+        order=(7,),
         flops=2 * cells * width * 3 * hidden,
         moved=14 * cells * hidden,
     )
     grad_right = call(
         grad_right_kernel,
-        shape(n_half, n_row, n_col, share, rows, cols),
+        shape(n_half, n_line, n_col, share, rows, cols),
         [],
-        (grad, left),
+        (grad, left, dzg),
         near=(0, 1),
         outs_near=True,
-        flops=2 * share * n_half * (n_row * rows) ** 2 * n_col * cols,
+        flops=2 * share * n_half * (n_line * rows) ** 2 * n_col * cols,
         moved=8 * cells * hidden,
     )
     grad_right = exchange_all(grad_right).reshape(n_half, n_place, share, rows, cols)
     grad_left = call(
         grad_left_kernel,
         pieces_shape,
-        [vmem(n_row, n_col, share, rows, cols)],
+        [vmem(n_line, n_col, share, rows, cols)],
         (grad, right),
         near=(0, 1),
         outs_near=True,
-        flops=2 * share * n_half * (n_row * rows) ** 2 * n_col * cols,
+        flops=2 * share * n_half * (n_line * rows) ** 2 * n_col * cols,
         moved=8 * cells * hidden,
     )
     grad_left = exchange_pieces(tuple(grad_left))
     dzg = call(
-        back_left_kernel,
+        functools.partial(back_left_kernel, n_row),
         shape(rows, width, cols, dtype=F32),
         [coef_v, wide, proj_v, wide, plane, sems(1), sems(n_groups), sems(n_groups)],
         (coef, dzg, proj_weight, *grad_left),
-        near=tuple(range(3, 3 + n_place)),
+        near=tuple(range(3, 3 + n_pieces)),
         flops=2 * cells * width * 2 * hidden,
         moved=18 * cells * width,
     )
@@ -573,10 +629,12 @@
 def solution(mesh):
     n_grp, n_row, n_col = (mesh.shape[name] for name in ("grp", "row", "col"))
     n_half = math.gcd(n_row, 2)
+    n_core = math.gcd(n_row // n_half, 2)
     split = jax.sharding.Mesh(
-        mesh.devices.reshape(n_grp, n_half, n_row // n_half, n_col), ("grp", "half", "row", "col")
-    )
-    cells = P(("grp", "half", "row"), "col", None)
+        mesh.devices.reshape(n_grp, n_half, n_row // (n_half * n_core), n_core, n_col),
+        ("grp", "half", "row", "core", "col"),
+    )
+    cells = P(("grp", "half", "row", "core"), "col", None)
     return jax.shard_map(
         body,
         mesh=split,

time: 122 us -> 116 us (0.951)
  waiting for transfers between devices: 11.8 us -> 49.7 us
  blocking collectives: 25.3 us -> 0 us
  starting transfers between devices: 51.5 us -> 30 us
  Pallas kernels: 31 us -> 33.5 us
    ppermute x30 -> x12, starting transfers between devices: 39.4 us -> 11.8 us  [permute(): lax.ppermute(values, axes, [(at, at ^ distance) for at in range(size)])]
    ppermute x30 -> x12, waiting for transfers between devices: 11.8 us -> 39.4 us  [permute(): lax.ppermute(values, axes, [(at, at ^ distance) for at in range(size)])]
    all_to_all x2 -> x0, blocking collectives: 25.3 us -> none  [exchange(): lax.all_to_all(values, ('row', 'col'), split_axis=0, concat_axis=0, tiled...]
    all_to_all x2 -> x4, waiting for transfers between devices: 0.01 us -> 10.3 us  [the longest x2 10.3 us: exchange(): lax.all_to_all(values, within, split_axis=0, concat_axis=0, tiled=True)]
    all_to_all x2 -> x4, starting transfers between devices: 12 us -> 18.2 us  [the longest x2 11 us: exchange_all(): lax.all_to_all(flat, ('half', *within), split_axis=0, concat_axis=0, tile...]
    pallas_call x10 -> x11, Pallas kernels: 31 us -> 33.5 us  [call(): pl.pallas_call(kernel, out_shape=outs if outs_near else jax.tree.map(lamb...]
  transfers between devices with their start and end apart: 32 -> 16, of which waited for: 4 -> 11; matrix products, arithmetic and copies ran while one was open for 0% -> 0% of each run, Pallas kernels for 16% -> 18%
where the time goes in v5:
time: 116 us; the launch traced here: 115 us
  waiting for transfers between devices  49.7 us (43%)
  Pallas kernels  33.5 us (29%)
  starting transfers between devices  30 us (26%)
    ppermute x12, waiting for transfers between devices, permute(): lax.ppermute(values, axes, [(at, at ^ distance) for at in range(size)])  39.4 us
    pallas_call x11, Pallas kernels, call(): pl.pallas_call(kernel, out_shape=outs if outs_near else jax.tree.map(lamb...  33.5 us
    ppermute x12, starting transfers between devices, permute(): lax.ppermute(values, axes, [(at, at ^ distance) for at in range(size)])  11.8 us
    all_to_all x2, starting transfers between devices, exchange_all(): lax.all_to_all(flat, ('half', *within), split_axis=0, concat_axis=0, tile...  11 us
    all_to_all x2, waiting for transfers between devices, exchange(): lax.all_to_all(values, within, split_axis=0, concat_axis=0, tiled=True)  10.3 us
    all_to_all x2, starting transfers between devices, exchange(): lax.all_to_all(values, within, split_axis=0, concat_axis=0, tiled=True)  7.16 us
  transfers between devices with their start and end apart: 16, of which 11 were waited for; matrix products, arithmetic and copies ran while one was open for 0% of the time, Pallas kernels for 18%

profile of v5, /device:TPU:0, one launch (start us, length us, event | category | flops | bytes accessed | tf_op | source)
XLA Modules:
  0.0 115.5 jit_solution(11157706407860768117)
XLA Ops:
  0.6 4.4 %shard_map.113 = bf16[2,16,8,16,128]{4,3,2,1,0:T(8,128)(2,1)} custom-call(bf16[16,128,128]{2,1,0:T(8,128)(2,1)} %pair_h.5, s32[256]{0:T(256)} %mask_h.5, s32[1,256]{1,0:T(1,128)} %bitcast.23, f32[1,128]{1,0:T(1,128)} %bitcast.26, f32[1,128]{1,0:T(1,128)} %bitcast.31, bf16[128,512]{1,0:T(8,128)(2,1)} %proj_h.9), custom_call_target="tpu_custom_call" | custom-call | flops 201326592 | bytes 1310720 | tf_op jit(solution)/shard_map/pallas_call | solution.py:427
  5.0 7.3 %all-to-all-start = ((bf16[32,8,16,128]{3,2,1,0:T(8,128)(2,1)}), bf16[32,8,16,128]{3,2,1,0:T(8,128)(2,1)S(1)}, u32[]{:S(2)}, u32[]{:S(2)}) async-start(bf16[32,8,16,128]{3,2,1,0:T(8,128)(2,1)} %bitcast.3), calls=%async_computation | async-start | bytes 2097152 | tf_op jit(solution)/shard_map/all_to_all | solution.py:478
  12.3 3.4 %shard_map.115 = (bf16[4,8,16,128]{3,2,1,0:T(8,128)(2,1)S(1)}, bf16[4,8,16,128]{3,2,1,0:T(8,128)(2,1)S(1)}, bf16[4,8,16,128]{3,2,1,0:T(8,128)(2,1)S(1)}, bf16[4,8,16,128]{3,2,1,0:T(8,128)(2,1)S(1)}) custom-call(bf16[16,128,128]{2,1,0:T(8,128)(2,1)} %pair_h.5, s32[256]{0:T(256)} %mask_h.5, s32[1,256]{1,0:T(1,128)} %bitcast.24, f32[1,128]{1,0:T(1,128)} %bitcast.27, ...), custom_call_target="tpu_custom_call" | custom-call | flops 201326592 | bytes 1310720 | tf_op jit(solution)/shard_map/pallas_call | solution.py:427
  15.7 1.8 %collective-permute-start = (bf16[4,8,16,128]{3,2,1,0:T(8,128)(2,1)S(1)}, bf16[4,8,16,128]{3,2,1,0:T(8,128)(2,1)S(1)}, u32[]{:S(2)}, u32[]{:S(2)}) collective-permute-start(bf16[4,8,16,128]{3,2,1,0:T(8,128)(2,1)S(1)} %get-tuple-element.20), channel_id=1, source_target_pairs={{0,1},{1,0},{2,3},{3,2},{4,5},{5,4},{6,7},{7,6},{8,9},{9,8},{10,11... | collective-permute-start | bytes 393224 | tf_op jit(solution)/shard_map/ppermute | solution.py:483
  18.0 9.1 %collective-permute-done.refs_1_ = bf16[4,8,16,128]{3,2,1,0:T(8,128)(2,1)S(1)} collective-permute-done((bf16[4,8,16,128]{3,2,1,0:T(8,128)(2,1)S(1)}, bf16[4,8,16,128]{3,2,1,0:T(8,128)(2,1)S(1)}, u32[]{:S(2)}, u32[]{:S(2)}) %collective-permute-start) | collective-permute-done | bytes 131104 | tf_op jit(solution)/shard_map/ppermute | solution.py:483
  27.1 2.4 %collective-permute-done.2.refs_3_ = bf16[4,8,16,128]{3,2,1,0:T(8,128)(2,1)S(1)} collective-permute-done((bf16[4,8,16,128]{3,2,1,0:T(8,128)(2,1)S(1)}, bf16[4,8,16,128]{3,2,1,0:T(8,128)(2,1)S(1)}, u32[]{:S(2)}, u32[]{:S(2)}) %collective-permute-start.2) | collective-permute-done | bytes 131104 | tf_op jit(solution)/shard_map/ppermute | solution.py:483
  31.6 1.7 %collective-permute-start.5 = (bf16[4,8,16,128]{3,2,1,0:T(8,128)(2,1)S(1)}, bf16[4,8,16,128]{3,2,1,0:T(8,128)(2,1)S(1)}, u32[]{:S(2)}, u32[]{:S(2)}) collective-permute-start(bf16[4,8,16,128]{3,2,1,0:T(8,128)(2,1)S(1)} %pad_maximum_fusion.2), channel_id=1, source_target_pairs={{0,12},{4,8},{8,4},{12,0},{1,13},{5,9},{9,5},{13,1},{2,14},{6,10},... | collective-permute-start | bytes 393224 | tf_op jit(solution)/shard_map/ppermute | solution.py:483
  33.2 4.9 %shard_map.114 = (f32[16,128,128]{2,1,0:T(8,128)}, f32[16,128]{1,0:T(8,128)}, f32[16,128,128]{2,1,0:T(8,128)}, f32[2048,128]{1,0:T(8,128)}) custom-call(bf16[16,128,128]{2,1,0:T(8,128)(2,1)} %pair_h.5, bf16[16,128,128]{2,1,0:T(8,128)(2,1)} %cot_h.3, f32[1,128]{1,0:T(1,128)} %bitcast.28, f32[1,128]{1,0:T(1,128)} %bitcast.33, bf16[128,128]{1,0:T(8,128)(2,1)} %gate_w_h.1, ...), custom_call_target="tpu_custom_call" | custom-call | flops 268435456 | bytes 4194304 | tf_op jit(solution)/shard_map/pallas_call | solution.py:427
  39.2 3.3 %collective-permute-done.5.refs_6_ = bf16[4,8,16,128]{3,2,1,0:T(8,128)(2,1)S(1)} collective-permute-done((bf16[4,8,16,128]{3,2,1,0:T(8,128)(2,1)S(1)}, bf16[4,8,16,128]{3,2,1,0:T(8,128)(2,1)S(1)}, u32[]{:S(2)}, u32[]{:S(2)}) %collective-permute-start.5) | collective-permute-done | bytes 131104 | tf_op jit(solution)/shard_map/ppermute | solution.py:483
  43.8 3.6 %all-to-all-start.1 = ((bf16[16,8,16,128]{3,2,1,0:T(8,128)(2,1)}), bf16[16,8,16,128]{3,2,1,0:T(8,128)(2,1)S(1)}, u32[]{:S(2)}, u32[]{:S(2)}) async-start(bf16[16,8,16,128]{3,2,1,0:T(8,128)(2,1)} %bitcast.6), calls=%async_computation.1 | async-start | bytes 1048576 | tf_op jit(solution)/shard_map/all_to_all | solution.py:474
  47.4 3.8 %shard_map.117.after.coef_h = f32[16,4,128,128]{3,2,1,0:T(8,128)} custom-call(f32[16,128,128]{2,1,0:T(8,128)} %get-tuple-element.26.zhat_h, s32[256]{0:T(256)} %mask_h.5, s32[1,256]{1,0:T(1,128)} %bitcast.25, f32[1,128]{1,0:T(1,128)} %bitcast.29, f32[1,128]{1,0:T(1,128)} %bitcast.34, bf16[128,512]{1,0:T(8,128)(2,1)} %proj_h.9, ...), custom_call_target="tpu_custom_call" | custom-call | flops 335544320 | bytes 5242880 | tf_op jit(solution)/shard_map/pallas_call | solution.py:427
  51.2 5.3 %all-to-all-done.1 = bf16[16,8,16,128]{3,2,1,0:T(8,128)(2,1)S(1)} async-done(((bf16[16,8,16,128]{3,2,1,0:T(8,128)(2,1)}), bf16[16,8,16,128]{3,2,1,0:T(8,128)(2,1)S(1)}, u32[]{:S(2)}, u32[]{:S(2)}) %all-to-all-start.1) | async-done | bytes 524320 | tf_op jit(solution)/shard_map/all_to_all | solution.py:474
  56.5 2.3 %shard_map.118.after = bf16[128,16,128]{2,1,0:T(8,128)(2,1)} custom-call(bf16[128,16,128]{2,1,0:T(8,128)(2,1)S(1)} %bitcast.16, f32[128,16,128]{2,1,0:T(8,128)} %bitcast.22, f32[16,4,128,128]{3,2,1,0:T(8,128)} %shard_map.117.after.coef_h), custom_call_target="tpu_custom_call" | custom-call | flops 5242880 | bytes 2097152 | tf_op jit(solution)/shard_map/pallas_call | solution.py:427
  58.8 3.6 %all-to-all-start.2 = ((bf16[16,8,16,128]{3,2,1,0:T(8,128)(2,1)}), bf16[16,8,16,128]{3,2,1,0:T(8,128)(2,1)S(1)}, u32[]{:S(2)}, u32[]{:S(2)}) async-start(bf16[16,8,16,128]{3,2,1,0:T(8,128)(2,1)} %bitcast.10), calls=%async_computation.2 | async-start | bytes 1048576 | tf_op jit(solution)/shard_map/all_to_all | solution.py:474
  62.4 4.1 %shard_map.119 = (bf16[16,128,128]{2,1,0:T(8,128)(2,1)}, f32[16,128,128]{2,1,0:T(8,128)}) custom-call(bf16[128,16,128]{2,1,0:T(8,128)(2,1)S(1)} %bitcast.17, f32[16,128,128]{2,1,0:T(8,128)} %get-tuple-element.24.gate_h, bf16[16,128,128]{2,1,0:T(8,128)(2,1)} %cot_h.3, f32[1,128]{1,0:T(1,128)} %bitcast.36, f32[1,128]{1,0:T(1,128)} %bitcast.37, ...), custom_call_target="tpu_custom_call" | custom-call | flops 201326592 | bytes 3670016 | tf_op jit(solution)/shard_map/pallas_call | solution.py:427
  66.6 5.0 %all-to-all-done.2 = bf16[16,8,16,128]{3,2,1,0:T(8,128)(2,1)S(1)} async-done(((bf16[16,8,16,128]{3,2,1,0:T(8,128)(2,1)}), bf16[16,8,16,128]{3,2,1,0:T(8,128)(2,1)S(1)}, u32[]{:S(2)}, u32[]{:S(2)}) %all-to-all-start.2) | async-done | bytes 524320 | tf_op jit(solution)/shard_map/all_to_all | solution.py:474
  73.1 3.7 %all-to-all-start.3 = ((bf16[32,8,16,128]{3,2,1,0:T(8,128)(2,1)}), bf16[32,8,16,128]{3,2,1,0:T(8,128)(2,1)S(1)}, u32[]{:S(2)}, u32[]{:S(2)}) async-start(bf16[32,8,16,128]{3,2,1,0:T(8,128)(2,1)} %bitcast.21), calls=%async_computation.3 | async-start | bytes 2097152 | tf_op jit(solution)/shard_map/all_to_all | solution.py:478
  79.5 12.0 %collective-permute-done.6.refs_1_ = bf16[4,8,16,128]{3,2,1,0:T(8,128)(2,1)S(1)} collective-permute-done((bf16[4,8,16,128]{3,2,1,0:T(8,128)(2,1)S(1)}, bf16[4,8,16,128]{3,2,1,0:T(8,128)(2,1)S(1)}, u32[]{:S(2)}, u32[]{:S(2)}) %collective-permute-start.6) | collective-permute-done | bytes 131104 | tf_op jit(solution)/shard_map/ppermute | solution.py:483
  91.5 2.4 %collective-permute-done.8.refs_3_ = bf16[4,8,16,128]{3,2,1,0:T(8,128)(2,1)S(1)} collective-permute-done((bf16[4,8,16,128]{3,2,1,0:T(8,128)(2,1)S(1)}, bf16[4,8,16,128]{3,2,1,0:T(8,128)(2,1)S(1)}, u32[]{:S(2)}, u32[]{:S(2)}) %collective-permute-start.8) | collective-permute-done | bytes 131104 | tf_op jit(solution)/shard_map/ppermute | solution.py:483
  97.6 3.7 %collective-permute-done.9.refs_4_ = bf16[4,8,16,128]{3,2,1,0:T(8,128)(2,1)S(1)} collective-permute-done((bf16[4,8,16,128]{3,2,1,0:T(8,128)(2,1)S(1)}, bf16[4,8,16,128]{3,2,1,0:T(8,128)(2,1)S(1)}, u32[]{:S(2)}, u32[]{:S(2)}) %collective-permute-start.9) | collective-permute-done | bytes 131104 | tf_op jit(solution)/shard_map/ppermute | solution.py:483
  101.3 2.2 %collective-permute-done.10.refs_5_ = bf16[4,8,16,128]{3,2,1,0:T(8,128)(2,1)S(1)} collective-permute-done((bf16[4,8,16,128]{3,2,1,0:T(8,128)(2,1)S(1)}, bf16[4,8,16,128]{3,2,1,0:T(8,128)(2,1)S(1)}, u32[]{:S(2)}, u32[]{:S(2)}) %collective-permute-start.10) | collective-permute-done | bytes 131104 | tf_op jit(solution)/shard_map/ppermute | solution.py:483
  103.5 3.3 %collective-permute-done.11.refs_6_ = bf16[4,8,16,128]{3,2,1,0:T(8,128)(2,1)S(1)} collective-permute-done((bf16[4,8,16,128]{3,2,1,0:T(8,128)(2,1)S(1)}, bf16[4,8,16,128]{3,2,1,0:T(8,128)(2,1)S(1)}, u32[]{:S(2)}, u32[]{:S(2)}) %collective-permute-start.11) | collective-permute-done | bytes 131104 | tf_op jit(solution)/shard_map/ppermute | solution.py:483
  106.9 3.8 %shard_map.122.dzg_h = f32[16,128,128]{2,1,0:T(8,128)} custom-call(f32[16,4,128,128]{3,2,1,0:T(8,128)} %shard_map.117.after.coef_h, f32[16,128,128]{2,1,0:T(8,128)} %get-tuple-element.29.after.dzg_h, bf16[128,512]{1,0:T(8,128)(2,1)} %proj_h.9, bf16[4,8,16,128]{3,2,1,0:T(8,128)(2,1)S(1)} %get-tuple-element.30.refs_0_, ...), custom_call_target="tpu_custom_call" | custom-call | flops 134217728 | bytes 4718592 | tf_op jit(solution)/shard_map/pallas_call | solution.py:427
  110.7 4.6 %shard_map.123 = bf16[16,128,128]{2,1,0:T(8,128)(2,1)} custom-call(bf16[2,16,8,16,128]{4,3,2,1,0:T(8,128)(2,1)S(1)} %bitcast.20, f32[16,4,128,128]{3,2,1,0:T(8,128)} %shard_map.117.after.coef_h, f32[16,128,128]{2,1,0:T(8,128)} %get-tuple-element.26.zhat_h, f32[16,128]{1,0:T(8,128)} %get-tuple-element.18.after.inv_h, f32[16,128,128]{2,1,0:T(8,128)} %shard_map.122.dzg_h, ...), custom_call_target="tpu_custom_call" | custom-call | flops 201326592 | bytes 5767168 | tf_op jit(solution)/shard_map/pallas_call | solution.py:427
  (35 shorter events, 12.7 us)
Async XLA Ops:
  5.0 37.5 %all-to-all-start = ((bf16[32,8,16,128]{3,2,1,0:T(8,128)(2,1)}), bf16[32,8,16,128]{3,2,1,0:T(8,128)(2,1)S(1)}, u32[]{:S(2)}, u32[]{:S(2)}) async-start(bf16[32,8,16,128]{3,2,1,0:T(8,128)(2,1)} %bitcast.3), calls=%async_computation | async-start | bytes 2097152 | tf_op jit(solution)/shard_map/all_to_all | solution.py:478
  15.7 11.3 %collective-permute-start = (bf16[4,8,16,128]{3,2,1,0:T(8,128)(2,1)S(1)}, bf16[4,8,16,128]{3,2,1,0:T(8,128)(2,1)S(1)}, u32[]{:S(2)}, u32[]{:S(2)}) collective-permute-start(bf16[4,8,16,128]{3,2,1,0:T(8,128)(2,1)S(1)} %get-tuple-element.20), channel_id=1, source_target_pairs={{0,1},{1,0},{2,3},{3,2},{4,5},{5,4},{6,7},{7,6},{8,9},{9,8},{10,11... | collective-permute-start | bytes 393224 | tf_op jit(solution)/shard_map/ppermute | solution.py:483
  17.6 9.5 %collective-permute-start.1 = (bf16[4,8,16,128]{3,2,1,0:T(8,128)(2,1)S(1)}, bf16[4,8,16,128]{3,2,1,0:T(8,128)(2,1)S(1)}, u32[]{:S(2)}, u32[]{:S(2)}) collective-permute-start(bf16[4,8,16,128]{3,2,1,0:T(8,128)(2,1)S(1)} %get-tuple-element.21), channel_id=1, source_target_pairs={{0,2},{1,3},{2,0},{3,1},{4,6},{5,7},{6,4},{7,5},{8,10},{9,11},{10,... | collective-permute-start | bytes 393224 | tf_op jit(solution)/shard_map/ppermute | solution.py:483
  17.6 11.9 %collective-permute-start.2 = (bf16[4,8,16,128]{3,2,1,0:T(8,128)(2,1)S(1)}, bf16[4,8,16,128]{3,2,1,0:T(8,128)(2,1)S(1)}, u32[]{:S(2)}, u32[]{:S(2)}) collective-permute-start(bf16[4,8,16,128]{3,2,1,0:T(8,128)(2,1)S(1)} %get-tuple-element.22), channel_id=1, source_target_pairs={{0,3},{1,2},{2,1},{3,0},{4,7},{5,6},{6,5},{7,4},{8,11},{9,10},{10,... | collective-permute-start | bytes 393224 | tf_op jit(solution)/shard_map/ppermute | solution.py:483
  29.5 8.7 %collective-permute-start.3 = (bf16[4,8,16,128]{3,2,1,0:T(8,128)(2,1)S(1)}, bf16[4,8,16,128]{3,2,1,0:T(8,128)(2,1)S(1)}, u32[]{:S(2)}, u32[]{:S(2)}) collective-permute-start(bf16[4,8,16,128]{3,2,1,0:T(8,128)(2,1)S(1)} %pad_maximum_fusion), channel_id=1, source_target_pairs={{0,4},{4,0},{8,12},{12,8},{1,5},{5,1},{9,13},{13,9},{2,6},{6,2},{1... | collective-permute-start | bytes 393224 | tf_op jit(solution)/shard_map/ppermute | solution.py:483
  30.2 8.9 %collective-permute-start.4 = (bf16[4,8,16,128]{3,2,1,0:T(8,128)(2,1)S(1)}, bf16[4,8,16,128]{3,2,1,0:T(8,128)(2,1)S(1)}, u32[]{:S(2)}, u32[]{:S(2)}) collective-permute-start(bf16[4,8,16,128]{3,2,1,0:T(8,128)(2,1)S(1)} %pad_maximum_fusion.1), channel_id=1, source_target_pairs={{0,8},{4,12},{8,0},{12,4},{1,9},{5,13},{9,1},{13,5},{2,10},{6,14},... | collective-permute-start | bytes 393224 | tf_op jit(solution)/shard_map/ppermute | solution.py:483
  31.6 11.0 %collective-permute-start.5 = (bf16[4,8,16,128]{3,2,1,0:T(8,128)(2,1)S(1)}, bf16[4,8,16,128]{3,2,1,0:T(8,128)(2,1)S(1)}, u32[]{:S(2)}, u32[]{:S(2)}) collective-permute-start(bf16[4,8,16,128]{3,2,1,0:T(8,128)(2,1)S(1)} %pad_maximum_fusion.2), channel_id=1, source_target_pairs={{0,12},{4,8},{8,4},{12,0},{1,13},{5,9},{9,5},{13,1},{2,14},{6,10},... | collective-permute-start | bytes 393224 | tf_op jit(solution)/shard_map/ppermute | solution.py:483
  43.8 12.7 %all-to-all-start.1 = ((bf16[16,8,16,128]{3,2,1,0:T(8,128)(2,1)}), bf16[16,8,16,128]{3,2,1,0:T(8,128)(2,1)S(1)}, u32[]{:S(2)}, u32[]{:S(2)}) async-start(bf16[16,8,16,128]{3,2,1,0:T(8,128)(2,1)} %bitcast.6), calls=%async_computation.1 | async-start | bytes 1048576 | tf_op jit(solution)/shard_map/all_to_all | solution.py:474
  58.8 12.7 %all-to-all-start.2 = ((bf16[16,8,16,128]{3,2,1,0:T(8,128)(2,1)}), bf16[16,8,16,128]{3,2,1,0:T(8,128)(2,1)S(1)}, u32[]{:S(2)}, u32[]{:S(2)}) async-start(bf16[16,8,16,128]{3,2,1,0:T(8,128)(2,1)} %bitcast.10), calls=%async_computation.2 | async-start | bytes 1048576 | tf_op jit(solution)/shard_map/all_to_all | solution.py:474
  72.0 1.1 copy-start
  73.1 37.6 %all-to-all-start.3 = ((bf16[32,8,16,128]{3,2,1,0:T(8,128)(2,1)}), bf16[32,8,16,128]{3,2,1,0:T(8,128)(2,1)S(1)}, u32[]{:S(2)}, u32[]{:S(2)}) async-start(bf16[32,8,16,128]{3,2,1,0:T(8,128)(2,1)} %bitcast.21), calls=%async_computation.3 | async-start | bytes 2097152 | tf_op jit(solution)/shard_map/all_to_all | solution.py:478
  77.2 14.2 %collective-permute-start.6 = (bf16[4,8,16,128]{3,2,1,0:T(8,128)(2,1)S(1)}, bf16[4,8,16,128]{3,2,1,0:T(8,128)(2,1)S(1)}, u32[]{:S(2)}, u32[]{:S(2)}) collective-permute-start(bf16[4,8,16,128]{3,2,1,0:T(8,128)(2,1)S(1)} %get-tuple-element.31), channel_id=1, source_target_pairs={{0,1},{1,0},{2,3},{3,2},{4,5},{5,4},{6,7},{7,6},{8,9},{9,8},{10,11... | collective-permute-start | bytes 393224 | tf_op jit(solution)/shard_map/ppermute | solution.py:483
  78.9 12.5 %collective-permute-start.7 = (bf16[4,8,16,128]{3,2,1,0:T(8,128)(2,1)S(1)}, bf16[4,8,16,128]{3,2,1,0:T(8,128)(2,1)S(1)}, u32[]{:S(2)}, u32[]{:S(2)}) collective-permute-start(bf16[4,8,16,128]{3,2,1,0:T(8,128)(2,1)S(1)} %get-tuple-element.32), channel_id=1, source_target_pairs={{0,2},{1,3},{2,0},{3,1},{4,6},{5,7},{6,4},{7,5},{8,10},{9,11},{10,... | collective-permute-start | bytes 393224 | tf_op jit(solution)/shard_map/ppermute | solution.py:483
  78.9 14.9 %collective-permute-start.8 = (bf16[4,8,16,128]{3,2,1,0:T(8,128)(2,1)S(1)}, bf16[4,8,16,128]{3,2,1,0:T(8,128)(2,1)S(1)}, u32[]{:S(2)}, u32[]{:S(2)}) collective-permute-start(bf16[4,8,16,128]{3,2,1,0:T(8,128)(2,1)S(1)} %get-tuple-element.33), channel_id=1, source_target_pairs={{0,3},{1,2},{2,1},{3,0},{4,7},{5,6},{6,5},{7,4},{8,11},{9,10},{10,... | collective-permute-start | bytes 393224 | tf_op jit(solution)/shard_map/ppermute | solution.py:483
  93.9 7.5 %collective-permute-start.9 = (bf16[4,8,16,128]{3,2,1,0:T(8,128)(2,1)S(1)}, bf16[4,8,16,128]{3,2,1,0:T(8,128)(2,1)S(1)}, u32[]{:S(2)}, u32[]{:S(2)}) collective-permute-start(bf16[4,8,16,128]{3,2,1,0:T(8,128)(2,1)S(1)} %pad_maximum_fusion.3), channel_id=1, source_target_pairs={{0,4},{4,0},{8,12},{12,8},{1,5},{5,1},{9,13},{13,9},{2,6},{6,2},{1... | collective-permute-start | bytes 393224 | tf_op jit(solution)/shard_map/ppermute | solution.py:483
  94.6 8.9 %collective-permute-start.10 = (bf16[4,8,16,128]{3,2,1,0:T(8,128)(2,1)S(1)}, bf16[4,8,16,128]{3,2,1,0:T(8,128)(2,1)S(1)}, u32[]{:S(2)}, u32[]{:S(2)}) collective-permute-start(bf16[4,8,16,128]{3,2,1,0:T(8,128)(2,1)S(1)} %pad_maximum_fusion.4), channel_id=1, source_target_pairs={{0,8},{4,12},{8,0},{12,4},{1,9},{5,13},{9,1},{13,5},{2,10},{6,14},... | collective-permute-start | bytes 393224 | tf_op jit(solution)/shard_map/ppermute | solution.py:483
  95.9 11.0 %collective-permute-start.11 = (bf16[4,8,16,128]{3,2,1,0:T(8,128)(2,1)S(1)}, bf16[4,8,16,128]{3,2,1,0:T(8,128)(2,1)S(1)}, u32[]{:S(2)}, u32[]{:S(2)}) collective-permute-start(bf16[4,8,16,128]{3,2,1,0:T(8,128)(2,1)S(1)} %pad_maximum_fusion.5), channel_id=1, source_target_pairs={{0,12},{4,8},{8,4},{12,0},{1,13},{5,9},{9,5},{13,1},{2,14},{6,10},... | collective-permute-start | bytes 393224 | tf_op jit(solution)/shard_map/ppermute | solution.py:483

commit v6 on v5

--- a/solution.py
+++ b/solution.py
@@ -87,17 +87,24 @@
     )
 
 
-def sources(n_row, n_quad):
-    row = lax.axis_index("row")
-    quad = lax.axis_index("core") * lax.axis_size("col") + lax.axis_index("col")
-    return [(m, n, (row ^ n) * n_quad + (quad ^ m)) for m in range(n_quad) for n in range(n_row)]
-
-
-def received(refs, n_row):
-    n_quad = len(refs) - n_row + 1
+def sources(n_chip, n_core):
+    n_col = lax.axis_size("col")
+    core = lax.axis_index("core")
+    chip = lax.axis_index("row") * n_col + lax.axis_index("col")
+    found = []
+    for n in range(n_chip):
+        other = chip ^ n
+        for m in range(n_core):
+            line = other // n_col * n_core + (core ^ m)
+            found.append((m, n, line * n_col + other % n_col))
+    return found
+
+
+def received(refs, n_chip):
+    n_core = len(refs) - n_chip + 1
     return [
-        (number, refs[m][0] if n == 0 else refs[n_quad + n - 1][m])
-        for m, n, number in sources(n_row, n_quad)
+        (number, refs[m][0] if n == 0 else refs[n_core + n - 1][m])
+        for m, n, number in sources(n_chip, n_core)
     ]
 
 
@@ -138,9 +145,9 @@
 
 
 def give_pieces(plane, outs):
-    n_row = outs[0].shape[0]
-    length = plane.shape[0] // (len(outs) * n_row)
-    for m, n, number in sources(n_row, len(outs)):
+    n_chip = outs[0].shape[0]
+    length = plane.shape[0] // (len(outs) * n_chip)
+    for m, n, number in sources(n_chip, len(outs)):
         first = pl.multiple_of(number * length, length)
         values = plane[pl.ds(first, length), :]
         outs[m][n] = values.reshape(outs[m].shape[1:]).astype(BF16)
@@ -245,10 +252,10 @@
         ref[(*lead, c, at)] = values[:, c * cols : (c + 1) * cols].reshape(*shape, rows, cols)
 
 
-def product_kernel(n_row, right, after, *refs):
+def product_kernel(n_chip, right, after, *refs):
     pieces, (out, left) = refs[:-2], refs[-2:]
     n_col, share = left.shape[1:3]
-    for number, piece in received(pieces, n_row):
+    for number, piece in received(pieces, n_chip):
         left[number // n_col, number % n_col] = piece
     for h in range(share):
         put_channel(out, h, dot(channel_matrix(left, h), channel_matrix(right, h), ((1,), (1,))))
@@ -334,7 +341,7 @@
     return dot(weight, jnp.concatenate(columns, axis=1))
 
 
-def back_left_kernel(n_row, coef_h, dzg_h, proj_h, *refs):
+def back_left_kernel(n_chip, coef_h, dzg_h, proj_h, *refs):
     pieces, out_h = refs[:-9], refs[-9]
     coef, dzg, proj_weight, out, plane, sems, coef_sems, dzg_sems = refs[-8:]
     rows, width, cols = out.shape
@@ -354,7 +361,7 @@
             [(dzg_h.at[pl.ds(at, size)], dzg.at[pl.ds(at, size)]) for at, size in groups],
         ),
     ]
-    arrived = received(pieces, n_row)
+    arrived = received(pieces, n_chip)
     length = plane.shape[0] // len(arrived)
     for number, piece in arrived:
         first = pl.multiple_of(number * length, length)
@@ -450,7 +457,7 @@
     n_row = lax.axis_size("row")
     n_core = lax.axis_size("core")
     n_col = lax.axis_size("col")
-    n_quad = n_core * n_col
+    n_chip = n_row * n_col
     n_line = n_row * n_core
     n_place = n_line * n_col
     within = ("row", "core", "col")
@@ -484,10 +491,10 @@
 
     def exchange_pieces(pieces):
         first = [pieces[0]]
-        first += [permute(pieces[m], ("core", "col"), n_quad, m) for m in range(1, n_quad)]
+        first += [permute(pieces[m], ("core",), n_core, m) for m in range(1, n_core)]
         second = [
-            permute(jnp.stack([piece[n] for piece in first]), ("row",), n_row, n)
-            for n in range(1, n_row)
+            permute(jnp.stack([piece[n] for piece in first]), ("row", "col"), n_chip, n)
+            for n in range(1, n_chip)
         ]
         return tuple(first + second)
 
@@ -500,8 +507,8 @@
     square = vmem(width, hidden)
     proj_v = vmem(width, 4 * hidden)
     coef_v = vmem(rows, 2, hidden, cols, dtype=F32)
-    pieces_shape = (shape(n_row, share, rows, cols),) * n_quad
-    n_pieces = n_quad + n_row - 1
+    pieces_shape = (shape(n_chip, share, rows, cols),) * n_core
+    n_pieces = n_core + n_chip - 1
 
     def front(part, outs):
         return call(
@@ -534,7 +541,7 @@
         moved=16 * cells * width,
     )
     product, left = call(
-        functools.partial(product_kernel, n_row),
+        functools.partial(product_kernel, n_chip),
         (shape(n_line, n_col, share, rows, cols), shape(n_line, n_col, share, rows, cols)),
         [],
         (right, inv, *left),
@@ -603,7 +610,7 @@
     )
     grad_left = exchange_pieces(tuple(grad_left))
     dzg = call(
-        functools.partial(back_left_kernel, n_row),
+        functools.partial(back_left_kernel, n_chip),
         shape(rows, width, cols, dtype=F32),
         [coef_v, wide, proj_v, wide, plane, sems(1), sems(n_groups), sems(n_groups)],
         (coef, dzg, proj_weight, *grad_left),

time: 116 us -> 109 us (0.940)
  waiting for transfers between devices: 49.7 us -> 35.2 us
  starting transfers between devices: 30 us -> 38 us
    ppermute x12 -> x16, waiting for transfers between devices: 39.4 us -> 24.8 us  [permute(): lax.ppermute(values, axes, [(at, at ^ distance) for at in range(size)])]
    ppermute x12 -> x16, starting transfers between devices: 11.8 us -> 18.8 us  [permute(): lax.ppermute(values, axes, [(at, at ^ distance) for at in range(size)])]
  transfers between devices with their start and end apart: 16 -> 20, of which waited for: 11 -> 14; matrix products, arithmetic and copies ran while one was open for 0% -> 0% of each run, Pallas kernels for 18% -> 19%
where the time goes in v6:
time: 109 us
  starting transfers between devices  38 us (35%)
  waiting for transfers between devices  35.2 us (32%)
  Pallas kernels  33.3 us (31%)
  local copies, waits for them, and re-layouts  1.14 us (1%)
    pallas_call x11, Pallas kernels, call(): pl.pallas_call(kernel, out_shape=outs if outs_near else jax.tree.map(lamb...  33.3 us
    ppermute x16, waiting for transfers between devices, permute(): lax.ppermute(values, axes, [(at, at ^ distance) for at in range(size)])  24.8 us
    ppermute x16, starting transfers between devices, permute(): lax.ppermute(values, axes, [(at, at ^ distance) for at in range(size)])  18.8 us
    all_to_all x2, starting transfers between devices, exchange_all(): lax.all_to_all(flat, ('half', *within), split_axis=0, concat_axis=0, tile...  11.6 us
    all_to_all x2, waiting for transfers between devices, exchange(): lax.all_to_all(values, within, split_axis=0, concat_axis=0, tiled=True)  10.4 us
    all_to_all x2, starting transfers between devices, exchange(): lax.all_to_all(values, within, split_axis=0, concat_axis=0, tiled=True)  7.51 us
  transfers between devices with their start and end apart: 20, of which 14 were waited for; matrix products, arithmetic and copies ran while one was open for 0% of the time, Pallas kernels for 19%

profile of v6, /device:TPU:0, one launch (start us, length us, event | category | flops | bytes accessed | tf_op | source)
XLA Modules:
  0.0 108.8 jit_solution(15613843663727036497)
XLA Ops:
  0.6 4.4 %shard_map.113 = bf16[2,16,8,16,128]{4,3,2,1,0:T(8,128)(2,1)} custom-call(bf16[16,128,128]{2,1,0:T(8,128)(2,1)} %pair_h.5, s32[256]{0:T(256)} %mask_h.5, s32[1,256]{1,0:T(1,128)} %bitcast.23, f32[1,128]{1,0:T(1,128)} %bitcast.26, f32[1,128]{1,0:T(1,128)} %bitcast.31, bf16[128,512]{1,0:T(8,128)(2,1)} %proj_h.9), custom_call_target="tpu_custom_call" | custom-call | flops 201326592 | bytes 1310720 | tf_op jit(solution)/shard_map/pallas_call | solution.py:434
  5.0 7.3 %all-to-all-start = ((bf16[32,8,16,128]{3,2,1,0:T(8,128)(2,1)}), bf16[32,8,16,128]{3,2,1,0:T(8,128)(2,1)S(1)}, u32[]{:S(2)}, u32[]{:S(2)}) async-start(bf16[32,8,16,128]{3,2,1,0:T(8,128)(2,1)} %bitcast.3), calls=%async_computation | async-start | bytes 2097152 | tf_op jit(solution)/shard_map/all_to_all | solution.py:485
  12.3 3.4 %shard_map.115 = (bf16[8,8,16,128]{3,2,1,0:T(8,128)(2,1)S(1)}, bf16[8,8,16,128]{3,2,1,0:T(8,128)(2,1)S(1)}) custom-call(bf16[16,128,128]{2,1,0:T(8,128)(2,1)} %pair_h.5, s32[256]{0:T(256)} %mask_h.5, s32[1,256]{1,0:T(1,128)} %bitcast.24, f32[1,128]{1,0:T(1,128)} %bitcast.27, f32[1,128]{1,0:T(1,128)} %bitcast.32, bf16[128,512]{1,0:T(8,128)(2,1)} %proj_h.9), custom_call_target="tpu_custom_call" | custom-call | flops 201326592 | bytes 1310720 | tf_op jit(solution)/shard_map/pallas_call | solution.py:434
  17.4 1.8 %collective-permute-start.1 = (bf16[2,8,16,128]{3,2,1,0:T(8,128)(2,1)S(1)}, bf16[2,8,16,128]{3,2,1,0:T(8,128)(2,1)S(1)}, u32[]{:S(2)}, u32[]{:S(2)}) collective-permute-start(bf16[2,8,16,128]{3,2,1,0:T(8,128)(2,1)S(1)} %pad_maximum_fusion), channel_id=1, source_target_pairs={{0,1},{1,0},{4,5},{5,4},{8,9},{9,8},{12,13},{13,12},{2,3},{3,2},{6... | collective-permute-start | bytes 196616 | tf_op jit(solution)/shard_map/ppermute | solution.py:490
  21.1 1.8 %collective-permute-start.4 = (bf16[2,8,16,128]{3,2,1,0:T(8,128)(2,1)S(1)}, bf16[2,8,16,128]{3,2,1,0:T(8,128)(2,1)S(1)}, u32[]{:S(2)}, u32[]{:S(2)}) collective-permute-start(bf16[2,8,16,128]{3,2,1,0:T(8,128)(2,1)S(1)} %pad_maximum_fusion.3), channel_id=1, source_target_pairs={{0,8},{1,9},{4,12},{5,13},{8,0},{9,1},{12,4},{13,5},{2,10},{3,11},... | collective-permute-start | bytes 196616 | tf_op jit(solution)/shard_map/ppermute | solution.py:490
  24.5 2.4 %collective-permute-start.6 = (bf16[2,8,16,128]{3,2,1,0:T(8,128)(2,1)S(1)}, bf16[2,8,16,128]{3,2,1,0:T(8,128)(2,1)S(1)}, u32[]{:S(2)}, u32[]{:S(2)}) collective-permute-start(bf16[2,8,16,128]{3,2,1,0:T(8,128)(2,1)S(1)} %pad_maximum_fusion.5), channel_id=1, source_target_pairs={{0,12},{1,13},{4,8},{5,9},{8,4},{9,5},{12,0},{13,1},{2,14},{3,15},... | collective-permute-start | bytes 196616 | tf_op jit(solution)/shard_map/ppermute | solution.py:490
  28.1 4.9 %shard_map.114 = (f32[16,128,128]{2,1,0:T(8,128)}, f32[16,128]{1,0:T(8,128)}, f32[16,128,128]{2,1,0:T(8,128)}, f32[2048,128]{1,0:T(8,128)}) custom-call(bf16[16,128,128]{2,1,0:T(8,128)(2,1)} %pair_h.5, bf16[16,128,128]{2,1,0:T(8,128)(2,1)} %cot_h.3, f32[1,128]{1,0:T(1,128)} %bitcast.28, f32[1,128]{1,0:T(1,128)} %bitcast.33, bf16[128,128]{1,0:T(8,128)(2,1)} %gate_w_h.1, ...), custom_call_target="tpu_custom_call" | custom-call | flops 268435456 | bytes 4194304 | tf_op jit(solution)/shard_map/pallas_call | solution.py:434
  33.2 2.7 %collective-permute-done.6.refs_7_ = bf16[2,8,16,128]{3,2,1,0:T(8,128)(2,1)S(1)} collective-permute-done((bf16[2,8,16,128]{3,2,1,0:T(8,128)(2,1)S(1)}, bf16[2,8,16,128]{3,2,1,0:T(8,128)(2,1)S(1)}, u32[]{:S(2)}, u32[]{:S(2)}) %collective-permute-start.6) | collective-permute-done | bytes 65568 | tf_op jit(solution)/shard_map/ppermute | solution.py:490
  35.9 2.9 %collective-permute-done.7.refs_8_ = bf16[2,8,16,128]{3,2,1,0:T(8,128)(2,1)S(1)} collective-permute-done((bf16[2,8,16,128]{3,2,1,0:T(8,128)(2,1)S(1)}, bf16[2,8,16,128]{3,2,1,0:T(8,128)(2,1)S(1)}, u32[]{:S(2)}, u32[]{:S(2)}) %collective-permute-start.7) | collective-permute-done | bytes 65568 | tf_op jit(solution)/shard_map/ppermute | solution.py:490
  40.1 3.9 %all-to-all-start.1 = ((bf16[16,8,16,128]{3,2,1,0:T(8,128)(2,1)}), bf16[16,8,16,128]{3,2,1,0:T(8,128)(2,1)S(1)}, u32[]{:S(2)}, u32[]{:S(2)}) async-start(bf16[16,8,16,128]{3,2,1,0:T(8,128)(2,1)} %bitcast.6), calls=%async_computation.1 | async-start | bytes 1048576 | tf_op jit(solution)/shard_map/all_to_all | solution.py:481
  44.1 3.8 %shard_map.117.after.coef_h = f32[16,4,128,128]{3,2,1,0:T(8,128)} custom-call(f32[16,128,128]{2,1,0:T(8,128)} %get-tuple-element.20.zhat_h, s32[256]{0:T(256)} %mask_h.5, s32[1,256]{1,0:T(1,128)} %bitcast.25, f32[1,128]{1,0:T(1,128)} %bitcast.29, f32[1,128]{1,0:T(1,128)} %bitcast.34, bf16[128,512]{1,0:T(8,128)(2,1)} %proj_h.9, ...), custom_call_target="tpu_custom_call" | custom-call | flops 335544320 | bytes 5242880 | tf_op jit(solution)/shard_map/pallas_call | solution.py:434
  47.9 5.4 %all-to-all-done.1 = bf16[16,8,16,128]{3,2,1,0:T(8,128)(2,1)S(1)} async-done(((bf16[16,8,16,128]{3,2,1,0:T(8,128)(2,1)}), bf16[16,8,16,128]{3,2,1,0:T(8,128)(2,1)S(1)}, u32[]{:S(2)}, u32[]{:S(2)}) %all-to-all-start.1) | async-done | bytes 524320 | tf_op jit(solution)/shard_map/all_to_all | solution.py:481
  53.2 2.3 %shard_map.118.after = bf16[128,16,128]{2,1,0:T(8,128)(2,1)} custom-call(bf16[128,16,128]{2,1,0:T(8,128)(2,1)S(1)} %bitcast.16, f32[128,16,128]{2,1,0:T(8,128)} %bitcast.22, f32[16,4,128,128]{3,2,1,0:T(8,128)} %shard_map.117.after.coef_h), custom_call_target="tpu_custom_call" | custom-call | flops 5242880 | bytes 2097152 | tf_op jit(solution)/shard_map/pallas_call | solution.py:434
  55.5 3.6 %all-to-all-start.2 = ((bf16[16,8,16,128]{3,2,1,0:T(8,128)(2,1)}), bf16[16,8,16,128]{3,2,1,0:T(8,128)(2,1)S(1)}, u32[]{:S(2)}, u32[]{:S(2)}) async-start(bf16[16,8,16,128]{3,2,1,0:T(8,128)(2,1)} %bitcast.10), calls=%async_computation.2 | async-start | bytes 1048576 | tf_op jit(solution)/shard_map/all_to_all | solution.py:481
  59.1 4.1 %shard_map.119 = (bf16[16,128,128]{2,1,0:T(8,128)(2,1)}, f32[16,128,128]{2,1,0:T(8,128)}) custom-call(bf16[128,16,128]{2,1,0:T(8,128)(2,1)S(1)} %bitcast.17, f32[16,128,128]{2,1,0:T(8,128)} %get-tuple-element.18.gate_h, bf16[16,128,128]{2,1,0:T(8,128)(2,1)} %cot_h.3, f32[1,128]{1,0:T(1,128)} %bitcast.36, f32[1,128]{1,0:T(1,128)} %bitcast.37, ...), custom_call_target="tpu_custom_call" | custom-call | flops 201326592 | bytes 3670016 | tf_op jit(solution)/shard_map/pallas_call | solution.py:434
  63.3 5.0 %all-to-all-done.2 = bf16[16,8,16,128]{3,2,1,0:T(8,128)(2,1)S(1)} async-done(((bf16[16,8,16,128]{3,2,1,0:T(8,128)(2,1)}), bf16[16,8,16,128]{3,2,1,0:T(8,128)(2,1)S(1)}, u32[]{:S(2)}, u32[]{:S(2)}) %all-to-all-start.2) | async-done | bytes 524320 | tf_op jit(solution)/shard_map/all_to_all | solution.py:481
  69.8 4.3 %all-to-all-start.3 = ((bf16[32,8,16,128]{3,2,1,0:T(8,128)(2,1)}), bf16[32,8,16,128]{3,2,1,0:T(8,128)(2,1)S(1)}, u32[]{:S(2)}, u32[]{:S(2)}) async-start(bf16[32,8,16,128]{3,2,1,0:T(8,128)(2,1)} %bitcast.21), calls=%async_computation.3 | async-start | bytes 2097152 | tf_op jit(solution)/shard_map/all_to_all | solution.py:485
  76.2 1.7 %collective-permute-start.9 = (bf16[2,8,16,128]{3,2,1,0:T(8,128)(2,1)S(1)}, bf16[2,8,16,128]{3,2,1,0:T(8,128)(2,1)S(1)}, u32[]{:S(2)}, u32[]{:S(2)}) collective-permute-start(bf16[2,8,16,128]{3,2,1,0:T(8,128)(2,1)S(1)} %pad_maximum_fusion.7), channel_id=1, source_target_pairs={{0,1},{1,0},{4,5},{5,4},{8,9},{9,8},{12,13},{13,12},{2,3},{3,2},{6... | collective-permute-start | bytes 196616 | tf_op jit(solution)/shard_map/ppermute | solution.py:490
  83.1 2.9 %collective-permute-done.9.refs_2_ = bf16[2,8,16,128]{3,2,1,0:T(8,128)(2,1)S(1)} collective-permute-done((bf16[2,8,16,128]{3,2,1,0:T(8,128)(2,1)S(1)}, bf16[2,8,16,128]{3,2,1,0:T(8,128)(2,1)S(1)}, u32[]{:S(2)}, u32[]{:S(2)}) %collective-permute-start.9) | collective-permute-done | bytes 65568 | tf_op jit(solution)/shard_map/ppermute | solution.py:490
  89.0 4.5 %collective-permute-done.12.refs_5_ = bf16[2,8,16,128]{3,2,1,0:T(8,128)(2,1)S(1)} collective-permute-done((bf16[2,8,16,128]{3,2,1,0:T(8,128)(2,1)S(1)}, bf16[2,8,16,128]{3,2,1,0:T(8,128)(2,1)S(1)}, u32[]{:S(2)}, u32[]{:S(2)}) %collective-permute-start.12) | collective-permute-done | bytes 65568 | tf_op jit(solution)/shard_map/ppermute | solution.py:490
  94.9 2.7 %collective-permute-done.14.refs_7_ = bf16[2,8,16,128]{3,2,1,0:T(8,128)(2,1)S(1)} collective-permute-done((bf16[2,8,16,128]{3,2,1,0:T(8,128)(2,1)S(1)}, bf16[2,8,16,128]{3,2,1,0:T(8,128)(2,1)S(1)}, u32[]{:S(2)}, u32[]{:S(2)}) %collective-permute-start.14) | collective-permute-done | bytes 65568 | tf_op jit(solution)/shard_map/ppermute | solution.py:490
  97.5 2.9 %collective-permute-done.15.refs_8_ = bf16[2,8,16,128]{3,2,1,0:T(8,128)(2,1)S(1)} collective-permute-done((bf16[2,8,16,128]{3,2,1,0:T(8,128)(2,1)S(1)}, bf16[2,8,16,128]{3,2,1,0:T(8,128)(2,1)S(1)}, u32[]{:S(2)}, u32[]{:S(2)}) %collective-permute-start.15) | collective-permute-done | bytes 65568 | tf_op jit(solution)/shard_map/ppermute | solution.py:490
  100.4 3.5 %shard_map.122.dzg_h = f32[16,128,128]{2,1,0:T(8,128)} custom-call(f32[16,4,128,128]{3,2,1,0:T(8,128)} %shard_map.117.after.coef_h, f32[16,128,128]{2,1,0:T(8,128)} %get-tuple-element.23.after.dzg_h, bf16[128,512]{1,0:T(8,128)(2,1)} %proj_h.9, bf16[8,8,16,128]{3,2,1,0:T(8,128)(2,1)S(1)} %get-tuple-element.24.refs_0_, ...), custom_call_target="tpu_custom_call" | custom-call | flops 134217728 | bytes 4718592 | tf_op jit(solution)/shard_map/pallas_call | solution.py:434
  103.9 4.6 %shard_map.123 = bf16[16,128,128]{2,1,0:T(8,128)(2,1)} custom-call(bf16[2,16,8,16,128]{4,3,2,1,0:T(8,128)(2,1)S(1)} %bitcast.20, f32[16,4,128,128]{3,2,1,0:T(8,128)} %shard_map.117.after.coef_h, f32[16,128,128]{2,1,0:T(8,128)} %get-tuple-element.20.zhat_h, f32[16,128]{1,0:T(8,128)} %get-tuple-element.14.after.inv_h, f32[16,128,128]{2,1,0:T(8,128)} %shard_map.122.dzg_h, ...), custom_call_target="tpu_custom_call" | custom-call | flops 201326592 | bytes 5767168 | tf_op jit(solution)/shard_map/pallas_call | solution.py:434
  (47 shorter events, 21.0 us)
Async XLA Ops:
  5.0 33.7 %all-to-all-start = ((bf16[32,8,16,128]{3,2,1,0:T(8,128)(2,1)}), bf16[32,8,16,128]{3,2,1,0:T(8,128)(2,1)S(1)}, u32[]{:S(2)}, u32[]{:S(2)}) async-start(bf16[32,8,16,128]{3,2,1,0:T(8,128)(2,1)} %bitcast.3), calls=%async_computation | async-start | bytes 2097152 | tf_op jit(solution)/shard_map/all_to_all | solution.py:485
  15.7 1.6 %collective-permute-start = (bf16[8,8,16,128]{3,2,1,0:T(8,128)(2,1)S(1)}, bf16[8,8,16,128]{3,2,1,0:T(8,128)(2,1)S(1)}, u32[]{:S(2)}, u32[]{:S(2)}) collective-permute-start(bf16[8,8,16,128]{3,2,1,0:T(8,128)(2,1)S(1)} %get-tuple-element.16), channel_id=1, source_target_pairs={{0,2},{2,0},{1,3},{3,1},{4,6},{6,4},{5,7},{7,5},{8,10},{10,8},{9,1... | collective-permute-start | bytes 786440 | tf_op jit(solution)/shard_map/ppermute | solution.py:490
  17.4 7.1 %collective-permute-start.1 = (bf16[2,8,16,128]{3,2,1,0:T(8,128)(2,1)S(1)}, bf16[2,8,16,128]{3,2,1,0:T(8,128)(2,1)S(1)}, u32[]{:S(2)}, u32[]{:S(2)}) collective-permute-start(bf16[2,8,16,128]{3,2,1,0:T(8,128)(2,1)S(1)} %pad_maximum_fusion), channel_id=1, source_target_pairs={{0,1},{1,0},{4,5},{5,4},{8,9},{9,8},{12,13},{13,12},{2,3},{3,2},{6... | collective-permute-start | bytes 196616 | tf_op jit(solution)/shard_map/ppermute | solution.py:490
  19.2 8.4 %collective-permute-start.2 = (bf16[2,8,16,128]{3,2,1,0:T(8,128)(2,1)S(1)}, bf16[2,8,16,128]{3,2,1,0:T(8,128)(2,1)S(1)}, u32[]{:S(2)}, u32[]{:S(2)}) collective-permute-start(bf16[2,8,16,128]{3,2,1,0:T(8,128)(2,1)S(1)} %pad_maximum_fusion.1), channel_id=1, source_target_pairs={{0,4},{1,5},{4,0},{5,1},{8,12},{9,13},{12,8},{13,9},{2,6},{3,7},{6... | collective-permute-start | bytes 196616 | tf_op jit(solution)/shard_map/ppermute | solution.py:490
  20.8 12.3 %collective-permute-start.3 = (bf16[2,8,16,128]{3,2,1,0:T(8,128)(2,1)S(1)}, bf16[2,8,16,128]{3,2,1,0:T(8,128)(2,1)S(1)}, u32[]{:S(2)}, u32[]{:S(2)}) collective-permute-start(bf16[2,8,16,128]{3,2,1,0:T(8,128)(2,1)S(1)} %pad_maximum_fusion.2), channel_id=1, source_target_pairs={{0,5},{1,4},{4,1},{5,0},{8,13},{9,12},{12,9},{13,8},{2,7},{3,6},{6... | collective-permute-start | bytes 196616 | tf_op jit(solution)/shard_map/ppermute | solution.py:490
  21.1 12.0 %collective-permute-start.4 = (bf16[2,8,16,128]{3,2,1,0:T(8,128)(2,1)S(1)}, bf16[2,8,16,128]{3,2,1,0:T(8,128)(2,1)S(1)}, u32[]{:S(2)}, u32[]{:S(2)}) collective-permute-start(bf16[2,8,16,128]{3,2,1,0:T(8,128)(2,1)S(1)} %pad_maximum_fusion.3), channel_id=1, source_target_pairs={{0,8},{1,9},{4,12},{5,13},{8,0},{9,1},{12,4},{13,5},{2,10},{3,11},... | collective-permute-start | bytes 196616 | tf_op jit(solution)/shard_map/ppermute | solution.py:490
  22.9 10.3 %collective-permute-start.5 = (bf16[2,8,16,128]{3,2,1,0:T(8,128)(2,1)S(1)}, bf16[2,8,16,128]{3,2,1,0:T(8,128)(2,1)S(1)}, u32[]{:S(2)}, u32[]{:S(2)}) collective-permute-start(bf16[2,8,16,128]{3,2,1,0:T(8,128)(2,1)S(1)} %pad_maximum_fusion.4), channel_id=1, source_target_pairs={{0,9},{1,8},{4,13},{5,12},{8,1},{9,0},{12,5},{13,4},{2,11},{3,10},... | collective-permute-start | bytes 196616 | tf_op jit(solution)/shard_map/ppermute | solution.py:490
  24.5 11.4 %collective-permute-start.6 = (bf16[2,8,16,128]{3,2,1,0:T(8,128)(2,1)S(1)}, bf16[2,8,16,128]{3,2,1,0:T(8,128)(2,1)S(1)}, u32[]{:S(2)}, u32[]{:S(2)}) collective-permute-start(bf16[2,8,16,128]{3,2,1,0:T(8,128)(2,1)S(1)} %pad_maximum_fusion.5), channel_id=1, source_target_pairs={{0,12},{1,13},{4,8},{5,9},{8,4},{9,5},{12,0},{13,1},{2,14},{3,15},... | collective-permute-start | bytes 196616 | tf_op jit(solution)/shard_map/ppermute | solution.py:490
  27.6 11.1 %collective-permute-start.7 = (bf16[2,8,16,128]{3,2,1,0:T(8,128)(2,1)S(1)}, bf16[2,8,16,128]{3,2,1,0:T(8,128)(2,1)S(1)}, u32[]{:S(2)}, u32[]{:S(2)}) collective-permute-start(bf16[2,8,16,128]{3,2,1,0:T(8,128)(2,1)S(1)} %pad_maximum_fusion.6), channel_id=1, source_target_pairs={{0,13},{1,12},{4,9},{5,8},{8,5},{9,4},{12,1},{13,0},{2,15},{3,14},... | collective-permute-start | bytes 196616 | tf_op jit(solution)/shard_map/ppermute | solution.py:490
  40.1 13.1 %all-to-all-start.1 = ((bf16[16,8,16,128]{3,2,1,0:T(8,128)(2,1)}), bf16[16,8,16,128]{3,2,1,0:T(8,128)(2,1)S(1)}, u32[]{:S(2)}, u32[]{:S(2)}) async-start(bf16[16,8,16,128]{3,2,1,0:T(8,128)(2,1)} %bitcast.6), calls=%async_computation.1 | async-start | bytes 1048576 | tf_op jit(solution)/shard_map/all_to_all | solution.py:481
  55.5 12.7 %all-to-all-start.2 = ((bf16[16,8,16,128]{3,2,1,0:T(8,128)(2,1)}), bf16[16,8,16,128]{3,2,1,0:T(8,128)(2,1)S(1)}, u32[]{:S(2)}, u32[]{:S(2)}) async-start(bf16[16,8,16,128]{3,2,1,0:T(8,128)(2,1)} %bitcast.10), calls=%async_computation.2 | async-start | bytes 1048576 | tf_op jit(solution)/shard_map/all_to_all | solution.py:481
  68.7 1.1 copy-start
  69.8 34.1 %all-to-all-start.3 = ((bf16[32,8,16,128]{3,2,1,0:T(8,128)(2,1)}), bf16[32,8,16,128]{3,2,1,0:T(8,128)(2,1)S(1)}, u32[]{:S(2)}, u32[]{:S(2)}) async-start(bf16[32,8,16,128]{3,2,1,0:T(8,128)(2,1)} %bitcast.21), calls=%async_computation.3 | async-start | bytes 2097152 | tf_op jit(solution)/shard_map/all_to_all | solution.py:485
  74.6 1.6 %collective-permute-start.8 = (bf16[8,8,16,128]{3,2,1,0:T(8,128)(2,1)S(1)}, bf16[8,8,16,128]{3,2,1,0:T(8,128)(2,1)S(1)}, u32[]{:S(2)}, u32[]{:S(2)}) collective-permute-start(bf16[8,8,16,128]{3,2,1,0:T(8,128)(2,1)S(1)} %get-tuple-element.25), channel_id=1, source_target_pairs={{0,2},{2,0},{1,3},{3,1},{4,6},{6,4},{5,7},{7,5},{8,10},{10,8},{9,1... | collective-permute-start | bytes 786440 | tf_op jit(solution)/shard_map/ppermute | solution.py:490
  76.2 9.8 %collective-permute-start.9 = (bf16[2,8,16,128]{3,2,1,0:T(8,128)(2,1)S(1)}, bf16[2,8,16,128]{3,2,1,0:T(8,128)(2,1)S(1)}, u32[]{:S(2)}, u32[]{:S(2)}) collective-permute-start(bf16[2,8,16,128]{3,2,1,0:T(8,128)(2,1)S(1)} %pad_maximum_fusion.7), channel_id=1, source_target_pairs={{0,1},{1,0},{4,5},{5,4},{8,9},{9,8},{12,13},{13,12},{2,3},{3,2},{6... | collective-permute-start | bytes 196616 | tf_op jit(solution)/shard_map/ppermute | solution.py:490
  77.9 9.9 %collective-permute-start.10 = (bf16[2,8,16,128]{3,2,1,0:T(8,128)(2,1)S(1)}, bf16[2,8,16,128]{3,2,1,0:T(8,128)(2,1)S(1)}, u32[]{:S(2)}, u32[]{:S(2)}) collective-permute-start(bf16[2,8,16,128]{3,2,1,0:T(8,128)(2,1)S(1)} %pad_maximum_fusion.8), channel_id=1, source_target_pairs={{0,4},{1,5},{4,0},{5,1},{8,12},{9,13},{12,8},{13,9},{2,6},{3,7},{6... | collective-permute-start | bytes 196616 | tf_op jit(solution)/shard_map/ppermute | solution.py:490
  79.4 9.6 %collective-permute-start.11 = (bf16[2,8,16,128]{3,2,1,0:T(8,128)(2,1)S(1)}, bf16[2,8,16,128]{3,2,1,0:T(8,128)(2,1)S(1)}, u32[]{:S(2)}, u32[]{:S(2)}) collective-permute-start(bf16[2,8,16,128]{3,2,1,0:T(8,128)(2,1)S(1)} %pad_maximum_fusion.9), channel_id=1, source_target_pairs={{0,5},{1,4},{4,1},{5,0},{8,13},{9,12},{12,9},{13,8},{2,7},{3,6},{6... | collective-permute-start | bytes 196616 | tf_op jit(solution)/shard_map/ppermute | solution.py:490
  79.9 13.6 %collective-permute-start.12 = (bf16[2,8,16,128]{3,2,1,0:T(8,128)(2,1)S(1)}, bf16[2,8,16,128]{3,2,1,0:T(8,128)(2,1)S(1)}, u32[]{:S(2)}, u32[]{:S(2)}) collective-permute-start(bf16[2,8,16,128]{3,2,1,0:T(8,128)(2,1)S(1)} %pad_maximum_fusion.10), channel_id=1, source_target_pairs={{0,8},{1,9},{4,12},{5,13},{8,0},{9,1},{12,4},{13,5},{2,10},{3,11},... | collective-permute-start | bytes 196616 | tf_op jit(solution)/shard_map/ppermute | solution.py:490
  81.6 13.3 %collective-permute-start.13 = (bf16[2,8,16,128]{3,2,1,0:T(8,128)(2,1)S(1)}, bf16[2,8,16,128]{3,2,1,0:T(8,128)(2,1)S(1)}, u32[]{:S(2)}, u32[]{:S(2)}) collective-permute-start(bf16[2,8,16,128]{3,2,1,0:T(8,128)(2,1)S(1)} %pad_maximum_fusion.11), channel_id=1, source_target_pairs={{0,9},{1,8},{4,13},{5,12},{8,1},{9,0},{12,5},{13,4},{2,11},{3,10},... | collective-permute-start | bytes 196616 | tf_op jit(solution)/shard_map/ppermute | solution.py:490
  86.0 11.5 %collective-permute-start.14 = (bf16[2,8,16,128]{3,2,1,0:T(8,128)(2,1)S(1)}, bf16[2,8,16,128]{3,2,1,0:T(8,128)(2,1)S(1)}, u32[]{:S(2)}, u32[]{:S(2)}) collective-permute-start(bf16[2,8,16,128]{3,2,1,0:T(8,128)(2,1)S(1)} %pad_maximum_fusion.12), channel_id=1, source_target_pairs={{0,12},{1,13},{4,8},{5,9},{8,4},{9,5},{12,0},{13,1},{2,14},{3,15},... | collective-permute-start | bytes 196616 | tf_op jit(solution)/shard_map/ppermute | solution.py:490
  87.8 12.6 %collective-permute-start.15 = (bf16[2,8,16,128]{3,2,1,0:T(8,128)(2,1)S(1)}, bf16[2,8,16,128]{3,2,1,0:T(8,128)(2,1)S(1)}, u32[]{:S(2)}, u32[]{:S(2)}) collective-permute-start(bf16[2,8,16,128]{3,2,1,0:T(8,128)(2,1)S(1)} %pad_maximum_fusion.13), channel_id=1, source_target_pairs={{0,13},{1,12},{4,9},{5,8},{8,5},{9,4},{12,1},{13,0},{2,15},{3,14},... | collective-permute-start | bytes 196616 | tf_op jit(solution)/shard_map/ppermute | solution.py:490

commit v7 on v6

--- a/solution.py
+++ b/solution.py
@@ -112,22 +112,26 @@
     part, n_out, pair_h, mask_h, mask_row_h, gain_h, bias_h, proj_h, *refs
 ):
     outs = refs[:n_out]
-    pair, mask_s, mask_v, gain, bias, proj_weight, plane, sems, row_sems = refs[n_out:]
+    pair, mask_s, mask_v, gain, bias, proj_weight, plane, sems, row_sems, *more = refs[n_out:]
     rows, cols, width = pair.shape
     hidden = plane.shape[0] // rows
     groups = groups_of(rows)
-    small = start(
-        sems,
-        [(gain_h, gain), (bias_h, bias), (proj_h, proj_weight), (mask_h, mask_s), (mask_row_h, mask_v)],
-    )
     blocks = start(
         row_sems,
         [(pair_h.at[pl.ds(at, size)], pair.at[pl.ds(at, size)]) for at, size in groups],
     )
+    small = start(
+        sems,
+        [
+            (gain_h, gain), (bias_h, bias),
+            (proj_h.at[:, pl.ds(part * hidden, 2 * hidden)], proj_weight),
+            (mask_h, mask_s), (mask_row_h, mask_v),
+        ],
+    )
     wait(small)
     gain_b = jnp.concatenate([down_lanes(gain[...], cols)] * groups[0][1], axis=1)
     bias_b = jnp.concatenate([down_lanes(bias[...], cols)] * groups[0][1], axis=1)
-    weight = turned_weight(proj_weight[:, part * hidden : (part + 2) * hidden])
+    weight = turned_weight(proj_weight[...])
     for (at, size), block in zip(groups, blocks):
         block.wait()
         zhat, _ = normalized(turned(pair[at : at + size].reshape(size * cols, width)))
@@ -136,12 +140,27 @@
         values = sigmoid(dot(weight[:hidden], zbar)) * dot(weight[hidden:], zbar) * pm
         for r in range(size):
             plane[pl.ds(at + r, hidden, stride=rows), :] = values[:, r * cols : (r + 1) * cols]
-    if n_out == 1:
-        values = plane[...].reshape(outs[0].shape[1:]).astype(BF16)
-        for half in range(outs[0].shape[0]):
-            outs[0][half] = values
+    if n_out > 1:
+        give_pieces(plane, outs)
     else:
-        give_pieces(plane, outs)
+        give_all(plane, outs[0], *more)
+
+
+def give_all(plane, out_h, ready, sems):
+    n_place = ready.shape[0]
+    size = math.gcd(n_place, 4)
+    length = plane.shape[0] // n_place * size
+    leaving = []
+    for n, at in enumerate(range(0, n_place, size)):
+        values = plane[n * length : (n + 1) * length]
+        ready[at : at + size] = values.reshape(size, *ready.shape[1:]).astype(BF16)
+        for half in range(out_h.shape[0]):
+            copy = pltpu.make_async_copy(
+                ready.at[pl.ds(at, size)], out_h.at[half, pl.ds(at, size)], sems.at[half, n]
+            )
+            copy.start()
+            leaving.append(copy)
+    wait(leaving)
 
 
 def give_pieces(plane, outs):
@@ -197,11 +216,12 @@
 
 
 def factors_kernel(
-    zhat_h, mask_h, mask_row_h, gain_h, bias_h, proj_h, after, coef_h,
-    zhat, mask_s, mask_v, gain, bias, proj_weight, coef, in_sems, out_sems,
+    zhat_h, mask_h, mask_row_h, gain_h, bias_h, proj_h, dxh_h, after, coef_h, dxh,
+    zhat, mask_s, mask_v, gain, bias, proj_weight, coef, in_sems, out_sems, fetch_sems,
 ):
     rows, width, cols = zhat.shape
     hidden = coef.shape[2]
+    fetched = start(fetch_sems, [(dxh_h, dxh)])
     wait(
         start(
             in_sems,
@@ -233,7 +253,7 @@
         )
         copy.start()
         leaving.append(copy)
-    wait(leaving)
+    wait(leaving + fetched)
 
 
 def channel_matrix(ref, at):
@@ -252,27 +272,48 @@
         ref[(*lead, c, at)] = values[:, c * cols : (c + 1) * cols].reshape(*shape, rows, cols)
 
 
+def leave(ready, out_h, at, sem):
+    lead = (slice(None),) * (len(ready.shape) - 3)
+    copy = pltpu.make_async_copy(
+        ready.at[(*lead, pl.ds(at, 1))], out_h.at[(*lead, pl.ds(at, 1))], sem
+    )
+    copy.start()
+    return copy
+
+
 def product_kernel(n_chip, right, after, *refs):
-    pieces, (out, left) = refs[:-2], refs[-2:]
+    pieces, (out_h, left, ready, sems) = refs[:-4], refs[-4:]
     n_col, share = left.shape[1:3]
     for number, piece in received(pieces, n_chip):
         left[number // n_col, number % n_col] = piece
+    leaving = []
     for h in range(share):
-        put_channel(out, h, dot(channel_matrix(left, h), channel_matrix(right, h), ((1,), (1,))))
-
-
-def middle_kernel(product, dxh_h, after, out, dxh, xhat, sems):
+        values = dot(channel_matrix(left, h), channel_matrix(right, h), ((1,), (1,)))
+        put_channel(ready, h, values)
+        leaving.append(leave(ready, out_h, h, sems.at[h]))
+    wait(leaving)
+
+
+def middle_kernel(product, dxh, out_h, xhat, ready, sems):
     hidden = product.shape[0]
-    (copy,) = start(sems, [(dxh_h, dxh)])
     values = product[...].astype(F32)
     mean = jnp.sum(values, axis=0) * (1.0 / hidden)
     centred = values - mean[None]
     var = jnp.sum(centred * centred, axis=0) * (1.0 / hidden)
     inverse = lax.rsqrt(var + EPS)
     xhat[...] = centred * inverse[None]
-    copy.wait()
     m2 = jnp.sum(dxh[...] * xhat[...], axis=0) * (1.0 / hidden)
-    out[...] = ((dxh[...] - xhat[...] * m2[None]) * inverse[None]).astype(BF16)
+    leaving = []
+    size = math.gcd(hidden, 32)
+    for n, at in enumerate(range(0, hidden, size)):
+        part = slice(at, at + size)
+        ready[part] = ((dxh[part] - xhat[part] * m2[None]) * inverse[None]).astype(BF16)
+        copy = pltpu.make_async_copy(
+            ready.at[pl.ds(at, size)], out_h.at[pl.ds(at, size)], sems.at[n]
+        )
+        copy.start()
+        leaving.append(copy)
+    wait(leaving)
 
 
 def update_kernel(
@@ -314,9 +355,13 @@
     wait(start(out_sems, [(update, update_h), (dzg, dzg_h)]))
 
 
-def grad_right_kernel(grad, left, after, out):
-    for h in range(out.shape[-3]):
-        put_channel(out, h, dot(channel_matrix(grad, h), channel_matrix(left, h), ((0,), (0,))))
+def grad_right_kernel(grad, left, after, out_h, ready, sems):
+    leaving = []
+    for h in range(ready.shape[-3]):
+        values = dot(channel_matrix(grad, h), channel_matrix(left, h), ((0,), (0,)))
+        put_channel(ready, h, values)
+        leaving.append(leave(ready, out_h, h, sems.at[h]))
+    wait(leaving)
 
 
 def grad_left_kernel(grad, right, *refs):
@@ -341,13 +386,19 @@
     return dot(weight, jnp.concatenate(columns, axis=1))
 
 
-def back_left_kernel(n_chip, coef_h, dzg_h, proj_h, *refs):
-    pieces, out_h = refs[:-9], refs[-9]
-    coef, dzg, proj_weight, out, plane, sems, coef_sems, dzg_sems = refs[-8:]
+def back_left_kernel(n_chip, coef_h, dzg_h, zhat_h, inv_h, proj_h, *refs):
+    pieces, (out, coef_right, zhat, inv) = refs[:-11], refs[-11:-7]
+    coef, dzg, proj_weight, plane, sems, coef_sems, dzg_sems = refs[-7:]
     rows, width, cols = out.shape
     hidden = plane.shape[0] // rows
     groups = groups_of(rows)
-    small = start(sems, [(proj_h, proj_weight)])
+    (small, *fetched) = start(
+        sems,
+        [
+            (proj_h, proj_weight), (coef_h.at[:, pl.ds(2, 2)], coef_right), (zhat_h, zhat),
+            (inv_h, inv),
+        ],
+    )
     blocks = [
         start(
             coef_sems,
@@ -366,50 +417,33 @@
     for number, piece in arrived:
         first = pl.multiple_of(number * length, length)
         plane[pl.ds(first, length), :] = piece.astype(F32).reshape(length, cols)
-    wait(small)
+    small.wait()
     weight = proj_weight[:, : 2 * hidden]
     for n, (at, size) in enumerate(groups):
         wait([copies[n] for copies in blocks])
         back = through_projection(plane, coef, weight, at, size, rows)
         for r in range(size):
             out[at + r] = back[:, r * cols : (r + 1) * cols] + dzg[at + r]
-    wait(start(sems, [(out, out_h)]))
+    wait(fetched)
 
 
 def back_kernel(
-    grads, coef_h, zhat_h, inv_h, dzg_h, gain_h, proj_h, out_h,
-    coef, zhat, inv, dzg, gain, proj_weight, out, plane,
-    sems, coef_sems, zhat_sems, dzg_sems, out_sems,
+    grads, coef, zhat, inv, dzg, gain_h, proj_h, out_h,
+    gain, proj_weight, out, plane, sems, out_sems,
 ):
     rows, cols, width = out.shape
     hidden = plane.shape[0] // rows
     groups = groups_of(rows)
-
-    def blocks_of(source, target):
-        return [(source.at[pl.ds(at, size)], target.at[pl.ds(at, size)]) for at, size in groups]
-
-    small = start(sems, [(gain_h, gain), (proj_h, proj_weight), (inv_h, inv)])
-    blocks = [
-        start(
-            coef_sems,
-            [
-                (coef_h.at[pl.ds(at, size), pl.ds(2, 2)], coef.at[pl.ds(at, size)])
-                for at, size in groups
-            ],
-        ),
-        start(zhat_sems, blocks_of(zhat_h, zhat)),
-        start(dzg_sems, blocks_of(dzg_h, dzg)),
-    ]
+    small = start(sems, [(gain_h, gain), (proj_h.at[:, pl.ds(2 * hidden, 2 * hidden)], proj_weight)])
     total = grads[0].astype(F32)
     for half in range(1, grads.shape[0]):
         total = total + grads[half].astype(F32)
     plane[...] = total.reshape(plane.shape)
     wait(small)
     gain_b = jnp.concatenate([down_lanes(gain[...], cols)] * groups[0][1], axis=1)
-    weight = proj_weight[:, 2 * hidden :]
+    weight = proj_weight[...]
     leaving = []
     for n, (at, size) in enumerate(groups):
-        wait([copies[n] for copies in blocks])
         back = through_projection(plane, coef, weight, at, size, rows)
         dzh = (back + side_by_side(dzg, at, size)) * gain_b
         z = side_by_side(zhat, at, size)
@@ -427,15 +461,17 @@
     wait(leaving)
 
 
-def call(kernel, outs, scratch, args, near=(), order=(), outs_near=False, flops=0, moved=0):
+def call(kernel, outs, scratch, args, near=(), outs_near=(), flops=0, moved=0):
     here, far = (pl.BlockSpec(memory_space=space) for space in (pltpu.VMEM, pltpu.HBM))
-    anywhere = pl.BlockSpec(memory_space=pl.ANY)
-    specs = [here if at in near else anywhere if at in order else far for at in range(len(args))]
+    specs = [here if at in near else far for at in range(len(args))]
     return pl.pallas_call(
         kernel,
-        out_shape=outs if outs_near else jax.tree.map(lambda o: pltpu.HBM(o.shape, o.dtype), outs),
+        out_shape=[
+            out if at in outs_near else pltpu.HBM(out.shape, out.dtype)
+            for at, out in enumerate(outs)
+        ],
         in_specs=specs,
-        out_specs=jax.tree.map(lambda _: here if outs_near else far, outs),
+        out_specs=[here if at in outs_near else far for at in range(len(outs))],
         scratch_shapes=scratch,
         compiler_params=pltpu.CompilerParams(vmem_limit_bytes=24 * MIB),
         cost_estimate=pl.CostEstimate(flops=flops, bytes_accessed=moved, transcendentals=0),
@@ -494,9 +530,9 @@
         first += [permute(pieces[m], ("core",), n_core, m) for m in range(1, n_core)]
         second = [
             permute(jnp.stack([piece[n] for piece in first]), ("row", "col"), n_chip, n)
-            for n in range(1, n_chip)
+            for n in range(n_chip - 1, 0, -1)
         ]
-        return tuple(first + second)
+        return tuple(first + second[::-1])
 
     mask_s = pltpu.SMEM(mask.shape, jnp.int32)
     mask_v = vmem(*mask_row.shape, dtype=jnp.int32)
@@ -510,20 +546,29 @@
     pieces_shape = (shape(n_chip, share, rows, cols),) * n_core
     n_pieces = n_core + n_chip - 1
 
-    def front(part, outs):
+    def front(part, outs, scratch, near):
         return call(
             functools.partial(front_kernel, part, len(outs)),
             outs,
-            [block, mask_s, mask_v, vector, vector, proj_v, plane, sems(5), sems(n_groups)],
+            [
+                block, mask_s, mask_v, vector, vector, vmem(width, 2 * hidden), plane,
+                sems(5), sems(n_groups), *scratch,
+            ],
             (pair, mask, mask_row, gain_in, bias_in, proj_weight),
-            outs_near=True,
+            outs_near=near,
             flops=2 * cells * width * 3 * hidden,
             moved=5 * cells * width,
         )
 
-    (right,) = front(2, (shape(n_half, n_place, share, rows, cols),))
+    everywhere = vmem(n_place, share, rows, cols)
+    (right,) = front(
+        2,
+        (shape(n_half, n_place, share, rows, cols),),
+        [everywhere, pltpu.SemaphoreType.DMA((n_half, n_place // math.gcd(n_place, 4)))],
+        (),
+    )
     right = exchange_all(right).reshape(n_half, n_line, n_col, share, rows, cols)
-    left = exchange_pieces(tuple(front(0, pieces_shape)))
+    left = exchange_pieces(tuple(front(0, pieces_shape, [], range(n_core))))
     zhat, inv, gate, dxh = call(
         side_kernel,
         (
@@ -543,39 +588,40 @@
     product, left = call(
         functools.partial(product_kernel, n_chip),
         (shape(n_line, n_col, share, rows, cols), shape(n_line, n_col, share, rows, cols)),
-        [],
+        [vmem(n_line, n_col, share, rows, cols), sems(share)],
         (right, inv, *left),
         near=(0, *range(2, 2 + n_pieces)),
-        outs_near=True,
+        outs_near=(1,),
         flops=2 * share * n_half * (n_line * rows) ** 2 * n_col * cols,
         moved=8 * cells * hidden,
     )
-    coef = call(
+    spread = vmem(hidden, rows, cols, dtype=F32)
+    coef, dxh = call(
         factors_kernel,
-        shape(rows, 4, hidden, cols, dtype=F32),
+        (shape(rows, 4, hidden, cols, dtype=F32), shape(hidden, rows, cols, dtype=F32)),
         [
             wide, mask_s, mask_v, vector, vector, proj_v, vmem(rows, 4, hidden, cols, dtype=F32),
-            sems(6), sems(n_groups),
+            sems(6), sems(n_groups), sems(1),
         ],
-        (zhat, mask, mask_row, gain_in, bias_in, proj_weight, product),
-        order=(6,),
+        (
+            zhat, mask, mask_row, gain_in, bias_in, proj_weight,
+            dxh.reshape(hidden, rows, cols), product,
+        ),
+        outs_near=(1,),
         flops=2 * cells * width * 5 * hidden,
         moved=20 * cells * width,
     )
     product = exchange(product.reshape(n_place, share, rows, cols)).reshape(hidden, rows, cols)
-    spread = vmem(hidden, rows, cols, dtype=F32)
-    grad = call(
+    (sent,) = call(
         middle_kernel,
-        shape(hidden, rows, cols),
-        [spread, spread, sems(1)],
-        (product, dxh.reshape(hidden, rows, cols), coef),
-        near=(0,),
-        outs_near=True,
+        (shape(hidden, rows, cols),),
+        [spread, vmem(hidden, rows, cols), sems(hidden // math.gcd(hidden, 32))],
+        (product, dxh),
+        near=(0, 1),
         flops=20 * cells * hidden,
         moved=8 * cells * hidden,
     )
-    sent = grad
-    grad = exchange(grad.reshape(n_place, share, rows, cols))
+    grad = exchange(sent.reshape(n_place, share, rows, cols))
     grad = grad.reshape(n_line, n_col, share, rows, cols)
     update, dzg = call(
         update_kernel,
@@ -583,17 +629,15 @@
         [wide, block, vector, vector, square, square, block, wide, plane, sems(6), sems(2)],
         (product, gate, cotangent, norm_gain, norm_bias, out_weight, gate_weight, sent),
         near=(0,),
-        order=(7,),
         flops=2 * cells * width * 3 * hidden,
         moved=14 * cells * hidden,
     )
-    grad_right = call(
+    (grad_right,) = call(
         grad_right_kernel,
-        shape(n_half, n_line, n_col, share, rows, cols),
-        [],
+        (shape(n_half, n_line, n_col, share, rows, cols),),
+        [vmem(n_half, n_line, n_col, share, rows, cols), sems(share)],
         (grad, left, dzg),
         near=(0, 1),
-        outs_near=True,
         flops=2 * share * n_half * (n_line * rows) ** 2 * n_col * cols,
         moved=8 * cells * hidden,
     )
@@ -604,29 +648,32 @@
         [vmem(n_line, n_col, share, rows, cols)],
         (grad, right),
         near=(0, 1),
-        outs_near=True,
+        outs_near=range(n_core),
         flops=2 * share * n_half * (n_line * rows) ** 2 * n_col * cols,
         moved=8 * cells * hidden,
     )
     grad_left = exchange_pieces(tuple(grad_left))
-    dzg = call(
+    dzg, coef, zhat, inv = call(
         functools.partial(back_left_kernel, n_chip),
-        shape(rows, width, cols, dtype=F32),
-        [coef_v, wide, proj_v, wide, plane, sems(1), sems(n_groups), sems(n_groups)],
-        (coef, dzg, proj_weight, *grad_left),
-        near=tuple(range(3, 3 + n_pieces)),
+        (
+            shape(rows, width, cols, dtype=F32),
+            shape(rows, 2, hidden, cols, dtype=F32),
+            shape(rows, width, cols, dtype=F32),
+            shape(rows, cols, dtype=F32),
+        ),
+        [coef_v, wide, proj_v, plane, sems(4), sems(n_groups), sems(n_groups)],
+        (coef, dzg, zhat, inv, proj_weight, *grad_left),
+        near=tuple(range(5, 5 + n_pieces)),
+        outs_near=range(4),
         flops=2 * cells * width * 2 * hidden,
         moved=18 * cells * width,
     )
-    grad_pair = call(
+    (grad_pair,) = call(
         back_kernel,
-        shape(rows, cols, width),
-        [
-            coef_v, wide, vmem(rows, cols, dtype=F32), wide, vector, proj_v, block, plane,
-            sems(3), sems(n_groups), sems(n_groups), sems(n_groups), sems(n_groups),
-        ],
+        (shape(rows, cols, width),),
+        [vector, vmem(width, 2 * hidden), block, plane, sems(2), sems(n_groups)],
         (grad_right, coef, zhat, inv, dzg, gain_in, proj_weight),
-        near=(0,),
+        near=range(5),
         flops=2 * cells * width * 3 * hidden,
         moved=22 * cells * width,
     )

time: 109 us -> 114 us (1.046)
  local copies, waits for them, and re-layouts: 1.14 us -> 7.09 us
  Pallas kernels: 33.3 us -> 31.7 us
    unnamed x2 -> x12, local copies, waits for them, and re-layouts: 1.07 us -> 7.03 us
    pallas_call x11, Pallas kernels: 33.3 us -> 31.7 us  [call(): pl.pallas_call(kernel, out_shape=[out if at in outs_near else pltpu.HBM(o...]
  transfers between devices with their start and end apart: 20 -> 20, of which waited for: 14 -> 14; matrix products, arithmetic and copies ran while one was open for 0% -> 0% of each run, Pallas kernels for 19% -> 18%
where the time goes in v7:
time: 114 us; the launch traced here: 113 us
  starting transfers between devices  38 us (33%)
  waiting for transfers between devices  34.9 us (31%)
  Pallas kernels  31.7 us (28%)
  local copies, waits for them, and re-layouts  7.09 us (6%)
    pallas_call x11, Pallas kernels, call(): pl.pallas_call(kernel, out_shape=[out if at in outs_near else pltpu.HBM(o...  31.7 us
    ppermute x16, waiting for transfers between devices, permute(): lax.ppermute(values, axes, [(at, at ^ distance) for at in range(size)])  24.9 us
    ppermute x16, starting transfers between devices, permute(): lax.ppermute(values, axes, [(at, at ^ distance) for at in range(size)])  18.8 us
    all_to_all x2, starting transfers between devices, exchange_all(): lax.all_to_all(flat, ('half', *within), split_axis=0, concat_axis=0, tile...  11.7 us
    all_to_all x2, waiting for transfers between devices, exchange(): lax.all_to_all(values, within, split_axis=0, concat_axis=0, tiled=True)  10 us
    all_to_all x2, starting transfers between devices, exchange(): lax.all_to_all(values, within, split_axis=0, concat_axis=0, tiled=True)  7.51 us
    unnamed x12, local copies, waits for them, and re-layouts  7.03 us
  transfers between devices with their start and end apart: 20, of which 14 were waited for; matrix products, arithmetic and copies ran while one was open for 0% of the time, Pallas kernels for 18%

profile of v7, /device:TPU:0, one launch (start us, length us, event | category | flops | bytes accessed | tf_op | source)
XLA Modules:
  0.0 112.8 jit_solution(287849063259420692)
XLA Ops:
  0.6 4.4 %shard_map.113 = bf16[2,16,8,16,128]{4,3,2,1,0:T(8,128)(2,1)} custom-call(bf16[16,128,128]{2,1,0:T(8,128)(2,1)} %pair_h.5, s32[256]{0:T(256)} %mask_h.5, s32[1,256]{1,0:T(1,128)} %bitcast.26, f32[1,128]{1,0:T(1,128)} %bitcast.29, f32[1,128]{1,0:T(1,128)} %bitcast.34, bf16[128,512]{1,0:T(8,128)(2,1)} %proj_h.9), custom_call_target="tpu_custom_call" | custom-call | flops 201326592 | bytes 1310720 | tf_op jit(solution)/shard_map/pallas_call | solution.py:467
  5.0 7.3 %all-to-all-start = ((bf16[32,8,16,128]{3,2,1,0:T(8,128)(2,1)}), bf16[32,8,16,128]{3,2,1,0:T(8,128)(2,1)S(1)}, u32[]{:S(2)}, u32[]{:S(2)}) async-start(bf16[32,8,16,128]{3,2,1,0:T(8,128)(2,1)} %bitcast.23), calls=%async_computation | async-start | bytes 2097152 | tf_op jit(solution)/shard_map/all_to_all | solution.py:521
  12.3 3.4 %shard_map.115 = (bf16[8,8,16,128]{3,2,1,0:T(8,128)(2,1)S(1)}, bf16[8,8,16,128]{3,2,1,0:T(8,128)(2,1)S(1)}) custom-call(bf16[16,128,128]{2,1,0:T(8,128)(2,1)} %pair_h.5, s32[256]{0:T(256)} %mask_h.5, s32[1,256]{1,0:T(1,128)} %bitcast.27, f32[1,128]{1,0:T(1,128)} %bitcast.30, f32[1,128]{1,0:T(1,128)} %bitcast.35, bf16[128,512]{1,0:T(8,128)(2,1)} %proj_h.9), custom_call_target="tpu_custom_call" | custom-call | flops 201326592 | bytes 1310720 | tf_op jit(solution)/shard_map/pallas_call | solution.py:467
  17.3 1.8 %collective-permute-start.1 = (bf16[2,8,16,128]{3,2,1,0:T(8,128)(2,1)S(1)}, bf16[2,8,16,128]{3,2,1,0:T(8,128)(2,1)S(1)}, u32[]{:S(2)}, u32[]{:S(2)}) collective-permute-start(bf16[2,8,16,128]{3,2,1,0:T(8,128)(2,1)S(1)} %pad_maximum_fusion), channel_id=1, source_target_pairs={{0,1},{1,0},{4,5},{5,4},{8,9},{9,8},{12,13},{13,12},{2,3},{3,2},{6... | collective-permute-start | bytes 196616 | tf_op jit(solution)/shard_map/ppermute | solution.py:526
  21.0 1.8 %collective-permute-start.4 = (bf16[2,8,16,128]{3,2,1,0:T(8,128)(2,1)S(1)}, bf16[2,8,16,128]{3,2,1,0:T(8,128)(2,1)S(1)}, u32[]{:S(2)}, u32[]{:S(2)}) collective-permute-start(bf16[2,8,16,128]{3,2,1,0:T(8,128)(2,1)S(1)} %pad_maximum_fusion.3), channel_id=1, source_target_pairs={{0,8},{1,9},{4,12},{5,13},{8,0},{9,1},{12,4},{13,5},{2,10},{3,11},... | collective-permute-start | bytes 196616 | tf_op jit(solution)/shard_map/ppermute | solution.py:526
  24.4 2.4 %collective-permute-start.6 = (bf16[2,8,16,128]{3,2,1,0:T(8,128)(2,1)S(1)}, bf16[2,8,16,128]{3,2,1,0:T(8,128)(2,1)S(1)}, u32[]{:S(2)}, u32[]{:S(2)}) collective-permute-start(bf16[2,8,16,128]{3,2,1,0:T(8,128)(2,1)S(1)} %pad_maximum_fusion.5), channel_id=1, source_target_pairs={{0,12},{1,13},{4,8},{5,9},{8,4},{9,5},{12,0},{13,1},{2,14},{3,15},... | collective-permute-start | bytes 196616 | tf_op jit(solution)/shard_map/ppermute | solution.py:526
  28.1 4.9 %shard_map.114 = (f32[16,128,128]{2,1,0:T(8,128)}, f32[16,128]{1,0:T(8,128)}, f32[16,128,128]{2,1,0:T(8,128)}, f32[2048,128]{1,0:T(8,128)}) custom-call(bf16[16,128,128]{2,1,0:T(8,128)(2,1)} %pair_h.5, bf16[16,128,128]{2,1,0:T(8,128)(2,1)} %cot_h.3, f32[1,128]{1,0:T(1,128)} %bitcast.31, f32[1,128]{1,0:T(1,128)} %bitcast.36, bf16[128,128]{1,0:T(8,128)(2,1)} %gate_w_h.1, ...), custom_call_target="tpu_custom_call" | custom-call | flops 268435456 | bytes 4194304 | tf_op jit(solution)/shard_map/pallas_call | solution.py:467
  33.2 2.7 %collective-permute-done.6.refs_7_ = bf16[2,8,16,128]{3,2,1,0:T(8,128)(2,1)S(1)} collective-permute-done((bf16[2,8,16,128]{3,2,1,0:T(8,128)(2,1)S(1)}, bf16[2,8,16,128]{3,2,1,0:T(8,128)(2,1)S(1)}, u32[]{:S(2)}, u32[]{:S(2)}) %collective-permute-start.6) | collective-permute-done | bytes 65568 | tf_op jit(solution)/shard_map/ppermute | solution.py:526
  35.9 2.9 %collective-permute-done.7.refs_8_ = bf16[2,8,16,128]{3,2,1,0:T(8,128)(2,1)S(1)} collective-permute-done((bf16[2,8,16,128]{3,2,1,0:T(8,128)(2,1)S(1)}, bf16[2,8,16,128]{3,2,1,0:T(8,128)(2,1)S(1)}, u32[]{:S(2)}, u32[]{:S(2)}) %collective-permute-start.7) | collective-permute-done | bytes 65568 | tf_op jit(solution)/shard_map/ppermute | solution.py:526
  40.9 3.9 %all-to-all-start.1 = ((bf16[16,8,16,128]{3,2,1,0:T(8,128)(2,1)}), bf16[16,8,16,128]{3,2,1,0:T(8,128)(2,1)S(1)}, u32[]{:S(2)}, u32[]{:S(2)}) async-start(bf16[16,8,16,128]{3,2,1,0:T(8,128)(2,1)} %bitcast.24), calls=%async_computation.1 | async-start | bytes 1048576 | tf_op jit(solution)/shard_map/all_to_all | solution.py:517
  44.8 4.1 %shard_map.117 = (f32[16,4,128,128]{3,2,1,0:T(8,128)}, f32[128,16,128]{2,1,0:T(8,128)S(1)}) custom-call(f32[16,128,128]{2,1,0:T(8,128)} %get-tuple-element.25.zhat_h, s32[256]{0:T(256)} %mask_h.5, s32[1,256]{1,0:T(1,128)} %bitcast.28, f32[1,128]{1,0:T(1,128)} %bitcast.32, f32[1,128]{1,0:T(1,128)} %bitcast.37, bf16[128,512]{1,0:T(8,128)(2,1)} %proj_h.9, ...), custom_call_target="tpu_custom_call" | custom-call | flops 335544320 | bytes 5242880 | tf_op jit(solution)/shard_map/pallas_call | solution.py:467
  49.0 5.0 %all-to-all-done.1 = bf16[16,8,16,128]{3,2,1,0:T(8,128)(2,1)S(1)} async-done(((bf16[16,8,16,128]{3,2,1,0:T(8,128)(2,1)}), bf16[16,8,16,128]{3,2,1,0:T(8,128)(2,1)S(1)}, u32[]{:S(2)}, u32[]{:S(2)}) %all-to-all-start.1) | async-done | bytes 524320 | tf_op jit(solution)/shard_map/all_to_all | solution.py:517
  55.3 3.6 %all-to-all-start.2 = ((bf16[16,8,16,128]{3,2,1,0:T(8,128)(2,1)}), bf16[16,8,16,128]{3,2,1,0:T(8,128)(2,1)S(1)}, u32[]{:S(2)}, u32[]{:S(2)}) async-start(bf16[16,8,16,128]{3,2,1,0:T(8,128)(2,1)} %bitcast.21), calls=%async_computation.2 | async-start | bytes 1048576 | tf_op jit(solution)/shard_map/all_to_all | solution.py:517
  58.9 4.1 %shard_map.119 = (bf16[16,128,128]{2,1,0:T(8,128)(2,1)}, f32[16,128,128]{2,1,0:T(8,128)}) custom-call(bf16[128,16,128]{2,1,0:T(8,128)(2,1)S(1)} %bitcast.19, f32[16,128,128]{2,1,0:T(8,128)} %get-tuple-element.24.gate_h, bf16[16,128,128]{2,1,0:T(8,128)(2,1)} %cot_h.3, f32[1,128]{1,0:T(1,128)} %bitcast.39, f32[1,128]{1,0:T(1,128)} %bitcast.40, ...), custom_call_target="tpu_custom_call" | custom-call | flops 201326592 | bytes 3670016 | tf_op jit(solution)/shard_map/pallas_call | solution.py:467
  63.0 5.0 %all-to-all-done.2 = bf16[16,8,16,128]{3,2,1,0:T(8,128)(2,1)S(1)} async-done(((bf16[16,8,16,128]{3,2,1,0:T(8,128)(2,1)}), bf16[16,8,16,128]{3,2,1,0:T(8,128)(2,1)S(1)}, u32[]{:S(2)}, u32[]{:S(2)}) %all-to-all-start.2) | async-done | bytes 524320 | tf_op jit(solution)/shard_map/all_to_all | solution.py:517
  70.4 4.3 %all-to-all-start.3 = ((bf16[32,8,16,128]{3,2,1,0:T(8,128)(2,1)}), bf16[32,8,16,128]{3,2,1,0:T(8,128)(2,1)S(1)}, u32[]{:S(2)}, u32[]{:S(2)}) async-start(bf16[32,8,16,128]{3,2,1,0:T(8,128)(2,1)} %bitcast.22), calls=%async_computation.3 | async-start | bytes 2097152 | tf_op jit(solution)/shard_map/all_to_all | solution.py:521
  76.8 1.7 %collective-permute-start.9 = (bf16[2,8,16,128]{3,2,1,0:T(8,128)(2,1)S(1)}, bf16[2,8,16,128]{3,2,1,0:T(8,128)(2,1)S(1)}, u32[]{:S(2)}, u32[]{:S(2)}) collective-permute-start(bf16[2,8,16,128]{3,2,1,0:T(8,128)(2,1)S(1)} %pad_maximum_fusion.7), channel_id=1, source_target_pairs={{0,1},{1,0},{4,5},{5,4},{8,9},{9,8},{12,13},{13,12},{2,3},{3,2},{6... | collective-permute-start | bytes 196616 | tf_op jit(solution)/shard_map/ppermute | solution.py:526
  80.5 1.7 %collective-permute-start.12 = (bf16[2,8,16,128]{3,2,1,0:T(8,128)(2,1)S(1)}, bf16[2,8,16,128]{3,2,1,0:T(8,128)(2,1)S(1)}, u32[]{:S(2)}, u32[]{:S(2)}) collective-permute-start(bf16[2,8,16,128]{3,2,1,0:T(8,128)(2,1)S(1)} %pad_maximum_fusion.10), channel_id=1, source_target_pairs={{0,8},{1,9},{4,12},{5,13},{8,0},{9,1},{12,4},{13,5},{2,10},{3,11},... | collective-permute-start | bytes 196616 | tf_op jit(solution)/shard_map/ppermute | solution.py:526
  83.8 2.9 %collective-permute-done.9.refs_2_ = bf16[2,8,16,128]{3,2,1,0:T(8,128)(2,1)S(1)} collective-permute-done((bf16[2,8,16,128]{3,2,1,0:T(8,128)(2,1)S(1)}, bf16[2,8,16,128]{3,2,1,0:T(8,128)(2,1)S(1)}, u32[]{:S(2)}, u32[]{:S(2)}) %collective-permute-start.9) | collective-permute-done | bytes 65568 | tf_op jit(solution)/shard_map/ppermute | solution.py:526
  89.6 4.5 %collective-permute-done.12.refs_5_ = bf16[2,8,16,128]{3,2,1,0:T(8,128)(2,1)S(1)} collective-permute-done((bf16[2,8,16,128]{3,2,1,0:T(8,128)(2,1)S(1)}, bf16[2,8,16,128]{3,2,1,0:T(8,128)(2,1)S(1)}, u32[]{:S(2)}, u32[]{:S(2)}) %collective-permute-start.12) | collective-permute-done | bytes 65568 | tf_op jit(solution)/shard_map/ppermute | solution.py:526
  95.5 2.7 %collective-permute-done.14.refs_7_ = bf16[2,8,16,128]{3,2,1,0:T(8,128)(2,1)S(1)} collective-permute-done((bf16[2,8,16,128]{3,2,1,0:T(8,128)(2,1)S(1)}, bf16[2,8,16,128]{3,2,1,0:T(8,128)(2,1)S(1)}, u32[]{:S(2)}, u32[]{:S(2)}) %collective-permute-start.14) | collective-permute-done | bytes 65568 | tf_op jit(solution)/shard_map/ppermute | solution.py:526
  98.2 2.9 %collective-permute-done.15.refs_8_ = bf16[2,8,16,128]{3,2,1,0:T(8,128)(2,1)S(1)} collective-permute-done((bf16[2,8,16,128]{3,2,1,0:T(8,128)(2,1)S(1)}, bf16[2,8,16,128]{3,2,1,0:T(8,128)(2,1)S(1)}, u32[]{:S(2)}, u32[]{:S(2)}) %collective-permute-start.15) | collective-permute-done | bytes 65568 | tf_op jit(solution)/shard_map/ppermute | solution.py:526
  101.0 3.3 %shard_map.122 = (f32[16,128,128]{2,1,0:T(8,128)S(1)}, f32[16,2,128,128]{3,2,1,0:T(8,128)S(1)}, f32[16,128,128]{2,1,0:T(8,128)S(1)}, f32[16,128]{1,0:T(8,128)S(1)}) custom-call(f32[16,4,128,128]{3,2,1,0:T(8,128)} %get-tuple-element.31.coef_h, f32[16,128,128]{2,1,0:T(8,128)} %get-tuple-element.30.after.dzg_h, f32[16,128,128]{2,1,0:T(8,128)} %get-tuple-element.25.zhat_h, ...), custom_call_target="tpu_custom_call" | custom-call | flops 134217728 | bytes 4718592 | tf_op jit(solution)/shard_map/pallas_call | solution.py:467
  109.5 3.1 %shard_map.123 = bf16[16,128,128]{2,1,0:T(8,128)(2,1)} custom-call(bf16[2,16,8,16,128]{4,3,2,1,0:T(8,128)(2,1)S(1)} %bitcast.20, f32[16,2,128,128]{3,2,1,0:T(8,128)S(1)} %copy-done.1, f32[16,128,128]{2,1,0:T(8,128)S(1)} %copy-done.3, f32[16,128]{1,0:T(8,128)S(1)} %get-tuple-element.36.inv, f32[16,128,128]{2,1,0:T(8,128)S(1)} %get-tuple-element.37.dzg, ...), custom_call_target="tpu_custom_call" | custom-call | flops 201326592 | bytes 5767168 | tf_op jit(solution)/shard_map/pallas_call | solution.py:467
  (57 shorter events, 27.4 us)
Async XLA Ops:
  5.0 33.7 %all-to-all-start = ((bf16[32,8,16,128]{3,2,1,0:T(8,128)(2,1)}), bf16[32,8,16,128]{3,2,1,0:T(8,128)(2,1)S(1)}, u32[]{:S(2)}, u32[]{:S(2)}) async-start(bf16[32,8,16,128]{3,2,1,0:T(8,128)(2,1)} %bitcast.23), calls=%async_computation | async-start | bytes 2097152 | tf_op jit(solution)/shard_map/all_to_all | solution.py:521
  15.7 1.6 %collective-permute-start = (bf16[8,8,16,128]{3,2,1,0:T(8,128)(2,1)S(1)}, bf16[8,8,16,128]{3,2,1,0:T(8,128)(2,1)S(1)}, u32[]{:S(2)}, u32[]{:S(2)}) collective-permute-start(bf16[8,8,16,128]{3,2,1,0:T(8,128)(2,1)S(1)} %get-tuple-element.22), channel_id=1, source_target_pairs={{0,2},{2,0},{1,3},{3,1},{4,6},{6,4},{5,7},{7,5},{8,10},{10,8},{9,1... | collective-permute-start | bytes 786440 | tf_op jit(solution)/shard_map/ppermute | solution.py:526
  17.3 7.1 %collective-permute-start.1 = (bf16[2,8,16,128]{3,2,1,0:T(8,128)(2,1)S(1)}, bf16[2,8,16,128]{3,2,1,0:T(8,128)(2,1)S(1)}, u32[]{:S(2)}, u32[]{:S(2)}) collective-permute-start(bf16[2,8,16,128]{3,2,1,0:T(8,128)(2,1)S(1)} %pad_maximum_fusion), channel_id=1, source_target_pairs={{0,1},{1,0},{4,5},{5,4},{8,9},{9,8},{12,13},{13,12},{2,3},{3,2},{6... | collective-permute-start | bytes 196616 | tf_op jit(solution)/shard_map/ppermute | solution.py:526
  19.2 8.4 %collective-permute-start.2 = (bf16[2,8,16,128]{3,2,1,0:T(8,128)(2,1)S(1)}, bf16[2,8,16,128]{3,2,1,0:T(8,128)(2,1)S(1)}, u32[]{:S(2)}, u32[]{:S(2)}) collective-permute-start(bf16[2,8,16,128]{3,2,1,0:T(8,128)(2,1)S(1)} %pad_maximum_fusion.1), channel_id=1, source_target_pairs={{0,4},{1,5},{4,0},{5,1},{8,12},{9,13},{12,8},{13,9},{2,6},{3,7},{6... | collective-permute-start | bytes 196616 | tf_op jit(solution)/shard_map/ppermute | solution.py:526
  20.7 12.3 %collective-permute-start.3 = (bf16[2,8,16,128]{3,2,1,0:T(8,128)(2,1)S(1)}, bf16[2,8,16,128]{3,2,1,0:T(8,128)(2,1)S(1)}, u32[]{:S(2)}, u32[]{:S(2)}) collective-permute-start(bf16[2,8,16,128]{3,2,1,0:T(8,128)(2,1)S(1)} %pad_maximum_fusion.2), channel_id=1, source_target_pairs={{0,5},{1,4},{4,1},{5,0},{8,13},{9,12},{12,9},{13,8},{2,7},{3,6},{6... | collective-permute-start | bytes 196616 | tf_op jit(solution)/shard_map/ppermute | solution.py:526
  21.0 11.9 %collective-permute-start.4 = (bf16[2,8,16,128]{3,2,1,0:T(8,128)(2,1)S(1)}, bf16[2,8,16,128]{3,2,1,0:T(8,128)(2,1)S(1)}, u32[]{:S(2)}, u32[]{:S(2)}) collective-permute-start(bf16[2,8,16,128]{3,2,1,0:T(8,128)(2,1)S(1)} %pad_maximum_fusion.3), channel_id=1, source_target_pairs={{0,8},{1,9},{4,12},{5,13},{8,0},{9,1},{12,4},{13,5},{2,10},{3,11},... | collective-permute-start | bytes 196616 | tf_op jit(solution)/shard_map/ppermute | solution.py:526
  22.9 10.3 %collective-permute-start.5 = (bf16[2,8,16,128]{3,2,1,0:T(8,128)(2,1)S(1)}, bf16[2,8,16,128]{3,2,1,0:T(8,128)(2,1)S(1)}, u32[]{:S(2)}, u32[]{:S(2)}) collective-permute-start(bf16[2,8,16,128]{3,2,1,0:T(8,128)(2,1)S(1)} %pad_maximum_fusion.4), channel_id=1, source_target_pairs={{0,9},{1,8},{4,13},{5,12},{8,1},{9,0},{12,5},{13,4},{2,11},{3,10},... | collective-permute-start | bytes 196616 | tf_op jit(solution)/shard_map/ppermute | solution.py:526
  24.4 11.4 %collective-permute-start.6 = (bf16[2,8,16,128]{3,2,1,0:T(8,128)(2,1)S(1)}, bf16[2,8,16,128]{3,2,1,0:T(8,128)(2,1)S(1)}, u32[]{:S(2)}, u32[]{:S(2)}) collective-permute-start(bf16[2,8,16,128]{3,2,1,0:T(8,128)(2,1)S(1)} %pad_maximum_fusion.5), channel_id=1, source_target_pairs={{0,12},{1,13},{4,8},{5,9},{8,4},{9,5},{12,0},{13,1},{2,14},{3,15},... | collective-permute-start | bytes 196616 | tf_op jit(solution)/shard_map/ppermute | solution.py:526
  27.6 11.1 %collective-permute-start.7 = (bf16[2,8,16,128]{3,2,1,0:T(8,128)(2,1)S(1)}, bf16[2,8,16,128]{3,2,1,0:T(8,128)(2,1)S(1)}, u32[]{:S(2)}, u32[]{:S(2)}) collective-permute-start(bf16[2,8,16,128]{3,2,1,0:T(8,128)(2,1)S(1)} %pad_maximum_fusion.6), channel_id=1, source_target_pairs={{0,13},{1,12},{4,9},{5,8},{8,5},{9,4},{12,1},{13,0},{2,15},{3,14},... | collective-permute-start | bytes 196616 | tf_op jit(solution)/shard_map/ppermute | solution.py:526
  40.9 13.1 %all-to-all-start.1 = ((bf16[16,8,16,128]{3,2,1,0:T(8,128)(2,1)}), bf16[16,8,16,128]{3,2,1,0:T(8,128)(2,1)S(1)}, u32[]{:S(2)}, u32[]{:S(2)}) async-start(bf16[16,8,16,128]{3,2,1,0:T(8,128)(2,1)} %bitcast.24), calls=%async_computation.1 | async-start | bytes 1048576 | tf_op jit(solution)/shard_map/all_to_all | solution.py:517
  55.3 12.7 %all-to-all-start.2 = ((bf16[16,8,16,128]{3,2,1,0:T(8,128)(2,1)}), bf16[16,8,16,128]{3,2,1,0:T(8,128)(2,1)S(1)}, u32[]{:S(2)}, u32[]{:S(2)}) async-start(bf16[16,8,16,128]{3,2,1,0:T(8,128)(2,1)} %bitcast.21), calls=%async_computation.2 | async-start | bytes 1048576 | tf_op jit(solution)/shard_map/all_to_all | solution.py:517
  68.0 1.0 copy-start.5
  70.4 36.2 %all-to-all-start.3 = ((bf16[32,8,16,128]{3,2,1,0:T(8,128)(2,1)}), bf16[32,8,16,128]{3,2,1,0:T(8,128)(2,1)S(1)}, u32[]{:S(2)}, u32[]{:S(2)}) async-start(bf16[32,8,16,128]{3,2,1,0:T(8,128)(2,1)} %bitcast.22), calls=%async_computation.3 | async-start | bytes 2097152 | tf_op jit(solution)/shard_map/all_to_all | solution.py:521
  75.2 1.6 %collective-permute-start.8 = (bf16[8,8,16,128]{3,2,1,0:T(8,128)(2,1)S(1)}, bf16[8,8,16,128]{3,2,1,0:T(8,128)(2,1)S(1)}, u32[]{:S(2)}, u32[]{:S(2)}) collective-permute-start(bf16[8,8,16,128]{3,2,1,0:T(8,128)(2,1)S(1)} %get-tuple-element.33), channel_id=1, source_target_pairs={{0,2},{2,0},{1,3},{3,1},{4,6},{6,4},{5,7},{7,5},{8,10},{10,8},{9,1... | collective-permute-start | bytes 786440 | tf_op jit(solution)/shard_map/ppermute | solution.py:526
  76.8 9.8 %collective-permute-start.9 = (bf16[2,8,16,128]{3,2,1,0:T(8,128)(2,1)S(1)}, bf16[2,8,16,128]{3,2,1,0:T(8,128)(2,1)S(1)}, u32[]{:S(2)}, u32[]{:S(2)}) collective-permute-start(bf16[2,8,16,128]{3,2,1,0:T(8,128)(2,1)S(1)} %pad_maximum_fusion.7), channel_id=1, source_target_pairs={{0,1},{1,0},{4,5},{5,4},{8,9},{9,8},{12,13},{13,12},{2,3},{3,2},{6... | collective-permute-start | bytes 196616 | tf_op jit(solution)/shard_map/ppermute | solution.py:526
  78.5 9.9 %collective-permute-start.10 = (bf16[2,8,16,128]{3,2,1,0:T(8,128)(2,1)S(1)}, bf16[2,8,16,128]{3,2,1,0:T(8,128)(2,1)S(1)}, u32[]{:S(2)}, u32[]{:S(2)}) collective-permute-start(bf16[2,8,16,128]{3,2,1,0:T(8,128)(2,1)S(1)} %pad_maximum_fusion.8), channel_id=1, source_target_pairs={{0,4},{1,5},{4,0},{5,1},{8,12},{9,13},{12,8},{13,9},{2,6},{3,7},{6... | collective-permute-start | bytes 196616 | tf_op jit(solution)/shard_map/ppermute | solution.py:526
  80.1 9.6 %collective-permute-start.11 = (bf16[2,8,16,128]{3,2,1,0:T(8,128)(2,1)S(1)}, bf16[2,8,16,128]{3,2,1,0:T(8,128)(2,1)S(1)}, u32[]{:S(2)}, u32[]{:S(2)}) collective-permute-start(bf16[2,8,16,128]{3,2,1,0:T(8,128)(2,1)S(1)} %pad_maximum_fusion.9), channel_id=1, source_target_pairs={{0,5},{1,4},{4,1},{5,0},{8,13},{9,12},{12,9},{13,8},{2,7},{3,6},{6... | collective-permute-start | bytes 196616 | tf_op jit(solution)/shard_map/ppermute | solution.py:526
  80.5 13.6 %collective-permute-start.12 = (bf16[2,8,16,128]{3,2,1,0:T(8,128)(2,1)S(1)}, bf16[2,8,16,128]{3,2,1,0:T(8,128)(2,1)S(1)}, u32[]{:S(2)}, u32[]{:S(2)}) collective-permute-start(bf16[2,8,16,128]{3,2,1,0:T(8,128)(2,1)S(1)} %pad_maximum_fusion.10), channel_id=1, source_target_pairs={{0,8},{1,9},{4,12},{5,13},{8,0},{9,1},{12,4},{13,5},{2,10},{3,11},... | collective-permute-start | bytes 196616 | tf_op jit(solution)/shard_map/ppermute | solution.py:526
  82.2 13.3 %collective-permute-start.13 = (bf16[2,8,16,128]{3,2,1,0:T(8,128)(2,1)S(1)}, bf16[2,8,16,128]{3,2,1,0:T(8,128)(2,1)S(1)}, u32[]{:S(2)}, u32[]{:S(2)}) collective-permute-start(bf16[2,8,16,128]{3,2,1,0:T(8,128)(2,1)S(1)} %pad_maximum_fusion.11), channel_id=1, source_target_pairs={{0,9},{1,8},{4,13},{5,12},{8,1},{9,0},{12,5},{13,4},{2,11},{3,10},... | collective-permute-start | bytes 196616 | tf_op jit(solution)/shard_map/ppermute | solution.py:526
  86.6 11.5 %collective-permute-start.14 = (bf16[2,8,16,128]{3,2,1,0:T(8,128)(2,1)S(1)}, bf16[2,8,16,128]{3,2,1,0:T(8,128)(2,1)S(1)}, u32[]{:S(2)}, u32[]{:S(2)}) collective-permute-start(bf16[2,8,16,128]{3,2,1,0:T(8,128)(2,1)S(1)} %pad_maximum_fusion.12), channel_id=1, source_target_pairs={{0,12},{1,13},{4,8},{5,9},{8,4},{9,5},{12,0},{13,1},{2,14},{3,15},... | collective-permute-start | bytes 196616 | tf_op jit(solution)/shard_map/ppermute | solution.py:526
  88.4 12.6 %collective-permute-start.15 = (bf16[2,8,16,128]{3,2,1,0:T(8,128)(2,1)S(1)}, bf16[2,8,16,128]{3,2,1,0:T(8,128)(2,1)S(1)}, u32[]{:S(2)}, u32[]{:S(2)}) collective-permute-start(bf16[2,8,16,128]{3,2,1,0:T(8,128)(2,1)S(1)} %pad_maximum_fusion.13), channel_id=1, source_target_pairs={{0,13},{1,12},{4,9},{5,8},{8,5},{9,4},{12,1},{13,0},{2,15},{3,14},... | collective-permute-start | bytes 196616 | tf_op jit(solution)/shard_map/ppermute | solution.py:526
  104.3 1.4 %copy-start = (f32[16,2,128,128]{3,2,1,0:T(8,128)}, f32[16,2,128,128]{3,2,1,0:T(8,128)S(1)}, u32[]{:S(2)}) copy-start(f32[16,2,128,128]{3,2,1,0:T(8,128)S(1)} %get-tuple-element.34.coef) | copy-start | bytes 6291460
  106.7 1.6 %copy-start.1 = (f32[16,2,128,128]{3,2,1,0:T(8,128)S(1)}, f32[16,2,128,128]{3,2,1,0:T(8,128)}, u32[]{:S(2)}) copy-start(f32[16,2,128,128]{3,2,1,0:T(8,128)} %copy-done) | copy-start | bytes 6291460
  108.3 1.2 %copy-start.3 = (f32[16,128,128]{2,1,0:T(8,128)S(1)}, f32[16,128,128]{2,1,0:T(8,128)}, u32[]{:S(2)}) copy-start(f32[16,128,128]{2,1,0:T(8,128)} %copy-done.2) | copy-start | bytes 3145732
  (2 other events, 1.8 us)

commit v8 on v7

--- a/solution.py
+++ b/solution.py
@@ -282,11 +282,11 @@
 
 
 def product_kernel(n_chip, right, after, *refs):
-    pieces, (out_h, left, ready, sems) = refs[:-4], refs[-4:]
+    pieces, (out_h, left_h, left, ready, sems, left_sem) = refs[:-6], refs[-6:]
     n_col, share = left.shape[1:3]
     for number, piece in received(pieces, n_chip):
         left[number // n_col, number % n_col] = piece
-    leaving = []
+    leaving = start(left_sem, [(left, left_h)])
     for h in range(share):
         values = dot(channel_matrix(left, h), channel_matrix(right, h), ((1,), (1,)))
         put_channel(ready, h, values)
@@ -317,12 +317,14 @@
 
 
 def update_kernel(
-    product, gate_h, cot_h, norm_gain_h, norm_bias_h, out_w_h, gate_w_h, after, update_h, dzg_h,
+    product, gate_h, cot_h, norm_gain_h, norm_bias_h, out_w_h, gate_w_h, left_h, after, update_h, dzg_h,
+    left,
     gate, cot, norm_gain, norm_bias, out_weight, gate_weight, update, dzg, spread,
-    in_sems, out_sems,
+    in_sems, out_sems, fetch_sems,
 ):
     hidden, rows, cols = product.shape
     width = cot.shape[2]
+    fetched = start(fetch_sems, [(left_h, left)])
     copies = start(
         in_sems,
         [
@@ -352,7 +354,7 @@
             lanes = slice(r * cols, (r + 1) * cols)
             update[at + r] = turned(done[:, lanes]).astype(BF16)
             dzg[at + r] = back[:, lanes]
-    wait(start(out_sems, [(update, update_h), (dzg, dzg_h)]))
+    wait(fetched + start(out_sems, [(update, update_h), (dzg, dzg_h)]))
 
 
 def grad_right_kernel(grad, left, after, out_h, ready, sems):
@@ -373,78 +375,57 @@
         outs[m][n] = ready[number // n_col, number % n_col]
 
 
-def through_projection(plane, coef, weight, at, size, rows):
-    hidden = plane.shape[0] // rows
-    columns = []
-    for r in range(size):
-        g = plane[pl.ds(at + r, hidden, stride=rows), :]
-        columns.append(
-            jnp.concatenate(
-                [(g * coef[at + r, part]).astype(BF16) for part in range(2)], axis=0
-            )
-        )
-    return dot(weight, jnp.concatenate(columns, axis=1))
-
-
-def back_left_kernel(n_chip, coef_h, dzg_h, zhat_h, inv_h, proj_h, *refs):
-    pieces, (out, coef_right, zhat, inv) = refs[:-11], refs[-11:-7]
-    coef, dzg, proj_weight, plane, sems, coef_sems, dzg_sems = refs[-7:]
-    rows, width, cols = out.shape
-    hidden = plane.shape[0] // rows
+def back_kernel(n_chip, grads, coef_h, zhat_h, inv_h, dzg_h, gain_h, proj_h, *refs):
+    pieces, out_h = refs[:-15], refs[-15]
+    (
+        coef, zhat, inv, dzg, gain, proj_weight, out, left, right,
+        sems, coef_sems, zhat_sems, dzg_sems, out_sems,
+    ) = refs[-14:]
+    rows, cols, width = out.shape
+    hidden = left.shape[0] // rows
     groups = groups_of(rows)
-    (small, *fetched) = start(
-        sems,
-        [
-            (proj_h, proj_weight), (coef_h.at[:, pl.ds(2, 2)], coef_right), (zhat_h, zhat),
-            (inv_h, inv),
-        ],
-    )
-    blocks = [
-        start(
-            coef_sems,
+    small = start(sems, [(gain_h, gain), (proj_h, proj_weight), (inv_h, inv)])
+    blocks = []
+    for n, (at, size) in enumerate(groups):
+        part = pl.ds(at, size)
+        blocks.append(
             [
-                (coef_h.at[pl.ds(at, size), pl.ds(0, 2)], coef.at[pl.ds(at, size)])
-                for at, size in groups
-            ],
-        ),
-        start(
-            dzg_sems,
-            [(dzg_h.at[pl.ds(at, size)], dzg.at[pl.ds(at, size)]) for at, size in groups],
-        ),
-    ]
+                pltpu.make_async_copy(source.at[part], target.at[part], sem.at[n])
+                for source, target, sem in (
+                    (coef_h, coef, coef_sems), (zhat_h, zhat, zhat_sems), (dzg_h, dzg, dzg_sems)
+                )
+            ]
+        )
+        for copy in blocks[-1]:
+            copy.start()
     arrived = received(pieces, n_chip)
-    length = plane.shape[0] // len(arrived)
+    length = left.shape[0] // len(arrived)
     for number, piece in arrived:
         first = pl.multiple_of(number * length, length)
-        plane[pl.ds(first, length), :] = piece.astype(F32).reshape(length, cols)
-    small.wait()
-    weight = proj_weight[:, : 2 * hidden]
-    for n, (at, size) in enumerate(groups):
-        wait([copies[n] for copies in blocks])
-        back = through_projection(plane, coef, weight, at, size, rows)
-        for r in range(size):
-            out[at + r] = back[:, r * cols : (r + 1) * cols] + dzg[at + r]
-    wait(fetched)
-
-
-def back_kernel(
-    grads, coef, zhat, inv, dzg, gain_h, proj_h, out_h,
-    gain, proj_weight, out, plane, sems, out_sems,
-):
-    rows, cols, width = out.shape
-    hidden = plane.shape[0] // rows
-    groups = groups_of(rows)
-    small = start(sems, [(gain_h, gain), (proj_h.at[:, pl.ds(2 * hidden, 2 * hidden)], proj_weight)])
+        left[pl.ds(first, length), :] = piece.astype(F32).reshape(length, cols)
     total = grads[0].astype(F32)
     for half in range(1, grads.shape[0]):
         total = total + grads[half].astype(F32)
-    plane[...] = total.reshape(plane.shape)
+    right[...] = total.reshape(right.shape)
     wait(small)
     gain_b = jnp.concatenate([down_lanes(gain[...], cols)] * groups[0][1], axis=1)
-    weight = proj_weight[...]
     leaving = []
     for n, (at, size) in enumerate(groups):
-        back = through_projection(plane, coef, weight, at, size, rows)
+        wait(blocks[n])
+        columns = []
+        for r in range(size):
+            gl = left[pl.ds(at + r, hidden, stride=rows), :]
+            gr = right[pl.ds(at + r, hidden, stride=rows), :]
+            columns.append(
+                jnp.concatenate(
+                    [
+                        (g * coef[at + r, part]).astype(BF16)
+                        for part, g in enumerate((gl, gl, gr, gr))
+                    ],
+                    axis=0,
+                )
+            )
+        back = dot(proj_weight[...], jnp.concatenate(columns, axis=1))
         dzh = (back + side_by_side(dzg, at, size)) * gain_b
         z = side_by_side(zhat, at, size)
         inverse = jnp.concatenate([inv[at + r : at + r + 1] for r in range(size)], axis=1)
@@ -473,7 +454,7 @@
         in_specs=specs,
         out_specs=[here if at in outs_near else far for at in range(len(outs))],
         scratch_shapes=scratch,
-        compiler_params=pltpu.CompilerParams(vmem_limit_bytes=24 * MIB),
+        compiler_params=pltpu.CompilerParams(vmem_limit_bytes=16 * MIB),
         cost_estimate=pl.CostEstimate(flops=flops, bytes_accessed=moved, transcendentals=0),
     )(
         *[
@@ -542,7 +523,6 @@
     wide = vmem(rows, width, cols, dtype=F32)
     square = vmem(width, hidden)
     proj_v = vmem(width, 4 * hidden)
-    coef_v = vmem(rows, 2, hidden, cols, dtype=F32)
     pieces_shape = (shape(n_chip, share, rows, cols),) * n_core
     n_pieces = n_core + n_chip - 1
 
@@ -588,10 +568,12 @@
     product, left = call(
         functools.partial(product_kernel, n_chip),
         (shape(n_line, n_col, share, rows, cols), shape(n_line, n_col, share, rows, cols)),
-        [vmem(n_line, n_col, share, rows, cols), sems(share)],
+        [
+            vmem(n_line, n_col, share, rows, cols), vmem(n_line, n_col, share, rows, cols),
+            sems(share), sems(1),
+        ],
         (right, inv, *left),
         near=(0, *range(2, 2 + n_pieces)),
-        outs_near=(1,),
         flops=2 * share * n_half * (n_line * rows) ** 2 * n_col * cols,
         moved=8 * cells * hidden,
     )
@@ -623,12 +605,20 @@
     )
     grad = exchange(sent.reshape(n_place, share, rows, cols))
     grad = grad.reshape(n_line, n_col, share, rows, cols)
-    update, dzg = call(
+    update, dzg, left = call(
         update_kernel,
-        (shape(rows, cols, width), shape(rows, width, cols, dtype=F32)),
-        [wide, block, vector, vector, square, square, block, wide, plane, sems(6), sems(2)],
-        (product, gate, cotangent, norm_gain, norm_bias, out_weight, gate_weight, sent),
+        (
+            shape(rows, cols, width),
+            shape(rows, width, cols, dtype=F32),
+            shape(n_line, n_col, share, rows, cols),
+        ),
+        [
+            wide, block, vector, vector, square, square, block, wide, plane,
+            sems(6), sems(2), sems(1),
+        ],
+        (product, gate, cotangent, norm_gain, norm_bias, out_weight, gate_weight, left, sent),
         near=(0,),
+        outs_near=(2,),
         flops=2 * cells * width * 3 * hidden,
         moved=14 * cells * hidden,
     )
@@ -653,29 +643,18 @@
         moved=8 * cells * hidden,
     )
     grad_left = exchange_pieces(tuple(grad_left))
-    dzg, coef, zhat, inv = call(
-        functools.partial(back_left_kernel, n_chip),
-        (
-            shape(rows, width, cols, dtype=F32),
-            shape(rows, 2, hidden, cols, dtype=F32),
-            shape(rows, width, cols, dtype=F32),
-            shape(rows, cols, dtype=F32),
-        ),
-        [coef_v, wide, proj_v, plane, sems(4), sems(n_groups), sems(n_groups)],
-        (coef, dzg, zhat, inv, proj_weight, *grad_left),
-        near=tuple(range(5, 5 + n_pieces)),
-        outs_near=range(4),
-        flops=2 * cells * width * 2 * hidden,
-        moved=18 * cells * width,
-    )
     (grad_pair,) = call(
-        back_kernel,
+        functools.partial(back_kernel, n_chip),
         (shape(rows, cols, width),),
-        [vector, vmem(width, 2 * hidden), block, plane, sems(2), sems(n_groups)],
-        (grad_right, coef, zhat, inv, dzg, gain_in, proj_weight),
-        near=range(5),
-        flops=2 * cells * width * 3 * hidden,
-        moved=22 * cells * width,
+        [
+            vmem(rows, 4, hidden, cols, dtype=F32), wide, vmem(rows, cols, dtype=F32), wide,
+            vector, proj_v, block, plane, plane,
+            sems(3), sems(n_groups), sems(n_groups), sems(n_groups), sems(n_groups),
+        ],
+        (grad_right, coef, zhat, inv, dzg, gain_in, proj_weight, *grad_left),
+        near=(0, *range(7, 7 + n_pieces)),
+        flops=2 * cells * width * 5 * hidden,
+        moved=30 * cells * width,
     )
     return (update, grad_pair)
 

time: 114 us -> 106 us (0.930)
  local copies, waits for them, and re-layouts: 7.09 us -> 0.06 us
    unnamed x12 -> x0, local copies, waits for them, and re-layouts: 7.03 us -> none
    pallas_call x11 -> x10, Pallas kernels: 31.7 us -> 31.3 us  [call(): pl.pallas_call(kernel, out_shape=[out if at in outs_near else pltpu.HBM(o...]
  transfers between devices with their start and end apart: 20 -> 20, of which waited for: 14 -> 14; matrix products, arithmetic and copies ran while one was open for 0% -> 0% of each run, Pallas kernels for 18% -> 16%
where the time goes in v8:
time: 106 us; the launch traced here: 105 us
  starting transfers between devices  38 us (36%)
  waiting for transfers between devices  34.8 us (33%)
  Pallas kernels  31.3 us (30%)
    pallas_call x10, Pallas kernels, call(): pl.pallas_call(kernel, out_shape=[out if at in outs_near else pltpu.HBM(o...  31.3 us
    ppermute x16, waiting for transfers between devices, permute(): lax.ppermute(values, axes, [(at, at ^ distance) for at in range(size)])  24.8 us
    ppermute x16, starting transfers between devices, permute(): lax.ppermute(values, axes, [(at, at ^ distance) for at in range(size)])  18.8 us
    all_to_all x2, starting transfers between devices, exchange_all(): lax.all_to_all(flat, ('half', *within), split_axis=0, concat_axis=0, tile...  11.7 us
    all_to_all x2, waiting for transfers between devices, exchange(): lax.all_to_all(values, within, split_axis=0, concat_axis=0, tiled=True)  9.98 us
    all_to_all x2, starting transfers between devices, exchange(): lax.all_to_all(values, within, split_axis=0, concat_axis=0, tiled=True)  7.53 us
  transfers between devices with their start and end apart: 20, of which 14 were waited for; matrix products, arithmetic and copies ran while one was open for 0% of the time, Pallas kernels for 16%

profile of v8, /device:TPU:0, one launch (start us, length us, event | category | flops | bytes accessed | tf_op | source)
XLA Modules:
  0.0 105.3 jit_solution(10453268900835703684)
XLA Ops:
  0.6 4.4 %shard_map.113 = bf16[2,16,8,16,128]{4,3,2,1,0:T(8,128)(2,1)} custom-call(bf16[16,128,128]{2,1,0:T(8,128)(2,1)} %pair_h.5, s32[256]{0:T(256)} %mask_h.5, s32[1,256]{1,0:T(1,128)} %bitcast.26, f32[1,128]{1,0:T(1,128)} %bitcast.29, f32[1,128]{1,0:T(1,128)} %bitcast.34, bf16[128,512]{1,0:T(8,128)(2,1)} %proj_h.7), custom_call_target="tpu_custom_call" | custom-call | flops 201326592 | bytes 1310720 | tf_op jit(solution)/shard_map/pallas_call | solution.py:448
  5.0 7.3 %all-to-all-start = ((bf16[32,8,16,128]{3,2,1,0:T(8,128)(2,1)}), bf16[32,8,16,128]{3,2,1,0:T(8,128)(2,1)S(1)}, u32[]{:S(2)}, u32[]{:S(2)}) async-start(bf16[32,8,16,128]{3,2,1,0:T(8,128)(2,1)} %bitcast.23), calls=%async_computation | async-start | bytes 2097152 | tf_op jit(solution)/shard_map/all_to_all | solution.py:502
  12.3 3.4 %shard_map.115 = (bf16[8,8,16,128]{3,2,1,0:T(8,128)(2,1)S(1)}, bf16[8,8,16,128]{3,2,1,0:T(8,128)(2,1)S(1)}) custom-call(bf16[16,128,128]{2,1,0:T(8,128)(2,1)} %pair_h.5, s32[256]{0:T(256)} %mask_h.5, s32[1,256]{1,0:T(1,128)} %bitcast.27, f32[1,128]{1,0:T(1,128)} %bitcast.30, f32[1,128]{1,0:T(1,128)} %bitcast.35, bf16[128,512]{1,0:T(8,128)(2,1)} %proj_h.7), custom_call_target="tpu_custom_call" | custom-call | flops 201326592 | bytes 1310720 | tf_op jit(solution)/shard_map/pallas_call | solution.py:448
  17.4 1.8 %collective-permute-start.1 = (bf16[2,8,16,128]{3,2,1,0:T(8,128)(2,1)S(1)}, bf16[2,8,16,128]{3,2,1,0:T(8,128)(2,1)S(1)}, u32[]{:S(2)}, u32[]{:S(2)}) collective-permute-start(bf16[2,8,16,128]{3,2,1,0:T(8,128)(2,1)S(1)} %pad_maximum_fusion), channel_id=1, source_target_pairs={{0,1},{1,0},{4,5},{5,4},{8,9},{9,8},{12,13},{13,12},{2,3},{3,2},{6... | collective-permute-start | bytes 196616 | tf_op jit(solution)/shard_map/ppermute | solution.py:507
  19.2 1.5 %collective-permute-start.2 = (bf16[2,8,16,128]{3,2,1,0:T(8,128)(2,1)S(1)}, bf16[2,8,16,128]{3,2,1,0:T(8,128)(2,1)S(1)}, u32[]{:S(2)}, u32[]{:S(2)}) collective-permute-start(bf16[2,8,16,128]{3,2,1,0:T(8,128)(2,1)S(1)} %pad_maximum_fusion.1), channel_id=1, source_target_pairs={{0,4},{1,5},{4,0},{5,1},{8,12},{9,13},{12,8},{13,9},{2,6},{3,7},{6... | collective-permute-start | bytes 196616 | tf_op jit(solution)/shard_map/ppermute | solution.py:507
  21.1 1.8 %collective-permute-start.4 = (bf16[2,8,16,128]{3,2,1,0:T(8,128)(2,1)S(1)}, bf16[2,8,16,128]{3,2,1,0:T(8,128)(2,1)S(1)}, u32[]{:S(2)}, u32[]{:S(2)}) collective-permute-start(bf16[2,8,16,128]{3,2,1,0:T(8,128)(2,1)S(1)} %pad_maximum_fusion.3), channel_id=1, source_target_pairs={{0,8},{1,9},{4,12},{5,13},{8,0},{9,1},{12,4},{13,5},{2,10},{3,11},... | collective-permute-start | bytes 196616 | tf_op jit(solution)/shard_map/ppermute | solution.py:507
  24.4 2.4 %collective-permute-start.6 = (bf16[2,8,16,128]{3,2,1,0:T(8,128)(2,1)S(1)}, bf16[2,8,16,128]{3,2,1,0:T(8,128)(2,1)S(1)}, u32[]{:S(2)}, u32[]{:S(2)}) collective-permute-start(bf16[2,8,16,128]{3,2,1,0:T(8,128)(2,1)S(1)} %pad_maximum_fusion.5), channel_id=1, source_target_pairs={{0,12},{1,13},{4,8},{5,9},{8,4},{9,5},{12,0},{13,1},{2,14},{3,15},... | collective-permute-start | bytes 196616 | tf_op jit(solution)/shard_map/ppermute | solution.py:507
  28.1 4.9 %shard_map.114 = (f32[16,128,128]{2,1,0:T(8,128)}, f32[16,128]{1,0:T(8,128)}, f32[16,128,128]{2,1,0:T(8,128)}, f32[2048,128]{1,0:T(8,128)}) custom-call(bf16[16,128,128]{2,1,0:T(8,128)(2,1)} %pair_h.5, bf16[16,128,128]{2,1,0:T(8,128)(2,1)} %cot_h.3, f32[1,128]{1,0:T(1,128)} %bitcast.31, f32[1,128]{1,0:T(1,128)} %bitcast.36, bf16[128,128]{1,0:T(8,128)(2,1)} %gate_w_h.1, ...), custom_call_target="tpu_custom_call" | custom-call | flops 268435456 | bytes 4194304 | tf_op jit(solution)/shard_map/pallas_call | solution.py:448
  33.2 2.7 %collective-permute-done.6.refs_7_ = bf16[2,8,16,128]{3,2,1,0:T(8,128)(2,1)S(1)} collective-permute-done((bf16[2,8,16,128]{3,2,1,0:T(8,128)(2,1)S(1)}, bf16[2,8,16,128]{3,2,1,0:T(8,128)(2,1)S(1)}, u32[]{:S(2)}, u32[]{:S(2)}) %collective-permute-start.6) | collective-permute-done | bytes 65568 | tf_op jit(solution)/shard_map/ppermute | solution.py:507
  35.9 2.9 %collective-permute-done.7.refs_8_ = bf16[2,8,16,128]{3,2,1,0:T(8,128)(2,1)S(1)} collective-permute-done((bf16[2,8,16,128]{3,2,1,0:T(8,128)(2,1)S(1)}, bf16[2,8,16,128]{3,2,1,0:T(8,128)(2,1)S(1)}, u32[]{:S(2)}, u32[]{:S(2)}) %collective-permute-start.7) | collective-permute-done | bytes 65568 | tf_op jit(solution)/shard_map/ppermute | solution.py:507
  40.2 3.9 %all-to-all-start.1 = ((bf16[16,8,16,128]{3,2,1,0:T(8,128)(2,1)}), bf16[16,8,16,128]{3,2,1,0:T(8,128)(2,1)S(1)}, u32[]{:S(2)}, u32[]{:S(2)}) async-start(bf16[16,8,16,128]{3,2,1,0:T(8,128)(2,1)} %bitcast.24), calls=%async_computation.1 | async-start | bytes 1048576 | tf_op jit(solution)/shard_map/all_to_all | solution.py:498
  44.1 4.1 %shard_map.117 = (f32[16,4,128,128]{3,2,1,0:T(8,128)}, f32[128,16,128]{2,1,0:T(8,128)S(1)}) custom-call(f32[16,128,128]{2,1,0:T(8,128)} %get-tuple-element.23.zhat_h, s32[256]{0:T(256)} %mask_h.5, s32[1,256]{1,0:T(1,128)} %bitcast.28, f32[1,128]{1,0:T(1,128)} %bitcast.32, f32[1,128]{1,0:T(1,128)} %bitcast.37, bf16[128,512]{1,0:T(8,128)(2,1)} %proj_h.7, ...), custom_call_target="tpu_custom_call" | custom-call | flops 335544320 | bytes 5242880 | tf_op jit(solution)/shard_map/pallas_call | solution.py:448
  48.2 5.1 %all-to-all-done.1 = bf16[16,8,16,128]{3,2,1,0:T(8,128)(2,1)S(1)} async-done(((bf16[16,8,16,128]{3,2,1,0:T(8,128)(2,1)}), bf16[16,8,16,128]{3,2,1,0:T(8,128)(2,1)S(1)}, u32[]{:S(2)}, u32[]{:S(2)}) %all-to-all-start.1) | async-done | bytes 524320 | tf_op jit(solution)/shard_map/all_to_all | solution.py:498
  54.6 3.6 %all-to-all-start.2 = ((bf16[16,8,16,128]{3,2,1,0:T(8,128)(2,1)}), bf16[16,8,16,128]{3,2,1,0:T(8,128)(2,1)S(1)}, u32[]{:S(2)}, u32[]{:S(2)}) async-start(bf16[16,8,16,128]{3,2,1,0:T(8,128)(2,1)} %bitcast.21), calls=%async_computation.2 | async-start | bytes 1048576 | tf_op jit(solution)/shard_map/all_to_all | solution.py:498
  58.2 4.2 %shard_map.119 = (bf16[16,128,128]{2,1,0:T(8,128)(2,1)}, f32[16,128,128]{2,1,0:T(8,128)}, bf16[8,2,8,16,128]{4,3,2,1,0:T(8,128)(2,1)S(1)}) custom-call(bf16[128,16,128]{2,1,0:T(8,128)(2,1)S(1)} %bitcast.19, f32[16,128,128]{2,1,0:T(8,128)} %get-tuple-element.21.gate_h, bf16[16,128,128]{2,1,0:T(8,128)(2,1)} %cot_h.3, f32[1,128]{1,0:T(1,128)} %bitcast.39, ...), custom_call_target="tpu_custom_call" | custom-call | flops 201326592 | bytes 3670016 | tf_op jit(solution)/shard_map/pallas_call | solution.py:448
  62.4 4.9 %all-to-all-done.2 = bf16[16,8,16,128]{3,2,1,0:T(8,128)(2,1)S(1)} async-done(((bf16[16,8,16,128]{3,2,1,0:T(8,128)(2,1)}), bf16[16,8,16,128]{3,2,1,0:T(8,128)(2,1)S(1)}, u32[]{:S(2)}, u32[]{:S(2)}) %all-to-all-start.2) | async-done | bytes 524320 | tf_op jit(solution)/shard_map/all_to_all | solution.py:498
  68.6 4.4 %all-to-all-start.3 = ((bf16[32,8,16,128]{3,2,1,0:T(8,128)(2,1)}), bf16[32,8,16,128]{3,2,1,0:T(8,128)(2,1)S(1)}, u32[]{:S(2)}, u32[]{:S(2)}) async-start(bf16[32,8,16,128]{3,2,1,0:T(8,128)(2,1)} %bitcast.22), calls=%async_computation.3 | async-start | bytes 2097152 | tf_op jit(solution)/shard_map/all_to_all | solution.py:502
  75.1 1.7 %collective-permute-start.9 = (bf16[2,8,16,128]{3,2,1,0:T(8,128)(2,1)S(1)}, bf16[2,8,16,128]{3,2,1,0:T(8,128)(2,1)S(1)}, u32[]{:S(2)}, u32[]{:S(2)}) collective-permute-start(bf16[2,8,16,128]{3,2,1,0:T(8,128)(2,1)S(1)} %pad_maximum_fusion.7), channel_id=1, source_target_pairs={{0,1},{1,0},{4,5},{5,4},{8,9},{9,8},{12,13},{13,12},{2,3},{3,2},{6... | collective-permute-start | bytes 196616 | tf_op jit(solution)/shard_map/ppermute | solution.py:507
  78.8 1.7 %collective-permute-start.12 = (bf16[2,8,16,128]{3,2,1,0:T(8,128)(2,1)S(1)}, bf16[2,8,16,128]{3,2,1,0:T(8,128)(2,1)S(1)}, u32[]{:S(2)}, u32[]{:S(2)}) collective-permute-start(bf16[2,8,16,128]{3,2,1,0:T(8,128)(2,1)S(1)} %pad_maximum_fusion.10), channel_id=1, source_target_pairs={{0,8},{1,9},{4,12},{5,13},{8,0},{9,1},{12,4},{13,5},{2,10},{3,11},... | collective-permute-start | bytes 196616 | tf_op jit(solution)/shard_map/ppermute | solution.py:507
  82.0 2.9 %collective-permute-done.9.refs_2_ = bf16[2,8,16,128]{3,2,1,0:T(8,128)(2,1)S(1)} collective-permute-done((bf16[2,8,16,128]{3,2,1,0:T(8,128)(2,1)S(1)}, bf16[2,8,16,128]{3,2,1,0:T(8,128)(2,1)S(1)}, u32[]{:S(2)}, u32[]{:S(2)}) %collective-permute-start.9) | collective-permute-done | bytes 65568 | tf_op jit(solution)/shard_map/ppermute | solution.py:507
  87.9 4.5 %collective-permute-done.12.refs_5_ = bf16[2,8,16,128]{3,2,1,0:T(8,128)(2,1)S(1)} collective-permute-done((bf16[2,8,16,128]{3,2,1,0:T(8,128)(2,1)S(1)}, bf16[2,8,16,128]{3,2,1,0:T(8,128)(2,1)S(1)}, u32[]{:S(2)}, u32[]{:S(2)}) %collective-permute-start.12) | collective-permute-done | bytes 65568 | tf_op jit(solution)/shard_map/ppermute | solution.py:507
  93.7 2.7 %collective-permute-done.14.refs_7_ = bf16[2,8,16,128]{3,2,1,0:T(8,128)(2,1)S(1)} collective-permute-done((bf16[2,8,16,128]{3,2,1,0:T(8,128)(2,1)S(1)}, bf16[2,8,16,128]{3,2,1,0:T(8,128)(2,1)S(1)}, u32[]{:S(2)}, u32[]{:S(2)}) %collective-permute-start.14) | collective-permute-done | bytes 65568 | tf_op jit(solution)/shard_map/ppermute | solution.py:507
  96.4 2.9 %collective-permute-done.15.refs_8_ = bf16[2,8,16,128]{3,2,1,0:T(8,128)(2,1)S(1)} collective-permute-done((bf16[2,8,16,128]{3,2,1,0:T(8,128)(2,1)S(1)}, bf16[2,8,16,128]{3,2,1,0:T(8,128)(2,1)S(1)}, u32[]{:S(2)}, u32[]{:S(2)}) %collective-permute-start.15) | collective-permute-done | bytes 65568 | tf_op jit(solution)/shard_map/ppermute | solution.py:507
  99.3 5.8 %shard_map.122 = bf16[16,128,128]{2,1,0:T(8,128)(2,1)} custom-call(bf16[2,16,8,16,128]{4,3,2,1,0:T(8,128)(2,1)S(1)} %bitcast.20, f32[16,4,128,128]{3,2,1,0:T(8,128)} %get-tuple-element.29.coef_h, f32[16,128,128]{2,1,0:T(8,128)} %get-tuple-element.23.zhat_h, f32[16,128]{1,0:T(8,128)} %get-tuple-element.17.after.inv_h, ...), custom_call_target="tpu_custom_call" | custom-call | flops 335544320 | bytes 7864320 | tf_op jit(solution)/shard_map/pallas_call | solution.py:448
  (44 shorter events, 18.9 us)
Async XLA Ops:
  5.0 33.7 %all-to-all-start = ((bf16[32,8,16,128]{3,2,1,0:T(8,128)(2,1)}), bf16[32,8,16,128]{3,2,1,0:T(8,128)(2,1)S(1)}, u32[]{:S(2)}, u32[]{:S(2)}) async-start(bf16[32,8,16,128]{3,2,1,0:T(8,128)(2,1)} %bitcast.23), calls=%async_computation | async-start | bytes 2097152 | tf_op jit(solution)/shard_map/all_to_all | solution.py:502
  15.7 1.6 %collective-permute-start = (bf16[8,8,16,128]{3,2,1,0:T(8,128)(2,1)S(1)}, bf16[8,8,16,128]{3,2,1,0:T(8,128)(2,1)S(1)}, u32[]{:S(2)}, u32[]{:S(2)}) collective-permute-start(bf16[8,8,16,128]{3,2,1,0:T(8,128)(2,1)S(1)} %get-tuple-element.19), channel_id=1, source_target_pairs={{0,2},{2,0},{1,3},{3,1},{4,6},{6,4},{5,7},{7,5},{8,10},{10,8},{9,1... | collective-permute-start | bytes 786440 | tf_op jit(solution)/shard_map/ppermute | solution.py:507
  17.4 7.1 %collective-permute-start.1 = (bf16[2,8,16,128]{3,2,1,0:T(8,128)(2,1)S(1)}, bf16[2,8,16,128]{3,2,1,0:T(8,128)(2,1)S(1)}, u32[]{:S(2)}, u32[]{:S(2)}) collective-permute-start(bf16[2,8,16,128]{3,2,1,0:T(8,128)(2,1)S(1)} %pad_maximum_fusion), channel_id=1, source_target_pairs={{0,1},{1,0},{4,5},{5,4},{8,9},{9,8},{12,13},{13,12},{2,3},{3,2},{6... | collective-permute-start | bytes 196616 | tf_op jit(solution)/shard_map/ppermute | solution.py:507
  19.2 8.4 %collective-permute-start.2 = (bf16[2,8,16,128]{3,2,1,0:T(8,128)(2,1)S(1)}, bf16[2,8,16,128]{3,2,1,0:T(8,128)(2,1)S(1)}, u32[]{:S(2)}, u32[]{:S(2)}) collective-permute-start(bf16[2,8,16,128]{3,2,1,0:T(8,128)(2,1)S(1)} %pad_maximum_fusion.1), channel_id=1, source_target_pairs={{0,4},{1,5},{4,0},{5,1},{8,12},{9,13},{12,8},{13,9},{2,6},{3,7},{6... | collective-permute-start | bytes 196616 | tf_op jit(solution)/shard_map/ppermute | solution.py:507
  20.7 12.3 %collective-permute-start.3 = (bf16[2,8,16,128]{3,2,1,0:T(8,128)(2,1)S(1)}, bf16[2,8,16,128]{3,2,1,0:T(8,128)(2,1)S(1)}, u32[]{:S(2)}, u32[]{:S(2)}) collective-permute-start(bf16[2,8,16,128]{3,2,1,0:T(8,128)(2,1)S(1)} %pad_maximum_fusion.2), channel_id=1, source_target_pairs={{0,5},{1,4},{4,1},{5,0},{8,13},{9,12},{12,9},{13,8},{2,7},{3,6},{6... | collective-permute-start | bytes 196616 | tf_op jit(solution)/shard_map/ppermute | solution.py:507
  21.1 12.0 %collective-permute-start.4 = (bf16[2,8,16,128]{3,2,1,0:T(8,128)(2,1)S(1)}, bf16[2,8,16,128]{3,2,1,0:T(8,128)(2,1)S(1)}, u32[]{:S(2)}, u32[]{:S(2)}) collective-permute-start(bf16[2,8,16,128]{3,2,1,0:T(8,128)(2,1)S(1)} %pad_maximum_fusion.3), channel_id=1, source_target_pairs={{0,8},{1,9},{4,12},{5,13},{8,0},{9,1},{12,4},{13,5},{2,10},{3,11},... | collective-permute-start | bytes 196616 | tf_op jit(solution)/shard_map/ppermute | solution.py:507
  22.9 10.3 %collective-permute-start.5 = (bf16[2,8,16,128]{3,2,1,0:T(8,128)(2,1)S(1)}, bf16[2,8,16,128]{3,2,1,0:T(8,128)(2,1)S(1)}, u32[]{:S(2)}, u32[]{:S(2)}) collective-permute-start(bf16[2,8,16,128]{3,2,1,0:T(8,128)(2,1)S(1)} %pad_maximum_fusion.4), channel_id=1, source_target_pairs={{0,9},{1,8},{4,13},{5,12},{8,1},{9,0},{12,5},{13,4},{2,11},{3,10},... | collective-permute-start | bytes 196616 | tf_op jit(solution)/shard_map/ppermute | solution.py:507
  24.4 11.4 %collective-permute-start.6 = (bf16[2,8,16,128]{3,2,1,0:T(8,128)(2,1)S(1)}, bf16[2,8,16,128]{3,2,1,0:T(8,128)(2,1)S(1)}, u32[]{:S(2)}, u32[]{:S(2)}) collective-permute-start(bf16[2,8,16,128]{3,2,1,0:T(8,128)(2,1)S(1)} %pad_maximum_fusion.5), channel_id=1, source_target_pairs={{0,12},{1,13},{4,8},{5,9},{8,4},{9,5},{12,0},{13,1},{2,14},{3,15},... | collective-permute-start | bytes 196616 | tf_op jit(solution)/shard_map/ppermute | solution.py:507
  27.6 11.1 %collective-permute-start.7 = (bf16[2,8,16,128]{3,2,1,0:T(8,128)(2,1)S(1)}, bf16[2,8,16,128]{3,2,1,0:T(8,128)(2,1)S(1)}, u32[]{:S(2)}, u32[]{:S(2)}) collective-permute-start(bf16[2,8,16,128]{3,2,1,0:T(8,128)(2,1)S(1)} %pad_maximum_fusion.6), channel_id=1, source_target_pairs={{0,13},{1,12},{4,9},{5,8},{8,5},{9,4},{12,1},{13,0},{2,15},{3,14},... | collective-permute-start | bytes 196616 | tf_op jit(solution)/shard_map/ppermute | solution.py:507
  40.2 13.1 %all-to-all-start.1 = ((bf16[16,8,16,128]{3,2,1,0:T(8,128)(2,1)}), bf16[16,8,16,128]{3,2,1,0:T(8,128)(2,1)S(1)}, u32[]{:S(2)}, u32[]{:S(2)}) async-start(bf16[16,8,16,128]{3,2,1,0:T(8,128)(2,1)} %bitcast.24), calls=%async_computation.1 | async-start | bytes 1048576 | tf_op jit(solution)/shard_map/all_to_all | solution.py:498
  54.6 12.7 %all-to-all-start.2 = ((bf16[16,8,16,128]{3,2,1,0:T(8,128)(2,1)}), bf16[16,8,16,128]{3,2,1,0:T(8,128)(2,1)S(1)}, u32[]{:S(2)}, u32[]{:S(2)}) async-start(bf16[16,8,16,128]{3,2,1,0:T(8,128)(2,1)} %bitcast.21), calls=%async_computation.2 | async-start | bytes 1048576 | tf_op jit(solution)/shard_map/all_to_all | solution.py:498
  68.6 30.6 %all-to-all-start.3 = ((bf16[32,8,16,128]{3,2,1,0:T(8,128)(2,1)}), bf16[32,8,16,128]{3,2,1,0:T(8,128)(2,1)S(1)}, u32[]{:S(2)}, u32[]{:S(2)}) async-start(bf16[32,8,16,128]{3,2,1,0:T(8,128)(2,1)} %bitcast.22), calls=%async_computation.3 | async-start | bytes 2097152 | tf_op jit(solution)/shard_map/all_to_all | solution.py:502
  73.4 1.6 %collective-permute-start.8 = (bf16[8,8,16,128]{3,2,1,0:T(8,128)(2,1)S(1)}, bf16[8,8,16,128]{3,2,1,0:T(8,128)(2,1)S(1)}, u32[]{:S(2)}, u32[]{:S(2)}) collective-permute-start(bf16[8,8,16,128]{3,2,1,0:T(8,128)(2,1)S(1)} %get-tuple-element.31), channel_id=1, source_target_pairs={{0,2},{2,0},{1,3},{3,1},{4,6},{6,4},{5,7},{7,5},{8,10},{10,8},{9,1... | collective-permute-start | bytes 786440 | tf_op jit(solution)/shard_map/ppermute | solution.py:507
  75.1 9.8 %collective-permute-start.9 = (bf16[2,8,16,128]{3,2,1,0:T(8,128)(2,1)S(1)}, bf16[2,8,16,128]{3,2,1,0:T(8,128)(2,1)S(1)}, u32[]{:S(2)}, u32[]{:S(2)}) collective-permute-start(bf16[2,8,16,128]{3,2,1,0:T(8,128)(2,1)S(1)} %pad_maximum_fusion.7), channel_id=1, source_target_pairs={{0,1},{1,0},{4,5},{5,4},{8,9},{9,8},{12,13},{13,12},{2,3},{3,2},{6... | collective-permute-start | bytes 196616 | tf_op jit(solution)/shard_map/ppermute | solution.py:507
  76.7 9.9 %collective-permute-start.10 = (bf16[2,8,16,128]{3,2,1,0:T(8,128)(2,1)S(1)}, bf16[2,8,16,128]{3,2,1,0:T(8,128)(2,1)S(1)}, u32[]{:S(2)}, u32[]{:S(2)}) collective-permute-start(bf16[2,8,16,128]{3,2,1,0:T(8,128)(2,1)S(1)} %pad_maximum_fusion.8), channel_id=1, source_target_pairs={{0,4},{1,5},{4,0},{5,1},{8,12},{9,13},{12,8},{13,9},{2,6},{3,7},{6... | collective-permute-start | bytes 196616 | tf_op jit(solution)/shard_map/ppermute | solution.py:507
  78.3 9.6 %collective-permute-start.11 = (bf16[2,8,16,128]{3,2,1,0:T(8,128)(2,1)S(1)}, bf16[2,8,16,128]{3,2,1,0:T(8,128)(2,1)S(1)}, u32[]{:S(2)}, u32[]{:S(2)}) collective-permute-start(bf16[2,8,16,128]{3,2,1,0:T(8,128)(2,1)S(1)} %pad_maximum_fusion.9), channel_id=1, source_target_pairs={{0,5},{1,4},{4,1},{5,0},{8,13},{9,12},{12,9},{13,8},{2,7},{3,6},{6... | collective-permute-start | bytes 196616 | tf_op jit(solution)/shard_map/ppermute | solution.py:507
  78.8 13.6 %collective-permute-start.12 = (bf16[2,8,16,128]{3,2,1,0:T(8,128)(2,1)S(1)}, bf16[2,8,16,128]{3,2,1,0:T(8,128)(2,1)S(1)}, u32[]{:S(2)}, u32[]{:S(2)}) collective-permute-start(bf16[2,8,16,128]{3,2,1,0:T(8,128)(2,1)S(1)} %pad_maximum_fusion.10), channel_id=1, source_target_pairs={{0,8},{1,9},{4,12},{5,13},{8,0},{9,1},{12,4},{13,5},{2,10},{3,11},... | collective-permute-start | bytes 196616 | tf_op jit(solution)/shard_map/ppermute | solution.py:507
  80.4 13.3 %collective-permute-start.13 = (bf16[2,8,16,128]{3,2,1,0:T(8,128)(2,1)S(1)}, bf16[2,8,16,128]{3,2,1,0:T(8,128)(2,1)S(1)}, u32[]{:S(2)}, u32[]{:S(2)}) collective-permute-start(bf16[2,8,16,128]{3,2,1,0:T(8,128)(2,1)S(1)} %pad_maximum_fusion.11), channel_id=1, source_target_pairs={{0,9},{1,8},{4,13},{5,12},{8,1},{9,0},{12,5},{13,4},{2,11},{3,10},... | collective-permute-start | bytes 196616 | tf_op jit(solution)/shard_map/ppermute | solution.py:507
  84.8 11.5 %collective-permute-start.14 = (bf16[2,8,16,128]{3,2,1,0:T(8,128)(2,1)S(1)}, bf16[2,8,16,128]{3,2,1,0:T(8,128)(2,1)S(1)}, u32[]{:S(2)}, u32[]{:S(2)}) collective-permute-start(bf16[2,8,16,128]{3,2,1,0:T(8,128)(2,1)S(1)} %pad_maximum_fusion.12), channel_id=1, source_target_pairs={{0,12},{1,13},{4,8},{5,9},{8,4},{9,5},{12,0},{13,1},{2,14},{3,15},... | collective-permute-start | bytes 196616 | tf_op jit(solution)/shard_map/ppermute | solution.py:507
  86.6 12.6 %collective-permute-start.15 = (bf16[2,8,16,128]{3,2,1,0:T(8,128)(2,1)S(1)}, bf16[2,8,16,128]{3,2,1,0:T(8,128)(2,1)S(1)}, u32[]{:S(2)}, u32[]{:S(2)}) collective-permute-start(bf16[2,8,16,128]{3,2,1,0:T(8,128)(2,1)S(1)} %pad_maximum_fusion.13), channel_id=1, source_target_pairs={{0,13},{1,12},{4,9},{5,8},{8,5},{9,4},{12,1},{13,0},{2,15},{3,14},... | collective-permute-start | bytes 196616 | tf_op jit(solution)/shard_map/ppermute | solution.py:507

commit v9 on v8

--- a/solution.py
+++ b/solution.py
@@ -112,51 +112,53 @@
     part, n_out, pair_h, mask_h, mask_row_h, gain_h, bias_h, proj_h, *refs
 ):
     outs = refs[:n_out]
-    pair, mask_s, mask_v, gain, bias, proj_weight, plane, sems, row_sems, *more = refs[n_out:]
+    pair, mask_s, mask_v, gain, bias, proj_weight, zbar, plane, sems, *more = refs[n_out:]
     rows, cols, width = pair.shape
     hidden = plane.shape[0] // rows
     groups = groups_of(rows)
-    blocks = start(
-        row_sems,
-        [(pair_h.at[pl.ds(at, size)], pair.at[pl.ds(at, size)]) for at, size in groups],
-    )
-    small = start(
-        sems,
-        [
-            (gain_h, gain), (bias_h, bias),
-            (proj_h.at[:, pl.ds(part * hidden, 2 * hidden)], proj_weight),
-            (mask_h, mask_s), (mask_row_h, mask_v),
-        ],
-    )
-    wait(small)
+    wait(
+        start(
+            sems,
+            [
+                (gain_h, gain), (bias_h, bias),
+                (proj_h.at[:, pl.ds(part * hidden, 2 * hidden)], proj_weight),
+                (mask_h, mask_s), (mask_row_h, mask_v), (pair_h, pair),
+            ],
+        )
+    )
     gain_b = jnp.concatenate([down_lanes(gain[...], cols)] * groups[0][1], axis=1)
     bias_b = jnp.concatenate([down_lanes(bias[...], cols)] * groups[0][1], axis=1)
+    for at, size in groups:
+        zhat, _ = normalized(turned(pair[at : at + size].reshape(size * cols, width)))
+        zbar[:, at * cols : (at + size) * cols] = (zhat * gain_b + bias_b).astype(BF16)
     weight = turned_weight(proj_weight[...])
-    for (at, size), block in zip(groups, blocks):
-        block.wait()
-        zhat, _ = normalized(turned(pair[at : at + size].reshape(size * cols, width)))
-        zbar = (zhat * gain_b + bias_b).astype(BF16)
-        pm = pair_mask(mask_s, mask_v, at, size, rows, cols)
-        values = sigmoid(dot(weight[:hidden], zbar)) * dot(weight[hidden:], zbar) * pm
-        for r in range(size):
-            plane[pl.ds(at + r, hidden, stride=rows), :] = values[:, r * cols : (r + 1) * cols]
+
+    def channels(first, count):
+        for at, size in groups:
+            z = zbar[:, at * cols : (at + size) * cols]
+            p = dot(weight[first : first + count], z)
+            q = dot(weight[hidden + first : hidden + first + count], z)
+            values = sigmoid(p) * q * pair_mask(mask_s, mask_v, at, size, rows, cols)
+            for r in range(size):
+                plane[pl.ds(first * rows + at + r, count, stride=rows), :] = values[
+                    :, r * cols : (r + 1) * cols
+                ]
+
     if n_out > 1:
+        channels(0, hidden)
         give_pieces(plane, outs)
-    else:
-        give_all(plane, outs[0], *more)
-
-
-def give_all(plane, out_h, ready, sems):
-    n_place = ready.shape[0]
-    size = math.gcd(n_place, 4)
-    length = plane.shape[0] // n_place * size
+        return
+    (out_h,), (ready, out_sems) = outs, more
+    n_place, share = ready.shape[:2]
+    size = n_place // math.gcd(n_place, 4)
     leaving = []
     for n, at in enumerate(range(0, n_place, size)):
-        values = plane[n * length : (n + 1) * length]
+        channels(at * share, size * share)
+        values = plane[at * share * rows : (at + size) * share * rows]
         ready[at : at + size] = values.reshape(size, *ready.shape[1:]).astype(BF16)
         for half in range(out_h.shape[0]):
             copy = pltpu.make_async_copy(
-                ready.at[pl.ds(at, size)], out_h.at[half, pl.ds(at, size)], sems.at[half, n]
+                ready.at[pl.ds(at, size)], out_h.at[half, pl.ds(at, size)], out_sems.at[half, n]
             )
             copy.start()
             leaving.append(copy)
@@ -174,9 +176,9 @@
 
 def side_kernel(
     pair_h, cot_h, gain_h, bias_h, gate_h, norm_gain_h, out_w_h,
-    zhat_h, inv_h, gate_out_h, dxh_h,
+    zhat_h, inv_h, gate_out_h, dxh_out,
     pair, cot, gain, bias, gate_weight, norm_gain, out_weight,
-    zhat_out, inv_out, gate_out, dxh_out, in_sems, out_sems,
+    zhat_out, inv_out, gate_out, in_sems, out_sems,
 ):
     rows, cols, width = pair.shape
     hidden = out_weight.shape[0]
@@ -210,18 +212,17 @@
     wait(
         start(
             out_sems,
-            [(zhat_out, zhat_h), (inv_out, inv_h), (gate_out, gate_out_h), (dxh_out, dxh_h)],
+            [(zhat_out, zhat_h), (inv_out, inv_h), (gate_out, gate_out_h)],
         )
     )
 
 
 def factors_kernel(
-    zhat_h, mask_h, mask_row_h, gain_h, bias_h, proj_h, dxh_h, after, coef_h, dxh,
-    zhat, mask_s, mask_v, gain, bias, proj_weight, coef, in_sems, out_sems, fetch_sems,
+    zhat_h, mask_h, mask_row_h, gain_h, bias_h, proj_h, after, coef_h,
+    zhat, mask_s, mask_v, gain, bias, proj_weight, coef, in_sems, out_sems,
 ):
     rows, width, cols = zhat.shape
     hidden = coef.shape[2]
-    fetched = start(fetch_sems, [(dxh_h, dxh)])
     wait(
         start(
             in_sems,
@@ -253,7 +254,7 @@
         )
         copy.start()
         leaving.append(copy)
-    wait(leaving + fetched)
+    wait(leaving)
 
 
 def channel_matrix(ref, at):
@@ -272,59 +273,35 @@
         ref[(*lead, c, at)] = values[:, c * cols : (c + 1) * cols].reshape(*shape, rows, cols)
 
 
-def leave(ready, out_h, at, sem):
-    lead = (slice(None),) * (len(ready.shape) - 3)
-    copy = pltpu.make_async_copy(
-        ready.at[(*lead, pl.ds(at, 1))], out_h.at[(*lead, pl.ds(at, 1))], sem
-    )
-    copy.start()
-    return copy
-
-
 def product_kernel(n_chip, right, after, *refs):
-    pieces, (out_h, left_h, left, ready, sems, left_sem) = refs[:-6], refs[-6:]
+    pieces, (out, left) = refs[:-2], refs[-2:]
     n_col, share = left.shape[1:3]
     for number, piece in received(pieces, n_chip):
         left[number // n_col, number % n_col] = piece
-    leaving = start(left_sem, [(left, left_h)])
     for h in range(share):
         values = dot(channel_matrix(left, h), channel_matrix(right, h), ((1,), (1,)))
-        put_channel(ready, h, values)
-        leaving.append(leave(ready, out_h, h, sems.at[h]))
-    wait(leaving)
-
-
-def middle_kernel(product, dxh, out_h, xhat, ready, sems):
+        put_channel(out, h, values)
+
+
+def middle_kernel(product, dxh, out, xhat):
     hidden = product.shape[0]
     values = product[...].astype(F32)
     mean = jnp.sum(values, axis=0) * (1.0 / hidden)
-    centred = values - mean[None]
+    centred = values - mean
     var = jnp.sum(centred * centred, axis=0) * (1.0 / hidden)
     inverse = lax.rsqrt(var + EPS)
-    xhat[...] = centred * inverse[None]
+    xhat[...] = centred * inverse
     m2 = jnp.sum(dxh[...] * xhat[...], axis=0) * (1.0 / hidden)
-    leaving = []
-    size = math.gcd(hidden, 32)
-    for n, at in enumerate(range(0, hidden, size)):
-        part = slice(at, at + size)
-        ready[part] = ((dxh[part] - xhat[part] * m2[None]) * inverse[None]).astype(BF16)
-        copy = pltpu.make_async_copy(
-            ready.at[pl.ds(at, size)], out_h.at[pl.ds(at, size)], sems.at[n]
-        )
-        copy.start()
-        leaving.append(copy)
-    wait(leaving)
+    out[...] = ((dxh[...] - xhat[...] * m2) * inverse).astype(BF16)
 
 
 def update_kernel(
-    product, gate_h, cot_h, norm_gain_h, norm_bias_h, out_w_h, gate_w_h, left_h, after, update_h, dzg_h,
-    left,
+    product, gate_h, cot_h, norm_gain_h, norm_bias_h, out_w_h, gate_w_h, after, update_h, dzg_h,
     gate, cot, norm_gain, norm_bias, out_weight, gate_weight, update, dzg, spread,
-    in_sems, out_sems, fetch_sems,
+    in_sems, out_sems,
 ):
     hidden, rows, cols = product.shape
     width = cot.shape[2]
-    fetched = start(fetch_sems, [(left_h, left)])
     copies = start(
         in_sems,
         [
@@ -354,15 +331,19 @@
             lanes = slice(r * cols, (r + 1) * cols)
             update[at + r] = turned(done[:, lanes]).astype(BF16)
             dzg[at + r] = back[:, lanes]
-    wait(fetched + start(out_sems, [(update, update_h), (dzg, dzg_h)]))
-
-
-def grad_right_kernel(grad, left, after, out_h, ready, sems):
+    wait(start(out_sems, [(update, update_h), (dzg, dzg_h)]))
+
+
+def grad_right_kernel(grad, left, out_h, ready, sems):
+    lead = (slice(None),) * (len(ready.shape) - 3)
     leaving = []
     for h in range(ready.shape[-3]):
         values = dot(channel_matrix(grad, h), channel_matrix(left, h), ((0,), (0,)))
         put_channel(ready, h, values)
-        leaving.append(leave(ready, out_h, h, sems.at[h]))
+        part = (*lead, pl.ds(h, 1))
+        copy = pltpu.make_async_copy(ready.at[part], out_h.at[part], sems.at[h])
+        copy.start()
+        leaving.append(copy)
     wait(leaving)
 
 
@@ -385,18 +366,17 @@
     hidden = left.shape[0] // rows
     groups = groups_of(rows)
     small = start(sems, [(gain_h, gain), (proj_h, proj_weight), (inv_h, inv)])
-    blocks = []
-    for n, (at, size) in enumerate(groups):
-        part = pl.ds(at, size)
-        blocks.append(
-            [
-                pltpu.make_async_copy(source.at[part], target.at[part], sem.at[n])
-                for source, target, sem in (
-                    (coef_h, coef, coef_sems), (zhat_h, zhat, zhat_sems), (dzg_h, dzg, dzg_sems)
-                )
-            ]
-        )
-        for copy in blocks[-1]:
+    ahead = rows // math.gcd(rows, 2)
+    blocks = {}
+    for n, at in enumerate(range(0, rows, ahead)):
+        part = pl.ds(at, ahead)
+        blocks[at] = [
+            pltpu.make_async_copy(source.at[part], target.at[part], sem.at[n])
+            for source, target, sem in (
+                (coef_h, coef, coef_sems), (zhat_h, zhat, zhat_sems), (dzg_h, dzg, dzg_sems)
+            )
+        ]
+        for copy in blocks[at]:
             copy.start()
     arrived = received(pieces, n_chip)
     length = left.shape[0] // len(arrived)
@@ -410,8 +390,8 @@
     wait(small)
     gain_b = jnp.concatenate([down_lanes(gain[...], cols)] * groups[0][1], axis=1)
     leaving = []
-    for n, (at, size) in enumerate(groups):
-        wait(blocks[n])
+    for at, size in groups:
+        wait(blocks.get(at, []))
         columns = []
         for r in range(size):
             gl = left[pl.ds(at + r, hidden, stride=rows), :]
@@ -434,11 +414,14 @@
         grad = ((dzh - m1 - z * m2) * inverse).astype(BF16)
         for r in range(size):
             out[at + r] = turned(grad[:, r * cols : (r + 1) * cols]).astype(BF16)
-        copy = pltpu.make_async_copy(
-            out.at[pl.ds(at, size)], out_h.at[pl.ds(at, size)], out_sems.at[n]
-        )
-        copy.start()
-        leaving.append(copy)
+        done = at + size
+        if done % ahead == 0:
+            part = pl.ds(done - ahead, ahead)
+            copy = pltpu.make_async_copy(
+                out.at[part], out_h.at[part], out_sems.at[done // ahead - 1]
+            )
+            copy.start()
+            leaving.append(copy)
     wait(leaving)
 
 
@@ -531,8 +514,8 @@
             functools.partial(front_kernel, part, len(outs)),
             outs,
             [
-                block, mask_s, mask_v, vector, vector, vmem(width, 2 * hidden), plane,
-                sems(5), sems(n_groups), *scratch,
+                block, mask_s, mask_v, vector, vector, vmem(width, 2 * hidden),
+                vmem(width, cells), plane, sems(6), *scratch,
             ],
             (pair, mask, mask_row, gain_in, bias_in, proj_weight),
             outs_near=near,
@@ -544,7 +527,7 @@
     (right,) = front(
         2,
         (shape(n_half, n_place, share, rows, cols),),
-        [everywhere, pltpu.SemaphoreType.DMA((n_half, n_place // math.gcd(n_place, 4)))],
+        [everywhere, pltpu.SemaphoreType.DMA((n_half, math.gcd(n_place, 4)))],
         (),
     )
     right = exchange_all(right).reshape(n_half, n_line, n_col, share, rows, cols)
@@ -559,74 +542,41 @@
         ),
         [
             block, block, vector, vector, square, vector, square,
-            wide, vmem(rows, cols, dtype=F32), wide, plane, sems(7), sems(4),
+            wide, vmem(rows, cols, dtype=F32), wide, sems(7), sems(3),
         ],
         (pair, cotangent, gain_in, bias_in, gate_weight, norm_gain, out_weight),
+        outs_near=(3,),
         flops=2 * cells * width * 4 * hidden,
         moved=16 * cells * width,
     )
     product, left = call(
         functools.partial(product_kernel, n_chip),
         (shape(n_line, n_col, share, rows, cols), shape(n_line, n_col, share, rows, cols)),
-        [
-            vmem(n_line, n_col, share, rows, cols), vmem(n_line, n_col, share, rows, cols),
-            sems(share), sems(1),
-        ],
+        [],
         (right, inv, *left),
         near=(0, *range(2, 2 + n_pieces)),
+        outs_near=(0, 1),
         flops=2 * share * n_half * (n_line * rows) ** 2 * n_col * cols,
         moved=8 * cells * hidden,
     )
-    spread = vmem(hidden, rows, cols, dtype=F32)
-    coef, dxh = call(
-        factors_kernel,
-        (shape(rows, 4, hidden, cols, dtype=F32), shape(hidden, rows, cols, dtype=F32)),
-        [
-            wide, mask_s, mask_v, vector, vector, proj_v, vmem(rows, 4, hidden, cols, dtype=F32),
-            sems(6), sems(n_groups), sems(1),
-        ],
-        (
-            zhat, mask, mask_row, gain_in, bias_in, proj_weight,
-            dxh.reshape(hidden, rows, cols), product,
-        ),
-        outs_near=(1,),
-        flops=2 * cells * width * 5 * hidden,
-        moved=20 * cells * width,
-    )
     product = exchange(product.reshape(n_place, share, rows, cols)).reshape(hidden, rows, cols)
-    (sent,) = call(
+    (grad,) = call(
         middle_kernel,
         (shape(hidden, rows, cols),),
-        [spread, vmem(hidden, rows, cols), sems(hidden // math.gcd(hidden, 32))],
-        (product, dxh),
+        [vmem(hidden, rows, cols, dtype=F32)],
+        (product, dxh.reshape(hidden, rows, cols)),
         near=(0, 1),
+        outs_near=(0,),
         flops=20 * cells * hidden,
         moved=8 * cells * hidden,
     )
-    grad = exchange(sent.reshape(n_place, share, rows, cols))
+    grad = exchange(grad.reshape(n_place, share, rows, cols))
     grad = grad.reshape(n_line, n_col, share, rows, cols)
-    update, dzg, left = call(
-        update_kernel,
-        (
-            shape(rows, cols, width),
-            shape(rows, width, cols, dtype=F32),
-            shape(n_line, n_col, share, rows, cols),
-        ),
-        [
-            wide, block, vector, vector, square, square, block, wide, plane,
-            sems(6), sems(2), sems(1),
-        ],
-        (product, gate, cotangent, norm_gain, norm_bias, out_weight, gate_weight, left, sent),
-        near=(0,),
-        outs_near=(2,),
-        flops=2 * cells * width * 3 * hidden,
-        moved=14 * cells * hidden,
-    )
     (grad_right,) = call(
         grad_right_kernel,
         (shape(n_half, n_line, n_col, share, rows, cols),),
         [vmem(n_half, n_line, n_col, share, rows, cols), sems(share)],
-        (grad, left, dzg),
+        (grad, left),
         near=(0, 1),
         flops=2 * share * n_half * (n_line * rows) ** 2 * n_col * cols,
         moved=8 * cells * hidden,
@@ -643,13 +593,35 @@
         moved=8 * cells * hidden,
     )
     grad_left = exchange_pieces(tuple(grad_left))
+    arrived = grad_left[-min(3, n_chip - 1)]
+    (coef,) = call(
+        factors_kernel,
+        (shape(rows, 4, hidden, cols, dtype=F32),),
+        [
+            wide, mask_s, mask_v, vector, vector, proj_v, vmem(rows, 4, hidden, cols, dtype=F32),
+            sems(6), sems(n_groups),
+        ],
+        (zhat, mask, mask_row, gain_in, bias_in, proj_weight, arrived),
+        near=(6,),
+        flops=2 * cells * width * 5 * hidden,
+        moved=20 * cells * width,
+    )
+    update, dzg = call(
+        update_kernel,
+        (shape(rows, cols, width), shape(rows, width, cols, dtype=F32)),
+        [wide, block, vector, vector, square, square, block, wide, plane, sems(6), sems(2)],
+        (product, gate, cotangent, norm_gain, norm_bias, out_weight, gate_weight, arrived),
+        near=(0, 7),
+        flops=2 * cells * width * 3 * hidden,
+        moved=14 * cells * hidden,
+    )
     (grad_pair,) = call(
         functools.partial(back_kernel, n_chip),
         (shape(rows, cols, width),),
         [
             vmem(rows, 4, hidden, cols, dtype=F32), wide, vmem(rows, cols, dtype=F32), wide,
             vector, proj_v, block, plane, plane,
-            sems(3), sems(n_groups), sems(n_groups), sems(n_groups), sems(n_groups),
+            sems(3), sems(2), sems(2), sems(2), sems(2),
         ],
         (grad_right, coef, zhat, inv, dzg, gain_in, proj_weight, *grad_left),
         near=(0, *range(7, 7 + n_pieces)),

time: 106 us -> 107 us (level)
  blocking collectives: 0 us -> 24.9 us
  waiting for transfers between devices: 34.8 us -> 21.6 us
  starting transfers between devices: 38 us -> 32.2 us
  Pallas kernels: 31.3 us -> 26.5 us
    all_to_all x0 -> x2, blocking collectives: none -> 24.9 us  [exchange(): lax.all_to_all(values, within, split_axis=0, concat_axis=0, tiled=True)]
    all_to_all x2 -> x0, waiting for transfers between devices: 9.98 us -> none  [exchange(): lax.all_to_all(values, within, split_axis=0, concat_axis=0, tiled=True)]
    all_to_all x2 -> x0, starting transfers between devices: 7.53 us -> none  [exchange(): lax.all_to_all(values, within, split_axis=0, concat_axis=0, tiled=True)]
    pallas_call x10, Pallas kernels: 31.3 us -> 26.5 us  [call(): pl.pallas_call(kernel, out_shape=[out if at in outs_near else pltpu.HBM(o...]
    ppermute x16, waiting for transfers between devices: 24.8 us -> 21.6 us  [permute(): lax.ppermute(values, axes, [(at, at ^ distance) for at in range(size)])]
    ppermute x16, starting transfers between devices: 18.8 us -> 21.2 us  [permute(): lax.ppermute(values, axes, [(at, at ^ distance) for at in range(size)])]
  transfers between devices with their start and end apart: 20 -> 18, of which waited for: 14 -> 9; matrix products, arithmetic and copies ran while one was open for 0% -> 0% of each run, Pallas kernels for 16% -> 14%
where the time goes in v9:
time: 107 us; the launch traced here: 106 us
  starting transfers between devices  32.2 us (30%)
  Pallas kernels  26.5 us (25%)
  blocking collectives  24.9 us (23%)
  waiting for transfers between devices  21.6 us (20%)
    pallas_call x10, Pallas kernels, call(): pl.pallas_call(kernel, out_shape=[out if at in outs_near else pltpu.HBM(o...  26.5 us
    all_to_all x2, blocking collectives, exchange(): lax.all_to_all(values, within, split_axis=0, concat_axis=0, tiled=True)  24.9 us
    ppermute x16, waiting for transfers between devices, permute(): lax.ppermute(values, axes, [(at, at ^ distance) for at in range(size)])  21.6 us
    ppermute x16, starting transfers between devices, permute(): lax.ppermute(values, axes, [(at, at ^ distance) for at in range(size)])  21.2 us
    all_to_all x2, starting transfers between devices, exchange_all(): lax.all_to_all(flat, ('half', *within), split_axis=0, concat_axis=0, tile...  10.9 us
  transfers between devices with their start and end apart: 18, of which 9 were waited for; matrix products, arithmetic and copies ran while one was open for 0% of the time, Pallas kernels for 14%

profile of v9, /device:TPU:0, one launch (start us, length us, event | category | flops | bytes accessed | tf_op | source)
XLA Modules:
  0.0 106.3 jit_solution(3596307511040289385)
XLA Ops:
  0.6 3.2 %shard_map.113 = bf16[2,16,8,16,128]{4,3,2,1,0:T(8,128)(2,1)} custom-call(bf16[16,128,128]{2,1,0:T(8,128)(2,1)} %pair_h.5, s32[256]{0:T(256)} %mask_h.5, s32[1,256]{1,0:T(1,128)} %bitcast.26, f32[1,128]{1,0:T(1,128)} %bitcast.29, f32[1,128]{1,0:T(1,128)} %bitcast.34, bf16[128,512]{1,0:T(8,128)(2,1)} %proj_h.7), custom_call_target="tpu_custom_call" | custom-call | flops 201326592 | bytes 1310720 | tf_op jit(solution)/shard_map/pallas_call | solution.py:431
  3.9 7.3 %all-to-all-start = ((bf16[32,8,16,128]{3,2,1,0:T(8,128)(2,1)}), bf16[32,8,16,128]{3,2,1,0:T(8,128)(2,1)S(1)}, u32[]{:S(2)}, u32[]{:S(2)}) async-start(bf16[32,8,16,128]{3,2,1,0:T(8,128)(2,1)} %bitcast.25), calls=%async_computation | async-start | bytes 2097152 | tf_op jit(solution)/shard_map/all_to_all | solution.py:485
  11.2 2.3 %shard_map.115 = (bf16[8,8,16,128]{3,2,1,0:T(8,128)(2,1)S(1)}, bf16[8,8,16,128]{3,2,1,0:T(8,128)(2,1)S(1)}) custom-call(bf16[16,128,128]{2,1,0:T(8,128)(2,1)} %pair_h.5, s32[256]{0:T(256)} %mask_h.5, s32[1,256]{1,0:T(1,128)} %bitcast.27, f32[1,128]{1,0:T(1,128)} %bitcast.30, f32[1,128]{1,0:T(1,128)} %bitcast.35, bf16[128,512]{1,0:T(8,128)(2,1)} %proj_h.7), custom_call_target="tpu_custom_call" | custom-call | flops 201326592 | bytes 1310720 | tf_op jit(solution)/shard_map/pallas_call | solution.py:431
  15.1 1.8 %collective-permute-start.1 = (bf16[2,8,16,128]{3,2,1,0:T(8,128)(2,1)S(1)}, bf16[2,8,16,128]{3,2,1,0:T(8,128)(2,1)S(1)}, u32[]{:S(2)}, u32[]{:S(2)}) collective-permute-start(bf16[2,8,16,128]{3,2,1,0:T(8,128)(2,1)S(1)} %pad_maximum_fusion), channel_id=1, source_target_pairs={{0,1},{1,0},{4,5},{5,4},{8,9},{9,8},{12,13},{13,12},{2,3},{3,2},{6... | collective-permute-start | bytes 196616 | tf_op jit(solution)/shard_map/ppermute | solution.py:490
  16.9 1.5 %collective-permute-start.2 = (bf16[2,8,16,128]{3,2,1,0:T(8,128)(2,1)S(1)}, bf16[2,8,16,128]{3,2,1,0:T(8,128)(2,1)S(1)}, u32[]{:S(2)}, u32[]{:S(2)}) collective-permute-start(bf16[2,8,16,128]{3,2,1,0:T(8,128)(2,1)S(1)} %pad_maximum_fusion.1), channel_id=1, source_target_pairs={{0,4},{1,5},{4,0},{5,1},{8,12},{9,13},{12,8},{13,9},{2,6},{3,7},{6... | collective-permute-start | bytes 196616 | tf_op jit(solution)/shard_map/ppermute | solution.py:490
  18.8 1.8 %collective-permute-start.4 = (bf16[2,8,16,128]{3,2,1,0:T(8,128)(2,1)S(1)}, bf16[2,8,16,128]{3,2,1,0:T(8,128)(2,1)S(1)}, u32[]{:S(2)}, u32[]{:S(2)}) collective-permute-start(bf16[2,8,16,128]{3,2,1,0:T(8,128)(2,1)S(1)} %pad_maximum_fusion.3), channel_id=1, source_target_pairs={{0,8},{1,9},{4,12},{5,13},{8,0},{9,1},{12,4},{13,5},{2,10},{3,11},... | collective-permute-start | bytes 196616 | tf_op jit(solution)/shard_map/ppermute | solution.py:490
  20.6 1.5 %collective-permute-start.5 = (bf16[2,8,16,128]{3,2,1,0:T(8,128)(2,1)S(1)}, bf16[2,8,16,128]{3,2,1,0:T(8,128)(2,1)S(1)}, u32[]{:S(2)}, u32[]{:S(2)}) collective-permute-start(bf16[2,8,16,128]{3,2,1,0:T(8,128)(2,1)S(1)} %pad_maximum_fusion.4), channel_id=1, source_target_pairs={{0,9},{1,8},{4,13},{5,12},{8,1},{9,0},{12,5},{13,4},{2,11},{3,10},... | collective-permute-start | bytes 196616 | tf_op jit(solution)/shard_map/ppermute | solution.py:490
  22.9 1.7 %collective-permute-start.6 = (bf16[2,8,16,128]{3,2,1,0:T(8,128)(2,1)S(1)}, bf16[2,8,16,128]{3,2,1,0:T(8,128)(2,1)S(1)}, u32[]{:S(2)}, u32[]{:S(2)}) collective-permute-start(bf16[2,8,16,128]{3,2,1,0:T(8,128)(2,1)S(1)} %pad_maximum_fusion.5), channel_id=1, source_target_pairs={{0,12},{1,13},{4,8},{5,9},{8,4},{9,5},{12,0},{13,1},{2,14},{3,15},... | collective-permute-start | bytes 196616 | tf_op jit(solution)/shard_map/ppermute | solution.py:490
  25.8 4.6 %shard_map.114 = (f32[16,128,128]{2,1,0:T(8,128)}, f32[16,128]{1,0:T(8,128)}, f32[16,128,128]{2,1,0:T(8,128)}, f32[2048,128]{1,0:T(8,128)S(1)}) custom-call(bf16[16,128,128]{2,1,0:T(8,128)(2,1)} %pair_h.5, bf16[16,128,128]{2,1,0:T(8,128)(2,1)} %cot_h.3, f32[1,128]{1,0:T(1,128)} %bitcast.31, f32[1,128]{1,0:T(1,128)} %bitcast.36, bf16[128,128]{1,0:T(8,128)(2,1)} %gate_w_h.1, ...), custom_call_target="tpu_custom_call" | custom-call | flops 268435456 | bytes 4194304 | tf_op jit(solution)/shard_map/pallas_call | solution.py:431
  30.6 1.5 %collective-permute-done.5.refs_6_ = bf16[2,8,16,128]{3,2,1,0:T(8,128)(2,1)S(1)} collective-permute-done((bf16[2,8,16,128]{3,2,1,0:T(8,128)(2,1)S(1)}, bf16[2,8,16,128]{3,2,1,0:T(8,128)(2,1)S(1)}, u32[]{:S(2)}, u32[]{:S(2)}) %collective-permute-start.5) | collective-permute-done | bytes 65568 | tf_op jit(solution)/shard_map/ppermute | solution.py:490
  32.1 2.7 %collective-permute-done.6.refs_7_ = bf16[2,8,16,128]{3,2,1,0:T(8,128)(2,1)S(1)} collective-permute-done((bf16[2,8,16,128]{3,2,1,0:T(8,128)(2,1)S(1)}, bf16[2,8,16,128]{3,2,1,0:T(8,128)(2,1)S(1)}, u32[]{:S(2)}, u32[]{:S(2)}) %collective-permute-start.6) | collective-permute-done | bytes 65568 | tf_op jit(solution)/shard_map/ppermute | solution.py:490
  34.7 2.9 %collective-permute-done.7.refs_8_ = bf16[2,8,16,128]{3,2,1,0:T(8,128)(2,1)S(1)} collective-permute-done((bf16[2,8,16,128]{3,2,1,0:T(8,128)(2,1)S(1)}, bf16[2,8,16,128]{3,2,1,0:T(8,128)(2,1)S(1)}, u32[]{:S(2)}, u32[]{:S(2)}) %collective-permute-start.7) | collective-permute-done | bytes 65568 | tf_op jit(solution)/shard_map/ppermute | solution.py:490
  38.2 12.9 %all_to_all.20 = bf16[16,8,16,128]{3,2,1,0:T(8,128)(2,1)S(1)} all-to-all(bf16[16,8,16,128]{3,2,1,0:T(8,128)(2,1)S(1)} %bitcast.23), channel_id=1, replica_groups=mesh['grp'=1,'half'=2,'row'=4,'core'=2,'col'=2] {'row','core','col'}, dimensions={0} | all-to-all | bytes 1048576 | tf_op jit(solution)/shard_map/all_to_all | solution.py:481
  51.6 12.0 %all_to_all.21 = bf16[16,8,16,128]{3,2,1,0:T(8,128)(2,1)S(1)} all-to-all(bf16[16,8,16,128]{3,2,1,0:T(8,128)(2,1)S(1)} %bitcast.21), channel_id=1, replica_groups=mesh['grp'=1,'half'=2,'row'=4,'core'=2,'col'=2] {'row','core','col'}, dimensions={0} | all-to-all | bytes 1048576 | tf_op jit(solution)/shard_map/all_to_all | solution.py:481
  65.0 3.6 %all-to-all-start.3 = ((bf16[32,8,16,128]{3,2,1,0:T(8,128)(2,1)}), bf16[32,8,16,128]{3,2,1,0:T(8,128)(2,1)S(1)}, u32[]{:S(2)}, u32[]{:S(2)}) async-start(bf16[32,8,16,128]{3,2,1,0:T(8,128)(2,1)} %bitcast.24), calls=%async_computation.3 | async-start | bytes 2097152 | tf_op jit(solution)/shard_map/all_to_all | solution.py:485
  69.2 1.4 %collective-permute-done.8.refs_1_ = bf16[8,8,16,128]{3,2,1,0:T(8,128)(2,1)S(1)} collective-permute-done((bf16[8,8,16,128]{3,2,1,0:T(8,128)(2,1)S(1)}, bf16[8,8,16,128]{3,2,1,0:T(8,128)(2,1)S(1)}, u32[]{:S(2)}, u32[]{:S(2)}) %collective-permute-start.8) | collective-permute-done | bytes 262176 | tf_op jit(solution)/shard_map/ppermute | solution.py:490
  70.7 2.6 %collective-permute-start.9 = (bf16[2,8,16,128]{3,2,1,0:T(8,128)(2,1)S(1)}, bf16[2,8,16,128]{3,2,1,0:T(8,128)(2,1)S(1)}, u32[]{:S(2)}, u32[]{:S(2)}) collective-permute-start(bf16[2,8,16,128]{3,2,1,0:T(8,128)(2,1)S(1)} %pad_maximum_fusion.7), channel_id=1, source_target_pairs={{0,9},{1,8},{4,13},{5,12},{8,1},{9,0},{12,5},{13,4},{2,11},{3,10},... | collective-permute-start | bytes 196616 | tf_op jit(solution)/shard_map/ppermute | solution.py:490
  73.9 1.5 %collective-permute-start.11 = (bf16[2,8,16,128]{3,2,1,0:T(8,128)(2,1)S(1)}, bf16[2,8,16,128]{3,2,1,0:T(8,128)(2,1)S(1)}, u32[]{:S(2)}, u32[]{:S(2)}) collective-permute-start(bf16[2,8,16,128]{3,2,1,0:T(8,128)(2,1)S(1)} %pad_maximum_fusion.9), channel_id=1, source_target_pairs={{0,4},{1,5},{4,0},{5,1},{8,12},{9,13},{12,8},{13,9},{2,6},{3,7},{6... | collective-permute-start | bytes 196616 | tf_op jit(solution)/shard_map/ppermute | solution.py:490
  75.4 1.5 %collective-permute-start.12 = (bf16[2,8,16,128]{3,2,1,0:T(8,128)(2,1)S(1)}, bf16[2,8,16,128]{3,2,1,0:T(8,128)(2,1)S(1)}, u32[]{:S(2)}, u32[]{:S(2)}) collective-permute-start(bf16[2,8,16,128]{3,2,1,0:T(8,128)(2,1)S(1)} %pad_maximum_fusion.10), channel_id=1, source_target_pairs={{0,5},{1,4},{4,1},{5,0},{8,13},{9,12},{12,9},{13,8},{2,7},{3,6},{6... | collective-permute-start | bytes 196616 | tf_op jit(solution)/shard_map/ppermute | solution.py:490
  77.6 10.4 %collective-permute-done.9.after.refs_6_ = bf16[2,8,16,128]{3,2,1,0:T(8,128)(2,1)S(1)} collective-permute-done((bf16[2,8,16,128]{3,2,1,0:T(8,128)(2,1)S(1)}, bf16[2,8,16,128]{3,2,1,0:T(8,128)(2,1)S(1)}, u32[]{:S(2)}, u32[]{:S(2)}) %collective-permute-start.9) | collective-permute-done | bytes 65568 | tf_op jit(solution)/shard_map/ppermute | solution.py:490
  87.9 4.5 %collective-permute-start.14 = (bf16[2,8,16,128]{3,2,1,0:T(8,128)(2,1)S(1)}, bf16[2,8,16,128]{3,2,1,0:T(8,128)(2,1)S(1)}, u32[]{:S(2)}, u32[]{:S(2)}) collective-permute-start(bf16[2,8,16,128]{3,2,1,0:T(8,128)(2,1)S(1)} %pad_maximum_fusion.12), channel_id=1, source_target_pairs={{0,12},{1,13},{4,8},{5,9},{8,4},{9,5},{12,0},{13,1},{2,14},{3,15},... | collective-permute-start | bytes 196616 | tf_op jit(solution)/shard_map/ppermute | solution.py:490
  92.5 4.1 %shard_map.119 = (bf16[16,128,128]{2,1,0:T(8,128)(2,1)}, f32[16,128,128]{2,1,0:T(8,128)}) custom-call(bf16[128,16,128]{2,1,0:T(8,128)(2,1)S(1)} %bitcast.19, f32[16,128,128]{2,1,0:T(8,128)} %get-tuple-element.18.gate_h, bf16[16,128,128]{2,1,0:T(8,128)(2,1)} %cot_h.3, f32[1,128]{1,0:T(1,128)} %bitcast.39, f32[1,128]{1,0:T(1,128)} %bitcast.40, ...), custom_call_target="tpu_custom_call" | custom-call | flops 201326592 | bytes 3670016 | tf_op jit(solution)/shard_map/pallas_call | solution.py:431
  96.6 3.8 %shard_map.121.coef_h = f32[16,4,128,128]{3,2,1,0:T(8,128)} custom-call(f32[16,128,128]{2,1,0:T(8,128)} %get-tuple-element.24.zhat_h, s32[256]{0:T(256)} %mask_h.5, s32[1,256]{1,0:T(1,128)} %bitcast.28, f32[1,128]{1,0:T(1,128)} %bitcast.32, f32[1,128]{1,0:T(1,128)} %bitcast.37, bf16[128,512]{1,0:T(8,128)(2,1)} %proj_h.7, ...), custom_call_target="tpu_custom_call" | custom-call | flops 335544320 | bytes 5242880 | tf_op jit(solution)/shard_map/pallas_call | solution.py:431
  100.4 5.7 %shard_map.122 = bf16[16,128,128]{2,1,0:T(8,128)(2,1)} custom-call(bf16[2,16,8,16,128]{4,3,2,1,0:T(8,128)(2,1)S(1)} %bitcast.20, f32[16,4,128,128]{3,2,1,0:T(8,128)} %shard_map.121.coef_h, f32[16,128,128]{2,1,0:T(8,128)} %get-tuple-element.24.zhat_h, f32[16,128]{1,0:T(8,128)} %get-tuple-element.14.after.inv_h, f32[16,128,128]{2,1,0:T(8,128)} %get-tuple-element.25.dzg_h, ...), custom_call_target="tpu_custom_call" | custom-call | flops 335544320 | bytes 7864320 | tf_op jit(solution)/shard_map/pallas_call | solution.py:431
  (42 shorter events, 8.5 us)
Async XLA Ops:
  3.9 33.7 %all-to-all-start = ((bf16[32,8,16,128]{3,2,1,0:T(8,128)(2,1)}), bf16[32,8,16,128]{3,2,1,0:T(8,128)(2,1)S(1)}, u32[]{:S(2)}, u32[]{:S(2)}) async-start(bf16[32,8,16,128]{3,2,1,0:T(8,128)(2,1)} %bitcast.25), calls=%async_computation | async-start | bytes 2097152 | tf_op jit(solution)/shard_map/all_to_all | solution.py:485
  13.4 1.6 %collective-permute-start = (bf16[8,8,16,128]{3,2,1,0:T(8,128)(2,1)S(1)}, bf16[8,8,16,128]{3,2,1,0:T(8,128)(2,1)S(1)}, u32[]{:S(2)}, u32[]{:S(2)}) collective-permute-start(bf16[8,8,16,128]{3,2,1,0:T(8,128)(2,1)S(1)} %get-tuple-element.16), channel_id=1, source_target_pairs={{0,2},{2,0},{1,3},{3,1},{4,6},{6,4},{5,7},{7,5},{8,10},{10,8},{9,1... | collective-permute-start | bytes 786440 | tf_op jit(solution)/shard_map/ppermute | solution.py:490
  15.1 7.8 %collective-permute-start.1 = (bf16[2,8,16,128]{3,2,1,0:T(8,128)(2,1)S(1)}, bf16[2,8,16,128]{3,2,1,0:T(8,128)(2,1)S(1)}, u32[]{:S(2)}, u32[]{:S(2)}) collective-permute-start(bf16[2,8,16,128]{3,2,1,0:T(8,128)(2,1)S(1)} %pad_maximum_fusion), channel_id=1, source_target_pairs={{0,1},{1,0},{4,5},{5,4},{8,9},{9,8},{12,13},{13,12},{2,3},{3,2},{6... | collective-permute-start | bytes 196616 | tf_op jit(solution)/shard_map/ppermute | solution.py:490
  16.9 8.2 %collective-permute-start.2 = (bf16[2,8,16,128]{3,2,1,0:T(8,128)(2,1)S(1)}, bf16[2,8,16,128]{3,2,1,0:T(8,128)(2,1)S(1)}, u32[]{:S(2)}, u32[]{:S(2)}) collective-permute-start(bf16[2,8,16,128]{3,2,1,0:T(8,128)(2,1)S(1)} %pad_maximum_fusion.1), channel_id=1, source_target_pairs={{0,4},{1,5},{4,0},{5,1},{8,12},{9,13},{12,8},{13,9},{2,6},{3,7},{6... | collective-permute-start | bytes 196616 | tf_op jit(solution)/shard_map/ppermute | solution.py:490
  18.4 11.9 %collective-permute-start.3 = (bf16[2,8,16,128]{3,2,1,0:T(8,128)(2,1)S(1)}, bf16[2,8,16,128]{3,2,1,0:T(8,128)(2,1)S(1)}, u32[]{:S(2)}, u32[]{:S(2)}) collective-permute-start(bf16[2,8,16,128]{3,2,1,0:T(8,128)(2,1)S(1)} %pad_maximum_fusion.2), channel_id=1, source_target_pairs={{0,5},{1,4},{4,1},{5,0},{8,13},{9,12},{12,9},{13,8},{2,7},{3,6},{6... | collective-permute-start | bytes 196616 | tf_op jit(solution)/shard_map/ppermute | solution.py:490
  18.8 11.8 %collective-permute-start.4 = (bf16[2,8,16,128]{3,2,1,0:T(8,128)(2,1)S(1)}, bf16[2,8,16,128]{3,2,1,0:T(8,128)(2,1)S(1)}, u32[]{:S(2)}, u32[]{:S(2)}) collective-permute-start(bf16[2,8,16,128]{3,2,1,0:T(8,128)(2,1)S(1)} %pad_maximum_fusion.3), channel_id=1, source_target_pairs={{0,8},{1,9},{4,12},{5,13},{8,0},{9,1},{12,4},{13,5},{2,10},{3,11},... | collective-permute-start | bytes 196616 | tf_op jit(solution)/shard_map/ppermute | solution.py:490
  20.6 11.5 %collective-permute-start.5 = (bf16[2,8,16,128]{3,2,1,0:T(8,128)(2,1)S(1)}, bf16[2,8,16,128]{3,2,1,0:T(8,128)(2,1)S(1)}, u32[]{:S(2)}, u32[]{:S(2)}) collective-permute-start(bf16[2,8,16,128]{3,2,1,0:T(8,128)(2,1)S(1)} %pad_maximum_fusion.4), channel_id=1, source_target_pairs={{0,9},{1,8},{4,13},{5,12},{8,1},{9,0},{12,5},{13,4},{2,11},{3,10},... | collective-permute-start | bytes 196616 | tf_op jit(solution)/shard_map/ppermute | solution.py:490
  22.9 11.8 %collective-permute-start.6 = (bf16[2,8,16,128]{3,2,1,0:T(8,128)(2,1)S(1)}, bf16[2,8,16,128]{3,2,1,0:T(8,128)(2,1)S(1)}, u32[]{:S(2)}, u32[]{:S(2)}) collective-permute-start(bf16[2,8,16,128]{3,2,1,0:T(8,128)(2,1)S(1)} %pad_maximum_fusion.5), channel_id=1, source_target_pairs={{0,12},{1,13},{4,8},{5,9},{8,4},{9,5},{12,0},{13,1},{2,14},{3,15},... | collective-permute-start | bytes 196616 | tf_op jit(solution)/shard_map/ppermute | solution.py:490
  25.1 12.5 %collective-permute-start.7 = (bf16[2,8,16,128]{3,2,1,0:T(8,128)(2,1)S(1)}, bf16[2,8,16,128]{3,2,1,0:T(8,128)(2,1)S(1)}, u32[]{:S(2)}, u32[]{:S(2)}) collective-permute-start(bf16[2,8,16,128]{3,2,1,0:T(8,128)(2,1)S(1)} %pad_maximum_fusion.6), channel_id=1, source_target_pairs={{0,13},{1,12},{4,9},{5,8},{8,5},{9,4},{12,1},{13,0},{2,15},{3,14},... | collective-permute-start | bytes 196616 | tf_op jit(solution)/shard_map/ppermute | solution.py:490
  65.0 35.5 %all-to-all-start.3 = ((bf16[32,8,16,128]{3,2,1,0:T(8,128)(2,1)}), bf16[32,8,16,128]{3,2,1,0:T(8,128)(2,1)S(1)}, u32[]{:S(2)}, u32[]{:S(2)}) async-start(bf16[32,8,16,128]{3,2,1,0:T(8,128)(2,1)} %bitcast.24), calls=%async_computation.3 | async-start | bytes 2097152 | tf_op jit(solution)/shard_map/all_to_all | solution.py:485
  69.0 1.6 %collective-permute-start.8 = (bf16[8,8,16,128]{3,2,1,0:T(8,128)(2,1)S(1)}, bf16[8,8,16,128]{3,2,1,0:T(8,128)(2,1)S(1)}, u32[]{:S(2)}, u32[]{:S(2)}) collective-permute-start(bf16[8,8,16,128]{3,2,1,0:T(8,128)(2,1)S(1)} %get-tuple-element.21), channel_id=1, source_target_pairs={{0,2},{2,0},{1,3},{3,1},{4,6},{6,4},{5,7},{7,5},{8,10},{10,8},{9,1... | collective-permute-start | bytes 786440 | tf_op jit(solution)/shard_map/ppermute | solution.py:490
  70.7 17.3 %collective-permute-start.9 = (bf16[2,8,16,128]{3,2,1,0:T(8,128)(2,1)S(1)}, bf16[2,8,16,128]{3,2,1,0:T(8,128)(2,1)S(1)}, u32[]{:S(2)}, u32[]{:S(2)}) collective-permute-start(bf16[2,8,16,128]{3,2,1,0:T(8,128)(2,1)S(1)} %pad_maximum_fusion.7), channel_id=1, source_target_pairs={{0,9},{1,8},{4,13},{5,12},{8,1},{9,0},{12,5},{13,4},{2,11},{3,10},... | collective-permute-start | bytes 196616 | tf_op jit(solution)/shard_map/ppermute | solution.py:490
  73.2 19.2 %collective-permute-start.10 = (bf16[2,8,16,128]{3,2,1,0:T(8,128)(2,1)S(1)}, bf16[2,8,16,128]{3,2,1,0:T(8,128)(2,1)S(1)}, u32[]{:S(2)}, u32[]{:S(2)}) collective-permute-start(bf16[2,8,16,128]{3,2,1,0:T(8,128)(2,1)S(1)} %pad_maximum_fusion.8), channel_id=1, source_target_pairs={{0,1},{1,0},{4,5},{5,4},{8,9},{9,8},{12,13},{13,12},{2,3},{3,2},{6... | collective-permute-start | bytes 196616 | tf_op jit(solution)/shard_map/ppermute | solution.py:490
  73.9 26.5 %collective-permute-start.11 = (bf16[2,8,16,128]{3,2,1,0:T(8,128)(2,1)S(1)}, bf16[2,8,16,128]{3,2,1,0:T(8,128)(2,1)S(1)}, u32[]{:S(2)}, u32[]{:S(2)}) collective-permute-start(bf16[2,8,16,128]{3,2,1,0:T(8,128)(2,1)S(1)} %pad_maximum_fusion.9), channel_id=1, source_target_pairs={{0,4},{1,5},{4,0},{5,1},{8,12},{9,13},{12,8},{13,9},{2,6},{3,7},{6... | collective-permute-start | bytes 196616 | tf_op jit(solution)/shard_map/ppermute | solution.py:490
  75.4 25.0 %collective-permute-start.12 = (bf16[2,8,16,128]{3,2,1,0:T(8,128)(2,1)S(1)}, bf16[2,8,16,128]{3,2,1,0:T(8,128)(2,1)S(1)}, u32[]{:S(2)}, u32[]{:S(2)}) collective-permute-start(bf16[2,8,16,128]{3,2,1,0:T(8,128)(2,1)S(1)} %pad_maximum_fusion.10), channel_id=1, source_target_pairs={{0,5},{1,4},{4,1},{5,0},{8,13},{9,12},{12,9},{13,8},{2,7},{3,6},{6... | collective-permute-start | bytes 196616 | tf_op jit(solution)/shard_map/ppermute | solution.py:490
  76.9 23.5 %collective-permute-start.13 = (bf16[2,8,16,128]{3,2,1,0:T(8,128)(2,1)S(1)}, bf16[2,8,16,128]{3,2,1,0:T(8,128)(2,1)S(1)}, u32[]{:S(2)}, u32[]{:S(2)}) collective-permute-start(bf16[2,8,16,128]{3,2,1,0:T(8,128)(2,1)S(1)} %pad_maximum_fusion.11), channel_id=1, source_target_pairs={{0,8},{1,9},{4,12},{5,13},{8,0},{9,1},{12,4},{13,5},{2,10},{3,11},... | collective-permute-start | bytes 196616 | tf_op jit(solution)/shard_map/ppermute | solution.py:490
  87.9 12.5 %collective-permute-start.14 = (bf16[2,8,16,128]{3,2,1,0:T(8,128)(2,1)S(1)}, bf16[2,8,16,128]{3,2,1,0:T(8,128)(2,1)S(1)}, u32[]{:S(2)}, u32[]{:S(2)}) collective-permute-start(bf16[2,8,16,128]{3,2,1,0:T(8,128)(2,1)S(1)} %pad_maximum_fusion.12), channel_id=1, source_target_pairs={{0,12},{1,13},{4,8},{5,9},{8,4},{9,5},{12,0},{13,1},{2,14},{3,15},... | collective-permute-start | bytes 196616 | tf_op jit(solution)/shard_map/ppermute | solution.py:490
  92.5 7.9 %collective-permute-start.15 = (bf16[2,8,16,128]{3,2,1,0:T(8,128)(2,1)S(1)}, bf16[2,8,16,128]{3,2,1,0:T(8,128)(2,1)S(1)}, u32[]{:S(2)}, u32[]{:S(2)}) collective-permute-start(bf16[2,8,16,128]{3,2,1,0:T(8,128)(2,1)S(1)} %pad_maximum_fusion.13), channel_id=1, source_target_pairs={{0,13},{1,12},{4,9},{5,8},{8,5},{9,4},{12,1},{13,0},{2,15},{3,14},... | collective-permute-start | bytes 196616 | tf_op jit(solution)/shard_map/ppermute | solution.py:490

commit v10 on v9

--- a/solution.py
+++ b/solution.py
@@ -218,7 +218,7 @@
 
 
 def factors_kernel(
-    zhat_h, mask_h, mask_row_h, gain_h, bias_h, proj_h, after, coef_h,
+    zhat_h, mask_h, mask_row_h, gain_h, bias_h, proj_h, coef_h,
     zhat, mask_s, mask_v, gain, bias, proj_weight, coef, in_sems, out_sems,
 ):
     rows, width, cols = zhat.shape
@@ -247,8 +247,8 @@
             first = second * q * (1.0 - s)
             for r in range(size):
                 lanes = slice(r * cols, (r + 1) * cols)
-                coef[at + r, part] = first[:, lanes]
-                coef[at + r, part + 1] = second[:, lanes]
+                coef[at + r, part] = first[:, lanes].astype(BF16)
+                coef[at + r, part + 1] = second[:, lanes].astype(BF16)
         copy = pltpu.make_async_copy(
             coef.at[pl.ds(at, size)], coef_h.at[pl.ds(at, size)], out_sems.at[n]
         )
@@ -394,15 +394,11 @@
         wait(blocks.get(at, []))
         columns = []
         for r in range(size):
-            gl = left[pl.ds(at + r, hidden, stride=rows), :]
-            gr = right[pl.ds(at + r, hidden, stride=rows), :]
+            gl = left[pl.ds(at + r, hidden, stride=rows), :].astype(BF16)
+            gr = right[pl.ds(at + r, hidden, stride=rows), :].astype(BF16)
             columns.append(
                 jnp.concatenate(
-                    [
-                        (g * coef[at + r, part]).astype(BF16)
-                        for part, g in enumerate((gl, gl, gr, gr))
-                    ],
-                    axis=0,
+                    [g * coef[at + r, part] for part, g in enumerate((gl, gl, gr, gr))], axis=0
                 )
             )
         back = dot(proj_weight[...], jnp.concatenate(columns, axis=1))
@@ -549,11 +545,22 @@
         flops=2 * cells * width * 4 * hidden,
         moved=16 * cells * width,
     )
+    (coef,) = call(
+        factors_kernel,
+        (shape(rows, 4, hidden, cols),),
+        [
+            wide, mask_s, mask_v, vector, vector, proj_v, vmem(rows, 4, hidden, cols),
+            sems(6), sems(n_groups),
+        ],
+        (zhat, mask, mask_row, gain_in, bias_in, proj_weight),
+        flops=2 * cells * width * 5 * hidden,
+        moved=16 * cells * width,
+    )
     product, left = call(
         functools.partial(product_kernel, n_chip),
         (shape(n_line, n_col, share, rows, cols), shape(n_line, n_col, share, rows, cols)),
         [],
-        (right, inv, *left),
+        (right, coef, *left),
         near=(0, *range(2, 2 + n_pieces)),
         outs_near=(0, 1),
         flops=2 * share * n_half * (n_line * rows) ** 2 * n_col * cols,
@@ -572,7 +579,7 @@
     )
     grad = exchange(grad.reshape(n_place, share, rows, cols))
     grad = grad.reshape(n_line, n_col, share, rows, cols)
-    (grad_right,) = call(
+    (sent,) = call(
         grad_right_kernel,
         (shape(n_half, n_line, n_col, share, rows, cols),),
         [vmem(n_half, n_line, n_col, share, rows, cols), sems(share)],
@@ -581,7 +588,7 @@
         flops=2 * share * n_half * (n_line * rows) ** 2 * n_col * cols,
         moved=8 * cells * hidden,
     )
-    grad_right = exchange_all(grad_right).reshape(n_half, n_place, share, rows, cols)
+    grad_right = exchange_all(sent).reshape(n_half, n_place, share, rows, cols)
     grad_left = call(
         grad_left_kernel,
         pieces_shape,
@@ -593,25 +600,12 @@
         moved=8 * cells * hidden,
     )
     grad_left = exchange_pieces(tuple(grad_left))
-    arrived = grad_left[-min(3, n_chip - 1)]
-    (coef,) = call(
-        factors_kernel,
-        (shape(rows, 4, hidden, cols, dtype=F32),),
-        [
-            wide, mask_s, mask_v, vector, vector, proj_v, vmem(rows, 4, hidden, cols, dtype=F32),
-            sems(6), sems(n_groups),
-        ],
-        (zhat, mask, mask_row, gain_in, bias_in, proj_weight, arrived),
-        near=(6,),
-        flops=2 * cells * width * 5 * hidden,
-        moved=20 * cells * width,
-    )
     update, dzg = call(
         update_kernel,
         (shape(rows, cols, width), shape(rows, width, cols, dtype=F32)),
         [wide, block, vector, vector, square, square, block, wide, plane, sems(6), sems(2)],
-        (product, gate, cotangent, norm_gain, norm_bias, out_weight, gate_weight, arrived),
-        near=(0, 7),
+        (product, gate, cotangent, norm_gain, norm_bias, out_weight, gate_weight, sent),
+        near=(0,),
         flops=2 * cells * width * 3 * hidden,
         moved=14 * cells * hidden,
     )
@@ -619,7 +613,7 @@
         functools.partial(back_kernel, n_chip),
         (shape(rows, cols, width),),
         [
-            vmem(rows, 4, hidden, cols, dtype=F32), wide, vmem(rows, cols, dtype=F32), wide,
+            vmem(rows, 4, hidden, cols), wide, vmem(rows, cols, dtype=F32), wide,
             vector, proj_v, block, plane, plane,
             sems(3), sems(2), sems(2), sems(2), sems(2),
         ],

time: 107 us -> 101 us (0.944)
  starting transfers between devices: 32.2 us -> 29.2 us
  waiting for transfers between devices: 21.6 us -> 19.5 us
  Pallas kernels: 26.5 us -> 25.3 us
    ppermute x16, starting transfers between devices: 21.2 us -> 18.2 us  [permute(): lax.ppermute(values, axes, [(at, at ^ distance) for at in range(size)])]
    ppermute x16, waiting for transfers between devices: 21.6 us -> 19.5 us  [permute(): lax.ppermute(values, axes, [(at, at ^ distance) for at in range(size)])]
    pallas_call x10, Pallas kernels: 26.5 us -> 25.3 us  [call(): pl.pallas_call(kernel, out_shape=[out if at in outs_near else pltpu.HBM(o...]
  transfers between devices with their start and end apart: 18 -> 18, of which waited for: 9 -> 12; matrix products, arithmetic and copies ran while one was open for 0% -> 0% of each run, Pallas kernels for 14% -> 15%
where the time goes in v10:
time: 101 us; the launch traced here: 100 us
  starting transfers between devices  29.2 us (29%)
  Pallas kernels  25.3 us (25%)
  blocking collectives  24.9 us (25%)
  waiting for transfers between devices  19.5 us (19%)
    pallas_call x10, Pallas kernels, call(): pl.pallas_call(kernel, out_shape=[out if at in outs_near else pltpu.HBM(o...  25.3 us
    all_to_all x2, blocking collectives, exchange(): lax.all_to_all(values, within, split_axis=0, concat_axis=0, tiled=True)  24.9 us
    ppermute x16, waiting for transfers between devices, permute(): lax.ppermute(values, axes, [(at, at ^ distance) for at in range(size)])  19.5 us
    ppermute x16, starting transfers between devices, permute(): lax.ppermute(values, axes, [(at, at ^ distance) for at in range(size)])  18.2 us
    all_to_all x2, starting transfers between devices, exchange_all(): lax.all_to_all(flat, ('half', *within), split_axis=0, concat_axis=0, tile...  10.9 us
  transfers between devices with their start and end apart: 18, of which 12 were waited for; matrix products, arithmetic and copies ran while one was open for 0% of the time, Pallas kernels for 15%

profile of v10, /device:TPU:0, one launch (start us, length us, event | category | flops | bytes accessed | tf_op | source)
XLA Modules:
  0.0 100.1 jit_solution(7982903304431338115)
XLA Ops:
  0.6 3.2 %shard_map.113 = bf16[2,16,8,16,128]{4,3,2,1,0:T(8,128)(2,1)} custom-call(bf16[16,128,128]{2,1,0:T(8,128)(2,1)} %pair_h.5, s32[256]{0:T(256)} %mask_h.5, s32[1,256]{1,0:T(1,128)} %bitcast.26, f32[1,128]{1,0:T(1,128)} %bitcast.29, f32[1,128]{1,0:T(1,128)} %bitcast.34, bf16[128,512]{1,0:T(8,128)(2,1)} %proj_h.7), custom_call_target="tpu_custom_call" | custom-call | flops 201326592 | bytes 1310720 | tf_op jit(solution)/shard_map/pallas_call | solution.py:427
  3.9 7.3 %all-to-all-start = ((bf16[32,8,16,128]{3,2,1,0:T(8,128)(2,1)}), bf16[32,8,16,128]{3,2,1,0:T(8,128)(2,1)S(1)}, u32[]{:S(2)}, u32[]{:S(2)}) async-start(bf16[32,8,16,128]{3,2,1,0:T(8,128)(2,1)} %bitcast.25), calls=%async_computation | async-start | bytes 2097152 | tf_op jit(solution)/shard_map/all_to_all | solution.py:481
  11.2 2.3 %shard_map.116 = (bf16[8,8,16,128]{3,2,1,0:T(8,128)(2,1)S(1)}, bf16[8,8,16,128]{3,2,1,0:T(8,128)(2,1)S(1)}) custom-call(bf16[16,128,128]{2,1,0:T(8,128)(2,1)} %pair_h.5, s32[256]{0:T(256)} %mask_h.5, s32[1,256]{1,0:T(1,128)} %bitcast.27, f32[1,128]{1,0:T(1,128)} %bitcast.30, f32[1,128]{1,0:T(1,128)} %bitcast.35, bf16[128,512]{1,0:T(8,128)(2,1)} %proj_h.7), custom_call_target="tpu_custom_call" | custom-call | flops 201326592 | bytes 1310720 | tf_op jit(solution)/shard_map/pallas_call | solution.py:427
  15.1 1.8 %collective-permute-start.1 = (bf16[2,8,16,128]{3,2,1,0:T(8,128)(2,1)S(1)}, bf16[2,8,16,128]{3,2,1,0:T(8,128)(2,1)S(1)}, u32[]{:S(2)}, u32[]{:S(2)}) collective-permute-start(bf16[2,8,16,128]{3,2,1,0:T(8,128)(2,1)S(1)} %pad_maximum_fusion), channel_id=1, source_target_pairs={{0,1},{1,0},{4,5},{5,4},{8,9},{9,8},{12,13},{13,12},{2,3},{3,2},{6... | collective-permute-start | bytes 196616 | tf_op jit(solution)/shard_map/ppermute | solution.py:486
  16.9 1.5 %collective-permute-start.2 = (bf16[2,8,16,128]{3,2,1,0:T(8,128)(2,1)S(1)}, bf16[2,8,16,128]{3,2,1,0:T(8,128)(2,1)S(1)}, u32[]{:S(2)}, u32[]{:S(2)}) collective-permute-start(bf16[2,8,16,128]{3,2,1,0:T(8,128)(2,1)S(1)} %pad_maximum_fusion.1), channel_id=1, source_target_pairs={{0,4},{1,5},{4,0},{5,1},{8,12},{9,13},{12,8},{13,9},{2,6},{3,7},{6... | collective-permute-start | bytes 196616 | tf_op jit(solution)/shard_map/ppermute | solution.py:486
  18.8 1.8 %collective-permute-start.4 = (bf16[2,8,16,128]{3,2,1,0:T(8,128)(2,1)S(1)}, bf16[2,8,16,128]{3,2,1,0:T(8,128)(2,1)S(1)}, u32[]{:S(2)}, u32[]{:S(2)}) collective-permute-start(bf16[2,8,16,128]{3,2,1,0:T(8,128)(2,1)S(1)} %pad_maximum_fusion.3), channel_id=1, source_target_pairs={{0,8},{1,9},{4,12},{5,13},{8,0},{9,1},{12,4},{13,5},{2,10},{3,11},... | collective-permute-start | bytes 196616 | tf_op jit(solution)/shard_map/ppermute | solution.py:486
  20.6 1.5 %collective-permute-start.5 = (bf16[2,8,16,128]{3,2,1,0:T(8,128)(2,1)S(1)}, bf16[2,8,16,128]{3,2,1,0:T(8,128)(2,1)S(1)}, u32[]{:S(2)}, u32[]{:S(2)}) collective-permute-start(bf16[2,8,16,128]{3,2,1,0:T(8,128)(2,1)S(1)} %pad_maximum_fusion.4), channel_id=1, source_target_pairs={{0,9},{1,8},{4,13},{5,12},{8,1},{9,0},{12,5},{13,4},{2,11},{3,10},... | collective-permute-start | bytes 196616 | tf_op jit(solution)/shard_map/ppermute | solution.py:486
  22.9 1.7 %collective-permute-start.6 = (bf16[2,8,16,128]{3,2,1,0:T(8,128)(2,1)S(1)}, bf16[2,8,16,128]{3,2,1,0:T(8,128)(2,1)S(1)}, u32[]{:S(2)}, u32[]{:S(2)}) collective-permute-start(bf16[2,8,16,128]{3,2,1,0:T(8,128)(2,1)S(1)} %pad_maximum_fusion.5), channel_id=1, source_target_pairs={{0,12},{1,13},{4,8},{5,9},{8,4},{9,5},{12,0},{13,1},{2,14},{3,15},... | collective-permute-start | bytes 196616 | tf_op jit(solution)/shard_map/ppermute | solution.py:486
  25.8 4.6 %shard_map.114 = (f32[16,128,128]{2,1,0:T(8,128)}, f32[16,128]{1,0:T(8,128)}, f32[16,128,128]{2,1,0:T(8,128)}, f32[2048,128]{1,0:T(8,128)S(1)}) custom-call(bf16[16,128,128]{2,1,0:T(8,128)(2,1)} %pair_h.5, bf16[16,128,128]{2,1,0:T(8,128)(2,1)} %cot_h.3, f32[1,128]{1,0:T(1,128)} %bitcast.31, f32[1,128]{1,0:T(1,128)} %bitcast.36, bf16[128,128]{1,0:T(8,128)(2,1)} %gate_w_h.1, ...), custom_call_target="tpu_custom_call" | custom-call | flops 268435456 | bytes 4194304 | tf_op jit(solution)/shard_map/pallas_call | solution.py:427
  30.4 3.2 %shard_map.115.after.coef_h = bf16[16,4,128,128]{3,2,1,0:T(8,128)(2,1)} custom-call(f32[16,128,128]{2,1,0:T(8,128)} %get-tuple-element.14.zhat_h, s32[256]{0:T(256)} %mask_h.5, s32[1,256]{1,0:T(1,128)} %bitcast.28, f32[1,128]{1,0:T(1,128)} %bitcast.32, f32[1,128]{1,0:T(1,128)} %bitcast.37, bf16[128,512]{1,0:T(8,128)(2,1)} %proj_h.7), custom_call_target="tpu_custom_call" | custom-call | flops 335544320 | bytes 4194304 | tf_op jit(solution)/shard_map/pallas_call | solution.py:427
  34.8 2.9 %collective-permute-done.7.refs_8_ = bf16[2,8,16,128]{3,2,1,0:T(8,128)(2,1)S(1)} collective-permute-done((bf16[2,8,16,128]{3,2,1,0:T(8,128)(2,1)S(1)}, bf16[2,8,16,128]{3,2,1,0:T(8,128)(2,1)S(1)}, u32[]{:S(2)}, u32[]{:S(2)}) %collective-permute-start.7) | collective-permute-done | bytes 65568 | tf_op jit(solution)/shard_map/ppermute | solution.py:486
  38.2 12.9 %all_to_all.20 = bf16[16,8,16,128]{3,2,1,0:T(8,128)(2,1)S(1)} all-to-all(bf16[16,8,16,128]{3,2,1,0:T(8,128)(2,1)S(1)} %bitcast.23), channel_id=1, replica_groups=mesh['grp'=1,'half'=2,'row'=4,'core'=2,'col'=2] {'row','core','col'}, dimensions={0} | all-to-all | bytes 1048576 | tf_op jit(solution)/shard_map/all_to_all | solution.py:477
  51.7 12.0 %all_to_all.21 = bf16[16,8,16,128]{3,2,1,0:T(8,128)(2,1)S(1)} all-to-all(bf16[16,8,16,128]{3,2,1,0:T(8,128)(2,1)S(1)} %bitcast.21), channel_id=1, replica_groups=mesh['grp'=1,'half'=2,'row'=4,'core'=2,'col'=2] {'row','core','col'}, dimensions={0} | all-to-all | bytes 1048576 | tf_op jit(solution)/shard_map/all_to_all | solution.py:477
  65.0 3.6 %all-to-all-start.3 = ((bf16[32,8,16,128]{3,2,1,0:T(8,128)(2,1)}), bf16[32,8,16,128]{3,2,1,0:T(8,128)(2,1)S(1)}, u32[]{:S(2)}, u32[]{:S(2)}) async-start(bf16[32,8,16,128]{3,2,1,0:T(8,128)(2,1)} %bitcast.24), calls=%async_computation.3 | async-start | bytes 2097152 | tf_op jit(solution)/shard_map/all_to_all | solution.py:481
  69.2 1.4 %collective-permute-done.8.refs_1_ = bf16[8,8,16,128]{3,2,1,0:T(8,128)(2,1)S(1)} collective-permute-done((bf16[8,8,16,128]{3,2,1,0:T(8,128)(2,1)S(1)}, bf16[8,8,16,128]{3,2,1,0:T(8,128)(2,1)S(1)}, u32[]{:S(2)}, u32[]{:S(2)}) %collective-permute-start.8) | collective-permute-done | bytes 262176 | tf_op jit(solution)/shard_map/ppermute | solution.py:486
  70.7 1.7 %collective-permute-start.9 = (bf16[2,8,16,128]{3,2,1,0:T(8,128)(2,1)S(1)}, bf16[2,8,16,128]{3,2,1,0:T(8,128)(2,1)S(1)}, u32[]{:S(2)}, u32[]{:S(2)}) collective-permute-start(bf16[2,8,16,128]{3,2,1,0:T(8,128)(2,1)S(1)} %pad_maximum_fusion.7), channel_id=1, source_target_pairs={{0,1},{1,0},{4,5},{5,4},{8,9},{9,8},{12,13},{13,12},{2,3},{3,2},{6... | collective-permute-start | bytes 196616 | tf_op jit(solution)/shard_map/ppermute | solution.py:486
  72.4 1.5 %collective-permute-start.10 = (bf16[2,8,16,128]{3,2,1,0:T(8,128)(2,1)S(1)}, bf16[2,8,16,128]{3,2,1,0:T(8,128)(2,1)S(1)}, u32[]{:S(2)}, u32[]{:S(2)}) collective-permute-start(bf16[2,8,16,128]{3,2,1,0:T(8,128)(2,1)S(1)} %pad_maximum_fusion.8), channel_id=1, source_target_pairs={{0,4},{1,5},{4,0},{5,1},{8,12},{9,13},{12,8},{13,9},{2,6},{3,7},{6... | collective-permute-start | bytes 196616 | tf_op jit(solution)/shard_map/ppermute | solution.py:486
  74.4 1.7 %collective-permute-start.12 = (bf16[2,8,16,128]{3,2,1,0:T(8,128)(2,1)S(1)}, bf16[2,8,16,128]{3,2,1,0:T(8,128)(2,1)S(1)}, u32[]{:S(2)}, u32[]{:S(2)}) collective-permute-start(bf16[2,8,16,128]{3,2,1,0:T(8,128)(2,1)S(1)} %pad_maximum_fusion.10), channel_id=1, source_target_pairs={{0,8},{1,9},{4,12},{5,13},{8,0},{9,1},{12,4},{13,5},{2,10},{3,11},... | collective-permute-start | bytes 196616 | tf_op jit(solution)/shard_map/ppermute | solution.py:486
  76.1 1.5 %collective-permute-start.13 = (bf16[2,8,16,128]{3,2,1,0:T(8,128)(2,1)S(1)}, bf16[2,8,16,128]{3,2,1,0:T(8,128)(2,1)S(1)}, u32[]{:S(2)}, u32[]{:S(2)}) collective-permute-start(bf16[2,8,16,128]{3,2,1,0:T(8,128)(2,1)S(1)} %pad_maximum_fusion.11), channel_id=1, source_target_pairs={{0,9},{1,8},{4,13},{5,12},{8,1},{9,0},{12,5},{13,4},{2,11},{3,10},... | collective-permute-start | bytes 196616 | tf_op jit(solution)/shard_map/ppermute | solution.py:486
  77.6 2.9 %collective-permute-done.9.refs_2_ = bf16[2,8,16,128]{3,2,1,0:T(8,128)(2,1)S(1)} collective-permute-done((bf16[2,8,16,128]{3,2,1,0:T(8,128)(2,1)S(1)}, bf16[2,8,16,128]{3,2,1,0:T(8,128)(2,1)S(1)}, u32[]{:S(2)}, u32[]{:S(2)}) %collective-permute-start.9) | collective-permute-done | bytes 65568 | tf_op jit(solution)/shard_map/ppermute | solution.py:486
  83.5 4.2 %shard_map.120 = (bf16[16,128,128]{2,1,0:T(8,128)(2,1)}, f32[16,128,128]{2,1,0:T(8,128)}) custom-call(bf16[128,16,128]{2,1,0:T(8,128)(2,1)S(1)} %bitcast.19, f32[16,128,128]{2,1,0:T(8,128)} %get-tuple-element.18.gate_h, bf16[16,128,128]{2,1,0:T(8,128)(2,1)} %cot_h.3, f32[1,128]{1,0:T(1,128)} %bitcast.39, f32[1,128]{1,0:T(1,128)} %bitcast.40, ...), custom_call_target="tpu_custom_call" | custom-call | flops 201326592 | bytes 3670016 | tf_op jit(solution)/shard_map/pallas_call | solution.py:427
  89.4 2.7 %collective-permute-done.14.refs_7_ = bf16[2,8,16,128]{3,2,1,0:T(8,128)(2,1)S(1)} collective-permute-done((bf16[2,8,16,128]{3,2,1,0:T(8,128)(2,1)S(1)}, bf16[2,8,16,128]{3,2,1,0:T(8,128)(2,1)S(1)}, u32[]{:S(2)}, u32[]{:S(2)}) %collective-permute-start.14) | collective-permute-done | bytes 65568 | tf_op jit(solution)/shard_map/ppermute | solution.py:486
  92.0 2.9 %collective-permute-done.15.refs_8_ = bf16[2,8,16,128]{3,2,1,0:T(8,128)(2,1)S(1)} collective-permute-done((bf16[2,8,16,128]{3,2,1,0:T(8,128)(2,1)S(1)}, bf16[2,8,16,128]{3,2,1,0:T(8,128)(2,1)S(1)}, u32[]{:S(2)}, u32[]{:S(2)}) %collective-permute-start.15) | collective-permute-done | bytes 65568 | tf_op jit(solution)/shard_map/ppermute | solution.py:486
  94.9 5.0 %shard_map.122 = bf16[16,128,128]{2,1,0:T(8,128)(2,1)} custom-call(bf16[2,16,8,16,128]{4,3,2,1,0:T(8,128)(2,1)S(1)} %bitcast.20, bf16[16,4,128,128]{3,2,1,0:T(8,128)(2,1)} %shard_map.115.after.coef_h, f32[16,128,128]{2,1,0:T(8,128)} %get-tuple-element.14.zhat_h, f32[16,128]{1,0:T(8,128)} %get-tuple-element.22.inv_h, ...), custom_call_target="tpu_custom_call" | custom-call | flops 335544320 | bytes 7864320 | tf_op jit(solution)/shard_map/pallas_call | solution.py:427
  (42 shorter events, 13.4 us)
Async XLA Ops:
  3.9 33.7 %all-to-all-start = ((bf16[32,8,16,128]{3,2,1,0:T(8,128)(2,1)}), bf16[32,8,16,128]{3,2,1,0:T(8,128)(2,1)S(1)}, u32[]{:S(2)}, u32[]{:S(2)}) async-start(bf16[32,8,16,128]{3,2,1,0:T(8,128)(2,1)} %bitcast.25), calls=%async_computation | async-start | bytes 2097152 | tf_op jit(solution)/shard_map/all_to_all | solution.py:481
  13.4 1.6 %collective-permute-start = (bf16[8,8,16,128]{3,2,1,0:T(8,128)(2,1)S(1)}, bf16[8,8,16,128]{3,2,1,0:T(8,128)(2,1)S(1)}, u32[]{:S(2)}, u32[]{:S(2)}) collective-permute-start(bf16[8,8,16,128]{3,2,1,0:T(8,128)(2,1)S(1)} %get-tuple-element.16), channel_id=1, source_target_pairs={{0,2},{2,0},{1,3},{3,1},{4,6},{6,4},{5,7},{7,5},{8,10},{10,8},{9,1... | collective-permute-start | bytes 786440 | tf_op jit(solution)/shard_map/ppermute | solution.py:486
  15.1 7.8 %collective-permute-start.1 = (bf16[2,8,16,128]{3,2,1,0:T(8,128)(2,1)S(1)}, bf16[2,8,16,128]{3,2,1,0:T(8,128)(2,1)S(1)}, u32[]{:S(2)}, u32[]{:S(2)}) collective-permute-start(bf16[2,8,16,128]{3,2,1,0:T(8,128)(2,1)S(1)} %pad_maximum_fusion), channel_id=1, source_target_pairs={{0,1},{1,0},{4,5},{5,4},{8,9},{9,8},{12,13},{13,12},{2,3},{3,2},{6... | collective-permute-start | bytes 196616 | tf_op jit(solution)/shard_map/ppermute | solution.py:486
  16.9 8.2 %collective-permute-start.2 = (bf16[2,8,16,128]{3,2,1,0:T(8,128)(2,1)S(1)}, bf16[2,8,16,128]{3,2,1,0:T(8,128)(2,1)S(1)}, u32[]{:S(2)}, u32[]{:S(2)}) collective-permute-start(bf16[2,8,16,128]{3,2,1,0:T(8,128)(2,1)S(1)} %pad_maximum_fusion.1), channel_id=1, source_target_pairs={{0,4},{1,5},{4,0},{5,1},{8,12},{9,13},{12,8},{13,9},{2,6},{3,7},{6... | collective-permute-start | bytes 196616 | tf_op jit(solution)/shard_map/ppermute | solution.py:486
  18.5 15.1 %collective-permute-start.3 = (bf16[2,8,16,128]{3,2,1,0:T(8,128)(2,1)S(1)}, bf16[2,8,16,128]{3,2,1,0:T(8,128)(2,1)S(1)}, u32[]{:S(2)}, u32[]{:S(2)}) collective-permute-start(bf16[2,8,16,128]{3,2,1,0:T(8,128)(2,1)S(1)} %pad_maximum_fusion.2), channel_id=1, source_target_pairs={{0,5},{1,4},{4,1},{5,0},{8,13},{9,12},{12,9},{13,8},{2,7},{3,6},{6... | collective-permute-start | bytes 196616 | tf_op jit(solution)/shard_map/ppermute | solution.py:486
  18.8 14.8 %collective-permute-start.4 = (bf16[2,8,16,128]{3,2,1,0:T(8,128)(2,1)S(1)}, bf16[2,8,16,128]{3,2,1,0:T(8,128)(2,1)S(1)}, u32[]{:S(2)}, u32[]{:S(2)}) collective-permute-start(bf16[2,8,16,128]{3,2,1,0:T(8,128)(2,1)S(1)} %pad_maximum_fusion.3), channel_id=1, source_target_pairs={{0,8},{1,9},{4,12},{5,13},{8,0},{9,1},{12,4},{13,5},{2,10},{3,11},... | collective-permute-start | bytes 196616 | tf_op jit(solution)/shard_map/ppermute | solution.py:486
  20.6 13.0 %collective-permute-start.5 = (bf16[2,8,16,128]{3,2,1,0:T(8,128)(2,1)S(1)}, bf16[2,8,16,128]{3,2,1,0:T(8,128)(2,1)S(1)}, u32[]{:S(2)}, u32[]{:S(2)}) collective-permute-start(bf16[2,8,16,128]{3,2,1,0:T(8,128)(2,1)S(1)} %pad_maximum_fusion.4), channel_id=1, source_target_pairs={{0,9},{1,8},{4,13},{5,12},{8,1},{9,0},{12,5},{13,4},{2,11},{3,10},... | collective-permute-start | bytes 196616 | tf_op jit(solution)/shard_map/ppermute | solution.py:486
  22.9 11.8 %collective-permute-start.6 = (bf16[2,8,16,128]{3,2,1,0:T(8,128)(2,1)S(1)}, bf16[2,8,16,128]{3,2,1,0:T(8,128)(2,1)S(1)}, u32[]{:S(2)}, u32[]{:S(2)}) collective-permute-start(bf16[2,8,16,128]{3,2,1,0:T(8,128)(2,1)S(1)} %pad_maximum_fusion.5), channel_id=1, source_target_pairs={{0,12},{1,13},{4,8},{5,9},{8,4},{9,5},{12,0},{13,1},{2,14},{3,15},... | collective-permute-start | bytes 196616 | tf_op jit(solution)/shard_map/ppermute | solution.py:486
  25.2 12.5 %collective-permute-start.7 = (bf16[2,8,16,128]{3,2,1,0:T(8,128)(2,1)S(1)}, bf16[2,8,16,128]{3,2,1,0:T(8,128)(2,1)S(1)}, u32[]{:S(2)}, u32[]{:S(2)}) collective-permute-start(bf16[2,8,16,128]{3,2,1,0:T(8,128)(2,1)S(1)} %pad_maximum_fusion.6), channel_id=1, source_target_pairs={{0,13},{1,12},{4,9},{5,8},{8,5},{9,4},{12,1},{13,0},{2,15},{3,14},... | collective-permute-start | bytes 196616 | tf_op jit(solution)/shard_map/ppermute | solution.py:486
  65.0 29.9 %all-to-all-start.3 = ((bf16[32,8,16,128]{3,2,1,0:T(8,128)(2,1)}), bf16[32,8,16,128]{3,2,1,0:T(8,128)(2,1)S(1)}, u32[]{:S(2)}, u32[]{:S(2)}) async-start(bf16[32,8,16,128]{3,2,1,0:T(8,128)(2,1)} %bitcast.24), calls=%async_computation.3 | async-start | bytes 2097152 | tf_op jit(solution)/shard_map/all_to_all | solution.py:481
  69.1 1.6 %collective-permute-start.8 = (bf16[8,8,16,128]{3,2,1,0:T(8,128)(2,1)S(1)}, bf16[8,8,16,128]{3,2,1,0:T(8,128)(2,1)S(1)}, u32[]{:S(2)}, u32[]{:S(2)}) collective-permute-start(bf16[8,8,16,128]{3,2,1,0:T(8,128)(2,1)S(1)} %get-tuple-element.25), channel_id=1, source_target_pairs={{0,2},{2,0},{1,3},{3,1},{4,6},{6,4},{5,7},{7,5},{8,10},{10,8},{9,1... | collective-permute-start | bytes 786440 | tf_op jit(solution)/shard_map/ppermute | solution.py:486
  70.7 9.8 %collective-permute-start.9 = (bf16[2,8,16,128]{3,2,1,0:T(8,128)(2,1)S(1)}, bf16[2,8,16,128]{3,2,1,0:T(8,128)(2,1)S(1)}, u32[]{:S(2)}, u32[]{:S(2)}) collective-permute-start(bf16[2,8,16,128]{3,2,1,0:T(8,128)(2,1)S(1)} %pad_maximum_fusion.7), channel_id=1, source_target_pairs={{0,1},{1,0},{4,5},{5,4},{8,9},{9,8},{12,13},{13,12},{2,3},{3,2},{6... | collective-permute-start | bytes 196616 | tf_op jit(solution)/shard_map/ppermute | solution.py:486
  72.4 9.9 %collective-permute-start.10 = (bf16[2,8,16,128]{3,2,1,0:T(8,128)(2,1)S(1)}, bf16[2,8,16,128]{3,2,1,0:T(8,128)(2,1)S(1)}, u32[]{:S(2)}, u32[]{:S(2)}) collective-permute-start(bf16[2,8,16,128]{3,2,1,0:T(8,128)(2,1)S(1)} %pad_maximum_fusion.8), channel_id=1, source_target_pairs={{0,4},{1,5},{4,0},{5,1},{8,12},{9,13},{12,8},{13,9},{2,6},{3,7},{6... | collective-permute-start | bytes 196616 | tf_op jit(solution)/shard_map/ppermute | solution.py:486
  73.9 13.8 %collective-permute-start.11 = (bf16[2,8,16,128]{3,2,1,0:T(8,128)(2,1)S(1)}, bf16[2,8,16,128]{3,2,1,0:T(8,128)(2,1)S(1)}, u32[]{:S(2)}, u32[]{:S(2)}) collective-permute-start(bf16[2,8,16,128]{3,2,1,0:T(8,128)(2,1)S(1)} %pad_maximum_fusion.9), channel_id=1, source_target_pairs={{0,5},{1,4},{4,1},{5,0},{8,13},{9,12},{12,9},{13,8},{2,7},{3,6},{6... | collective-permute-start | bytes 196616 | tf_op jit(solution)/shard_map/ppermute | solution.py:486
  74.4 13.6 %collective-permute-start.12 = (bf16[2,8,16,128]{3,2,1,0:T(8,128)(2,1)S(1)}, bf16[2,8,16,128]{3,2,1,0:T(8,128)(2,1)S(1)}, u32[]{:S(2)}, u32[]{:S(2)}) collective-permute-start(bf16[2,8,16,128]{3,2,1,0:T(8,128)(2,1)S(1)} %pad_maximum_fusion.10), channel_id=1, source_target_pairs={{0,8},{1,9},{4,12},{5,13},{8,0},{9,1},{12,4},{13,5},{2,10},{3,11},... | collective-permute-start | bytes 196616 | tf_op jit(solution)/shard_map/ppermute | solution.py:486
  76.1 13.3 %collective-permute-start.13 = (bf16[2,8,16,128]{3,2,1,0:T(8,128)(2,1)S(1)}, bf16[2,8,16,128]{3,2,1,0:T(8,128)(2,1)S(1)}, u32[]{:S(2)}, u32[]{:S(2)}) collective-permute-start(bf16[2,8,16,128]{3,2,1,0:T(8,128)(2,1)S(1)} %pad_maximum_fusion.11), channel_id=1, source_target_pairs={{0,9},{1,8},{4,13},{5,12},{8,1},{9,0},{12,5},{13,4},{2,11},{3,10},... | collective-permute-start | bytes 196616 | tf_op jit(solution)/shard_map/ppermute | solution.py:486
  80.5 11.5 %collective-permute-start.14 = (bf16[2,8,16,128]{3,2,1,0:T(8,128)(2,1)S(1)}, bf16[2,8,16,128]{3,2,1,0:T(8,128)(2,1)S(1)}, u32[]{:S(2)}, u32[]{:S(2)}) collective-permute-start(bf16[2,8,16,128]{3,2,1,0:T(8,128)(2,1)S(1)} %pad_maximum_fusion.12), channel_id=1, source_target_pairs={{0,12},{1,13},{4,8},{5,9},{8,4},{9,5},{12,0},{13,1},{2,14},{3,15},... | collective-permute-start | bytes 196616 | tf_op jit(solution)/shard_map/ppermute | solution.py:486
  82.3 12.6 %collective-permute-start.15 = (bf16[2,8,16,128]{3,2,1,0:T(8,128)(2,1)S(1)}, bf16[2,8,16,128]{3,2,1,0:T(8,128)(2,1)S(1)}, u32[]{:S(2)}, u32[]{:S(2)}) collective-permute-start(bf16[2,8,16,128]{3,2,1,0:T(8,128)(2,1)S(1)} %pad_maximum_fusion.13), channel_id=1, source_target_pairs={{0,13},{1,12},{4,9},{5,8},{8,5},{9,4},{12,1},{13,0},{2,15},{3,14},... | collective-permute-start | bytes 196616 | tf_op jit(solution)/shard_map/ppermute | solution.py:486

commit v11 on v10

--- a/solution.py
+++ b/solution.py
@@ -109,69 +109,43 @@
 
 
 def front_kernel(
-    part, n_out, pair_h, mask_h, mask_row_h, gain_h, bias_h, proj_h, *refs
+    n_out, pair_h, mask_h, mask_row_h, gain_h, bias_h, proj_h, *refs
 ):
     outs = refs[:n_out]
-    pair, mask_s, mask_v, gain, bias, proj_weight, zbar, plane, sems, *more = refs[n_out:]
+    pair, mask_s, mask_v, gain, bias, proj_weight, left, right, sems = refs[n_out:]
     rows, cols, width = pair.shape
-    hidden = plane.shape[0] // rows
+    hidden = left.shape[0] // rows
     groups = groups_of(rows)
     wait(
         start(
             sems,
             [
-                (gain_h, gain), (bias_h, bias),
-                (proj_h.at[:, pl.ds(part * hidden, 2 * hidden)], proj_weight),
+                (gain_h, gain), (bias_h, bias), (proj_h, proj_weight),
                 (mask_h, mask_s), (mask_row_h, mask_v), (pair_h, pair),
             ],
         )
     )
     gain_b = jnp.concatenate([down_lanes(gain[...], cols)] * groups[0][1], axis=1)
     bias_b = jnp.concatenate([down_lanes(bias[...], cols)] * groups[0][1], axis=1)
+    weight = turned_weight(proj_weight[...])
     for at, size in groups:
         zhat, _ = normalized(turned(pair[at : at + size].reshape(size * cols, width)))
-        zbar[:, at * cols : (at + size) * cols] = (zhat * gain_b + bias_b).astype(BF16)
-    weight = turned_weight(proj_weight[...])
-
-    def channels(first, count):
-        for at, size in groups:
-            z = zbar[:, at * cols : (at + size) * cols]
-            p = dot(weight[first : first + count], z)
-            q = dot(weight[hidden + first : hidden + first + count], z)
-            values = sigmoid(p) * q * pair_mask(mask_s, mask_v, at, size, rows, cols)
+        zbar = (zhat * gain_b + bias_b).astype(BF16)
+        pm = pair_mask(mask_s, mask_v, at, size, rows, cols)
+        for part, plane in ((0, left), (2, right)):
+            p = dot(weight[part * hidden : (part + 1) * hidden], zbar)
+            q = dot(weight[(part + 1) * hidden : (part + 2) * hidden], zbar)
+            values = sigmoid(p) * q * pm
             for r in range(size):
-                plane[pl.ds(first * rows + at + r, count, stride=rows), :] = values[
-                    :, r * cols : (r + 1) * cols
-                ]
-
-    if n_out > 1:
-        channels(0, hidden)
-        give_pieces(plane, outs)
-        return
-    (out_h,), (ready, out_sems) = outs, more
-    n_place, share = ready.shape[:2]
-    size = n_place // math.gcd(n_place, 4)
-    leaving = []
-    for n, at in enumerate(range(0, n_place, size)):
-        channels(at * share, size * share)
-        values = plane[at * share * rows : (at + size) * share * rows]
-        ready[at : at + size] = values.reshape(size, *ready.shape[1:]).astype(BF16)
-        for half in range(out_h.shape[0]):
-            copy = pltpu.make_async_copy(
-                ready.at[pl.ds(at, size)], out_h.at[half, pl.ds(at, size)], out_sems.at[half, n]
-            )
-            copy.start()
-            leaving.append(copy)
-    wait(leaving)
-
-
-def give_pieces(plane, outs):
-    n_chip = outs[0].shape[0]
-    length = plane.shape[0] // (len(outs) * n_chip)
-    for m, n, number in sources(n_chip, len(outs)):
+                plane[pl.ds(at + r, hidden, stride=rows), :] = values[:, r * cols : (r + 1) * cols]
+    n_chip, share2 = outs[0].shape[:2]
+    share = share2 // 2
+    length = share * rows
+    for m, n, number in sources(n_chip, n_out):
         first = pl.multiple_of(number * length, length)
-        values = plane[pl.ds(first, length), :]
-        outs[m][n] = values.reshape(outs[m].shape[1:]).astype(BF16)
+        for part, plane in enumerate((left, right)):
+            values = plane[pl.ds(first, length), :].reshape(share, rows, cols)
+            outs[m][n, part * share : (part + 1) * share] = values.astype(BF16)
 
 
 def side_kernel(
@@ -265,22 +239,37 @@
     )
 
 
-def put_channel(ref, at, values):
-    *shape, n_col, _, rows, cols = ref.shape
-    lead = (slice(None),) * len(shape)
+def half_columns(ref, which):
+    count = ref.shape[1] // lax.axis_size("half")
+    first = (lax.axis_index("half") ^ which) * count
+    return [first + c for c in range(count)]
+
+
+def half_matrix(ref, at, which):
+    cols = ref.shape[-1]
+    return jnp.concatenate(
+        [ref[:, c, at].reshape(-1, cols) for c in half_columns(ref, which)], axis=1
+    )
+
+
+def put_channel(ref, at, values, columns):
+    n_line, _, _, rows, cols = ref.shape
     values = values.astype(BF16)
-    for c in range(n_col):
-        ref[(*lead, c, at)] = values[:, c * cols : (c + 1) * cols].reshape(*shape, rows, cols)
-
-
-def product_kernel(n_chip, right, after, *refs):
-    pieces, (out, left) = refs[:-2], refs[-2:]
-    n_col, share = left.shape[1:3]
+    for n, c in enumerate(columns):
+        ref[:, c, at] = values[:, n * cols : (n + 1) * cols].reshape(n_line, rows, cols)
+
+
+def product_kernel(n_chip, n_core, after, *refs):
+    pieces, crossed, (out, own, other) = refs[: n_core + n_chip - 1], refs[-3 - n_chip : -3], refs[-3:]
+    n_col, share = other.shape[1:3]
     for number, piece in received(pieces, n_chip):
-        left[number // n_col, number % n_col] = piece
+        own[number // n_col, number % n_col] = piece
+    for m, n, number in sources(n_chip, n_core):
+        other[number // n_col, number % n_col] = crossed[n][m]
     for h in range(share):
-        values = dot(channel_matrix(left, h), channel_matrix(right, h), ((1,), (1,)))
-        put_channel(out, h, values)
+        left = channel_matrix(own, h)
+        for which, right in enumerate((channel_matrix(own, share + h), channel_matrix(other, h))):
+            put_channel(out, h, dot(left, right, ((1,), (1,))), half_columns(out, which))
 
 
 def middle_kernel(product, dxh, out, xhat):
@@ -334,30 +323,23 @@
     wait(start(out_sems, [(update, update_h), (dzg, dzg_h)]))
 
 
-def grad_right_kernel(grad, left, out_h, ready, sems):
-    lead = (slice(None),) * (len(ready.shape) - 3)
-    leaving = []
-    for h in range(ready.shape[-3]):
-        values = dot(channel_matrix(grad, h), channel_matrix(left, h), ((0,), (0,)))
-        put_channel(ready, h, values)
-        part = (*lead, pl.ds(h, 1))
-        copy = pltpu.make_async_copy(ready.at[part], out_h.at[part], sems.at[h])
-        copy.start()
-        leaving.append(copy)
-    wait(leaving)
-
-
-def grad_left_kernel(grad, right, *refs):
-    outs, ready = refs[:-1], refs[-1]
-    n_col, share = ready.shape[1:3]
+def grads_kernel(n_out, grad, own, other, *refs):
+    outs, ready = refs[:n_out], refs[n_out]
+    n_col, share = other.shape[1:3]
+    everywhere = range(n_col)
     for h in range(share):
-        put_channel(ready, h, dot(channel_matrix(grad, h), channel_matrix(right, h)))
-    for m, n, number in sources(outs[0].shape[0], len(outs)):
+        left, right = channel_matrix(own, h), channel_matrix(own, share + h)
+        here, there = half_matrix(grad, h, 0), half_matrix(grad, h, 1)
+        back = dot(here, right) + dot(there, channel_matrix(other, h))
+        put_channel(ready, h, back, everywhere)
+        put_channel(ready, share + h, dot(here, left, ((0,), (0,))), everywhere)
+        put_channel(ready, 2 * share + h, dot(there, left, ((0,), (0,))), everywhere)
+    for m, n, number in sources(outs[0].shape[0], n_out):
         outs[m][n] = ready[number // n_col, number % n_col]
 
 
-def back_kernel(n_chip, grads, coef_h, zhat_h, inv_h, dzg_h, gain_h, proj_h, *refs):
-    pieces, out_h = refs[:-15], refs[-15]
+def back_kernel(n_chip, n_core, coef_h, zhat_h, inv_h, dzg_h, gain_h, proj_h, *refs):
+    pieces, crossed, out_h = refs[: n_core + n_chip - 1], refs[-15 - n_chip : -15], refs[-15]
     (
         coef, zhat, inv, dzg, gain, proj_weight, out, left, right,
         sems, coef_sems, zhat_sems, dzg_sems, out_sems,
@@ -378,15 +360,15 @@
         ]
         for copy in blocks[at]:
             copy.start()
-    arrived = received(pieces, n_chip)
-    length = left.shape[0] // len(arrived)
-    for number, piece in arrived:
-        first = pl.multiple_of(number * length, length)
-        left[pl.ds(first, length), :] = piece.astype(F32).reshape(length, cols)
-    total = grads[0].astype(F32)
-    for half in range(1, grads.shape[0]):
-        total = total + grads[half].astype(F32)
-    right[...] = total.reshape(right.shape)
+    share = crossed[0].shape[1]
+    length = share * rows
+    got = {(m, n): ref[m] for n, ref in enumerate(crossed) for m in range(n_core)}
+    places = sources(n_chip, n_core)
+    for (number, piece), (m, n, _) in zip(received(pieces, n_chip), places):
+        part = pl.ds(pl.multiple_of(number * length, length), length)
+        left[part, :] = piece[:share].astype(F32).reshape(length, cols)
+        total = piece[share : 2 * share].astype(F32) + got[m, n].astype(F32)
+        right[part, :] = total.reshape(length, cols)
     wait(small)
     gain_b = jnp.concatenate([down_lanes(gain[...], cols)] * groups[0][1], axis=1)
     leaving = []
@@ -476,23 +458,24 @@
     def exchange(values):
         return lax.all_to_all(values, within, split_axis=0, concat_axis=0, tiled=True)
 
-    def exchange_all(values):
-        flat = values.reshape(n_half * n_place, share, rows, cols)
-        return lax.all_to_all(
-            flat, ("half", *within), split_axis=0, concat_axis=0, tiled=True
-        )
-
     def permute(values, axes, size, distance):
         return lax.ppermute(values, axes, [(at, at ^ distance) for at in range(size)])
 
-    def exchange_pieces(pieces):
+    def exchange_pieces(pieces, crossing):
         first = [pieces[0]]
         first += [permute(pieces[m], ("core",), n_core, m) for m in range(1, n_core)]
-        second = [
-            permute(jnp.stack([piece[n] for piece in first]), ("row", "col"), n_chip, n)
-            for n in range(n_chip - 1, 0, -1)
-        ]
-        return tuple(first + second[::-1])
+        inside, crossed = {}, {}
+        for n in range(n_chip - 1, -1, -1):
+            values = jnp.stack([piece[n, crossing : crossing + share] for piece in first])
+            crossed[n] = permute(values, ("half", "row", "col"), n_half * n_chip, n_chip + n)
+            if n > 0:
+                values = jnp.stack([piece[n, : 2 * share] for piece in first])
+                inside[n] = permute(values, ("row", "col"), n_chip, n)
+        return (
+            *first,
+            *[inside[n] for n in range(1, n_chip)],
+            *[crossed[n] for n in range(n_chip)],
+        )
 
     mask_s = pltpu.SMEM(mask.shape, jnp.int32)
     mask_v = vmem(*mask_row.shape, dtype=jnp.int32)
@@ -502,32 +485,17 @@
     wide = vmem(rows, width, cols, dtype=F32)
     square = vmem(width, hidden)
     proj_v = vmem(width, 4 * hidden)
-    pieces_shape = (shape(n_chip, share, rows, cols),) * n_core
-    n_pieces = n_core + n_chip - 1
-
-    def front(part, outs, scratch, near):
-        return call(
-            functools.partial(front_kernel, part, len(outs)),
-            outs,
-            [
-                block, mask_s, mask_v, vector, vector, vmem(width, 2 * hidden),
-                vmem(width, cells), plane, sems(6), *scratch,
-            ],
-            (pair, mask, mask_row, gain_in, bias_in, proj_weight),
-            outs_near=near,
-            flops=2 * cells * width * 3 * hidden,
-            moved=5 * cells * width,
-        )
-
-    everywhere = vmem(n_place, share, rows, cols)
-    (right,) = front(
-        2,
-        (shape(n_half, n_place, share, rows, cols),),
-        [everywhere, pltpu.SemaphoreType.DMA((n_half, math.gcd(n_place, 4)))],
-        (),
-    )
-    right = exchange_all(right).reshape(n_half, n_line, n_col, share, rows, cols)
-    left = exchange_pieces(tuple(front(0, pieces_shape, [], range(n_core))))
+    n_pieces = n_core + 2 * n_chip - 1
+    pieces = call(
+        functools.partial(front_kernel, n_core),
+        (shape(n_chip, 2 * share, rows, cols),) * n_core,
+        [block, mask_s, mask_v, vector, vector, proj_v, plane, plane, sems(6)],
+        (pair, mask, mask_row, gain_in, bias_in, proj_weight),
+        outs_near=range(n_core),
+        flops=2 * cells * width * 5 * hidden,
+        moved=6 * cells * width,
+    )
+    arrived = exchange_pieces(pieces, share)
     zhat, inv, gate, dxh = call(
         side_kernel,
         (
@@ -556,13 +524,17 @@
         flops=2 * cells * width * 5 * hidden,
         moved=16 * cells * width,
     )
-    product, left = call(
-        functools.partial(product_kernel, n_chip),
-        (shape(n_line, n_col, share, rows, cols), shape(n_line, n_col, share, rows, cols)),
+    product, own, other = call(
+        functools.partial(product_kernel, n_chip, n_core),
+        (
+            shape(n_line, n_col, share, rows, cols),
+            shape(n_line, n_col, 2 * share, rows, cols),
+            shape(n_line, n_col, share, rows, cols),
+        ),
         [],
-        (right, coef, *left),
-        near=(0, *range(2, 2 + n_pieces)),
-        outs_near=(0, 1),
+        (coef, *arrived),
+        near=range(1, 1 + n_pieces),
+        outs_near=range(3),
         flops=2 * share * n_half * (n_line * rows) ** 2 * n_col * cols,
         moved=8 * cells * hidden,
     )
@@ -579,46 +551,36 @@
     )
     grad = exchange(grad.reshape(n_place, share, rows, cols))
     grad = grad.reshape(n_line, n_col, share, rows, cols)
-    (sent,) = call(
-        grad_right_kernel,
-        (shape(n_half, n_line, n_col, share, rows, cols),),
-        [vmem(n_half, n_line, n_col, share, rows, cols), sems(share)],
-        (grad, left),
-        near=(0, 1),
-        flops=2 * share * n_half * (n_line * rows) ** 2 * n_col * cols,
-        moved=8 * cells * hidden,
-    )
-    grad_right = exchange_all(sent).reshape(n_half, n_place, share, rows, cols)
-    grad_left = call(
-        grad_left_kernel,
-        pieces_shape,
-        [vmem(n_line, n_col, share, rows, cols)],
-        (grad, right),
-        near=(0, 1),
+    pieces = call(
+        functools.partial(grads_kernel, n_core),
+        (shape(n_chip, 3 * share, rows, cols),) * n_core,
+        [vmem(n_line, n_col, 3 * share, rows, cols)],
+        (grad, own, other),
+        near=range(3),
         outs_near=range(n_core),
-        flops=2 * share * n_half * (n_line * rows) ** 2 * n_col * cols,
-        moved=8 * cells * hidden,
-    )
-    grad_left = exchange_pieces(tuple(grad_left))
+        flops=4 * share * n_half * (n_line * rows) ** 2 * n_col * cols,
+        moved=12 * cells * hidden,
+    )
+    arrived = exchange_pieces(pieces, 2 * share)
     update, dzg = call(
         update_kernel,
         (shape(rows, cols, width), shape(rows, width, cols, dtype=F32)),
         [wide, block, vector, vector, square, square, block, wide, plane, sems(6), sems(2)],
-        (product, gate, cotangent, norm_gain, norm_bias, out_weight, gate_weight, sent),
-        near=(0,),
+        (product, gate, cotangent, norm_gain, norm_bias, out_weight, gate_weight, pieces[0]),
+        near=(0, 7),
         flops=2 * cells * width * 3 * hidden,
         moved=14 * cells * hidden,
     )
     (grad_pair,) = call(
-        functools.partial(back_kernel, n_chip),
+        functools.partial(back_kernel, n_chip, n_core),
         (shape(rows, cols, width),),
         [
             vmem(rows, 4, hidden, cols), wide, vmem(rows, cols, dtype=F32), wide,
             vector, proj_v, block, plane, plane,
             sems(3), sems(2), sems(2), sems(2), sems(2),
         ],
-        (grad_right, coef, zhat, inv, dzg, gain_in, proj_weight, *grad_left),
-        near=(0, *range(7, 7 + n_pieces)),
+        (coef, zhat, inv, dzg, gain_in, proj_weight, *arrived),
+        near=range(6, 6 + n_pieces),
         flops=2 * cells * width * 5 * hidden,
         moved=30 * cells * width,
     )

time: 101 us -> 125 us (1.24)
  starting transfers between devices: 29.2 us -> 52.5 us
  Pallas kernels: 25.3 us -> 22.5 us
  waiting for transfers between devices: 19.5 us -> 21.9 us
    ppermute x16 -> x32, starting transfers between devices: 18.2 us -> 52.5 us  [permute(): lax.ppermute(values, axes, [(at, at ^ distance) for at in range(size)])]
    all_to_all x2 -> x0, starting transfers between devices: 10.9 us -> none  [exchange_all(): lax.all_to_all(flat, ('half', *within), split_axis=0, concat_axis=0, tile...]
    pallas_call x10 -> x8, Pallas kernels: 25.3 us -> 22.5 us  [call(): pl.pallas_call(kernel, out_shape=[out if at in outs_near else pltpu.HBM(o...]
    ppermute x16 -> x32, waiting for transfers between devices: 19.5 us -> 21.9 us  [permute(): lax.ppermute(values, axes, [(at, at ^ distance) for at in range(size)])]
  transfers between devices with their start and end apart: 18 -> 32, of which waited for: 12 -> 12; matrix products, arithmetic and copies ran while one was open for 0% -> 0% of each run, Pallas kernels for 15% -> 10%
where the time goes in v11:
time: 125 us; the launch traced here: 124 us
  starting transfers between devices  52.5 us (42%)
  blocking collectives  25.8 us (21%)
  Pallas kernels  22.5 us (18%)
  waiting for transfers between devices  21.9 us (18%)
    ppermute x32, starting transfers between devices, permute(): lax.ppermute(values, axes, [(at, at ^ distance) for at in range(size)])  52.5 us
    all_to_all x2, blocking collectives, exchange(): lax.all_to_all(values, within, split_axis=0, concat_axis=0, tiled=True)  25.8 us
    pallas_call x8, Pallas kernels, call(): pl.pallas_call(kernel, out_shape=[out if at in outs_near else pltpu.HBM(o...  22.5 us
    ppermute x32, waiting for transfers between devices, permute(): lax.ppermute(values, axes, [(at, at ^ distance) for at in range(size)])  21.9 us
  transfers between devices with their start and end apart: 32, of which 12 were waited for; matrix products, arithmetic and copies ran while one was open for 0% of the time, Pallas kernels for 10%

profile of v11, /device:TPU:0, one launch (start us, length us, event | category | flops | bytes accessed | tf_op | source)
XLA Modules:
  0.0 124.4 jit_solution(9615285782584072061)
XLA Ops:
  0.6 3.4 %shard_map.115 = (bf16[8,16,16,128]{3,2,1,0:T(8,128)(2,1)S(1)}, bf16[8,16,16,128]{3,2,1,0:T(8,128)(2,1)S(1)}) custom-call(bf16[16,128,128]{2,1,0:T(8,128)(2,1)} %pair_h.3, s32[256]{0:T(256)} %mask_h.3, s32[1,256]{1,0:T(1,128)} %bitcast.20, f32[1,128]{1,0:T(1,128)} %bitcast.16, f32[1,128]{1,0:T(1,128)} %bitcast.22, bf16[128,512]{1,0:T(8,128)(2,1)} %proj_h.5), custom_call_target="tpu_custom_call" | custom-call | flops 335544320 | bytes 1572864 | tf_op jit(solution)/shard_map/pallas_call | solution.py:409
  6.1 4.0 %collective-permute-start.8 = (bf16[2,8,16,128]{3,2,1,0:T(8,128)(2,1)S(1)}, bf16[2,8,16,128]{3,2,1,0:T(8,128)(2,1)S(1)}, u32[]{:S(2)}, u32[]{:S(2)}) collective-permute-start(bf16[2,8,16,128]{3,2,1,0:T(8,128)(2,1)S(1)} %pad_maximum_fusion.14), channel_id=1, source_target_pairs={{0,16},{1,17},{4,20},{5,21},{8,24},{9,25},{12,28},{13,29},{16,0},{... | collective-permute-start | bytes 196616 | tf_op jit(solution)/shard_map/ppermute | solution.py:462
  11.5 3.6 %collective-permute-start.10 = (bf16[2,8,16,128]{3,2,1,0:T(8,128)(2,1)S(1)}, bf16[2,8,16,128]{3,2,1,0:T(8,128)(2,1)S(1)}, u32[]{:S(2)}, u32[]{:S(2)}) collective-permute-start(bf16[2,8,16,128]{3,2,1,0:T(8,128)(2,1)S(1)} %pad_maximum_fusion.16), channel_id=1, source_target_pairs={{0,20},{1,21},{4,16},{5,17},{8,28},{9,29},{12,24},{13,25},{16,4},{... | collective-permute-start | bytes 196616 | tf_op jit(solution)/shard_map/ppermute | solution.py:462
  15.2 3.9 %collective-permute-start.12 = (bf16[2,8,16,128]{3,2,1,0:T(8,128)(2,1)S(1)}, bf16[2,8,16,128]{3,2,1,0:T(8,128)(2,1)S(1)}, u32[]{:S(2)}, u32[]{:S(2)}) collective-permute-start(bf16[2,8,16,128]{3,2,1,0:T(8,128)(2,1)S(1)} %pad_maximum_fusion.18), channel_id=1, source_target_pairs={{0,24},{1,25},{4,28},{5,29},{8,16},{9,17},{12,20},{13,21},{16,8},{... | collective-permute-start | bytes 196616 | tf_op jit(solution)/shard_map/ppermute | solution.py:462
  22.4 2.7 %collective-permute-done.10.refs_11_ = bf16[2,8,16,128]{3,2,1,0:T(8,128)(2,1)S(1)} collective-permute-done((bf16[2,8,16,128]{3,2,1,0:T(8,128)(2,1)S(1)}, bf16[2,8,16,128]{3,2,1,0:T(8,128)(2,1)S(1)}, u32[]{:S(2)}, u32[]{:S(2)}) %collective-permute-start.10) | collective-permute-done | bytes 65568 | tf_op jit(solution)/shard_map/ppermute | solution.py:462
  25.0 2.9 %collective-permute-start.13 = (bf16[2,8,16,128]{3,2,1,0:T(8,128)(2,1)S(1)}, bf16[2,8,16,128]{3,2,1,0:T(8,128)(2,1)S(1)}, u32[]{:S(2)}, u32[]{:S(2)}) collective-permute-start(bf16[2,8,16,128]{3,2,1,0:T(8,128)(2,1)S(1)} %pad_maximum_fusion.19), channel_id=1, source_target_pairs={{0,25},{1,24},{4,29},{5,28},{8,17},{9,16},{12,21},{13,20},{16,9},{... | collective-permute-start | bytes 196616 | tf_op jit(solution)/shard_map/ppermute | solution.py:462
  29.3 3.3 %collective-permute-start.15 = (bf16[2,8,16,128]{3,2,1,0:T(8,128)(2,1)S(1)}, bf16[2,8,16,128]{3,2,1,0:T(8,128)(2,1)S(1)}, u32[]{:S(2)}, u32[]{:S(2)}) collective-permute-start(bf16[2,8,16,128]{3,2,1,0:T(8,128)(2,1)S(1)} %pad_maximum_fusion.21), channel_id=1, source_target_pairs={{0,29},{1,28},{4,25},{5,24},{8,21},{9,20},{12,17},{13,16},{16,13},... | collective-permute-start | bytes 196616 | tf_op jit(solution)/shard_map/ppermute | solution.py:462
  35.8 2.2 %collective-permute-done.15.refs_16_ = bf16[2,8,16,128]{3,2,1,0:T(8,128)(2,1)S(1)} collective-permute-done((bf16[2,8,16,128]{3,2,1,0:T(8,128)(2,1)S(1)}, bf16[2,8,16,128]{3,2,1,0:T(8,128)(2,1)S(1)}, u32[]{:S(2)}, u32[]{:S(2)}) %collective-permute-start.15) | collective-permute-done | bytes 65568 | tf_op jit(solution)/shard_map/ppermute | solution.py:462
  38.0 3.3 %collective-permute-start.6 = (bf16[2,16,16,128]{3,2,1,0:T(8,128)(2,1)S(1)}, bf16[2,16,16,128]{3,2,1,0:T(8,128)(2,1)S(1)}, u32[]{:S(2)}, u32[]{:S(2)}) collective-permute-start(bf16[2,16,16,128]{3,2,1,0:T(8,128)(2,1)S(1)} %pad_maximum_fusion.5), channel_id=1, source_target_pairs={{0,12},{1,13},{4,8},{5,9},{8,4},{9,5},{12,0},{13,1},{2,14},{3,15},... | collective-permute-start | bytes 393224 | tf_op jit(solution)/shard_map/ppermute | solution.py:462
  41.6 4.6 %shard_map.113 = (f32[16,128,128]{2,1,0:T(8,128)}, f32[16,128]{1,0:T(8,128)}, f32[16,128,128]{2,1,0:T(8,128)}, f32[2048,128]{1,0:T(8,128)S(1)}) custom-call(bf16[16,128,128]{2,1,0:T(8,128)(2,1)} %pair_h.3, bf16[16,128,128]{2,1,0:T(8,128)(2,1)} %cot_h.3, f32[1,128]{1,0:T(1,128)} %bitcast.17, f32[1,128]{1,0:T(1,128)} %bitcast.23, bf16[128,128]{1,0:T(8,128)(2,1)} %gate_w_h.1, ...), custom_call_target="tpu_custom_call" | custom-call | flops 268435456 | bytes 4194304 | tf_op jit(solution)/shard_map/pallas_call | solution.py:409
  46.2 3.2 %shard_map.114.after.coef_h = bf16[16,4,128,128]{3,2,1,0:T(8,128)(2,1)} custom-call(f32[16,128,128]{2,1,0:T(8,128)} %get-tuple-element.15.zhat_h, s32[256]{0:T(256)} %mask_h.3, s32[1,256]{1,0:T(1,128)} %bitcast.21, f32[1,128]{1,0:T(1,128)} %bitcast.18, f32[1,128]{1,0:T(1,128)} %bitcast.24, bf16[128,512]{1,0:T(8,128)(2,1)} %proj_h.5), custom_call_target="tpu_custom_call" | custom-call | flops 335544320 | bytes 4194304 | tf_op jit(solution)/shard_map/pallas_call | solution.py:409
  50.2 13.8 %all_to_all.10 = bf16[16,8,16,128]{3,2,1,0:T(8,128)(2,1)S(1)} all-to-all(bf16[16,8,16,128]{3,2,1,0:T(8,128)(2,1)S(1)} %bitcast.15), channel_id=1, replica_groups=mesh['grp'=1,'half'=2,'row'=4,'core'=2,'col'=2] {'row','core','col'}, dimensions={0} | all-to-all | bytes 1048576 | tf_op jit(solution)/shard_map/all_to_all | solution.py:459
  64.5 12.0 %all_to_all.11 = bf16[16,8,16,128]{3,2,1,0:T(8,128)(2,1)S(1)} all-to-all(bf16[16,8,16,128]{3,2,1,0:T(8,128)(2,1)S(1)} %bitcast.13), channel_id=1, replica_groups=mesh['grp'=1,'half'=2,'row'=4,'core'=2,'col'=2] {'row','core','col'}, dimensions={0} | all-to-all | bytes 1048576 | tf_op jit(solution)/shard_map/all_to_all | solution.py:459
  77.7 2.0 %collective-permute-done.16.refs_1_ = bf16[8,24,16,128]{3,2,1,0:T(8,128)(2,1)S(1)} collective-permute-done((bf16[8,24,16,128]{3,2,1,0:T(8,128)(2,1)S(1)}, bf16[8,24,16,128]{3,2,1,0:T(8,128)(2,1)S(1)}, u32[]{:S(2)}, u32[]{:S(2)}) %collective-permute-start.16) | collective-permute-done | bytes 786464 | tf_op jit(solution)/shard_map/ppermute | solution.py:462
  80.8 2.9 %collective-permute-start.25 = (bf16[2,8,16,128]{3,2,1,0:T(8,128)(2,1)S(1)}, bf16[2,8,16,128]{3,2,1,0:T(8,128)(2,1)S(1)}, u32[]{:S(2)}, u32[]{:S(2)}) collective-permute-start(bf16[2,8,16,128]{3,2,1,0:T(8,128)(2,1)S(1)} %pad_maximum_fusion.23), channel_id=1, source_target_pairs={{0,17},{1,16},{4,21},{5,20},{8,25},{9,24},{12,29},{13,28},{16,1},{... | collective-permute-start | bytes 196616 | tf_op jit(solution)/shard_map/ppermute | solution.py:462
  84.9 2.8 %collective-permute-start.27 = (bf16[2,8,16,128]{3,2,1,0:T(8,128)(2,1)S(1)}, bf16[2,8,16,128]{3,2,1,0:T(8,128)(2,1)S(1)}, u32[]{:S(2)}, u32[]{:S(2)}) collective-permute-start(bf16[2,8,16,128]{3,2,1,0:T(8,128)(2,1)S(1)} %pad_maximum_fusion.25), channel_id=1, source_target_pairs={{0,21},{1,20},{4,17},{5,16},{8,29},{9,28},{12,25},{13,24},{16,5},{... | collective-permute-start | bytes 196616 | tf_op jit(solution)/shard_map/ppermute | solution.py:462
  91.5 2.2 %collective-permute-done.25.refs_10_ = bf16[2,8,16,128]{3,2,1,0:T(8,128)(2,1)S(1)} collective-permute-done((bf16[2,8,16,128]{3,2,1,0:T(8,128)(2,1)S(1)}, bf16[2,8,16,128]{3,2,1,0:T(8,128)(2,1)S(1)}, u32[]{:S(2)}, u32[]{:S(2)}) %collective-permute-start.25) | collective-permute-done | bytes 65568 | tf_op jit(solution)/shard_map/ppermute | solution.py:462
  95.9 1.7 %collective-permute-start.29 = (bf16[2,8,16,128]{3,2,1,0:T(8,128)(2,1)S(1)}, bf16[2,8,16,128]{3,2,1,0:T(8,128)(2,1)S(1)}, u32[]{:S(2)}, u32[]{:S(2)}) collective-permute-start(bf16[2,8,16,128]{3,2,1,0:T(8,128)(2,1)S(1)} %pad_maximum_fusion.27), channel_id=1, source_target_pairs={{0,25},{1,24},{4,29},{5,28},{8,17},{9,16},{12,21},{13,20},{16,9},{... | collective-permute-start | bytes 196616 | tf_op jit(solution)/shard_map/ppermute | solution.py:462
  97.6 3.0 %collective-permute-start.30 = (bf16[2,8,16,128]{3,2,1,0:T(8,128)(2,1)S(1)}, bf16[2,8,16,128]{3,2,1,0:T(8,128)(2,1)S(1)}, u32[]{:S(2)}, u32[]{:S(2)}) collective-permute-start(bf16[2,8,16,128]{3,2,1,0:T(8,128)(2,1)S(1)} %pad_maximum_fusion.28), channel_id=1, source_target_pairs={{0,28},{1,29},{4,24},{5,25},{8,20},{9,21},{12,16},{13,17},{16,12},... | collective-permute-start | bytes 196616 | tf_op jit(solution)/shard_map/ppermute | solution.py:462
  100.6 2.7 %collective-permute-start.31 = (bf16[2,8,16,128]{3,2,1,0:T(8,128)(2,1)S(1)}, bf16[2,8,16,128]{3,2,1,0:T(8,128)(2,1)S(1)}, u32[]{:S(2)}, u32[]{:S(2)}) collective-permute-start(bf16[2,8,16,128]{3,2,1,0:T(8,128)(2,1)S(1)} %pad_maximum_fusion.29), channel_id=1, source_target_pairs={{0,29},{1,28},{4,25},{5,24},{8,21},{9,20},{12,17},{13,16},{16,13},... | collective-permute-start | bytes 196616 | tf_op jit(solution)/shard_map/ppermute | solution.py:462
  104.8 4.3 %collective-permute-done.31.refs_16_ = bf16[2,8,16,128]{3,2,1,0:T(8,128)(2,1)S(1)} collective-permute-done((bf16[2,8,16,128]{3,2,1,0:T(8,128)(2,1)S(1)}, bf16[2,8,16,128]{3,2,1,0:T(8,128)(2,1)S(1)}, u32[]{:S(2)}, u32[]{:S(2)}) %collective-permute-start.31) | collective-permute-done | bytes 65568 | tf_op jit(solution)/shard_map/ppermute | solution.py:462
  109.1 3.0 %collective-permute-start.22 = (bf16[2,16,16,128]{3,2,1,0:T(8,128)(2,1)S(1)}, bf16[2,16,16,128]{3,2,1,0:T(8,128)(2,1)S(1)}, u32[]{:S(2)}, u32[]{:S(2)}) collective-permute-start(bf16[2,16,16,128]{3,2,1,0:T(8,128)(2,1)S(1)} %pad_maximum_fusion.12), channel_id=1, source_target_pairs={{0,12},{1,13},{4,8},{5,9},{8,4},{9,5},{12,0},{13,1},{2,14},{3,15},... | collective-permute-start | bytes 393224 | tf_op jit(solution)/shard_map/ppermute | solution.py:462
  112.1 4.1 %shard_map.119 = (bf16[16,128,128]{2,1,0:T(8,128)(2,1)}, f32[16,128,128]{2,1,0:T(8,128)}) custom-call(bf16[128,16,128]{2,1,0:T(8,128)(2,1)S(1)} %bitcast.11, f32[16,128,128]{2,1,0:T(8,128)} %get-tuple-element.19.gate_h, bf16[16,128,128]{2,1,0:T(8,128)(2,1)} %cot_h.3, f32[1,128]{1,0:T(1,128)} %bitcast.26, f32[1,128]{1,0:T(1,128)} %bitcast.27, ...), custom_call_target="tpu_custom_call" | custom-call | flops 201326592 | bytes 3670016 | tf_op jit(solution)/shard_map/pallas_call | solution.py:409
  119.1 5.1 %shard_map.120 = bf16[16,128,128]{2,1,0:T(8,128)(2,1)} custom-call(bf16[16,4,128,128]{3,2,1,0:T(8,128)(2,1)} %shard_map.114.after.coef_h, f32[16,128,128]{2,1,0:T(8,128)} %get-tuple-element.15.zhat_h, f32[16,128]{1,0:T(8,128)} %get-tuple-element.25.inv_h, f32[16,128,128]{2,1,0:T(8,128)} %get-tuple-element.26.dzg_h, f32[1,128]{1,0:T(1,128)} %bitcast.19, ...), custom_call_target="tpu_custom_call" | custom-call | flops 335544320 | bytes 7864320 | tf_op jit(solution)/shard_map/pallas_call | solution.py:409
  (88 shorter events, 26.7 us)
Async XLA Ops:
  6.1 13.2 %collective-permute-start.8 = (bf16[2,8,16,128]{3,2,1,0:T(8,128)(2,1)S(1)}, bf16[2,8,16,128]{3,2,1,0:T(8,128)(2,1)S(1)}, u32[]{:S(2)}, u32[]{:S(2)}) collective-permute-start(bf16[2,8,16,128]{3,2,1,0:T(8,128)(2,1)S(1)} %pad_maximum_fusion.14), channel_id=1, source_target_pairs={{0,16},{1,17},{4,20},{5,21},{8,24},{9,25},{12,28},{13,29},{16,0},{... | collective-permute-start | bytes 196616 | tf_op jit(solution)/shard_map/ppermute | solution.py:462
  10.1 10.7 %collective-permute-start.9 = (bf16[2,8,16,128]{3,2,1,0:T(8,128)(2,1)S(1)}, bf16[2,8,16,128]{3,2,1,0:T(8,128)(2,1)S(1)}, u32[]{:S(2)}, u32[]{:S(2)}) collective-permute-start(bf16[2,8,16,128]{3,2,1,0:T(8,128)(2,1)S(1)} %pad_maximum_fusion.15), channel_id=1, source_target_pairs={{0,17},{1,16},{4,21},{5,20},{8,25},{9,24},{12,29},{13,28},{16,1},{... | collective-permute-start | bytes 196616 | tf_op jit(solution)/shard_map/ppermute | solution.py:462
  11.5 13.6 %collective-permute-start.10 = (bf16[2,8,16,128]{3,2,1,0:T(8,128)(2,1)S(1)}, bf16[2,8,16,128]{3,2,1,0:T(8,128)(2,1)S(1)}, u32[]{:S(2)}, u32[]{:S(2)}) collective-permute-start(bf16[2,8,16,128]{3,2,1,0:T(8,128)(2,1)S(1)} %pad_maximum_fusion.16), channel_id=1, source_target_pairs={{0,20},{1,21},{4,16},{5,17},{8,28},{9,29},{12,24},{13,25},{16,4},{... | collective-permute-start | bytes 196616 | tf_op jit(solution)/shard_map/ppermute | solution.py:462
  15.1 12.9 %collective-permute-start.11 = (bf16[2,8,16,128]{3,2,1,0:T(8,128)(2,1)S(1)}, bf16[2,8,16,128]{3,2,1,0:T(8,128)(2,1)S(1)}, u32[]{:S(2)}, u32[]{:S(2)}) collective-permute-start(bf16[2,8,16,128]{3,2,1,0:T(8,128)(2,1)S(1)} %pad_maximum_fusion.17), channel_id=1, source_target_pairs={{0,21},{1,20},{4,17},{5,16},{8,29},{9,28},{12,25},{13,24},{16,5},{... | collective-permute-start | bytes 196616 | tf_op jit(solution)/shard_map/ppermute | solution.py:462
  15.2 14.2 %collective-permute-start.12 = (bf16[2,8,16,128]{3,2,1,0:T(8,128)(2,1)S(1)}, bf16[2,8,16,128]{3,2,1,0:T(8,128)(2,1)S(1)}, u32[]{:S(2)}, u32[]{:S(2)}) collective-permute-start(bf16[2,8,16,128]{3,2,1,0:T(8,128)(2,1)S(1)} %pad_maximum_fusion.18), channel_id=1, source_target_pairs={{0,24},{1,25},{4,28},{5,29},{8,16},{9,17},{12,20},{13,21},{16,8},{... | collective-permute-start | bytes 196616 | tf_op jit(solution)/shard_map/ppermute | solution.py:462
  19.3 18.7 %collective-permute-start.1 = (bf16[2,16,16,128]{3,2,1,0:T(8,128)(2,1)S(1)}, bf16[2,16,16,128]{3,2,1,0:T(8,128)(2,1)S(1)}, u32[]{:S(2)}, u32[]{:S(2)}) collective-permute-start(bf16[2,16,16,128]{3,2,1,0:T(8,128)(2,1)S(1)} %pad_maximum_fusion), channel_id=1, source_target_pairs={{0,1},{1,0},{4,5},{5,4},{8,9},{9,8},{12,13},{13,12},{2,3},{3,2},{6... | collective-permute-start | bytes 393224 | tf_op jit(solution)/shard_map/ppermute | solution.py:462
  20.8 20.4 %collective-permute-start.2 = (bf16[2,16,16,128]{3,2,1,0:T(8,128)(2,1)S(1)}, bf16[2,16,16,128]{3,2,1,0:T(8,128)(2,1)S(1)}, u32[]{:S(2)}, u32[]{:S(2)}) collective-permute-start(bf16[2,16,16,128]{3,2,1,0:T(8,128)(2,1)S(1)} %pad_maximum_fusion.1), channel_id=1, source_target_pairs={{0,4},{1,5},{4,0},{5,1},{8,12},{9,13},{12,8},{13,9},{2,6},{3,7},{6... | collective-permute-start | bytes 393224 | tf_op jit(solution)/shard_map/ppermute | solution.py:462
  29.3 8.6 %collective-permute-start.15 = (bf16[2,8,16,128]{3,2,1,0:T(8,128)(2,1)S(1)}, bf16[2,8,16,128]{3,2,1,0:T(8,128)(2,1)S(1)}, u32[]{:S(2)}, u32[]{:S(2)}) collective-permute-start(bf16[2,8,16,128]{3,2,1,0:T(8,128)(2,1)S(1)} %pad_maximum_fusion.21), channel_id=1, source_target_pairs={{0,29},{1,28},{4,25},{5,24},{8,21},{9,20},{12,17},{13,16},{16,13},... | collective-permute-start | bytes 196616 | tf_op jit(solution)/shard_map/ppermute | solution.py:462
  32.6 16.8 %collective-permute-start.3 = (bf16[2,16,16,128]{3,2,1,0:T(8,128)(2,1)S(1)}, bf16[2,16,16,128]{3,2,1,0:T(8,128)(2,1)S(1)}, u32[]{:S(2)}, u32[]{:S(2)}) collective-permute-start(bf16[2,16,16,128]{3,2,1,0:T(8,128)(2,1)S(1)} %pad_maximum_fusion.2), channel_id=1, source_target_pairs={{0,5},{1,4},{4,1},{5,0},{8,13},{9,12},{12,9},{13,8},{2,7},{3,6},{6... | collective-permute-start | bytes 393224 | tf_op jit(solution)/shard_map/ppermute | solution.py:462
  35.8 13.7 %collective-permute-start.4 = (bf16[2,16,16,128]{3,2,1,0:T(8,128)(2,1)S(1)}, bf16[2,16,16,128]{3,2,1,0:T(8,128)(2,1)S(1)}, u32[]{:S(2)}, u32[]{:S(2)}) collective-permute-start(bf16[2,16,16,128]{3,2,1,0:T(8,128)(2,1)S(1)} %pad_maximum_fusion.3), channel_id=1, source_target_pairs={{0,8},{1,9},{4,12},{5,13},{8,0},{9,1},{12,4},{13,5},{2,10},{3,11},... | collective-permute-start | bytes 393224 | tf_op jit(solution)/shard_map/ppermute | solution.py:462
  38.0 11.5 %collective-permute-start.5 = (bf16[2,16,16,128]{3,2,1,0:T(8,128)(2,1)S(1)}, bf16[2,16,16,128]{3,2,1,0:T(8,128)(2,1)S(1)}, u32[]{:S(2)}, u32[]{:S(2)}) collective-permute-start(bf16[2,16,16,128]{3,2,1,0:T(8,128)(2,1)S(1)} %pad_maximum_fusion.4), channel_id=1, source_target_pairs={{0,9},{1,8},{4,13},{5,12},{8,1},{9,0},{12,5},{13,4},{2,11},{3,10},... | collective-permute-start | bytes 393224 | tf_op jit(solution)/shard_map/ppermute | solution.py:462
  38.0 11.5 %collective-permute-start.6 = (bf16[2,16,16,128]{3,2,1,0:T(8,128)(2,1)S(1)}, bf16[2,16,16,128]{3,2,1,0:T(8,128)(2,1)S(1)}, u32[]{:S(2)}, u32[]{:S(2)}) collective-permute-start(bf16[2,16,16,128]{3,2,1,0:T(8,128)(2,1)S(1)} %pad_maximum_fusion.5), channel_id=1, source_target_pairs={{0,12},{1,13},{4,8},{5,9},{8,4},{9,5},{12,0},{13,1},{2,14},{3,15},... | collective-permute-start | bytes 393224 | tf_op jit(solution)/shard_map/ppermute | solution.py:462
  41.3 8.2 %collective-permute-start.7 = (bf16[2,16,16,128]{3,2,1,0:T(8,128)(2,1)S(1)}, bf16[2,16,16,128]{3,2,1,0:T(8,128)(2,1)S(1)}, u32[]{:S(2)}, u32[]{:S(2)}) collective-permute-start(bf16[2,16,16,128]{3,2,1,0:T(8,128)(2,1)S(1)} %pad_maximum_fusion.6), channel_id=1, source_target_pairs={{0,13},{1,12},{4,9},{5,8},{8,5},{9,4},{12,1},{13,0},{2,15},{3,14},... | collective-permute-start | bytes 393224 | tf_op jit(solution)/shard_map/ppermute | solution.py:462
  79.7 10.3 %collective-permute-start.24 = (bf16[2,8,16,128]{3,2,1,0:T(8,128)(2,1)S(1)}, bf16[2,8,16,128]{3,2,1,0:T(8,128)(2,1)S(1)}, u32[]{:S(2)}, u32[]{:S(2)}) collective-permute-start(bf16[2,8,16,128]{3,2,1,0:T(8,128)(2,1)S(1)} %pad_maximum_fusion.22), channel_id=1, source_target_pairs={{0,16},{1,17},{4,20},{5,21},{8,24},{9,25},{12,28},{13,29},{16,0},{... | collective-permute-start | bytes 196616 | tf_op jit(solution)/shard_map/ppermute | solution.py:462
  80.8 12.9 %collective-permute-start.25 = (bf16[2,8,16,128]{3,2,1,0:T(8,128)(2,1)S(1)}, bf16[2,8,16,128]{3,2,1,0:T(8,128)(2,1)S(1)}, u32[]{:S(2)}, u32[]{:S(2)}) collective-permute-start(bf16[2,8,16,128]{3,2,1,0:T(8,128)(2,1)S(1)} %pad_maximum_fusion.23), channel_id=1, source_target_pairs={{0,17},{1,16},{4,21},{5,20},{8,25},{9,24},{12,29},{13,28},{16,1},{... | collective-permute-start | bytes 196616 | tf_op jit(solution)/shard_map/ppermute | solution.py:462
  83.7 12.2 %collective-permute-start.26 = (bf16[2,8,16,128]{3,2,1,0:T(8,128)(2,1)S(1)}, bf16[2,8,16,128]{3,2,1,0:T(8,128)(2,1)S(1)}, u32[]{:S(2)}, u32[]{:S(2)}) collective-permute-start(bf16[2,8,16,128]{3,2,1,0:T(8,128)(2,1)S(1)} %pad_maximum_fusion.24), channel_id=1, source_target_pairs={{0,20},{1,21},{4,16},{5,17},{8,28},{9,29},{12,24},{13,25},{16,4},{... | collective-permute-start | bytes 196616 | tf_op jit(solution)/shard_map/ppermute | solution.py:462
  84.9 12.7 %collective-permute-start.27 = (bf16[2,8,16,128]{3,2,1,0:T(8,128)(2,1)S(1)}, bf16[2,8,16,128]{3,2,1,0:T(8,128)(2,1)S(1)}, u32[]{:S(2)}, u32[]{:S(2)}) collective-permute-start(bf16[2,8,16,128]{3,2,1,0:T(8,128)(2,1)S(1)} %pad_maximum_fusion.25), channel_id=1, source_target_pairs={{0,21},{1,20},{4,17},{5,16},{8,29},{9,28},{12,25},{13,24},{16,5},{... | collective-permute-start | bytes 196616 | tf_op jit(solution)/shard_map/ppermute | solution.py:462
  87.7 12.9 %collective-permute-start.28 = (bf16[2,8,16,128]{3,2,1,0:T(8,128)(2,1)S(1)}, bf16[2,8,16,128]{3,2,1,0:T(8,128)(2,1)S(1)}, u32[]{:S(2)}, u32[]{:S(2)}) collective-permute-start(bf16[2,8,16,128]{3,2,1,0:T(8,128)(2,1)S(1)} %pad_maximum_fusion.26), channel_id=1, source_target_pairs={{0,24},{1,25},{4,28},{5,29},{8,16},{9,17},{12,20},{13,21},{16,8},{... | collective-permute-start | bytes 196616 | tf_op jit(solution)/shard_map/ppermute | solution.py:462
  90.0 19.0 %collective-permute-start.17 = (bf16[2,16,16,128]{3,2,1,0:T(8,128)(2,1)S(1)}, bf16[2,16,16,128]{3,2,1,0:T(8,128)(2,1)S(1)}, u32[]{:S(2)}, u32[]{:S(2)}) collective-permute-start(bf16[2,16,16,128]{3,2,1,0:T(8,128)(2,1)S(1)} %pad_maximum_fusion.7), channel_id=1, source_target_pairs={{0,1},{1,0},{4,5},{5,4},{8,9},{9,8},{12,13},{13,12},{2,3},{3,2},{6... | collective-permute-start | bytes 393224 | tf_op jit(solution)/shard_map/ppermute | solution.py:462
  93.7 18.3 %collective-permute-start.18 = (bf16[2,16,16,128]{3,2,1,0:T(8,128)(2,1)S(1)}, bf16[2,16,16,128]{3,2,1,0:T(8,128)(2,1)S(1)}, u32[]{:S(2)}, u32[]{:S(2)}) collective-permute-start(bf16[2,16,16,128]{3,2,1,0:T(8,128)(2,1)S(1)} %pad_maximum_fusion.8), channel_id=1, source_target_pairs={{0,4},{1,5},{4,0},{5,1},{8,12},{9,13},{12,8},{13,9},{2,6},{3,7},{6... | collective-permute-start | bytes 393224 | tf_op jit(solution)/shard_map/ppermute | solution.py:462
  100.6 8.5 %collective-permute-start.31 = (bf16[2,8,16,128]{3,2,1,0:T(8,128)(2,1)S(1)}, bf16[2,8,16,128]{3,2,1,0:T(8,128)(2,1)S(1)}, u32[]{:S(2)}, u32[]{:S(2)}) collective-permute-start(bf16[2,8,16,128]{3,2,1,0:T(8,128)(2,1)S(1)} %pad_maximum_fusion.29), channel_id=1, source_target_pairs={{0,29},{1,28},{4,25},{5,24},{8,21},{9,20},{12,17},{13,16},{16,13},... | collective-permute-start | bytes 196616 | tf_op jit(solution)/shard_map/ppermute | solution.py:462
  103.3 13.0 %collective-permute-start.19 = (bf16[2,16,16,128]{3,2,1,0:T(8,128)(2,1)S(1)}, bf16[2,16,16,128]{3,2,1,0:T(8,128)(2,1)S(1)}, u32[]{:S(2)}, u32[]{:S(2)}) collective-permute-start(bf16[2,16,16,128]{3,2,1,0:T(8,128)(2,1)S(1)} %pad_maximum_fusion.9), channel_id=1, source_target_pairs={{0,5},{1,4},{4,1},{5,0},{8,13},{9,12},{12,9},{13,8},{2,7},{3,6},{6... | collective-permute-start | bytes 393224 | tf_op jit(solution)/shard_map/ppermute | solution.py:462
  104.8 11.5 %collective-permute-start.20 = (bf16[2,16,16,128]{3,2,1,0:T(8,128)(2,1)S(1)}, bf16[2,16,16,128]{3,2,1,0:T(8,128)(2,1)S(1)}, u32[]{:S(2)}, u32[]{:S(2)}) collective-permute-start(bf16[2,16,16,128]{3,2,1,0:T(8,128)(2,1)S(1)} %pad_maximum_fusion.10), channel_id=1, source_target_pairs={{0,8},{1,9},{4,12},{5,13},{8,0},{9,1},{12,4},{13,5},{2,10},{3,11},... | collective-permute-start | bytes 393224 | tf_op jit(solution)/shard_map/ppermute | solution.py:462
  109.1 8.4 %collective-permute-start.22 = (bf16[2,16,16,128]{3,2,1,0:T(8,128)(2,1)S(1)}, bf16[2,16,16,128]{3,2,1,0:T(8,128)(2,1)S(1)}, u32[]{:S(2)}, u32[]{:S(2)}) collective-permute-start(bf16[2,16,16,128]{3,2,1,0:T(8,128)(2,1)S(1)} %pad_maximum_fusion.12), channel_id=1, source_target_pairs={{0,12},{1,13},{4,8},{5,9},{8,4},{9,5},{12,0},{13,1},{2,14},{3,15},... | collective-permute-start | bytes 393224 | tf_op jit(solution)/shard_map/ppermute | solution.py:462
  (8 other events, 48.7 us)

commit v12 on v10

--- a/solution.py
+++ b/solution.py
@@ -296,9 +296,10 @@
 
 
 def update_kernel(
-    product, gate_h, cot_h, norm_gain_h, norm_bias_h, out_w_h, gate_w_h, after, update_h, dzg_h,
-    gate, cot, norm_gain, norm_bias, out_weight, gate_weight, update, dzg, spread,
-    in_sems, out_sems,
+    product, gate_h, cot_h, norm_gain_h, norm_bias_h, out_w_h, gate_w_h, after, coef_h, zhat_h,
+    inv_h, update_h, dzg, coef, zhat, inv,
+    gate, cot, norm_gain, norm_bias, out_weight, gate_weight, update, spread,
+    in_sems, out_sems, fetch_sems,
 ):
     hidden, rows, cols = product.shape
     width = cot.shape[2]
@@ -309,6 +310,7 @@
             (out_w_h, out_weight), (gate_w_h, gate_weight),
         ],
     )
+    fetched = start(fetch_sems, [(coef_h, coef), (zhat_h, zhat), (inv_h, inv)])
     spread[...] = product[...].astype(F32).reshape(hidden * rows, cols)
     wait(copies)
     groups = groups_of(rows)
@@ -331,17 +333,19 @@
             lanes = slice(r * cols, (r + 1) * cols)
             update[at + r] = turned(done[:, lanes]).astype(BF16)
             dzg[at + r] = back[:, lanes]
-    wait(start(out_sems, [(update, update_h), (dzg, dzg_h)]))
+    wait(fetched + start(out_sems, [(update, update_h)]))
 
 
 def grad_right_kernel(grad, left, out_h, ready, sems):
-    lead = (slice(None),) * (len(ready.shape) - 3)
+    share = ready.shape[-3]
+    columns = ready.shape[1] * ready.shape[-2]
+    factors = [(channel_matrix(grad, h), channel_matrix(left, h)) for h in range(share)]
     leaving = []
-    for h in range(ready.shape[-3]):
-        values = dot(channel_matrix(grad, h), channel_matrix(left, h), ((0,), (0,)))
-        put_channel(ready, h, values)
-        part = (*lead, pl.ds(h, 1))
-        copy = pltpu.make_async_copy(ready.at[part], out_h.at[part], sems.at[h])
+    for half in range(ready.shape[0]):
+        for h, (g, other) in enumerate(factors):
+            part = g[:, half * columns : (half + 1) * columns]
+            put_channel(ready.at[half], h, dot(part, other, ((0,), (0,))))
+        copy = pltpu.make_async_copy(ready.at[half], out_h.at[half], sems.at[half])
         copy.start()
         leaving.append(copy)
     wait(leaving)
@@ -356,28 +360,14 @@
         outs[m][n] = ready[number // n_col, number % n_col]
 
 
-def back_kernel(n_chip, grads, coef_h, zhat_h, inv_h, dzg_h, gain_h, proj_h, *refs):
-    pieces, out_h = refs[:-15], refs[-15]
-    (
-        coef, zhat, inv, dzg, gain, proj_weight, out, left, right,
-        sems, coef_sems, zhat_sems, dzg_sems, out_sems,
-    ) = refs[-14:]
+def back_kernel(n_chip, grads, coef, zhat, inv, dzg, gain_h, proj_h, *refs):
+    pieces, out_h = refs[:-8], refs[-8]
+    gain, proj_weight, out, left, right, sems, out_sems = refs[-7:]
     rows, cols, width = out.shape
     hidden = left.shape[0] // rows
     groups = groups_of(rows)
-    small = start(sems, [(gain_h, gain), (proj_h, proj_weight), (inv_h, inv)])
     ahead = rows // math.gcd(rows, 2)
-    blocks = {}
-    for n, at in enumerate(range(0, rows, ahead)):
-        part = pl.ds(at, ahead)
-        blocks[at] = [
-            pltpu.make_async_copy(source.at[part], target.at[part], sem.at[n])
-            for source, target, sem in (
-                (coef_h, coef, coef_sems), (zhat_h, zhat, zhat_sems), (dzg_h, dzg, dzg_sems)
-            )
-        ]
-        for copy in blocks[at]:
-            copy.start()
+    small = start(sems, [(gain_h, gain), (proj_h, proj_weight)])
     arrived = received(pieces, n_chip)
     length = left.shape[0] // len(arrived)
     for number, piece in arrived:
@@ -391,7 +381,6 @@
     gain_b = jnp.concatenate([down_lanes(gain[...], cols)] * groups[0][1], axis=1)
     leaving = []
     for at, size in groups:
-        wait(blocks.get(at, []))
         columns = []
         for r in range(size):
             gl = left[pl.ds(at + r, hidden, stride=rows), :].astype(BF16)
@@ -582,7 +571,7 @@
     (sent,) = call(
         grad_right_kernel,
         (shape(n_half, n_line, n_col, share, rows, cols),),
-        [vmem(n_half, n_line, n_col, share, rows, cols), sems(share)],
+        [vmem(n_half, n_line, n_col, share, rows, cols), sems(n_half)],
         (grad, left),
         near=(0, 1),
         flops=2 * share * n_half * (n_line * rows) ** 2 * n_col * cols,
@@ -600,27 +589,33 @@
         moved=8 * cells * hidden,
     )
     grad_left = exchange_pieces(tuple(grad_left))
-    update, dzg = call(
+    update, dzg, coef, zhat, inv = call(
         update_kernel,
-        (shape(rows, cols, width), shape(rows, width, cols, dtype=F32)),
-        [wide, block, vector, vector, square, square, block, wide, plane, sems(6), sems(2)],
-        (product, gate, cotangent, norm_gain, norm_bias, out_weight, gate_weight, sent),
+        (
+            shape(rows, cols, width),
+            shape(rows, width, cols, dtype=F32),
+            shape(rows, 4, hidden, cols),
+            shape(rows, width, cols, dtype=F32),
+            shape(rows, cols, dtype=F32),
+        ),
+        [wide, block, vector, vector, square, square, block, plane, sems(6), sems(1), sems(3)],
+        (
+            product, gate, cotangent, norm_gain, norm_bias, out_weight, gate_weight, sent,
+            coef, zhat, inv,
+        ),
         near=(0,),
+        outs_near=range(1, 5),
         flops=2 * cells * width * 3 * hidden,
-        moved=14 * cells * hidden,
+        moved=24 * cells * hidden,
     )
     (grad_pair,) = call(
         functools.partial(back_kernel, n_chip),
         (shape(rows, cols, width),),
-        [
-            vmem(rows, 4, hidden, cols), wide, vmem(rows, cols, dtype=F32), wide,
-            vector, proj_v, block, plane, plane,
-            sems(3), sems(2), sems(2), sems(2), sems(2),
-        ],
+        [vector, proj_v, block, plane, plane, sems(2), sems(2)],
         (grad_right, coef, zhat, inv, dzg, gain_in, proj_weight, *grad_left),
-        near=(0, *range(7, 7 + n_pieces)),
+        near=(*range(5), *range(7, 7 + n_pieces)),
         flops=2 * cells * width * 5 * hidden,
-        moved=30 * cells * width,
+        moved=24 * cells * width,
     )
     return (update, grad_pair)
 

time: 101 us -> 104 us (1.030)
  local copies, waits for them, and re-layouts: 0.06 us -> 6.67 us
  waiting for transfers between devices: 19.5 us -> 16.7 us
    unnamed x0 -> x12, local copies, waits for them, and re-layouts: none -> 6.61 us
    ppermute x16, waiting for transfers between devices: 19.5 us -> 16.7 us  [permute(): lax.ppermute(values, axes, [(at, at ^ distance) for at in range(size)])]
  transfers between devices with their start and end apart: 18 -> 18, of which waited for: 12 -> 10; matrix products, arithmetic and copies ran while one was open for 0% -> 0% of each run, Pallas kernels for 15% -> 15%
where the time goes in v12:
time: 104 us; the launch traced here: 103 us
  starting transfers between devices  29.2 us (28%)
  blocking collectives  24.9 us (24%)
  Pallas kernels  24.5 us (24%)
  waiting for transfers between devices  16.7 us (16%)
  local copies, waits for them, and re-layouts  6.67 us (6%)
    all_to_all x2, blocking collectives, exchange(): lax.all_to_all(values, within, split_axis=0, concat_axis=0, tiled=True)  24.9 us
    pallas_call x10, Pallas kernels, call(): pl.pallas_call(kernel, out_shape=[out if at in outs_near else pltpu.HBM(o...  24.5 us
    ppermute x16, starting transfers between devices, permute(): lax.ppermute(values, axes, [(at, at ^ distance) for at in range(size)])  18.2 us
    ppermute x16, waiting for transfers between devices, permute(): lax.ppermute(values, axes, [(at, at ^ distance) for at in range(size)])  16.7 us
    all_to_all x2, starting transfers between devices, exchange_all(): lax.all_to_all(flat, ('half', *within), split_axis=0, concat_axis=0, tile...  10.9 us
    unnamed x12, local copies, waits for them, and re-layouts  6.61 us
  transfers between devices with their start and end apart: 18, of which 10 were waited for; matrix products, arithmetic and copies ran while one was open for 0% of the time, Pallas kernels for 15%

profile of v12, /device:TPU:0, one launch (start us, length us, event | category | flops | bytes accessed | tf_op | source)
XLA Modules:
  0.0 103.0 jit_solution(3150163192304508755)
XLA Ops:
  0.6 3.2 %shard_map.113 = bf16[2,16,8,16,128]{4,3,2,1,0:T(8,128)(2,1)} custom-call(bf16[16,128,128]{2,1,0:T(8,128)(2,1)} %pair_h.5, s32[256]{0:T(256)} %mask_h.5, s32[1,256]{1,0:T(1,128)} %bitcast.26, f32[1,128]{1,0:T(1,128)} %bitcast.29, f32[1,128]{1,0:T(1,128)} %bitcast.34, bf16[128,512]{1,0:T(8,128)(2,1)} %proj_h.7), custom_call_target="tpu_custom_call" | custom-call | flops 201326592 | bytes 1310720 | tf_op jit(solution)/shard_map/pallas_call | solution.py:416
  3.8 7.3 %all-to-all-start = ((bf16[32,8,16,128]{3,2,1,0:T(8,128)(2,1)}), bf16[32,8,16,128]{3,2,1,0:T(8,128)(2,1)S(1)}, u32[]{:S(2)}, u32[]{:S(2)}) async-start(bf16[32,8,16,128]{3,2,1,0:T(8,128)(2,1)} %bitcast.25), calls=%async_computation | async-start | bytes 2097152 | tf_op jit(solution)/shard_map/all_to_all | solution.py:470
  11.1 2.3 %shard_map.116 = (bf16[8,8,16,128]{3,2,1,0:T(8,128)(2,1)S(1)}, bf16[8,8,16,128]{3,2,1,0:T(8,128)(2,1)S(1)}) custom-call(bf16[16,128,128]{2,1,0:T(8,128)(2,1)} %pair_h.5, s32[256]{0:T(256)} %mask_h.5, s32[1,256]{1,0:T(1,128)} %bitcast.27, f32[1,128]{1,0:T(1,128)} %bitcast.30, f32[1,128]{1,0:T(1,128)} %bitcast.35, bf16[128,512]{1,0:T(8,128)(2,1)} %proj_h.7), custom_call_target="tpu_custom_call" | custom-call | flops 201326592 | bytes 1310720 | tf_op jit(solution)/shard_map/pallas_call | solution.py:416
  15.0 1.8 %collective-permute-start.1 = (bf16[2,8,16,128]{3,2,1,0:T(8,128)(2,1)S(1)}, bf16[2,8,16,128]{3,2,1,0:T(8,128)(2,1)S(1)}, u32[]{:S(2)}, u32[]{:S(2)}) collective-permute-start(bf16[2,8,16,128]{3,2,1,0:T(8,128)(2,1)S(1)} %pad_maximum_fusion), channel_id=1, source_target_pairs={{0,1},{1,0},{4,5},{5,4},{8,9},{9,8},{12,13},{13,12},{2,3},{3,2},{6... | collective-permute-start | bytes 196616 | tf_op jit(solution)/shard_map/ppermute | solution.py:475
  16.9 1.5 %collective-permute-start.2 = (bf16[2,8,16,128]{3,2,1,0:T(8,128)(2,1)S(1)}, bf16[2,8,16,128]{3,2,1,0:T(8,128)(2,1)S(1)}, u32[]{:S(2)}, u32[]{:S(2)}) collective-permute-start(bf16[2,8,16,128]{3,2,1,0:T(8,128)(2,1)S(1)} %pad_maximum_fusion.1), channel_id=1, source_target_pairs={{0,4},{1,5},{4,0},{5,1},{8,12},{9,13},{12,8},{13,9},{2,6},{3,7},{6... | collective-permute-start | bytes 196616 | tf_op jit(solution)/shard_map/ppermute | solution.py:475
  18.7 1.8 %collective-permute-start.4 = (bf16[2,8,16,128]{3,2,1,0:T(8,128)(2,1)S(1)}, bf16[2,8,16,128]{3,2,1,0:T(8,128)(2,1)S(1)}, u32[]{:S(2)}, u32[]{:S(2)}) collective-permute-start(bf16[2,8,16,128]{3,2,1,0:T(8,128)(2,1)S(1)} %pad_maximum_fusion.3), channel_id=1, source_target_pairs={{0,8},{1,9},{4,12},{5,13},{8,0},{9,1},{12,4},{13,5},{2,10},{3,11},... | collective-permute-start | bytes 196616 | tf_op jit(solution)/shard_map/ppermute | solution.py:475
  20.6 1.5 %collective-permute-start.5 = (bf16[2,8,16,128]{3,2,1,0:T(8,128)(2,1)S(1)}, bf16[2,8,16,128]{3,2,1,0:T(8,128)(2,1)S(1)}, u32[]{:S(2)}, u32[]{:S(2)}) collective-permute-start(bf16[2,8,16,128]{3,2,1,0:T(8,128)(2,1)S(1)} %pad_maximum_fusion.4), channel_id=1, source_target_pairs={{0,9},{1,8},{4,13},{5,12},{8,1},{9,0},{12,5},{13,4},{2,11},{3,10},... | collective-permute-start | bytes 196616 | tf_op jit(solution)/shard_map/ppermute | solution.py:475
  22.9 1.7 %collective-permute-start.6 = (bf16[2,8,16,128]{3,2,1,0:T(8,128)(2,1)S(1)}, bf16[2,8,16,128]{3,2,1,0:T(8,128)(2,1)S(1)}, u32[]{:S(2)}, u32[]{:S(2)}) collective-permute-start(bf16[2,8,16,128]{3,2,1,0:T(8,128)(2,1)S(1)} %pad_maximum_fusion.5), channel_id=1, source_target_pairs={{0,12},{1,13},{4,8},{5,9},{8,4},{9,5},{12,0},{13,1},{2,14},{3,15},... | collective-permute-start | bytes 196616 | tf_op jit(solution)/shard_map/ppermute | solution.py:475
  25.8 4.6 %shard_map.114 = (f32[16,128,128]{2,1,0:T(8,128)}, f32[16,128]{1,0:T(8,128)}, f32[16,128,128]{2,1,0:T(8,128)}, f32[2048,128]{1,0:T(8,128)S(1)}) custom-call(bf16[16,128,128]{2,1,0:T(8,128)(2,1)} %pair_h.5, bf16[16,128,128]{2,1,0:T(8,128)(2,1)} %cot_h.3, f32[1,128]{1,0:T(1,128)} %bitcast.31, f32[1,128]{1,0:T(1,128)} %bitcast.36, bf16[128,128]{1,0:T(8,128)(2,1)} %gate_w_h.1, ...), custom_call_target="tpu_custom_call" | custom-call | flops 268435456 | bytes 4194304 | tf_op jit(solution)/shard_map/pallas_call | solution.py:416
  30.4 3.2 %shard_map.115.after.coef_h = bf16[16,4,128,128]{3,2,1,0:T(8,128)(2,1)} custom-call(f32[16,128,128]{2,1,0:T(8,128)} %get-tuple-element.17.zhat_h, s32[256]{0:T(256)} %mask_h.5, s32[1,256]{1,0:T(1,128)} %bitcast.28, f32[1,128]{1,0:T(1,128)} %bitcast.32, f32[1,128]{1,0:T(1,128)} %bitcast.37, bf16[128,512]{1,0:T(8,128)(2,1)} %proj_h.7), custom_call_target="tpu_custom_call" | custom-call | flops 335544320 | bytes 4194304 | tf_op jit(solution)/shard_map/pallas_call | solution.py:416
  34.7 2.9 %collective-permute-done.7.refs_8_ = bf16[2,8,16,128]{3,2,1,0:T(8,128)(2,1)S(1)} collective-permute-done((bf16[2,8,16,128]{3,2,1,0:T(8,128)(2,1)S(1)}, bf16[2,8,16,128]{3,2,1,0:T(8,128)(2,1)S(1)}, u32[]{:S(2)}, u32[]{:S(2)}) %collective-permute-start.7) | collective-permute-done | bytes 65568 | tf_op jit(solution)/shard_map/ppermute | solution.py:475
  38.2 12.9 %all_to_all.20 = bf16[16,8,16,128]{3,2,1,0:T(8,128)(2,1)S(1)} all-to-all(bf16[16,8,16,128]{3,2,1,0:T(8,128)(2,1)S(1)} %bitcast.23), channel_id=1, replica_groups=mesh['grp'=1,'half'=2,'row'=4,'core'=2,'col'=2] {'row','core','col'}, dimensions={0} | all-to-all | bytes 1048576 | tf_op jit(solution)/shard_map/all_to_all | solution.py:466
  51.6 12.0 %all_to_all.21 = bf16[16,8,16,128]{3,2,1,0:T(8,128)(2,1)S(1)} all-to-all(bf16[16,8,16,128]{3,2,1,0:T(8,128)(2,1)S(1)} %bitcast.21), channel_id=1, replica_groups=mesh['grp'=1,'half'=2,'row'=4,'core'=2,'col'=2] {'row','core','col'}, dimensions={0} | all-to-all | bytes 1048576 | tf_op jit(solution)/shard_map/all_to_all | solution.py:466
  64.9 3.6 %all-to-all-start.3 = ((bf16[32,8,16,128]{3,2,1,0:T(8,128)(2,1)}), bf16[32,8,16,128]{3,2,1,0:T(8,128)(2,1)S(1)}, u32[]{:S(2)}, u32[]{:S(2)}) async-start(bf16[32,8,16,128]{3,2,1,0:T(8,128)(2,1)} %bitcast.24), calls=%async_computation.3 | async-start | bytes 2097152 | tf_op jit(solution)/shard_map/all_to_all | solution.py:470
  70.6 1.7 %collective-permute-start.9 = (bf16[2,8,16,128]{3,2,1,0:T(8,128)(2,1)S(1)}, bf16[2,8,16,128]{3,2,1,0:T(8,128)(2,1)S(1)}, u32[]{:S(2)}, u32[]{:S(2)}) collective-permute-start(bf16[2,8,16,128]{3,2,1,0:T(8,128)(2,1)S(1)} %pad_maximum_fusion.7), channel_id=1, source_target_pairs={{0,1},{1,0},{4,5},{5,4},{8,9},{9,8},{12,13},{13,12},{2,3},{3,2},{6... | collective-permute-start | bytes 196616 | tf_op jit(solution)/shard_map/ppermute | solution.py:475
  72.3 1.5 %collective-permute-start.10 = (bf16[2,8,16,128]{3,2,1,0:T(8,128)(2,1)S(1)}, bf16[2,8,16,128]{3,2,1,0:T(8,128)(2,1)S(1)}, u32[]{:S(2)}, u32[]{:S(2)}) collective-permute-start(bf16[2,8,16,128]{3,2,1,0:T(8,128)(2,1)S(1)} %pad_maximum_fusion.8), channel_id=1, source_target_pairs={{0,4},{1,5},{4,0},{5,1},{8,12},{9,13},{12,8},{13,9},{2,6},{3,7},{6... | collective-permute-start | bytes 196616 | tf_op jit(solution)/shard_map/ppermute | solution.py:475
  74.3 1.7 %collective-permute-start.12 = (bf16[2,8,16,128]{3,2,1,0:T(8,128)(2,1)S(1)}, bf16[2,8,16,128]{3,2,1,0:T(8,128)(2,1)S(1)}, u32[]{:S(2)}, u32[]{:S(2)}) collective-permute-start(bf16[2,8,16,128]{3,2,1,0:T(8,128)(2,1)S(1)} %pad_maximum_fusion.10), channel_id=1, source_target_pairs={{0,8},{1,9},{4,12},{5,13},{8,0},{9,1},{12,4},{13,5},{2,10},{3,11},... | collective-permute-start | bytes 196616 | tf_op jit(solution)/shard_map/ppermute | solution.py:475
  76.0 1.5 %collective-permute-start.13 = (bf16[2,8,16,128]{3,2,1,0:T(8,128)(2,1)S(1)}, bf16[2,8,16,128]{3,2,1,0:T(8,128)(2,1)S(1)}, u32[]{:S(2)}, u32[]{:S(2)}) collective-permute-start(bf16[2,8,16,128]{3,2,1,0:T(8,128)(2,1)S(1)} %pad_maximum_fusion.11), channel_id=1, source_target_pairs={{0,9},{1,8},{4,13},{5,12},{8,1},{9,0},{12,5},{13,4},{2,11},{3,10},... | collective-permute-start | bytes 196616 | tf_op jit(solution)/shard_map/ppermute | solution.py:475
  77.5 2.9 %collective-permute-done.9.refs_2_ = bf16[2,8,16,128]{3,2,1,0:T(8,128)(2,1)S(1)} collective-permute-done((bf16[2,8,16,128]{3,2,1,0:T(8,128)(2,1)S(1)}, bf16[2,8,16,128]{3,2,1,0:T(8,128)(2,1)S(1)}, u32[]{:S(2)}, u32[]{:S(2)}) %collective-permute-start.9) | collective-permute-done | bytes 65568 | tf_op jit(solution)/shard_map/ppermute | solution.py:475
  83.4 4.6 %shard_map.120 = (bf16[16,128,128]{2,1,0:T(8,128)(2,1)}, f32[16,128,128]{2,1,0:T(8,128)S(1)}, bf16[16,4,128,128]{3,2,1,0:T(8,128)(2,1)S(1)}, f32[16,128,128]{2,1,0:T(8,128)S(1)}, f32[16,128]{1,0:T(8,128)S(1)}) custom-call(bf16[128,16,128]{2,1,0:T(8,128)(2,1)S(1)} %bitcast.19, f32[16,128,128]{2,1,0:T(8,128)} %get-tuple-element.21.gate_h, ...), custom_call_target="tpu_custom_call" | custom-call | flops 201326592 | bytes 6291456 | tf_op jit(solution)/shard_map/pallas_call | solution.py:416
  90.4 1.5 %collective-permute-done.14.refs_7_ = bf16[2,8,16,128]{3,2,1,0:T(8,128)(2,1)S(1)} collective-permute-done((bf16[2,8,16,128]{3,2,1,0:T(8,128)(2,1)S(1)}, bf16[2,8,16,128]{3,2,1,0:T(8,128)(2,1)S(1)}, u32[]{:S(2)}, u32[]{:S(2)}) %collective-permute-start.14) | collective-permute-done | bytes 65568 | tf_op jit(solution)/shard_map/ppermute | solution.py:475
  92.0 2.9 %collective-permute-done.15.refs_8_ = bf16[2,8,16,128]{3,2,1,0:T(8,128)(2,1)S(1)} collective-permute-done((bf16[2,8,16,128]{3,2,1,0:T(8,128)(2,1)S(1)}, bf16[2,8,16,128]{3,2,1,0:T(8,128)(2,1)S(1)}, u32[]{:S(2)}, u32[]{:S(2)}) %collective-permute-start.15) | collective-permute-done | bytes 65568 | tf_op jit(solution)/shard_map/ppermute | solution.py:475
  95.5 1.6 %copy-done.1 = bf16[16,4,128,128]{3,2,1,0:T(8,128)(2,1)S(1)} copy-done((bf16[16,4,128,128]{3,2,1,0:T(8,128)(2,1)S(1)}, bf16[16,4,128,128]{3,2,1,0:T(8,128)(2,1)}, u32[]{:S(2)}) %copy-start.1) | copy-done | bytes 2097176
  99.1 3.7 %shard_map.122 = bf16[16,128,128]{2,1,0:T(8,128)(2,1)} custom-call(bf16[2,16,8,16,128]{4,3,2,1,0:T(8,128)(2,1)S(1)} %bitcast.20, bf16[16,4,128,128]{3,2,1,0:T(8,128)(2,1)S(1)} %copy-done.1, f32[16,128,128]{2,1,0:T(8,128)S(1)} %copy-done.3, f32[16,128]{1,0:T(8,128)S(1)} %get-tuple-element.28.inv, f32[16,128,128]{2,1,0:T(8,128)S(1)} %get-tuple-element.29.dzg, ...), custom_call_target="tpu_custom_call" | custom-call | flops 335544320 | bytes 6291456 | tf_op jit(solution)/shard_map/pallas_call | solution.py:416
  (54 shorter events, 18.1 us)
Async XLA Ops:
  3.8 33.7 %all-to-all-start = ((bf16[32,8,16,128]{3,2,1,0:T(8,128)(2,1)}), bf16[32,8,16,128]{3,2,1,0:T(8,128)(2,1)S(1)}, u32[]{:S(2)}, u32[]{:S(2)}) async-start(bf16[32,8,16,128]{3,2,1,0:T(8,128)(2,1)} %bitcast.25), calls=%async_computation | async-start | bytes 2097152 | tf_op jit(solution)/shard_map/all_to_all | solution.py:470
  13.4 1.6 %collective-permute-start = (bf16[8,8,16,128]{3,2,1,0:T(8,128)(2,1)S(1)}, bf16[8,8,16,128]{3,2,1,0:T(8,128)(2,1)S(1)}, u32[]{:S(2)}, u32[]{:S(2)}) collective-permute-start(bf16[8,8,16,128]{3,2,1,0:T(8,128)(2,1)S(1)} %get-tuple-element.19), channel_id=1, source_target_pairs={{0,2},{2,0},{1,3},{3,1},{4,6},{6,4},{5,7},{7,5},{8,10},{10,8},{9,1... | collective-permute-start | bytes 786440 | tf_op jit(solution)/shard_map/ppermute | solution.py:475
  15.0 7.8 %collective-permute-start.1 = (bf16[2,8,16,128]{3,2,1,0:T(8,128)(2,1)S(1)}, bf16[2,8,16,128]{3,2,1,0:T(8,128)(2,1)S(1)}, u32[]{:S(2)}, u32[]{:S(2)}) collective-permute-start(bf16[2,8,16,128]{3,2,1,0:T(8,128)(2,1)S(1)} %pad_maximum_fusion), channel_id=1, source_target_pairs={{0,1},{1,0},{4,5},{5,4},{8,9},{9,8},{12,13},{13,12},{2,3},{3,2},{6... | collective-permute-start | bytes 196616 | tf_op jit(solution)/shard_map/ppermute | solution.py:475
  16.9 8.2 %collective-permute-start.2 = (bf16[2,8,16,128]{3,2,1,0:T(8,128)(2,1)S(1)}, bf16[2,8,16,128]{3,2,1,0:T(8,128)(2,1)S(1)}, u32[]{:S(2)}, u32[]{:S(2)}) collective-permute-start(bf16[2,8,16,128]{3,2,1,0:T(8,128)(2,1)S(1)} %pad_maximum_fusion.1), channel_id=1, source_target_pairs={{0,4},{1,5},{4,0},{5,1},{8,12},{9,13},{12,8},{13,9},{2,6},{3,7},{6... | collective-permute-start | bytes 196616 | tf_op jit(solution)/shard_map/ppermute | solution.py:475
  18.4 15.2 %collective-permute-start.3 = (bf16[2,8,16,128]{3,2,1,0:T(8,128)(2,1)S(1)}, bf16[2,8,16,128]{3,2,1,0:T(8,128)(2,1)S(1)}, u32[]{:S(2)}, u32[]{:S(2)}) collective-permute-start(bf16[2,8,16,128]{3,2,1,0:T(8,128)(2,1)S(1)} %pad_maximum_fusion.2), channel_id=1, source_target_pairs={{0,5},{1,4},{4,1},{5,0},{8,13},{9,12},{12,9},{13,8},{2,7},{3,6},{6... | collective-permute-start | bytes 196616 | tf_op jit(solution)/shard_map/ppermute | solution.py:475
  18.7 14.9 %collective-permute-start.4 = (bf16[2,8,16,128]{3,2,1,0:T(8,128)(2,1)S(1)}, bf16[2,8,16,128]{3,2,1,0:T(8,128)(2,1)S(1)}, u32[]{:S(2)}, u32[]{:S(2)}) collective-permute-start(bf16[2,8,16,128]{3,2,1,0:T(8,128)(2,1)S(1)} %pad_maximum_fusion.3), channel_id=1, source_target_pairs={{0,8},{1,9},{4,12},{5,13},{8,0},{9,1},{12,4},{13,5},{2,10},{3,11},... | collective-permute-start | bytes 196616 | tf_op jit(solution)/shard_map/ppermute | solution.py:475
  20.6 13.0 %collective-permute-start.5 = (bf16[2,8,16,128]{3,2,1,0:T(8,128)(2,1)S(1)}, bf16[2,8,16,128]{3,2,1,0:T(8,128)(2,1)S(1)}, u32[]{:S(2)}, u32[]{:S(2)}) collective-permute-start(bf16[2,8,16,128]{3,2,1,0:T(8,128)(2,1)S(1)} %pad_maximum_fusion.4), channel_id=1, source_target_pairs={{0,9},{1,8},{4,13},{5,12},{8,1},{9,0},{12,5},{13,4},{2,11},{3,10},... | collective-permute-start | bytes 196616 | tf_op jit(solution)/shard_map/ppermute | solution.py:475
  22.9 11.8 %collective-permute-start.6 = (bf16[2,8,16,128]{3,2,1,0:T(8,128)(2,1)S(1)}, bf16[2,8,16,128]{3,2,1,0:T(8,128)(2,1)S(1)}, u32[]{:S(2)}, u32[]{:S(2)}) collective-permute-start(bf16[2,8,16,128]{3,2,1,0:T(8,128)(2,1)S(1)} %pad_maximum_fusion.5), channel_id=1, source_target_pairs={{0,12},{1,13},{4,8},{5,9},{8,4},{9,5},{12,0},{13,1},{2,14},{3,15},... | collective-permute-start | bytes 196616 | tf_op jit(solution)/shard_map/ppermute | solution.py:475
  25.1 12.5 %collective-permute-start.7 = (bf16[2,8,16,128]{3,2,1,0:T(8,128)(2,1)S(1)}, bf16[2,8,16,128]{3,2,1,0:T(8,128)(2,1)S(1)}, u32[]{:S(2)}, u32[]{:S(2)}) collective-permute-start(bf16[2,8,16,128]{3,2,1,0:T(8,128)(2,1)S(1)} %pad_maximum_fusion.6), channel_id=1, source_target_pairs={{0,13},{1,12},{4,9},{5,8},{8,5},{9,4},{12,1},{13,0},{2,15},{3,14},... | collective-permute-start | bytes 196616 | tf_op jit(solution)/shard_map/ppermute | solution.py:475
  64.9 30.5 %all-to-all-start.3 = ((bf16[32,8,16,128]{3,2,1,0:T(8,128)(2,1)}), bf16[32,8,16,128]{3,2,1,0:T(8,128)(2,1)S(1)}, u32[]{:S(2)}, u32[]{:S(2)}) async-start(bf16[32,8,16,128]{3,2,1,0:T(8,128)(2,1)} %bitcast.24), calls=%async_computation.3 | async-start | bytes 2097152 | tf_op jit(solution)/shard_map/all_to_all | solution.py:470
  69.0 1.6 %collective-permute-start.8 = (bf16[8,8,16,128]{3,2,1,0:T(8,128)(2,1)S(1)}, bf16[8,8,16,128]{3,2,1,0:T(8,128)(2,1)S(1)}, u32[]{:S(2)}, u32[]{:S(2)}) collective-permute-start(bf16[8,8,16,128]{3,2,1,0:T(8,128)(2,1)S(1)} %get-tuple-element.31), channel_id=1, source_target_pairs={{0,2},{2,0},{1,3},{3,1},{4,6},{6,4},{5,7},{7,5},{8,10},{10,8},{9,1... | collective-permute-start | bytes 786440 | tf_op jit(solution)/shard_map/ppermute | solution.py:475
  70.6 9.8 %collective-permute-start.9 = (bf16[2,8,16,128]{3,2,1,0:T(8,128)(2,1)S(1)}, bf16[2,8,16,128]{3,2,1,0:T(8,128)(2,1)S(1)}, u32[]{:S(2)}, u32[]{:S(2)}) collective-permute-start(bf16[2,8,16,128]{3,2,1,0:T(8,128)(2,1)S(1)} %pad_maximum_fusion.7), channel_id=1, source_target_pairs={{0,1},{1,0},{4,5},{5,4},{8,9},{9,8},{12,13},{13,12},{2,3},{3,2},{6... | collective-permute-start | bytes 196616 | tf_op jit(solution)/shard_map/ppermute | solution.py:475
  72.3 9.9 %collective-permute-start.10 = (bf16[2,8,16,128]{3,2,1,0:T(8,128)(2,1)S(1)}, bf16[2,8,16,128]{3,2,1,0:T(8,128)(2,1)S(1)}, u32[]{:S(2)}, u32[]{:S(2)}) collective-permute-start(bf16[2,8,16,128]{3,2,1,0:T(8,128)(2,1)S(1)} %pad_maximum_fusion.8), channel_id=1, source_target_pairs={{0,4},{1,5},{4,0},{5,1},{8,12},{9,13},{12,8},{13,9},{2,6},{3,7},{6... | collective-permute-start | bytes 196616 | tf_op jit(solution)/shard_map/ppermute | solution.py:475
  73.8 16.6 %collective-permute-start.11 = (bf16[2,8,16,128]{3,2,1,0:T(8,128)(2,1)S(1)}, bf16[2,8,16,128]{3,2,1,0:T(8,128)(2,1)S(1)}, u32[]{:S(2)}, u32[]{:S(2)}) collective-permute-start(bf16[2,8,16,128]{3,2,1,0:T(8,128)(2,1)S(1)} %pad_maximum_fusion.9), channel_id=1, source_target_pairs={{0,5},{1,4},{4,1},{5,0},{8,13},{9,12},{12,9},{13,8},{2,7},{3,6},{6... | collective-permute-start | bytes 196616 | tf_op jit(solution)/shard_map/ppermute | solution.py:475
  74.3 16.1 %collective-permute-start.12 = (bf16[2,8,16,128]{3,2,1,0:T(8,128)(2,1)S(1)}, bf16[2,8,16,128]{3,2,1,0:T(8,128)(2,1)S(1)}, u32[]{:S(2)}, u32[]{:S(2)}) collective-permute-start(bf16[2,8,16,128]{3,2,1,0:T(8,128)(2,1)S(1)} %pad_maximum_fusion.10), channel_id=1, source_target_pairs={{0,8},{1,9},{4,12},{5,13},{8,0},{9,1},{12,4},{13,5},{2,10},{3,11},... | collective-permute-start | bytes 196616 | tf_op jit(solution)/shard_map/ppermute | solution.py:475
  76.0 14.4 %collective-permute-start.13 = (bf16[2,8,16,128]{3,2,1,0:T(8,128)(2,1)S(1)}, bf16[2,8,16,128]{3,2,1,0:T(8,128)(2,1)S(1)}, u32[]{:S(2)}, u32[]{:S(2)}) collective-permute-start(bf16[2,8,16,128]{3,2,1,0:T(8,128)(2,1)S(1)} %pad_maximum_fusion.11), channel_id=1, source_target_pairs={{0,9},{1,8},{4,13},{5,12},{8,1},{9,0},{12,5},{13,4},{2,11},{3,10},... | collective-permute-start | bytes 196616 | tf_op jit(solution)/shard_map/ppermute | solution.py:475
  80.4 11.5 %collective-permute-start.14 = (bf16[2,8,16,128]{3,2,1,0:T(8,128)(2,1)S(1)}, bf16[2,8,16,128]{3,2,1,0:T(8,128)(2,1)S(1)}, u32[]{:S(2)}, u32[]{:S(2)}) collective-permute-start(bf16[2,8,16,128]{3,2,1,0:T(8,128)(2,1)S(1)} %pad_maximum_fusion.12), channel_id=1, source_target_pairs={{0,12},{1,13},{4,8},{5,9},{8,4},{9,5},{12,0},{13,1},{2,14},{3,15},... | collective-permute-start | bytes 196616 | tf_op jit(solution)/shard_map/ppermute | solution.py:475
  82.2 12.6 %collective-permute-start.15 = (bf16[2,8,16,128]{3,2,1,0:T(8,128)(2,1)S(1)}, bf16[2,8,16,128]{3,2,1,0:T(8,128)(2,1)S(1)}, u32[]{:S(2)}, u32[]{:S(2)}) collective-permute-start(bf16[2,8,16,128]{3,2,1,0:T(8,128)(2,1)S(1)} %pad_maximum_fusion.13), channel_id=1, source_target_pairs={{0,13},{1,12},{4,9},{5,8},{8,5},{9,4},{12,1},{13,0},{2,15},{3,14},... | collective-permute-start | bytes 196616 | tf_op jit(solution)/shard_map/ppermute | solution.py:475
  88.1 1.4 %copy-start = (bf16[16,4,128,128]{3,2,1,0:T(8,128)(2,1)}, bf16[16,4,128,128]{3,2,1,0:T(8,128)(2,1)S(1)}, u32[]{:S(2)}) copy-start(bf16[16,4,128,128]{3,2,1,0:T(8,128)(2,1)S(1)} %get-tuple-element.26.coef) | copy-start | bytes 6291460
  89.4 1.0 copy-start.2
  94.8 0.6 copy-start.4
  95.5 1.6 %copy-start.1 = (bf16[16,4,128,128]{3,2,1,0:T(8,128)(2,1)S(1)}, bf16[16,4,128,128]{3,2,1,0:T(8,128)(2,1)}, u32[]{:S(2)}) copy-start(bf16[16,4,128,128]{3,2,1,0:T(8,128)(2,1)} %copy-done) | copy-start | bytes 6291460
  97.1 1.2 %copy-start.3 = (f32[16,128,128]{2,1,0:T(8,128)S(1)}, f32[16,128,128]{2,1,0:T(8,128)}, u32[]{:S(2)}) copy-start(f32[16,128,128]{2,1,0:T(8,128)} %copy-done.2) | copy-start | bytes 3145732
  98.3 0.8 copy-start.5

commit v13 on v10

--- a/solution.py
+++ b/solution.py
@@ -116,22 +116,22 @@
     rows, cols, width = pair.shape
     hidden = plane.shape[0] // rows
     groups = groups_of(rows)
-    wait(
-        start(
-            sems,
-            [
-                (gain_h, gain), (bias_h, bias),
-                (proj_h.at[:, pl.ds(part * hidden, 2 * hidden)], proj_weight),
-                (mask_h, mask_s), (mask_row_h, mask_v), (pair_h, pair),
-            ],
-        )
-    )
+    *small, whole = start(
+        sems,
+        [
+            (gain_h, gain), (bias_h, bias),
+            (proj_h.at[:, pl.ds(part * hidden, 2 * hidden)], proj_weight),
+            (mask_h, mask_s), (mask_row_h, mask_v), (pair_h, pair),
+        ],
+    )
+    wait(small)
     gain_b = jnp.concatenate([down_lanes(gain[...], cols)] * groups[0][1], axis=1)
     bias_b = jnp.concatenate([down_lanes(bias[...], cols)] * groups[0][1], axis=1)
+    weight = turned_weight(proj_weight[...])
+    whole.wait()
     for at, size in groups:
         zhat, _ = normalized(turned(pair[at : at + size].reshape(size * cols, width)))
         zbar[:, at * cols : (at + size) * cols] = (zhat * gain_b + bias_b).astype(BF16)
-    weight = turned_weight(proj_weight[...])
 
     def channels(first, count):
         for at, size in groups:
@@ -176,9 +176,9 @@
 
 def side_kernel(
     pair_h, cot_h, gain_h, bias_h, gate_h, norm_gain_h, out_w_h,
-    zhat_h, inv_h, gate_out_h, dxh_out,
+    zhat_h, short_h, inv_h, gate_out_h, dxh_out,
     pair, cot, gain, bias, gate_weight, norm_gain, out_weight,
-    zhat_out, inv_out, gate_out, in_sems, out_sems,
+    zhat_out, short_out, inv_out, gate_out, in_sems, out_sems,
 ):
     rows, cols, width = pair.shape
     hidden = out_weight.shape[0]
@@ -206,13 +206,17 @@
         for r in range(size):
             lanes = slice(r * cols, (r + 1) * cols)
             zhat_out[at + r] = zhat[:, lanes]
+            short_out[at + r] = zhat[:, lanes].astype(BF16)
             inv_out[at + r : at + r + 1] = inverse[:, lanes]
             gate_out[at + r] = gate[:, lanes]
             dxh_out[pl.ds(at + r, hidden, stride=rows), :] = dxh[:, lanes]
     wait(
         start(
             out_sems,
-            [(zhat_out, zhat_h), (inv_out, inv_h), (gate_out, gate_out_h)],
+            [
+                (zhat_out, zhat_h), (short_out, short_h), (inv_out, inv_h),
+                (gate_out, gate_out_h),
+            ],
         )
     )
 
@@ -330,7 +334,7 @@
         for r in range(size):
             lanes = slice(r * cols, (r + 1) * cols)
             update[at + r] = turned(done[:, lanes]).astype(BF16)
-            dzg[at + r] = back[:, lanes]
+            dzg[at + r] = back[:, lanes].astype(BF16)
     wait(start(out_sems, [(update, update_h), (dzg, dzg_h)]))
 
 
@@ -367,17 +371,19 @@
     groups = groups_of(rows)
     small = start(sems, [(gain_h, gain), (proj_h, proj_weight), (inv_h, inv)])
     ahead = rows // math.gcd(rows, 2)
-    blocks = {}
-    for n, at in enumerate(range(0, rows, ahead)):
-        part = pl.ds(at, ahead)
-        blocks[at] = [
-            pltpu.make_async_copy(source.at[part], target.at[part], sem.at[n])
+    blocks = [
+        [
+            pltpu.make_async_copy(
+                source.at[pl.ds(at, size)], target.at[pl.ds(at, size)], sem.at[n]
+            )
             for source, target, sem in (
                 (coef_h, coef, coef_sems), (zhat_h, zhat, zhat_sems), (dzg_h, dzg, dzg_sems)
             )
         ]
-        for copy in blocks[at]:
-            copy.start()
+        for n, (at, size) in enumerate(groups)
+    ]
+    for copy in sum(blocks[:2], []):
+        copy.start()
     arrived = received(pieces, n_chip)
     length = left.shape[0] // len(arrived)
     for number, piece in arrived:
@@ -390,8 +396,10 @@
     wait(small)
     gain_b = jnp.concatenate([down_lanes(gain[...], cols)] * groups[0][1], axis=1)
     leaving = []
-    for at, size in groups:
-        wait(blocks.get(at, []))
+    for copy in sum(blocks[2:], []):
+        copy.start()
+    for n, (at, size) in enumerate(groups):
+        wait(blocks[n])
         columns = []
         for r in range(size):
             gl = left[pl.ds(at + r, hidden, stride=rows), :].astype(BF16)
@@ -402,8 +410,8 @@
                 )
             )
         back = dot(proj_weight[...], jnp.concatenate(columns, axis=1))
-        dzh = (back + side_by_side(dzg, at, size)) * gain_b
-        z = side_by_side(zhat, at, size)
+        dzh = (back + side_by_side(dzg, at, size).astype(F32)) * gain_b
+        z = side_by_side(zhat, at, size).astype(F32)
         inverse = jnp.concatenate([inv[at + r : at + r + 1] for r in range(size)], axis=1)
         m1 = jnp.mean(dzh, axis=0, keepdims=True)
         m2 = jnp.mean(dzh * z, axis=0, keepdims=True)
@@ -500,6 +508,7 @@
     plane = vmem(hidden * rows, cols, dtype=F32)
     block = vmem(rows, cols, width)
     wide = vmem(rows, width, cols, dtype=F32)
+    short = vmem(rows, width, cols)
     square = vmem(width, hidden)
     proj_v = vmem(width, 4 * hidden)
     pieces_shape = (shape(n_chip, share, rows, cols),) * n_core
@@ -528,20 +537,21 @@
     )
     right = exchange_all(right).reshape(n_half, n_line, n_col, share, rows, cols)
     left = exchange_pieces(tuple(front(0, pieces_shape, [], range(n_core))))
-    zhat, inv, gate, dxh = call(
+    zhat, short_zhat, inv, gate, dxh = call(
         side_kernel,
         (
             shape(rows, width, cols, dtype=F32),
+            shape(rows, width, cols),
             shape(rows, cols, dtype=F32),
             shape(rows, width, cols, dtype=F32),
             shape(hidden * rows, cols, dtype=F32),
         ),
         [
             block, block, vector, vector, square, vector, square,
-            wide, vmem(rows, cols, dtype=F32), wide, sems(7), sems(3),
+            wide, short, vmem(rows, cols, dtype=F32), wide, sems(7), sems(4),
         ],
         (pair, cotangent, gain_in, bias_in, gate_weight, norm_gain, out_weight),
-        outs_near=(3,),
+        outs_near=(4,),
         flops=2 * cells * width * 4 * hidden,
         moved=16 * cells * width,
     )
@@ -602,8 +612,8 @@
     grad_left = exchange_pieces(tuple(grad_left))
     update, dzg = call(
         update_kernel,
-        (shape(rows, cols, width), shape(rows, width, cols, dtype=F32)),
-        [wide, block, vector, vector, square, square, block, wide, plane, sems(6), sems(2)],
+        (shape(rows, cols, width), shape(rows, width, cols)),
+        [wide, block, vector, vector, square, square, block, short, plane, sems(6), sems(2)],
         (product, gate, cotangent, norm_gain, norm_bias, out_weight, gate_weight, sent),
         near=(0,),
         flops=2 * cells * width * 3 * hidden,
@@ -613,11 +623,11 @@
         functools.partial(back_kernel, n_chip),
         (shape(rows, cols, width),),
         [
-            vmem(rows, 4, hidden, cols), wide, vmem(rows, cols, dtype=F32), wide,
+            vmem(rows, 4, hidden, cols), short, vmem(rows, cols, dtype=F32), short,
             vector, proj_v, block, plane, plane,
-            sems(3), sems(2), sems(2), sems(2), sems(2),
+            sems(3), sems(n_groups), sems(n_groups), sems(n_groups), sems(2),
         ],
-        (grad_right, coef, zhat, inv, dzg, gain_in, proj_weight, *grad_left),
+        (grad_right, coef, short_zhat, inv, dzg, gain_in, proj_weight, *grad_left),
         near=(0, *range(7, 7 + n_pieces)),
         flops=2 * cells * width * 5 * hidden,
         moved=30 * cells * width,

time: 101 us -> 100 us (0.990)
  no operation moved by 1% of the time
where the time goes in v13:
time: 100 us; the launch traced here: 99.7 us
  starting transfers between devices  29.3 us (29%)
  Pallas kernels  25.1 us (25%)
  blocking collectives  24.9 us (25%)
  waiting for transfers between devices  19.4 us (19%)
    pallas_call x10, Pallas kernels, call(): pl.pallas_call(kernel, out_shape=[out if at in outs_near else pltpu.HBM(o...  25.1 us
    all_to_all x2, blocking collectives, exchange(): lax.all_to_all(values, within, split_axis=0, concat_axis=0, tiled=True)  24.9 us
    ppermute x16, waiting for transfers between devices, permute(): lax.ppermute(values, axes, [(at, at ^ distance) for at in range(size)])  19.4 us
    ppermute x16, starting transfers between devices, permute(): lax.ppermute(values, axes, [(at, at ^ distance) for at in range(size)])  18.3 us
    all_to_all x2, starting transfers between devices, exchange_all(): lax.all_to_all(flat, ('half', *within), split_axis=0, concat_axis=0, tile...  10.9 us
  transfers between devices with their start and end apart: 18, of which 12 were waited for; matrix products, arithmetic and copies ran while one was open for 0% of the time, Pallas kernels for 15%

profile of v13, /device:TPU:0, one launch (start us, length us, event | category | flops | bytes accessed | tf_op | source)
XLA Modules:
  0.0 99.7 jit_solution(18444663861707785764)
XLA Ops:
  0.6 3.2 %shard_map.113 = bf16[2,16,8,16,128]{4,3,2,1,0:T(8,128)(2,1)} custom-call(bf16[16,128,128]{2,1,0:T(8,128)(2,1)} %pair_h.5, s32[256]{0:T(256)} %mask_h.5, s32[1,256]{1,0:T(1,128)} %bitcast.26, f32[1,128]{1,0:T(1,128)} %bitcast.29, f32[1,128]{1,0:T(1,128)} %bitcast.34, bf16[128,512]{1,0:T(8,128)(2,1)} %proj_h.7), custom_call_target="tpu_custom_call" | custom-call | flops 201326592 | bytes 1310720 | tf_op jit(solution)/shard_map/pallas_call | solution.py:435
  3.8 7.3 %all-to-all-start = ((bf16[32,8,16,128]{3,2,1,0:T(8,128)(2,1)}), bf16[32,8,16,128]{3,2,1,0:T(8,128)(2,1)S(1)}, u32[]{:S(2)}, u32[]{:S(2)}) async-start(bf16[32,8,16,128]{3,2,1,0:T(8,128)(2,1)} %bitcast.25), calls=%async_computation | async-start | bytes 2097152 | tf_op jit(solution)/shard_map/all_to_all | solution.py:489
  11.1 2.3 %shard_map.116 = (bf16[8,8,16,128]{3,2,1,0:T(8,128)(2,1)S(1)}, bf16[8,8,16,128]{3,2,1,0:T(8,128)(2,1)S(1)}) custom-call(bf16[16,128,128]{2,1,0:T(8,128)(2,1)} %pair_h.5, s32[256]{0:T(256)} %mask_h.5, s32[1,256]{1,0:T(1,128)} %bitcast.27, f32[1,128]{1,0:T(1,128)} %bitcast.30, f32[1,128]{1,0:T(1,128)} %bitcast.35, bf16[128,512]{1,0:T(8,128)(2,1)} %proj_h.7), custom_call_target="tpu_custom_call" | custom-call | flops 201326592 | bytes 1310720 | tf_op jit(solution)/shard_map/pallas_call | solution.py:435
  15.1 1.8 %collective-permute-start.1 = (bf16[2,8,16,128]{3,2,1,0:T(8,128)(2,1)S(1)}, bf16[2,8,16,128]{3,2,1,0:T(8,128)(2,1)S(1)}, u32[]{:S(2)}, u32[]{:S(2)}) collective-permute-start(bf16[2,8,16,128]{3,2,1,0:T(8,128)(2,1)S(1)} %pad_maximum_fusion), channel_id=1, source_target_pairs={{0,1},{1,0},{4,5},{5,4},{8,9},{9,8},{12,13},{13,12},{2,3},{3,2},{6... | collective-permute-start | bytes 196616 | tf_op jit(solution)/shard_map/ppermute | solution.py:494
  16.9 1.5 %collective-permute-start.2 = (bf16[2,8,16,128]{3,2,1,0:T(8,128)(2,1)S(1)}, bf16[2,8,16,128]{3,2,1,0:T(8,128)(2,1)S(1)}, u32[]{:S(2)}, u32[]{:S(2)}) collective-permute-start(bf16[2,8,16,128]{3,2,1,0:T(8,128)(2,1)S(1)} %pad_maximum_fusion.1), channel_id=1, source_target_pairs={{0,4},{1,5},{4,0},{5,1},{8,12},{9,13},{12,8},{13,9},{2,6},{3,7},{6... | collective-permute-start | bytes 196616 | tf_op jit(solution)/shard_map/ppermute | solution.py:494
  18.8 1.8 %collective-permute-start.4 = (bf16[2,8,16,128]{3,2,1,0:T(8,128)(2,1)S(1)}, bf16[2,8,16,128]{3,2,1,0:T(8,128)(2,1)S(1)}, u32[]{:S(2)}, u32[]{:S(2)}) collective-permute-start(bf16[2,8,16,128]{3,2,1,0:T(8,128)(2,1)S(1)} %pad_maximum_fusion.3), channel_id=1, source_target_pairs={{0,8},{1,9},{4,12},{5,13},{8,0},{9,1},{12,4},{13,5},{2,10},{3,11},... | collective-permute-start | bytes 196616 | tf_op jit(solution)/shard_map/ppermute | solution.py:494
  20.6 1.5 %collective-permute-start.5 = (bf16[2,8,16,128]{3,2,1,0:T(8,128)(2,1)S(1)}, bf16[2,8,16,128]{3,2,1,0:T(8,128)(2,1)S(1)}, u32[]{:S(2)}, u32[]{:S(2)}) collective-permute-start(bf16[2,8,16,128]{3,2,1,0:T(8,128)(2,1)S(1)} %pad_maximum_fusion.4), channel_id=1, source_target_pairs={{0,9},{1,8},{4,13},{5,12},{8,1},{9,0},{12,5},{13,4},{2,11},{3,10},... | collective-permute-start | bytes 196616 | tf_op jit(solution)/shard_map/ppermute | solution.py:494
  22.8 1.7 %collective-permute-start.6 = (bf16[2,8,16,128]{3,2,1,0:T(8,128)(2,1)S(1)}, bf16[2,8,16,128]{3,2,1,0:T(8,128)(2,1)S(1)}, u32[]{:S(2)}, u32[]{:S(2)}) collective-permute-start(bf16[2,8,16,128]{3,2,1,0:T(8,128)(2,1)S(1)} %pad_maximum_fusion.5), channel_id=1, source_target_pairs={{0,12},{1,13},{4,8},{5,9},{8,4},{9,5},{12,0},{13,1},{2,14},{3,15},... | collective-permute-start | bytes 196616 | tf_op jit(solution)/shard_map/ppermute | solution.py:494
  25.8 4.8 %shard_map.114 = (f32[16,128,128]{2,1,0:T(8,128)}, bf16[16,128,128]{2,1,0:T(8,128)(2,1)}, f32[16,128]{1,0:T(8,128)}, f32[16,128,128]{2,1,0:T(8,128)}, f32[2048,128]{1,0:T(8,128)S(1)}) custom-call(bf16[16,128,128]{2,1,0:T(8,128)(2,1)} %pair_h.5, bf16[16,128,128]{2,1,0:T(8,128)(2,1)} %cot_h.3, f32[1,128]{1,0:T(1,128)} %bitcast.31, f32[1,128]{1,0:T(1,128)} %bitcast.36, ...), custom_call_target="tpu_custom_call" | custom-call | flops 268435456 | bytes 4194304 | tf_op jit(solution)/shard_map/pallas_call | solution.py:435
  30.6 3.2 %shard_map.115.after.coef_h = bf16[16,4,128,128]{3,2,1,0:T(8,128)(2,1)} custom-call(f32[16,128,128]{2,1,0:T(8,128)} %get-tuple-element.15.zhat_h, s32[256]{0:T(256)} %mask_h.5, s32[1,256]{1,0:T(1,128)} %bitcast.28, f32[1,128]{1,0:T(1,128)} %bitcast.32, f32[1,128]{1,0:T(1,128)} %bitcast.37, bf16[128,512]{1,0:T(8,128)(2,1)} %proj_h.7), custom_call_target="tpu_custom_call" | custom-call | flops 335544320 | bytes 4194304 | tf_op jit(solution)/shard_map/pallas_call | solution.py:435
  34.7 2.9 %collective-permute-done.7.refs_8_ = bf16[2,8,16,128]{3,2,1,0:T(8,128)(2,1)S(1)} collective-permute-done((bf16[2,8,16,128]{3,2,1,0:T(8,128)(2,1)S(1)}, bf16[2,8,16,128]{3,2,1,0:T(8,128)(2,1)S(1)}, u32[]{:S(2)}, u32[]{:S(2)}) %collective-permute-start.7) | collective-permute-done | bytes 65568 | tf_op jit(solution)/shard_map/ppermute | solution.py:494
  38.1 12.9 %all_to_all.20 = bf16[16,8,16,128]{3,2,1,0:T(8,128)(2,1)S(1)} all-to-all(bf16[16,8,16,128]{3,2,1,0:T(8,128)(2,1)S(1)} %bitcast.23), channel_id=1, replica_groups=mesh['grp'=1,'half'=2,'row'=4,'core'=2,'col'=2] {'row','core','col'}, dimensions={0} | all-to-all | bytes 1048576 | tf_op jit(solution)/shard_map/all_to_all | solution.py:485
  51.6 12.0 %all_to_all.21 = bf16[16,8,16,128]{3,2,1,0:T(8,128)(2,1)S(1)} all-to-all(bf16[16,8,16,128]{3,2,1,0:T(8,128)(2,1)S(1)} %bitcast.21), channel_id=1, replica_groups=mesh['grp'=1,'half'=2,'row'=4,'core'=2,'col'=2] {'row','core','col'}, dimensions={0} | all-to-all | bytes 1048576 | tf_op jit(solution)/shard_map/all_to_all | solution.py:485
  64.9 3.6 %all-to-all-start.3 = ((bf16[32,8,16,128]{3,2,1,0:T(8,128)(2,1)}), bf16[32,8,16,128]{3,2,1,0:T(8,128)(2,1)S(1)}, u32[]{:S(2)}, u32[]{:S(2)}) async-start(bf16[32,8,16,128]{3,2,1,0:T(8,128)(2,1)} %bitcast.24), calls=%async_computation.3 | async-start | bytes 2097152 | tf_op jit(solution)/shard_map/all_to_all | solution.py:489
  69.1 1.4 %collective-permute-done.8.refs_1_ = bf16[8,8,16,128]{3,2,1,0:T(8,128)(2,1)S(1)} collective-permute-done((bf16[8,8,16,128]{3,2,1,0:T(8,128)(2,1)S(1)}, bf16[8,8,16,128]{3,2,1,0:T(8,128)(2,1)S(1)}, u32[]{:S(2)}, u32[]{:S(2)}) %collective-permute-start.8) | collective-permute-done | bytes 262176 | tf_op jit(solution)/shard_map/ppermute | solution.py:494
  70.6 1.7 %collective-permute-start.9 = (bf16[2,8,16,128]{3,2,1,0:T(8,128)(2,1)S(1)}, bf16[2,8,16,128]{3,2,1,0:T(8,128)(2,1)S(1)}, u32[]{:S(2)}, u32[]{:S(2)}) collective-permute-start(bf16[2,8,16,128]{3,2,1,0:T(8,128)(2,1)S(1)} %pad_maximum_fusion.7), channel_id=1, source_target_pairs={{0,1},{1,0},{4,5},{5,4},{8,9},{9,8},{12,13},{13,12},{2,3},{3,2},{6... | collective-permute-start | bytes 196616 | tf_op jit(solution)/shard_map/ppermute | solution.py:494
  72.3 1.5 %collective-permute-start.10 = (bf16[2,8,16,128]{3,2,1,0:T(8,128)(2,1)S(1)}, bf16[2,8,16,128]{3,2,1,0:T(8,128)(2,1)S(1)}, u32[]{:S(2)}, u32[]{:S(2)}) collective-permute-start(bf16[2,8,16,128]{3,2,1,0:T(8,128)(2,1)S(1)} %pad_maximum_fusion.8), channel_id=1, source_target_pairs={{0,4},{1,5},{4,0},{5,1},{8,12},{9,13},{12,8},{13,9},{2,6},{3,7},{6... | collective-permute-start | bytes 196616 | tf_op jit(solution)/shard_map/ppermute | solution.py:494
  74.3 1.7 %collective-permute-start.12 = (bf16[2,8,16,128]{3,2,1,0:T(8,128)(2,1)S(1)}, bf16[2,8,16,128]{3,2,1,0:T(8,128)(2,1)S(1)}, u32[]{:S(2)}, u32[]{:S(2)}) collective-permute-start(bf16[2,8,16,128]{3,2,1,0:T(8,128)(2,1)S(1)} %pad_maximum_fusion.10), channel_id=1, source_target_pairs={{0,8},{1,9},{4,12},{5,13},{8,0},{9,1},{12,4},{13,5},{2,10},{3,11},... | collective-permute-start | bytes 196616 | tf_op jit(solution)/shard_map/ppermute | solution.py:494
  76.0 1.5 %collective-permute-start.13 = (bf16[2,8,16,128]{3,2,1,0:T(8,128)(2,1)S(1)}, bf16[2,8,16,128]{3,2,1,0:T(8,128)(2,1)S(1)}, u32[]{:S(2)}, u32[]{:S(2)}) collective-permute-start(bf16[2,8,16,128]{3,2,1,0:T(8,128)(2,1)S(1)} %pad_maximum_fusion.11), channel_id=1, source_target_pairs={{0,9},{1,8},{4,13},{5,12},{8,1},{9,0},{12,5},{13,4},{2,11},{3,10},... | collective-permute-start | bytes 196616 | tf_op jit(solution)/shard_map/ppermute | solution.py:494
  77.5 2.9 %collective-permute-done.9.refs_2_ = bf16[2,8,16,128]{3,2,1,0:T(8,128)(2,1)S(1)} collective-permute-done((bf16[2,8,16,128]{3,2,1,0:T(8,128)(2,1)S(1)}, bf16[2,8,16,128]{3,2,1,0:T(8,128)(2,1)S(1)}, u32[]{:S(2)}, u32[]{:S(2)}) %collective-permute-start.9) | collective-permute-done | bytes 65568 | tf_op jit(solution)/shard_map/ppermute | solution.py:494
  83.4 4.0 %shard_map.120 = (bf16[16,128,128]{2,1,0:T(8,128)(2,1)}, bf16[16,128,128]{2,1,0:T(8,128)(2,1)}) custom-call(bf16[128,16,128]{2,1,0:T(8,128)(2,1)S(1)} %bitcast.19, f32[16,128,128]{2,1,0:T(8,128)} %get-tuple-element.19.gate_h, bf16[16,128,128]{2,1,0:T(8,128)(2,1)} %cot_h.3, f32[1,128]{1,0:T(1,128)} %bitcast.39, f32[1,128]{1,0:T(1,128)} %bitcast.40, ...), custom_call_target="tpu_custom_call" | custom-call | flops 201326592 | bytes 3670016 | tf_op jit(solution)/shard_map/pallas_call | solution.py:435
  89.3 2.7 %collective-permute-done.14.refs_7_ = bf16[2,8,16,128]{3,2,1,0:T(8,128)(2,1)S(1)} collective-permute-done((bf16[2,8,16,128]{3,2,1,0:T(8,128)(2,1)S(1)}, bf16[2,8,16,128]{3,2,1,0:T(8,128)(2,1)S(1)}, u32[]{:S(2)}, u32[]{:S(2)}) %collective-permute-start.14) | collective-permute-done | bytes 65568 | tf_op jit(solution)/shard_map/ppermute | solution.py:494
  91.9 2.9 %collective-permute-done.15.refs_8_ = bf16[2,8,16,128]{3,2,1,0:T(8,128)(2,1)S(1)} collective-permute-done((bf16[2,8,16,128]{3,2,1,0:T(8,128)(2,1)S(1)}, bf16[2,8,16,128]{3,2,1,0:T(8,128)(2,1)S(1)}, u32[]{:S(2)}, u32[]{:S(2)}) %collective-permute-start.15) | collective-permute-done | bytes 65568 | tf_op jit(solution)/shard_map/ppermute | solution.py:494
  94.8 4.8 %shard_map.122 = bf16[16,128,128]{2,1,0:T(8,128)(2,1)} custom-call(bf16[2,16,8,16,128]{4,3,2,1,0:T(8,128)(2,1)S(1)} %bitcast.20, bf16[16,4,128,128]{3,2,1,0:T(8,128)(2,1)} %shard_map.115.after.coef_h, bf16[16,128,128]{2,1,0:T(8,128)(2,1)} %get-tuple-element.23.zhat_h, f32[16,128]{1,0:T(8,128)} %get-tuple-element.24.inv_h, ...), custom_call_target="tpu_custom_call" | custom-call | flops 335544320 | bytes 7864320 | tf_op jit(solution)/shard_map/pallas_call | solution.py:435
  (42 shorter events, 13.2 us)
Async XLA Ops:
  3.8 33.7 %all-to-all-start = ((bf16[32,8,16,128]{3,2,1,0:T(8,128)(2,1)}), bf16[32,8,16,128]{3,2,1,0:T(8,128)(2,1)S(1)}, u32[]{:S(2)}, u32[]{:S(2)}) async-start(bf16[32,8,16,128]{3,2,1,0:T(8,128)(2,1)} %bitcast.25), calls=%async_computation | async-start | bytes 2097152 | tf_op jit(solution)/shard_map/all_to_all | solution.py:489
  13.4 1.6 %collective-permute-start = (bf16[8,8,16,128]{3,2,1,0:T(8,128)(2,1)S(1)}, bf16[8,8,16,128]{3,2,1,0:T(8,128)(2,1)S(1)}, u32[]{:S(2)}, u32[]{:S(2)}) collective-permute-start(bf16[8,8,16,128]{3,2,1,0:T(8,128)(2,1)S(1)} %get-tuple-element.17), channel_id=1, source_target_pairs={{0,2},{2,0},{1,3},{3,1},{4,6},{6,4},{5,7},{7,5},{8,10},{10,8},{9,1... | collective-permute-start | bytes 786440 | tf_op jit(solution)/shard_map/ppermute | solution.py:494
  15.1 7.8 %collective-permute-start.1 = (bf16[2,8,16,128]{3,2,1,0:T(8,128)(2,1)S(1)}, bf16[2,8,16,128]{3,2,1,0:T(8,128)(2,1)S(1)}, u32[]{:S(2)}, u32[]{:S(2)}) collective-permute-start(bf16[2,8,16,128]{3,2,1,0:T(8,128)(2,1)S(1)} %pad_maximum_fusion), channel_id=1, source_target_pairs={{0,1},{1,0},{4,5},{5,4},{8,9},{9,8},{12,13},{13,12},{2,3},{3,2},{6... | collective-permute-start | bytes 196616 | tf_op jit(solution)/shard_map/ppermute | solution.py:494
  16.9 8.2 %collective-permute-start.2 = (bf16[2,8,16,128]{3,2,1,0:T(8,128)(2,1)S(1)}, bf16[2,8,16,128]{3,2,1,0:T(8,128)(2,1)S(1)}, u32[]{:S(2)}, u32[]{:S(2)}) collective-permute-start(bf16[2,8,16,128]{3,2,1,0:T(8,128)(2,1)S(1)} %pad_maximum_fusion.1), channel_id=1, source_target_pairs={{0,4},{1,5},{4,0},{5,1},{8,12},{9,13},{12,8},{13,9},{2,6},{3,7},{6... | collective-permute-start | bytes 196616 | tf_op jit(solution)/shard_map/ppermute | solution.py:494
  18.4 15.4 %collective-permute-start.3 = (bf16[2,8,16,128]{3,2,1,0:T(8,128)(2,1)S(1)}, bf16[2,8,16,128]{3,2,1,0:T(8,128)(2,1)S(1)}, u32[]{:S(2)}, u32[]{:S(2)}) collective-permute-start(bf16[2,8,16,128]{3,2,1,0:T(8,128)(2,1)S(1)} %pad_maximum_fusion.2), channel_id=1, source_target_pairs={{0,5},{1,4},{4,1},{5,0},{8,13},{9,12},{12,9},{13,8},{2,7},{3,6},{6... | collective-permute-start | bytes 196616 | tf_op jit(solution)/shard_map/ppermute | solution.py:494
  18.8 15.1 %collective-permute-start.4 = (bf16[2,8,16,128]{3,2,1,0:T(8,128)(2,1)S(1)}, bf16[2,8,16,128]{3,2,1,0:T(8,128)(2,1)S(1)}, u32[]{:S(2)}, u32[]{:S(2)}) collective-permute-start(bf16[2,8,16,128]{3,2,1,0:T(8,128)(2,1)S(1)} %pad_maximum_fusion.3), channel_id=1, source_target_pairs={{0,8},{1,9},{4,12},{5,13},{8,0},{9,1},{12,4},{13,5},{2,10},{3,11},... | collective-permute-start | bytes 196616 | tf_op jit(solution)/shard_map/ppermute | solution.py:494
  20.6 13.2 %collective-permute-start.5 = (bf16[2,8,16,128]{3,2,1,0:T(8,128)(2,1)S(1)}, bf16[2,8,16,128]{3,2,1,0:T(8,128)(2,1)S(1)}, u32[]{:S(2)}, u32[]{:S(2)}) collective-permute-start(bf16[2,8,16,128]{3,2,1,0:T(8,128)(2,1)S(1)} %pad_maximum_fusion.4), channel_id=1, source_target_pairs={{0,9},{1,8},{4,13},{5,12},{8,1},{9,0},{12,5},{13,4},{2,11},{3,10},... | collective-permute-start | bytes 196616 | tf_op jit(solution)/shard_map/ppermute | solution.py:494
  22.8 11.8 %collective-permute-start.6 = (bf16[2,8,16,128]{3,2,1,0:T(8,128)(2,1)S(1)}, bf16[2,8,16,128]{3,2,1,0:T(8,128)(2,1)S(1)}, u32[]{:S(2)}, u32[]{:S(2)}) collective-permute-start(bf16[2,8,16,128]{3,2,1,0:T(8,128)(2,1)S(1)} %pad_maximum_fusion.5), channel_id=1, source_target_pairs={{0,12},{1,13},{4,8},{5,9},{8,4},{9,5},{12,0},{13,1},{2,14},{3,15},... | collective-permute-start | bytes 196616 | tf_op jit(solution)/shard_map/ppermute | solution.py:494
  25.1 12.5 %collective-permute-start.7 = (bf16[2,8,16,128]{3,2,1,0:T(8,128)(2,1)S(1)}, bf16[2,8,16,128]{3,2,1,0:T(8,128)(2,1)S(1)}, u32[]{:S(2)}, u32[]{:S(2)}) collective-permute-start(bf16[2,8,16,128]{3,2,1,0:T(8,128)(2,1)S(1)} %pad_maximum_fusion.6), channel_id=1, source_target_pairs={{0,13},{1,12},{4,9},{5,8},{8,5},{9,4},{12,1},{13,0},{2,15},{3,14},... | collective-permute-start | bytes 196616 | tf_op jit(solution)/shard_map/ppermute | solution.py:494
  64.9 29.9 %all-to-all-start.3 = ((bf16[32,8,16,128]{3,2,1,0:T(8,128)(2,1)}), bf16[32,8,16,128]{3,2,1,0:T(8,128)(2,1)S(1)}, u32[]{:S(2)}, u32[]{:S(2)}) async-start(bf16[32,8,16,128]{3,2,1,0:T(8,128)(2,1)} %bitcast.24), calls=%async_computation.3 | async-start | bytes 2097152 | tf_op jit(solution)/shard_map/all_to_all | solution.py:489
  69.0 1.6 %collective-permute-start.8 = (bf16[8,8,16,128]{3,2,1,0:T(8,128)(2,1)S(1)}, bf16[8,8,16,128]{3,2,1,0:T(8,128)(2,1)S(1)}, u32[]{:S(2)}, u32[]{:S(2)}) collective-permute-start(bf16[8,8,16,128]{3,2,1,0:T(8,128)(2,1)S(1)} %get-tuple-element.27), channel_id=1, source_target_pairs={{0,2},{2,0},{1,3},{3,1},{4,6},{6,4},{5,7},{7,5},{8,10},{10,8},{9,1... | collective-permute-start | bytes 786440 | tf_op jit(solution)/shard_map/ppermute | solution.py:494
  70.6 9.8 %collective-permute-start.9 = (bf16[2,8,16,128]{3,2,1,0:T(8,128)(2,1)S(1)}, bf16[2,8,16,128]{3,2,1,0:T(8,128)(2,1)S(1)}, u32[]{:S(2)}, u32[]{:S(2)}) collective-permute-start(bf16[2,8,16,128]{3,2,1,0:T(8,128)(2,1)S(1)} %pad_maximum_fusion.7), channel_id=1, source_target_pairs={{0,1},{1,0},{4,5},{5,4},{8,9},{9,8},{12,13},{13,12},{2,3},{3,2},{6... | collective-permute-start | bytes 196616 | tf_op jit(solution)/shard_map/ppermute | solution.py:494
  72.3 9.9 %collective-permute-start.10 = (bf16[2,8,16,128]{3,2,1,0:T(8,128)(2,1)S(1)}, bf16[2,8,16,128]{3,2,1,0:T(8,128)(2,1)S(1)}, u32[]{:S(2)}, u32[]{:S(2)}) collective-permute-start(bf16[2,8,16,128]{3,2,1,0:T(8,128)(2,1)S(1)} %pad_maximum_fusion.8), channel_id=1, source_target_pairs={{0,4},{1,5},{4,0},{5,1},{8,12},{9,13},{12,8},{13,9},{2,6},{3,7},{6... | collective-permute-start | bytes 196616 | tf_op jit(solution)/shard_map/ppermute | solution.py:494
  73.8 13.6 %collective-permute-start.11 = (bf16[2,8,16,128]{3,2,1,0:T(8,128)(2,1)S(1)}, bf16[2,8,16,128]{3,2,1,0:T(8,128)(2,1)S(1)}, u32[]{:S(2)}, u32[]{:S(2)}) collective-permute-start(bf16[2,8,16,128]{3,2,1,0:T(8,128)(2,1)S(1)} %pad_maximum_fusion.9), channel_id=1, source_target_pairs={{0,5},{1,4},{4,1},{5,0},{8,13},{9,12},{12,9},{13,8},{2,7},{3,6},{6... | collective-permute-start | bytes 196616 | tf_op jit(solution)/shard_map/ppermute | solution.py:494
  74.3 13.6 %collective-permute-start.12 = (bf16[2,8,16,128]{3,2,1,0:T(8,128)(2,1)S(1)}, bf16[2,8,16,128]{3,2,1,0:T(8,128)(2,1)S(1)}, u32[]{:S(2)}, u32[]{:S(2)}) collective-permute-start(bf16[2,8,16,128]{3,2,1,0:T(8,128)(2,1)S(1)} %pad_maximum_fusion.10), channel_id=1, source_target_pairs={{0,8},{1,9},{4,12},{5,13},{8,0},{9,1},{12,4},{13,5},{2,10},{3,11},... | collective-permute-start | bytes 196616 | tf_op jit(solution)/shard_map/ppermute | solution.py:494
  76.0 13.3 %collective-permute-start.13 = (bf16[2,8,16,128]{3,2,1,0:T(8,128)(2,1)S(1)}, bf16[2,8,16,128]{3,2,1,0:T(8,128)(2,1)S(1)}, u32[]{:S(2)}, u32[]{:S(2)}) collective-permute-start(bf16[2,8,16,128]{3,2,1,0:T(8,128)(2,1)S(1)} %pad_maximum_fusion.11), channel_id=1, source_target_pairs={{0,9},{1,8},{4,13},{5,12},{8,1},{9,0},{12,5},{13,4},{2,11},{3,10},... | collective-permute-start | bytes 196616 | tf_op jit(solution)/shard_map/ppermute | solution.py:494
  80.4 11.5 %collective-permute-start.14 = (bf16[2,8,16,128]{3,2,1,0:T(8,128)(2,1)S(1)}, bf16[2,8,16,128]{3,2,1,0:T(8,128)(2,1)S(1)}, u32[]{:S(2)}, u32[]{:S(2)}) collective-permute-start(bf16[2,8,16,128]{3,2,1,0:T(8,128)(2,1)S(1)} %pad_maximum_fusion.12), channel_id=1, source_target_pairs={{0,12},{1,13},{4,8},{5,9},{8,4},{9,5},{12,0},{13,1},{2,14},{3,15},... | collective-permute-start | bytes 196616 | tf_op jit(solution)/shard_map/ppermute | solution.py:494
  82.2 12.6 %collective-permute-start.15 = (bf16[2,8,16,128]{3,2,1,0:T(8,128)(2,1)S(1)}, bf16[2,8,16,128]{3,2,1,0:T(8,128)(2,1)S(1)}, u32[]{:S(2)}, u32[]{:S(2)}) collective-permute-start(bf16[2,8,16,128]{3,2,1,0:T(8,128)(2,1)S(1)} %pad_maximum_fusion.13), channel_id=1, source_target_pairs={{0,13},{1,12},{4,9},{5,8},{8,5},{9,4},{12,1},{13,0},{2,15},{3,14},... | collective-permute-start | bytes 196616 | tf_op jit(solution)/shard_map/ppermute | solution.py:494

commit v14 on v13

--- a/solution.py
+++ b/solution.py
@@ -134,11 +134,13 @@
         zbar[:, at * cols : (at + size) * cols] = (zhat * gain_b + bias_b).astype(BF16)
 
     def channels(first, count):
+        block = jnp.concatenate(
+            [weight[first : first + count], weight[hidden + first : hidden + first + count]], axis=0
+        )
         for at, size in groups:
-            z = zbar[:, at * cols : (at + size) * cols]
-            p = dot(weight[first : first + count], z)
-            q = dot(weight[hidden + first : hidden + first + count], z)
-            values = sigmoid(p) * q * pair_mask(mask_s, mask_v, at, size, rows, cols)
+            proj = dot(block, zbar[:, at * cols : (at + size) * cols])
+            pm = pair_mask(mask_s, mask_v, at, size, rows, cols)
+            values = sigmoid(proj[:count]) * proj[count:] * pm
             for r in range(size):
                 plane[pl.ds(first * rows + at + r, count, stride=rows), :] = values[
                     :, r * cols : (r + 1) * cols
@@ -150,7 +152,7 @@
         return
     (out_h,), (ready, out_sems) = outs, more
     n_place, share = ready.shape[:2]
-    size = n_place // math.gcd(n_place, 4)
+    size = n_place // math.gcd(n_place, 2)
     leaving = []
     for n, at in enumerate(range(0, n_place, size)):
         channels(at * share, size * share)
@@ -369,7 +371,6 @@
     rows, cols, width = out.shape
     hidden = left.shape[0] // rows
     groups = groups_of(rows)
-    small = start(sems, [(gain_h, gain), (proj_h, proj_weight), (inv_h, inv)])
     ahead = rows // math.gcd(rows, 2)
     blocks = [
         [
@@ -382,13 +383,16 @@
         ]
         for n, (at, size) in enumerate(groups)
     ]
-    for copy in sum(blocks[:2], []):
+    for copy in blocks[0]:
         copy.start()
+    small = start(sems, [(gain_h, gain), (proj_h, proj_weight), (inv_h, inv)])
     arrived = received(pieces, n_chip)
     length = left.shape[0] // len(arrived)
     for number, piece in arrived:
         first = pl.multiple_of(number * length, length)
         left[pl.ds(first, length), :] = piece.astype(F32).reshape(length, cols)
+    for copy in sum(blocks[1:], []):
+        copy.start()
     total = grads[0].astype(F32)
     for half in range(1, grads.shape[0]):
         total = total + grads[half].astype(F32)
@@ -396,14 +400,14 @@
     wait(small)
     gain_b = jnp.concatenate([down_lanes(gain[...], cols)] * groups[0][1], axis=1)
     leaving = []
-    for copy in sum(blocks[2:], []):
-        copy.start()
     for n, (at, size) in enumerate(groups):
+        both = [
+            [plane[pl.ds(at + r, hidden, stride=rows), :].astype(BF16) for plane in (left, right)]
+            for r in range(size)
+        ]
         wait(blocks[n])
         columns = []
-        for r in range(size):
-            gl = left[pl.ds(at + r, hidden, stride=rows), :].astype(BF16)
-            gr = right[pl.ds(at + r, hidden, stride=rows), :].astype(BF16)
+        for r, (gl, gr) in enumerate(both):
             columns.append(
                 jnp.concatenate(
                     [g * coef[at + r, part] for part, g in enumerate((gl, gl, gr, gr))], axis=0
@@ -532,7 +536,7 @@
     (right,) = front(
         2,
         (shape(n_half, n_place, share, rows, cols),),
-        [everywhere, pltpu.SemaphoreType.DMA((n_half, math.gcd(n_place, 4)))],
+        [everywhere, pltpu.SemaphoreType.DMA((n_half, math.gcd(n_place, 2)))],
         (),
     )
     right = exchange_all(right).reshape(n_half, n_line, n_col, share, rows, cols)

time: 100 us -> 101 us (1.010)
  no operation moved by 1% of the time
where the time goes in v14:
time: 101 us; the launch traced here: 100 us
  starting transfers between devices  29.1 us (29%)
  Pallas kernels  25.7 us (25%)
  blocking collectives  24.9 us (25%)
  waiting for transfers between devices  19.5 us (19%)
    pallas_call x10, Pallas kernels, call(): pl.pallas_call(kernel, out_shape=[out if at in outs_near else pltpu.HBM(o...  25.7 us
    all_to_all x2, blocking collectives, exchange(): lax.all_to_all(values, within, split_axis=0, concat_axis=0, tiled=True)  24.9 us
    ppermute x16, waiting for transfers between devices, permute(): lax.ppermute(values, axes, [(at, at ^ distance) for at in range(size)])  19.5 us
    ppermute x16, starting transfers between devices, permute(): lax.ppermute(values, axes, [(at, at ^ distance) for at in range(size)])  18.2 us
    all_to_all x2, starting transfers between devices, exchange_all(): lax.all_to_all(flat, ('half', *within), split_axis=0, concat_axis=0, tile...  10.9 us
  transfers between devices with their start and end apart: 18, of which 12 were waited for; matrix products, arithmetic and copies ran while one was open for 0% of the time, Pallas kernels for 15%

profile of v14, /device:TPU:0, one launch (start us, length us, event | category | flops | bytes accessed | tf_op | source)
XLA Modules:
  0.0 100.4 jit_solution(13182205076889048229)
XLA Ops:
  0.6 3.1 %shard_map.113 = bf16[2,16,8,16,128]{4,3,2,1,0:T(8,128)(2,1)} custom-call(bf16[16,128,128]{2,1,0:T(8,128)(2,1)} %pair_h.5, s32[256]{0:T(256)} %mask_h.5, s32[1,256]{1,0:T(1,128)} %bitcast.26, f32[1,128]{1,0:T(1,128)} %bitcast.29, f32[1,128]{1,0:T(1,128)} %bitcast.34, bf16[128,512]{1,0:T(8,128)(2,1)} %proj_h.7), custom_call_target="tpu_custom_call" | custom-call | flops 201326592 | bytes 1310720 | tf_op jit(solution)/shard_map/pallas_call | solution.py:439
  3.7 7.3 %all-to-all-start = ((bf16[32,8,16,128]{3,2,1,0:T(8,128)(2,1)}), bf16[32,8,16,128]{3,2,1,0:T(8,128)(2,1)S(1)}, u32[]{:S(2)}, u32[]{:S(2)}) async-start(bf16[32,8,16,128]{3,2,1,0:T(8,128)(2,1)} %bitcast.25), calls=%async_computation | async-start | bytes 2097152 | tf_op jit(solution)/shard_map/all_to_all | solution.py:493
  11.0 2.2 %shard_map.116 = (bf16[8,8,16,128]{3,2,1,0:T(8,128)(2,1)S(1)}, bf16[8,8,16,128]{3,2,1,0:T(8,128)(2,1)S(1)}) custom-call(bf16[16,128,128]{2,1,0:T(8,128)(2,1)} %pair_h.5, s32[256]{0:T(256)} %mask_h.5, s32[1,256]{1,0:T(1,128)} %bitcast.27, f32[1,128]{1,0:T(1,128)} %bitcast.30, f32[1,128]{1,0:T(1,128)} %bitcast.35, bf16[128,512]{1,0:T(8,128)(2,1)} %proj_h.7), custom_call_target="tpu_custom_call" | custom-call | flops 201326592 | bytes 1310720 | tf_op jit(solution)/shard_map/pallas_call | solution.py:439
  14.9 1.8 %collective-permute-start.1 = (bf16[2,8,16,128]{3,2,1,0:T(8,128)(2,1)S(1)}, bf16[2,8,16,128]{3,2,1,0:T(8,128)(2,1)S(1)}, u32[]{:S(2)}, u32[]{:S(2)}) collective-permute-start(bf16[2,8,16,128]{3,2,1,0:T(8,128)(2,1)S(1)} %pad_maximum_fusion), channel_id=1, source_target_pairs={{0,1},{1,0},{4,5},{5,4},{8,9},{9,8},{12,13},{13,12},{2,3},{3,2},{6... | collective-permute-start | bytes 196616 | tf_op jit(solution)/shard_map/ppermute | solution.py:498
  16.8 1.5 %collective-permute-start.2 = (bf16[2,8,16,128]{3,2,1,0:T(8,128)(2,1)S(1)}, bf16[2,8,16,128]{3,2,1,0:T(8,128)(2,1)S(1)}, u32[]{:S(2)}, u32[]{:S(2)}) collective-permute-start(bf16[2,8,16,128]{3,2,1,0:T(8,128)(2,1)S(1)} %pad_maximum_fusion.1), channel_id=1, source_target_pairs={{0,4},{1,5},{4,0},{5,1},{8,12},{9,13},{12,8},{13,9},{2,6},{3,7},{6... | collective-permute-start | bytes 196616 | tf_op jit(solution)/shard_map/ppermute | solution.py:498
  18.6 1.8 %collective-permute-start.4 = (bf16[2,8,16,128]{3,2,1,0:T(8,128)(2,1)S(1)}, bf16[2,8,16,128]{3,2,1,0:T(8,128)(2,1)S(1)}, u32[]{:S(2)}, u32[]{:S(2)}) collective-permute-start(bf16[2,8,16,128]{3,2,1,0:T(8,128)(2,1)S(1)} %pad_maximum_fusion.3), channel_id=1, source_target_pairs={{0,8},{1,9},{4,12},{5,13},{8,0},{9,1},{12,4},{13,5},{2,10},{3,11},... | collective-permute-start | bytes 196616 | tf_op jit(solution)/shard_map/ppermute | solution.py:498
  20.5 1.5 %collective-permute-start.5 = (bf16[2,8,16,128]{3,2,1,0:T(8,128)(2,1)S(1)}, bf16[2,8,16,128]{3,2,1,0:T(8,128)(2,1)S(1)}, u32[]{:S(2)}, u32[]{:S(2)}) collective-permute-start(bf16[2,8,16,128]{3,2,1,0:T(8,128)(2,1)S(1)} %pad_maximum_fusion.4), channel_id=1, source_target_pairs={{0,9},{1,8},{4,13},{5,12},{8,1},{9,0},{12,5},{13,4},{2,11},{3,10},... | collective-permute-start | bytes 196616 | tf_op jit(solution)/shard_map/ppermute | solution.py:498
  22.8 1.6 %collective-permute-start.6 = (bf16[2,8,16,128]{3,2,1,0:T(8,128)(2,1)S(1)}, bf16[2,8,16,128]{3,2,1,0:T(8,128)(2,1)S(1)}, u32[]{:S(2)}, u32[]{:S(2)}) collective-permute-start(bf16[2,8,16,128]{3,2,1,0:T(8,128)(2,1)S(1)} %pad_maximum_fusion.5), channel_id=1, source_target_pairs={{0,12},{1,13},{4,8},{5,9},{8,4},{9,5},{12,0},{13,1},{2,14},{3,15},... | collective-permute-start | bytes 196616 | tf_op jit(solution)/shard_map/ppermute | solution.py:498
  25.6 4.8 %shard_map.114 = (f32[16,128,128]{2,1,0:T(8,128)}, bf16[16,128,128]{2,1,0:T(8,128)(2,1)}, f32[16,128]{1,0:T(8,128)}, f32[16,128,128]{2,1,0:T(8,128)}, f32[2048,128]{1,0:T(8,128)S(1)}) custom-call(bf16[16,128,128]{2,1,0:T(8,128)(2,1)} %pair_h.5, bf16[16,128,128]{2,1,0:T(8,128)(2,1)} %cot_h.3, f32[1,128]{1,0:T(1,128)} %bitcast.31, f32[1,128]{1,0:T(1,128)} %bitcast.36, ...), custom_call_target="tpu_custom_call" | custom-call | flops 268435456 | bytes 4194304 | tf_op jit(solution)/shard_map/pallas_call | solution.py:439
  30.5 3.2 %shard_map.115.after.coef_h = bf16[16,4,128,128]{3,2,1,0:T(8,128)(2,1)} custom-call(f32[16,128,128]{2,1,0:T(8,128)} %get-tuple-element.15.zhat_h, s32[256]{0:T(256)} %mask_h.5, s32[1,256]{1,0:T(1,128)} %bitcast.28, f32[1,128]{1,0:T(1,128)} %bitcast.32, f32[1,128]{1,0:T(1,128)} %bitcast.37, bf16[128,512]{1,0:T(8,128)(2,1)} %proj_h.7), custom_call_target="tpu_custom_call" | custom-call | flops 335544320 | bytes 4194304 | tf_op jit(solution)/shard_map/pallas_call | solution.py:439
  34.6 2.9 %collective-permute-done.7.refs_8_ = bf16[2,8,16,128]{3,2,1,0:T(8,128)(2,1)S(1)} collective-permute-done((bf16[2,8,16,128]{3,2,1,0:T(8,128)(2,1)S(1)}, bf16[2,8,16,128]{3,2,1,0:T(8,128)(2,1)S(1)}, u32[]{:S(2)}, u32[]{:S(2)}) %collective-permute-start.7) | collective-permute-done | bytes 65568 | tf_op jit(solution)/shard_map/ppermute | solution.py:498
  38.0 12.9 %all_to_all.20 = bf16[16,8,16,128]{3,2,1,0:T(8,128)(2,1)S(1)} all-to-all(bf16[16,8,16,128]{3,2,1,0:T(8,128)(2,1)S(1)} %bitcast.23), channel_id=1, replica_groups=mesh['grp'=1,'half'=2,'row'=4,'core'=2,'col'=2] {'row','core','col'}, dimensions={0} | all-to-all | bytes 1048576 | tf_op jit(solution)/shard_map/all_to_all | solution.py:489
  51.5 12.0 %all_to_all.21 = bf16[16,8,16,128]{3,2,1,0:T(8,128)(2,1)S(1)} all-to-all(bf16[16,8,16,128]{3,2,1,0:T(8,128)(2,1)S(1)} %bitcast.21), channel_id=1, replica_groups=mesh['grp'=1,'half'=2,'row'=4,'core'=2,'col'=2] {'row','core','col'}, dimensions={0} | all-to-all | bytes 1048576 | tf_op jit(solution)/shard_map/all_to_all | solution.py:489
  64.8 3.6 %all-to-all-start.3 = ((bf16[32,8,16,128]{3,2,1,0:T(8,128)(2,1)}), bf16[32,8,16,128]{3,2,1,0:T(8,128)(2,1)S(1)}, u32[]{:S(2)}, u32[]{:S(2)}) async-start(bf16[32,8,16,128]{3,2,1,0:T(8,128)(2,1)} %bitcast.24), calls=%async_computation.3 | async-start | bytes 2097152 | tf_op jit(solution)/shard_map/all_to_all | solution.py:493
  69.0 1.4 %collective-permute-done.8.refs_1_ = bf16[8,8,16,128]{3,2,1,0:T(8,128)(2,1)S(1)} collective-permute-done((bf16[8,8,16,128]{3,2,1,0:T(8,128)(2,1)S(1)}, bf16[8,8,16,128]{3,2,1,0:T(8,128)(2,1)S(1)}, u32[]{:S(2)}, u32[]{:S(2)}) %collective-permute-start.8) | collective-permute-done | bytes 262176 | tf_op jit(solution)/shard_map/ppermute | solution.py:498
  70.5 1.7 %collective-permute-start.9 = (bf16[2,8,16,128]{3,2,1,0:T(8,128)(2,1)S(1)}, bf16[2,8,16,128]{3,2,1,0:T(8,128)(2,1)S(1)}, u32[]{:S(2)}, u32[]{:S(2)}) collective-permute-start(bf16[2,8,16,128]{3,2,1,0:T(8,128)(2,1)S(1)} %pad_maximum_fusion.7), channel_id=1, source_target_pairs={{0,1},{1,0},{4,5},{5,4},{8,9},{9,8},{12,13},{13,12},{2,3},{3,2},{6... | collective-permute-start | bytes 196616 | tf_op jit(solution)/shard_map/ppermute | solution.py:498
  72.2 1.5 %collective-permute-start.10 = (bf16[2,8,16,128]{3,2,1,0:T(8,128)(2,1)S(1)}, bf16[2,8,16,128]{3,2,1,0:T(8,128)(2,1)S(1)}, u32[]{:S(2)}, u32[]{:S(2)}) collective-permute-start(bf16[2,8,16,128]{3,2,1,0:T(8,128)(2,1)S(1)} %pad_maximum_fusion.8), channel_id=1, source_target_pairs={{0,4},{1,5},{4,0},{5,1},{8,12},{9,13},{12,8},{13,9},{2,6},{3,7},{6... | collective-permute-start | bytes 196616 | tf_op jit(solution)/shard_map/ppermute | solution.py:498
  74.2 1.7 %collective-permute-start.12 = (bf16[2,8,16,128]{3,2,1,0:T(8,128)(2,1)S(1)}, bf16[2,8,16,128]{3,2,1,0:T(8,128)(2,1)S(1)}, u32[]{:S(2)}, u32[]{:S(2)}) collective-permute-start(bf16[2,8,16,128]{3,2,1,0:T(8,128)(2,1)S(1)} %pad_maximum_fusion.10), channel_id=1, source_target_pairs={{0,8},{1,9},{4,12},{5,13},{8,0},{9,1},{12,4},{13,5},{2,10},{3,11},... | collective-permute-start | bytes 196616 | tf_op jit(solution)/shard_map/ppermute | solution.py:498
  75.9 1.5 %collective-permute-start.13 = (bf16[2,8,16,128]{3,2,1,0:T(8,128)(2,1)S(1)}, bf16[2,8,16,128]{3,2,1,0:T(8,128)(2,1)S(1)}, u32[]{:S(2)}, u32[]{:S(2)}) collective-permute-start(bf16[2,8,16,128]{3,2,1,0:T(8,128)(2,1)S(1)} %pad_maximum_fusion.11), channel_id=1, source_target_pairs={{0,9},{1,8},{4,13},{5,12},{8,1},{9,0},{12,5},{13,4},{2,11},{3,10},... | collective-permute-start | bytes 196616 | tf_op jit(solution)/shard_map/ppermute | solution.py:498
  77.4 2.9 %collective-permute-done.9.refs_2_ = bf16[2,8,16,128]{3,2,1,0:T(8,128)(2,1)S(1)} collective-permute-done((bf16[2,8,16,128]{3,2,1,0:T(8,128)(2,1)S(1)}, bf16[2,8,16,128]{3,2,1,0:T(8,128)(2,1)S(1)}, u32[]{:S(2)}, u32[]{:S(2)}) %collective-permute-start.9) | collective-permute-done | bytes 65568 | tf_op jit(solution)/shard_map/ppermute | solution.py:498
  83.3 4.0 %shard_map.120 = (bf16[16,128,128]{2,1,0:T(8,128)(2,1)}, bf16[16,128,128]{2,1,0:T(8,128)(2,1)}) custom-call(bf16[128,16,128]{2,1,0:T(8,128)(2,1)S(1)} %bitcast.19, f32[16,128,128]{2,1,0:T(8,128)} %get-tuple-element.19.gate_h, bf16[16,128,128]{2,1,0:T(8,128)(2,1)} %cot_h.3, f32[1,128]{1,0:T(1,128)} %bitcast.39, f32[1,128]{1,0:T(1,128)} %bitcast.40, ...), custom_call_target="tpu_custom_call" | custom-call | flops 201326592 | bytes 3670016 | tf_op jit(solution)/shard_map/pallas_call | solution.py:439
  89.2 2.7 %collective-permute-done.14.refs_7_ = bf16[2,8,16,128]{3,2,1,0:T(8,128)(2,1)S(1)} collective-permute-done((bf16[2,8,16,128]{3,2,1,0:T(8,128)(2,1)S(1)}, bf16[2,8,16,128]{3,2,1,0:T(8,128)(2,1)S(1)}, u32[]{:S(2)}, u32[]{:S(2)}) %collective-permute-start.14) | collective-permute-done | bytes 65568 | tf_op jit(solution)/shard_map/ppermute | solution.py:498
  91.8 2.9 %collective-permute-done.15.refs_8_ = bf16[2,8,16,128]{3,2,1,0:T(8,128)(2,1)S(1)} collective-permute-done((bf16[2,8,16,128]{3,2,1,0:T(8,128)(2,1)S(1)}, bf16[2,8,16,128]{3,2,1,0:T(8,128)(2,1)S(1)}, u32[]{:S(2)}, u32[]{:S(2)}) %collective-permute-start.15) | collective-permute-done | bytes 65568 | tf_op jit(solution)/shard_map/ppermute | solution.py:498
  94.7 5.5 %shard_map.122 = bf16[16,128,128]{2,1,0:T(8,128)(2,1)} custom-call(bf16[2,16,8,16,128]{4,3,2,1,0:T(8,128)(2,1)S(1)} %bitcast.20, bf16[16,4,128,128]{3,2,1,0:T(8,128)(2,1)} %shard_map.115.after.coef_h, bf16[16,128,128]{2,1,0:T(8,128)(2,1)} %get-tuple-element.23.zhat_h, f32[16,128]{1,0:T(8,128)} %get-tuple-element.24.inv_h, ...), custom_call_target="tpu_custom_call" | custom-call | flops 335544320 | bytes 7864320 | tf_op jit(solution)/shard_map/pallas_call | solution.py:439
  (42 shorter events, 13.3 us)
Async XLA Ops:
  3.7 33.7 %all-to-all-start = ((bf16[32,8,16,128]{3,2,1,0:T(8,128)(2,1)}), bf16[32,8,16,128]{3,2,1,0:T(8,128)(2,1)S(1)}, u32[]{:S(2)}, u32[]{:S(2)}) async-start(bf16[32,8,16,128]{3,2,1,0:T(8,128)(2,1)} %bitcast.25), calls=%async_computation | async-start | bytes 2097152 | tf_op jit(solution)/shard_map/all_to_all | solution.py:493
  13.3 1.6 %collective-permute-start = (bf16[8,8,16,128]{3,2,1,0:T(8,128)(2,1)S(1)}, bf16[8,8,16,128]{3,2,1,0:T(8,128)(2,1)S(1)}, u32[]{:S(2)}, u32[]{:S(2)}) collective-permute-start(bf16[8,8,16,128]{3,2,1,0:T(8,128)(2,1)S(1)} %get-tuple-element.17), channel_id=1, source_target_pairs={{0,2},{2,0},{1,3},{3,1},{4,6},{6,4},{5,7},{7,5},{8,10},{10,8},{9,1... | collective-permute-start | bytes 786440 | tf_op jit(solution)/shard_map/ppermute | solution.py:498
  14.9 7.9 %collective-permute-start.1 = (bf16[2,8,16,128]{3,2,1,0:T(8,128)(2,1)S(1)}, bf16[2,8,16,128]{3,2,1,0:T(8,128)(2,1)S(1)}, u32[]{:S(2)}, u32[]{:S(2)}) collective-permute-start(bf16[2,8,16,128]{3,2,1,0:T(8,128)(2,1)S(1)} %pad_maximum_fusion), channel_id=1, source_target_pairs={{0,1},{1,0},{4,5},{5,4},{8,9},{9,8},{12,13},{13,12},{2,3},{3,2},{6... | collective-permute-start | bytes 196616 | tf_op jit(solution)/shard_map/ppermute | solution.py:498
  16.8 8.2 %collective-permute-start.2 = (bf16[2,8,16,128]{3,2,1,0:T(8,128)(2,1)S(1)}, bf16[2,8,16,128]{3,2,1,0:T(8,128)(2,1)S(1)}, u32[]{:S(2)}, u32[]{:S(2)}) collective-permute-start(bf16[2,8,16,128]{3,2,1,0:T(8,128)(2,1)S(1)} %pad_maximum_fusion.1), channel_id=1, source_target_pairs={{0,4},{1,5},{4,0},{5,1},{8,12},{9,13},{12,8},{13,9},{2,6},{3,7},{6... | collective-permute-start | bytes 196616 | tf_op jit(solution)/shard_map/ppermute | solution.py:498
  18.3 15.4 %collective-permute-start.3 = (bf16[2,8,16,128]{3,2,1,0:T(8,128)(2,1)S(1)}, bf16[2,8,16,128]{3,2,1,0:T(8,128)(2,1)S(1)}, u32[]{:S(2)}, u32[]{:S(2)}) collective-permute-start(bf16[2,8,16,128]{3,2,1,0:T(8,128)(2,1)S(1)} %pad_maximum_fusion.2), channel_id=1, source_target_pairs={{0,5},{1,4},{4,1},{5,0},{8,13},{9,12},{12,9},{13,8},{2,7},{3,6},{6... | collective-permute-start | bytes 196616 | tf_op jit(solution)/shard_map/ppermute | solution.py:498
  18.6 15.1 %collective-permute-start.4 = (bf16[2,8,16,128]{3,2,1,0:T(8,128)(2,1)S(1)}, bf16[2,8,16,128]{3,2,1,0:T(8,128)(2,1)S(1)}, u32[]{:S(2)}, u32[]{:S(2)}) collective-permute-start(bf16[2,8,16,128]{3,2,1,0:T(8,128)(2,1)S(1)} %pad_maximum_fusion.3), channel_id=1, source_target_pairs={{0,8},{1,9},{4,12},{5,13},{8,0},{9,1},{12,4},{13,5},{2,10},{3,11},... | collective-permute-start | bytes 196616 | tf_op jit(solution)/shard_map/ppermute | solution.py:498
  20.5 13.3 %collective-permute-start.5 = (bf16[2,8,16,128]{3,2,1,0:T(8,128)(2,1)S(1)}, bf16[2,8,16,128]{3,2,1,0:T(8,128)(2,1)S(1)}, u32[]{:S(2)}, u32[]{:S(2)}) collective-permute-start(bf16[2,8,16,128]{3,2,1,0:T(8,128)(2,1)S(1)} %pad_maximum_fusion.4), channel_id=1, source_target_pairs={{0,9},{1,8},{4,13},{5,12},{8,1},{9,0},{12,5},{13,4},{2,11},{3,10},... | collective-permute-start | bytes 196616 | tf_op jit(solution)/shard_map/ppermute | solution.py:498
  22.8 11.8 %collective-permute-start.6 = (bf16[2,8,16,128]{3,2,1,0:T(8,128)(2,1)S(1)}, bf16[2,8,16,128]{3,2,1,0:T(8,128)(2,1)S(1)}, u32[]{:S(2)}, u32[]{:S(2)}) collective-permute-start(bf16[2,8,16,128]{3,2,1,0:T(8,128)(2,1)S(1)} %pad_maximum_fusion.5), channel_id=1, source_target_pairs={{0,12},{1,13},{4,8},{5,9},{8,4},{9,5},{12,0},{13,1},{2,14},{3,15},... | collective-permute-start | bytes 196616 | tf_op jit(solution)/shard_map/ppermute | solution.py:498
  25.0 12.5 %collective-permute-start.7 = (bf16[2,8,16,128]{3,2,1,0:T(8,128)(2,1)S(1)}, bf16[2,8,16,128]{3,2,1,0:T(8,128)(2,1)S(1)}, u32[]{:S(2)}, u32[]{:S(2)}) collective-permute-start(bf16[2,8,16,128]{3,2,1,0:T(8,128)(2,1)S(1)} %pad_maximum_fusion.6), channel_id=1, source_target_pairs={{0,13},{1,12},{4,9},{5,8},{8,5},{9,4},{12,1},{13,0},{2,15},{3,14},... | collective-permute-start | bytes 196616 | tf_op jit(solution)/shard_map/ppermute | solution.py:498
  64.8 29.9 %all-to-all-start.3 = ((bf16[32,8,16,128]{3,2,1,0:T(8,128)(2,1)}), bf16[32,8,16,128]{3,2,1,0:T(8,128)(2,1)S(1)}, u32[]{:S(2)}, u32[]{:S(2)}) async-start(bf16[32,8,16,128]{3,2,1,0:T(8,128)(2,1)} %bitcast.24), calls=%async_computation.3 | async-start | bytes 2097152 | tf_op jit(solution)/shard_map/all_to_all | solution.py:493
  68.9 1.6 %collective-permute-start.8 = (bf16[8,8,16,128]{3,2,1,0:T(8,128)(2,1)S(1)}, bf16[8,8,16,128]{3,2,1,0:T(8,128)(2,1)S(1)}, u32[]{:S(2)}, u32[]{:S(2)}) collective-permute-start(bf16[8,8,16,128]{3,2,1,0:T(8,128)(2,1)S(1)} %get-tuple-element.27), channel_id=1, source_target_pairs={{0,2},{2,0},{1,3},{3,1},{4,6},{6,4},{5,7},{7,5},{8,10},{10,8},{9,1... | collective-permute-start | bytes 786440 | tf_op jit(solution)/shard_map/ppermute | solution.py:498
  70.5 9.8 %collective-permute-start.9 = (bf16[2,8,16,128]{3,2,1,0:T(8,128)(2,1)S(1)}, bf16[2,8,16,128]{3,2,1,0:T(8,128)(2,1)S(1)}, u32[]{:S(2)}, u32[]{:S(2)}) collective-permute-start(bf16[2,8,16,128]{3,2,1,0:T(8,128)(2,1)S(1)} %pad_maximum_fusion.7), channel_id=1, source_target_pairs={{0,1},{1,0},{4,5},{5,4},{8,9},{9,8},{12,13},{13,12},{2,3},{3,2},{6... | collective-permute-start | bytes 196616 | tf_op jit(solution)/shard_map/ppermute | solution.py:498
  72.2 9.9 %collective-permute-start.10 = (bf16[2,8,16,128]{3,2,1,0:T(8,128)(2,1)S(1)}, bf16[2,8,16,128]{3,2,1,0:T(8,128)(2,1)S(1)}, u32[]{:S(2)}, u32[]{:S(2)}) collective-permute-start(bf16[2,8,16,128]{3,2,1,0:T(8,128)(2,1)S(1)} %pad_maximum_fusion.8), channel_id=1, source_target_pairs={{0,4},{1,5},{4,0},{5,1},{8,12},{9,13},{12,8},{13,9},{2,6},{3,7},{6... | collective-permute-start | bytes 196616 | tf_op jit(solution)/shard_map/ppermute | solution.py:498
  73.7 13.6 %collective-permute-start.11 = (bf16[2,8,16,128]{3,2,1,0:T(8,128)(2,1)S(1)}, bf16[2,8,16,128]{3,2,1,0:T(8,128)(2,1)S(1)}, u32[]{:S(2)}, u32[]{:S(2)}) collective-permute-start(bf16[2,8,16,128]{3,2,1,0:T(8,128)(2,1)S(1)} %pad_maximum_fusion.9), channel_id=1, source_target_pairs={{0,5},{1,4},{4,1},{5,0},{8,13},{9,12},{12,9},{13,8},{2,7},{3,6},{6... | collective-permute-start | bytes 196616 | tf_op jit(solution)/shard_map/ppermute | solution.py:498
  74.2 13.6 %collective-permute-start.12 = (bf16[2,8,16,128]{3,2,1,0:T(8,128)(2,1)S(1)}, bf16[2,8,16,128]{3,2,1,0:T(8,128)(2,1)S(1)}, u32[]{:S(2)}, u32[]{:S(2)}) collective-permute-start(bf16[2,8,16,128]{3,2,1,0:T(8,128)(2,1)S(1)} %pad_maximum_fusion.10), channel_id=1, source_target_pairs={{0,8},{1,9},{4,12},{5,13},{8,0},{9,1},{12,4},{13,5},{2,10},{3,11},... | collective-permute-start | bytes 196616 | tf_op jit(solution)/shard_map/ppermute | solution.py:498
  75.9 13.3 %collective-permute-start.13 = (bf16[2,8,16,128]{3,2,1,0:T(8,128)(2,1)S(1)}, bf16[2,8,16,128]{3,2,1,0:T(8,128)(2,1)S(1)}, u32[]{:S(2)}, u32[]{:S(2)}) collective-permute-start(bf16[2,8,16,128]{3,2,1,0:T(8,128)(2,1)S(1)} %pad_maximum_fusion.11), channel_id=1, source_target_pairs={{0,9},{1,8},{4,13},{5,12},{8,1},{9,0},{12,5},{13,4},{2,11},{3,10},... | collective-permute-start | bytes 196616 | tf_op jit(solution)/shard_map/ppermute | solution.py:498
  80.3 11.5 %collective-permute-start.14 = (bf16[2,8,16,128]{3,2,1,0:T(8,128)(2,1)S(1)}, bf16[2,8,16,128]{3,2,1,0:T(8,128)(2,1)S(1)}, u32[]{:S(2)}, u32[]{:S(2)}) collective-permute-start(bf16[2,8,16,128]{3,2,1,0:T(8,128)(2,1)S(1)} %pad_maximum_fusion.12), channel_id=1, source_target_pairs={{0,12},{1,13},{4,8},{5,9},{8,4},{9,5},{12,0},{13,1},{2,14},{3,15},... | collective-permute-start | bytes 196616 | tf_op jit(solution)/shard_map/ppermute | solution.py:498
  82.1 12.6 %collective-permute-start.15 = (bf16[2,8,16,128]{3,2,1,0:T(8,128)(2,1)S(1)}, bf16[2,8,16,128]{3,2,1,0:T(8,128)(2,1)S(1)}, u32[]{:S(2)}, u32[]{:S(2)}) collective-permute-start(bf16[2,8,16,128]{3,2,1,0:T(8,128)(2,1)S(1)} %pad_maximum_fusion.13), channel_id=1, source_target_pairs={{0,13},{1,12},{4,9},{5,8},{8,5},{9,4},{12,1},{13,0},{2,15},{3,14},... | collective-permute-start | bytes 196616 | tf_op jit(solution)/shard_map/ppermute | solution.py:498

commit v15 on v14

--- a/solution.py
+++ b/solution.py
@@ -363,36 +363,31 @@
 
 
 def back_kernel(n_chip, grads, coef_h, zhat_h, inv_h, dzg_h, gain_h, proj_h, *refs):
-    pieces, out_h = refs[:-15], refs[-15]
+    pieces, out_h = refs[:-14], refs[-14]
     (
         coef, zhat, inv, dzg, gain, proj_weight, out, left, right,
-        sems, coef_sems, zhat_sems, dzg_sems, out_sems,
-    ) = refs[-14:]
+        sems, near_sems, far_sems, out_sems,
+    ) = refs[-13:]
     rows, cols, width = out.shape
     hidden = left.shape[0] // rows
     groups = groups_of(rows)
     ahead = rows // math.gcd(rows, 2)
-    blocks = [
-        [
-            pltpu.make_async_copy(
-                source.at[pl.ds(at, size)], target.at[pl.ds(at, size)], sem.at[n]
-            )
-            for source, target, sem in (
-                (coef_h, coef, coef_sems), (zhat_h, zhat, zhat_sems), (dzg_h, dzg, dzg_sems)
-            )
-        ]
-        for n, (at, size) in enumerate(groups)
-    ]
-    for copy in blocks[0]:
-        copy.start()
+    blocks = {
+        at: start(
+            sem,
+            [
+                (source.at[pl.ds(at, ahead)], target.at[pl.ds(at, ahead)])
+                for source, target in ((coef_h, coef), (zhat_h, zhat), (dzg_h, dzg))
+            ],
+        )
+        for at, sem in zip(range(0, rows, ahead), (near_sems, far_sems))
+    }
     small = start(sems, [(gain_h, gain), (proj_h, proj_weight), (inv_h, inv)])
     arrived = received(pieces, n_chip)
     length = left.shape[0] // len(arrived)
     for number, piece in arrived:
         first = pl.multiple_of(number * length, length)
         left[pl.ds(first, length), :] = piece.astype(F32).reshape(length, cols)
-    for copy in sum(blocks[1:], []):
-        copy.start()
     total = grads[0].astype(F32)
     for half in range(1, grads.shape[0]):
         total = total + grads[half].astype(F32)
@@ -400,12 +395,12 @@
     wait(small)
     gain_b = jnp.concatenate([down_lanes(gain[...], cols)] * groups[0][1], axis=1)
     leaving = []
-    for n, (at, size) in enumerate(groups):
+    for at, size in groups:
         both = [
             [plane[pl.ds(at + r, hidden, stride=rows), :].astype(BF16) for plane in (left, right)]
             for r in range(size)
         ]
-        wait(blocks[n])
+        wait(blocks.get(at, []))
         columns = []
         for r, (gl, gr) in enumerate(both):
             columns.append(
@@ -629,7 +624,7 @@
         [
             vmem(rows, 4, hidden, cols), short, vmem(rows, cols, dtype=F32), short,
             vector, proj_v, block, plane, plane,
-            sems(3), sems(n_groups), sems(n_groups), sems(n_groups), sems(2),
+            sems(3), sems(3), sems(3), sems(2),
         ],
         (grad_right, coef, short_zhat, inv, dzg, gain_in, proj_weight, *grad_left),
         near=(0, *range(7, 7 + n_pieces)),

time: 101 us -> 101 us (level)
  no operation moved by 1% of the time
where the time goes in v15:
time: 101 us; the launch traced here: 100 us
  starting transfers between devices  29.1 us (29%)
  Pallas kernels  25.4 us (25%)
  blocking collectives  24.9 us (25%)
  waiting for transfers between devices  19.5 us (19%)
    pallas_call x10, Pallas kernels, call(): pl.pallas_call(kernel, out_shape=[out if at in outs_near else pltpu.HBM(o...  25.4 us
    all_to_all x2, blocking collectives, exchange(): lax.all_to_all(values, within, split_axis=0, concat_axis=0, tiled=True)  24.9 us
    ppermute x16, waiting for transfers between devices, permute(): lax.ppermute(values, axes, [(at, at ^ distance) for at in range(size)])  19.5 us
    ppermute x16, starting transfers between devices, permute(): lax.ppermute(values, axes, [(at, at ^ distance) for at in range(size)])  18.2 us
    all_to_all x2, starting transfers between devices, exchange_all(): lax.all_to_all(flat, ('half', *within), split_axis=0, concat_axis=0, tile...  10.9 us
  transfers between devices with their start and end apart: 18, of which 12 were waited for; matrix products, arithmetic and copies ran while one was open for 0% of the time, Pallas kernels for 15%

profile of v15, /device:TPU:0, one launch (start us, length us, event | category | flops | bytes accessed | tf_op | source)
XLA Modules:
  0.0 100.1 jit_solution(6539914418484826363)
XLA Ops:
  0.6 3.1 %shard_map.113 = bf16[2,16,8,16,128]{4,3,2,1,0:T(8,128)(2,1)} custom-call(bf16[16,128,128]{2,1,0:T(8,128)(2,1)} %pair_h.5, s32[256]{0:T(256)} %mask_h.5, s32[1,256]{1,0:T(1,128)} %bitcast.26, f32[1,128]{1,0:T(1,128)} %bitcast.29, f32[1,128]{1,0:T(1,128)} %bitcast.34, bf16[128,512]{1,0:T(8,128)(2,1)} %proj_h.7), custom_call_target="tpu_custom_call" | custom-call | flops 201326592 | bytes 1310720 | tf_op jit(solution)/shard_map/pallas_call | solution.py:434
  3.7 7.3 %all-to-all-start = ((bf16[32,8,16,128]{3,2,1,0:T(8,128)(2,1)}), bf16[32,8,16,128]{3,2,1,0:T(8,128)(2,1)S(1)}, u32[]{:S(2)}, u32[]{:S(2)}) async-start(bf16[32,8,16,128]{3,2,1,0:T(8,128)(2,1)} %bitcast.25), calls=%async_computation | async-start | bytes 2097152 | tf_op jit(solution)/shard_map/all_to_all | solution.py:488
  11.0 2.2 %shard_map.116 = (bf16[8,8,16,128]{3,2,1,0:T(8,128)(2,1)S(1)}, bf16[8,8,16,128]{3,2,1,0:T(8,128)(2,1)S(1)}) custom-call(bf16[16,128,128]{2,1,0:T(8,128)(2,1)} %pair_h.5, s32[256]{0:T(256)} %mask_h.5, s32[1,256]{1,0:T(1,128)} %bitcast.27, f32[1,128]{1,0:T(1,128)} %bitcast.30, f32[1,128]{1,0:T(1,128)} %bitcast.35, bf16[128,512]{1,0:T(8,128)(2,1)} %proj_h.7), custom_call_target="tpu_custom_call" | custom-call | flops 201326592 | bytes 1310720 | tf_op jit(solution)/shard_map/pallas_call | solution.py:434
  14.9 1.8 %collective-permute-start.1 = (bf16[2,8,16,128]{3,2,1,0:T(8,128)(2,1)S(1)}, bf16[2,8,16,128]{3,2,1,0:T(8,128)(2,1)S(1)}, u32[]{:S(2)}, u32[]{:S(2)}) collective-permute-start(bf16[2,8,16,128]{3,2,1,0:T(8,128)(2,1)S(1)} %pad_maximum_fusion), channel_id=1, source_target_pairs={{0,1},{1,0},{4,5},{5,4},{8,9},{9,8},{12,13},{13,12},{2,3},{3,2},{6... | collective-permute-start | bytes 196616 | tf_op jit(solution)/shard_map/ppermute | solution.py:493
  16.8 1.5 %collective-permute-start.2 = (bf16[2,8,16,128]{3,2,1,0:T(8,128)(2,1)S(1)}, bf16[2,8,16,128]{3,2,1,0:T(8,128)(2,1)S(1)}, u32[]{:S(2)}, u32[]{:S(2)}) collective-permute-start(bf16[2,8,16,128]{3,2,1,0:T(8,128)(2,1)S(1)} %pad_maximum_fusion.1), channel_id=1, source_target_pairs={{0,4},{1,5},{4,0},{5,1},{8,12},{9,13},{12,8},{13,9},{2,6},{3,7},{6... | collective-permute-start | bytes 196616 | tf_op jit(solution)/shard_map/ppermute | solution.py:493
  18.6 1.8 %collective-permute-start.4 = (bf16[2,8,16,128]{3,2,1,0:T(8,128)(2,1)S(1)}, bf16[2,8,16,128]{3,2,1,0:T(8,128)(2,1)S(1)}, u32[]{:S(2)}, u32[]{:S(2)}) collective-permute-start(bf16[2,8,16,128]{3,2,1,0:T(8,128)(2,1)S(1)} %pad_maximum_fusion.3), channel_id=1, source_target_pairs={{0,8},{1,9},{4,12},{5,13},{8,0},{9,1},{12,4},{13,5},{2,10},{3,11},... | collective-permute-start | bytes 196616 | tf_op jit(solution)/shard_map/ppermute | solution.py:493
  20.5 1.5 %collective-permute-start.5 = (bf16[2,8,16,128]{3,2,1,0:T(8,128)(2,1)S(1)}, bf16[2,8,16,128]{3,2,1,0:T(8,128)(2,1)S(1)}, u32[]{:S(2)}, u32[]{:S(2)}) collective-permute-start(bf16[2,8,16,128]{3,2,1,0:T(8,128)(2,1)S(1)} %pad_maximum_fusion.4), channel_id=1, source_target_pairs={{0,9},{1,8},{4,13},{5,12},{8,1},{9,0},{12,5},{13,4},{2,11},{3,10},... | collective-permute-start | bytes 196616 | tf_op jit(solution)/shard_map/ppermute | solution.py:493
  22.8 1.6 %collective-permute-start.6 = (bf16[2,8,16,128]{3,2,1,0:T(8,128)(2,1)S(1)}, bf16[2,8,16,128]{3,2,1,0:T(8,128)(2,1)S(1)}, u32[]{:S(2)}, u32[]{:S(2)}) collective-permute-start(bf16[2,8,16,128]{3,2,1,0:T(8,128)(2,1)S(1)} %pad_maximum_fusion.5), channel_id=1, source_target_pairs={{0,12},{1,13},{4,8},{5,9},{8,4},{9,5},{12,0},{13,1},{2,14},{3,15},... | collective-permute-start | bytes 196616 | tf_op jit(solution)/shard_map/ppermute | solution.py:493
  25.6 4.8 %shard_map.114 = (f32[16,128,128]{2,1,0:T(8,128)}, bf16[16,128,128]{2,1,0:T(8,128)(2,1)}, f32[16,128]{1,0:T(8,128)}, f32[16,128,128]{2,1,0:T(8,128)}, f32[2048,128]{1,0:T(8,128)S(1)}) custom-call(bf16[16,128,128]{2,1,0:T(8,128)(2,1)} %pair_h.5, bf16[16,128,128]{2,1,0:T(8,128)(2,1)} %cot_h.3, f32[1,128]{1,0:T(1,128)} %bitcast.31, f32[1,128]{1,0:T(1,128)} %bitcast.36, ...), custom_call_target="tpu_custom_call" | custom-call | flops 268435456 | bytes 4194304 | tf_op jit(solution)/shard_map/pallas_call | solution.py:434
  30.5 3.2 %shard_map.115.after.coef_h = bf16[16,4,128,128]{3,2,1,0:T(8,128)(2,1)} custom-call(f32[16,128,128]{2,1,0:T(8,128)} %get-tuple-element.15.zhat_h, s32[256]{0:T(256)} %mask_h.5, s32[1,256]{1,0:T(1,128)} %bitcast.28, f32[1,128]{1,0:T(1,128)} %bitcast.32, f32[1,128]{1,0:T(1,128)} %bitcast.37, bf16[128,512]{1,0:T(8,128)(2,1)} %proj_h.7), custom_call_target="tpu_custom_call" | custom-call | flops 335544320 | bytes 4194304 | tf_op jit(solution)/shard_map/pallas_call | solution.py:434
  34.6 2.9 %collective-permute-done.7.refs_8_ = bf16[2,8,16,128]{3,2,1,0:T(8,128)(2,1)S(1)} collective-permute-done((bf16[2,8,16,128]{3,2,1,0:T(8,128)(2,1)S(1)}, bf16[2,8,16,128]{3,2,1,0:T(8,128)(2,1)S(1)}, u32[]{:S(2)}, u32[]{:S(2)}) %collective-permute-start.7) | collective-permute-done | bytes 65568 | tf_op jit(solution)/shard_map/ppermute | solution.py:493
  38.0 12.9 %all_to_all.20 = bf16[16,8,16,128]{3,2,1,0:T(8,128)(2,1)S(1)} all-to-all(bf16[16,8,16,128]{3,2,1,0:T(8,128)(2,1)S(1)} %bitcast.23), channel_id=1, replica_groups=mesh['grp'=1,'half'=2,'row'=4,'core'=2,'col'=2] {'row','core','col'}, dimensions={0} | all-to-all | bytes 1048576 | tf_op jit(solution)/shard_map/all_to_all | solution.py:484
  51.5 12.0 %all_to_all.21 = bf16[16,8,16,128]{3,2,1,0:T(8,128)(2,1)S(1)} all-to-all(bf16[16,8,16,128]{3,2,1,0:T(8,128)(2,1)S(1)} %bitcast.21), channel_id=1, replica_groups=mesh['grp'=1,'half'=2,'row'=4,'core'=2,'col'=2] {'row','core','col'}, dimensions={0} | all-to-all | bytes 1048576 | tf_op jit(solution)/shard_map/all_to_all | solution.py:484
  64.8 3.6 %all-to-all-start.3 = ((bf16[32,8,16,128]{3,2,1,0:T(8,128)(2,1)}), bf16[32,8,16,128]{3,2,1,0:T(8,128)(2,1)S(1)}, u32[]{:S(2)}, u32[]{:S(2)}) async-start(bf16[32,8,16,128]{3,2,1,0:T(8,128)(2,1)} %bitcast.24), calls=%async_computation.3 | async-start | bytes 2097152 | tf_op jit(solution)/shard_map/all_to_all | solution.py:488
  69.0 1.4 %collective-permute-done.8.refs_1_ = bf16[8,8,16,128]{3,2,1,0:T(8,128)(2,1)S(1)} collective-permute-done((bf16[8,8,16,128]{3,2,1,0:T(8,128)(2,1)S(1)}, bf16[8,8,16,128]{3,2,1,0:T(8,128)(2,1)S(1)}, u32[]{:S(2)}, u32[]{:S(2)}) %collective-permute-start.8) | collective-permute-done | bytes 262176 | tf_op jit(solution)/shard_map/ppermute | solution.py:493
  70.5 1.7 %collective-permute-start.9 = (bf16[2,8,16,128]{3,2,1,0:T(8,128)(2,1)S(1)}, bf16[2,8,16,128]{3,2,1,0:T(8,128)(2,1)S(1)}, u32[]{:S(2)}, u32[]{:S(2)}) collective-permute-start(bf16[2,8,16,128]{3,2,1,0:T(8,128)(2,1)S(1)} %pad_maximum_fusion.7), channel_id=1, source_target_pairs={{0,1},{1,0},{4,5},{5,4},{8,9},{9,8},{12,13},{13,12},{2,3},{3,2},{6... | collective-permute-start | bytes 196616 | tf_op jit(solution)/shard_map/ppermute | solution.py:493
  72.2 1.5 %collective-permute-start.10 = (bf16[2,8,16,128]{3,2,1,0:T(8,128)(2,1)S(1)}, bf16[2,8,16,128]{3,2,1,0:T(8,128)(2,1)S(1)}, u32[]{:S(2)}, u32[]{:S(2)}) collective-permute-start(bf16[2,8,16,128]{3,2,1,0:T(8,128)(2,1)S(1)} %pad_maximum_fusion.8), channel_id=1, source_target_pairs={{0,4},{1,5},{4,0},{5,1},{8,12},{9,13},{12,8},{13,9},{2,6},{3,7},{6... | collective-permute-start | bytes 196616 | tf_op jit(solution)/shard_map/ppermute | solution.py:493
  74.2 1.7 %collective-permute-start.12 = (bf16[2,8,16,128]{3,2,1,0:T(8,128)(2,1)S(1)}, bf16[2,8,16,128]{3,2,1,0:T(8,128)(2,1)S(1)}, u32[]{:S(2)}, u32[]{:S(2)}) collective-permute-start(bf16[2,8,16,128]{3,2,1,0:T(8,128)(2,1)S(1)} %pad_maximum_fusion.10), channel_id=1, source_target_pairs={{0,8},{1,9},{4,12},{5,13},{8,0},{9,1},{12,4},{13,5},{2,10},{3,11},... | collective-permute-start | bytes 196616 | tf_op jit(solution)/shard_map/ppermute | solution.py:493
  75.9 1.5 %collective-permute-start.13 = (bf16[2,8,16,128]{3,2,1,0:T(8,128)(2,1)S(1)}, bf16[2,8,16,128]{3,2,1,0:T(8,128)(2,1)S(1)}, u32[]{:S(2)}, u32[]{:S(2)}) collective-permute-start(bf16[2,8,16,128]{3,2,1,0:T(8,128)(2,1)S(1)} %pad_maximum_fusion.11), channel_id=1, source_target_pairs={{0,9},{1,8},{4,13},{5,12},{8,1},{9,0},{12,5},{13,4},{2,11},{3,10},... | collective-permute-start | bytes 196616 | tf_op jit(solution)/shard_map/ppermute | solution.py:493
  77.4 2.9 %collective-permute-done.9.refs_2_ = bf16[2,8,16,128]{3,2,1,0:T(8,128)(2,1)S(1)} collective-permute-done((bf16[2,8,16,128]{3,2,1,0:T(8,128)(2,1)S(1)}, bf16[2,8,16,128]{3,2,1,0:T(8,128)(2,1)S(1)}, u32[]{:S(2)}, u32[]{:S(2)}) %collective-permute-start.9) | collective-permute-done | bytes 65568 | tf_op jit(solution)/shard_map/ppermute | solution.py:493
  83.3 4.0 %shard_map.120 = (bf16[16,128,128]{2,1,0:T(8,128)(2,1)}, bf16[16,128,128]{2,1,0:T(8,128)(2,1)}) custom-call(bf16[128,16,128]{2,1,0:T(8,128)(2,1)S(1)} %bitcast.19, f32[16,128,128]{2,1,0:T(8,128)} %get-tuple-element.19.gate_h, bf16[16,128,128]{2,1,0:T(8,128)(2,1)} %cot_h.3, f32[1,128]{1,0:T(1,128)} %bitcast.39, f32[1,128]{1,0:T(1,128)} %bitcast.40, ...), custom_call_target="tpu_custom_call" | custom-call | flops 201326592 | bytes 3670016 | tf_op jit(solution)/shard_map/pallas_call | solution.py:434
  89.2 2.7 %collective-permute-done.14.refs_7_ = bf16[2,8,16,128]{3,2,1,0:T(8,128)(2,1)S(1)} collective-permute-done((bf16[2,8,16,128]{3,2,1,0:T(8,128)(2,1)S(1)}, bf16[2,8,16,128]{3,2,1,0:T(8,128)(2,1)S(1)}, u32[]{:S(2)}, u32[]{:S(2)}) %collective-permute-start.14) | collective-permute-done | bytes 65568 | tf_op jit(solution)/shard_map/ppermute | solution.py:493
  91.8 2.9 %collective-permute-done.15.refs_8_ = bf16[2,8,16,128]{3,2,1,0:T(8,128)(2,1)S(1)} collective-permute-done((bf16[2,8,16,128]{3,2,1,0:T(8,128)(2,1)S(1)}, bf16[2,8,16,128]{3,2,1,0:T(8,128)(2,1)S(1)}, u32[]{:S(2)}, u32[]{:S(2)}) %collective-permute-start.15) | collective-permute-done | bytes 65568 | tf_op jit(solution)/shard_map/ppermute | solution.py:493
  94.7 5.2 %shard_map.122 = bf16[16,128,128]{2,1,0:T(8,128)(2,1)} custom-call(bf16[2,16,8,16,128]{4,3,2,1,0:T(8,128)(2,1)S(1)} %bitcast.20, bf16[16,4,128,128]{3,2,1,0:T(8,128)(2,1)} %shard_map.115.after.coef_h, bf16[16,128,128]{2,1,0:T(8,128)(2,1)} %get-tuple-element.23.zhat_h, f32[16,128]{1,0:T(8,128)} %get-tuple-element.24.inv_h, ...), custom_call_target="tpu_custom_call" | custom-call | flops 335544320 | bytes 7864320 | tf_op jit(solution)/shard_map/pallas_call | solution.py:434
  (42 shorter events, 13.3 us)
Async XLA Ops:
  3.7 33.7 %all-to-all-start = ((bf16[32,8,16,128]{3,2,1,0:T(8,128)(2,1)}), bf16[32,8,16,128]{3,2,1,0:T(8,128)(2,1)S(1)}, u32[]{:S(2)}, u32[]{:S(2)}) async-start(bf16[32,8,16,128]{3,2,1,0:T(8,128)(2,1)} %bitcast.25), calls=%async_computation | async-start | bytes 2097152 | tf_op jit(solution)/shard_map/all_to_all | solution.py:488
  13.3 1.6 %collective-permute-start = (bf16[8,8,16,128]{3,2,1,0:T(8,128)(2,1)S(1)}, bf16[8,8,16,128]{3,2,1,0:T(8,128)(2,1)S(1)}, u32[]{:S(2)}, u32[]{:S(2)}) collective-permute-start(bf16[8,8,16,128]{3,2,1,0:T(8,128)(2,1)S(1)} %get-tuple-element.17), channel_id=1, source_target_pairs={{0,2},{2,0},{1,3},{3,1},{4,6},{6,4},{5,7},{7,5},{8,10},{10,8},{9,1... | collective-permute-start | bytes 786440 | tf_op jit(solution)/shard_map/ppermute | solution.py:493
  14.9 7.9 %collective-permute-start.1 = (bf16[2,8,16,128]{3,2,1,0:T(8,128)(2,1)S(1)}, bf16[2,8,16,128]{3,2,1,0:T(8,128)(2,1)S(1)}, u32[]{:S(2)}, u32[]{:S(2)}) collective-permute-start(bf16[2,8,16,128]{3,2,1,0:T(8,128)(2,1)S(1)} %pad_maximum_fusion), channel_id=1, source_target_pairs={{0,1},{1,0},{4,5},{5,4},{8,9},{9,8},{12,13},{13,12},{2,3},{3,2},{6... | collective-permute-start | bytes 196616 | tf_op jit(solution)/shard_map/ppermute | solution.py:493
  16.8 8.2 %collective-permute-start.2 = (bf16[2,8,16,128]{3,2,1,0:T(8,128)(2,1)S(1)}, bf16[2,8,16,128]{3,2,1,0:T(8,128)(2,1)S(1)}, u32[]{:S(2)}, u32[]{:S(2)}) collective-permute-start(bf16[2,8,16,128]{3,2,1,0:T(8,128)(2,1)S(1)} %pad_maximum_fusion.1), channel_id=1, source_target_pairs={{0,4},{1,5},{4,0},{5,1},{8,12},{9,13},{12,8},{13,9},{2,6},{3,7},{6... | collective-permute-start | bytes 196616 | tf_op jit(solution)/shard_map/ppermute | solution.py:493
  18.3 15.4 %collective-permute-start.3 = (bf16[2,8,16,128]{3,2,1,0:T(8,128)(2,1)S(1)}, bf16[2,8,16,128]{3,2,1,0:T(8,128)(2,1)S(1)}, u32[]{:S(2)}, u32[]{:S(2)}) collective-permute-start(bf16[2,8,16,128]{3,2,1,0:T(8,128)(2,1)S(1)} %pad_maximum_fusion.2), channel_id=1, source_target_pairs={{0,5},{1,4},{4,1},{5,0},{8,13},{9,12},{12,9},{13,8},{2,7},{3,6},{6... | collective-permute-start | bytes 196616 | tf_op jit(solution)/shard_map/ppermute | solution.py:493
  18.6 15.1 %collective-permute-start.4 = (bf16[2,8,16,128]{3,2,1,0:T(8,128)(2,1)S(1)}, bf16[2,8,16,128]{3,2,1,0:T(8,128)(2,1)S(1)}, u32[]{:S(2)}, u32[]{:S(2)}) collective-permute-start(bf16[2,8,16,128]{3,2,1,0:T(8,128)(2,1)S(1)} %pad_maximum_fusion.3), channel_id=1, source_target_pairs={{0,8},{1,9},{4,12},{5,13},{8,0},{9,1},{12,4},{13,5},{2,10},{3,11},... | collective-permute-start | bytes 196616 | tf_op jit(solution)/shard_map/ppermute | solution.py:493
  20.5 13.3 %collective-permute-start.5 = (bf16[2,8,16,128]{3,2,1,0:T(8,128)(2,1)S(1)}, bf16[2,8,16,128]{3,2,1,0:T(8,128)(2,1)S(1)}, u32[]{:S(2)}, u32[]{:S(2)}) collective-permute-start(bf16[2,8,16,128]{3,2,1,0:T(8,128)(2,1)S(1)} %pad_maximum_fusion.4), channel_id=1, source_target_pairs={{0,9},{1,8},{4,13},{5,12},{8,1},{9,0},{12,5},{13,4},{2,11},{3,10},... | collective-permute-start | bytes 196616 | tf_op jit(solution)/shard_map/ppermute | solution.py:493
  22.8 11.8 %collective-permute-start.6 = (bf16[2,8,16,128]{3,2,1,0:T(8,128)(2,1)S(1)}, bf16[2,8,16,128]{3,2,1,0:T(8,128)(2,1)S(1)}, u32[]{:S(2)}, u32[]{:S(2)}) collective-permute-start(bf16[2,8,16,128]{3,2,1,0:T(8,128)(2,1)S(1)} %pad_maximum_fusion.5), channel_id=1, source_target_pairs={{0,12},{1,13},{4,8},{5,9},{8,4},{9,5},{12,0},{13,1},{2,14},{3,15},... | collective-permute-start | bytes 196616 | tf_op jit(solution)/shard_map/ppermute | solution.py:493
  25.0 12.5 %collective-permute-start.7 = (bf16[2,8,16,128]{3,2,1,0:T(8,128)(2,1)S(1)}, bf16[2,8,16,128]{3,2,1,0:T(8,128)(2,1)S(1)}, u32[]{:S(2)}, u32[]{:S(2)}) collective-permute-start(bf16[2,8,16,128]{3,2,1,0:T(8,128)(2,1)S(1)} %pad_maximum_fusion.6), channel_id=1, source_target_pairs={{0,13},{1,12},{4,9},{5,8},{8,5},{9,4},{12,1},{13,0},{2,15},{3,14},... | collective-permute-start | bytes 196616 | tf_op jit(solution)/shard_map/ppermute | solution.py:493
  64.8 29.9 %all-to-all-start.3 = ((bf16[32,8,16,128]{3,2,1,0:T(8,128)(2,1)}), bf16[32,8,16,128]{3,2,1,0:T(8,128)(2,1)S(1)}, u32[]{:S(2)}, u32[]{:S(2)}) async-start(bf16[32,8,16,128]{3,2,1,0:T(8,128)(2,1)} %bitcast.24), calls=%async_computation.3 | async-start | bytes 2097152 | tf_op jit(solution)/shard_map/all_to_all | solution.py:488
  68.9 1.6 %collective-permute-start.8 = (bf16[8,8,16,128]{3,2,1,0:T(8,128)(2,1)S(1)}, bf16[8,8,16,128]{3,2,1,0:T(8,128)(2,1)S(1)}, u32[]{:S(2)}, u32[]{:S(2)}) collective-permute-start(bf16[8,8,16,128]{3,2,1,0:T(8,128)(2,1)S(1)} %get-tuple-element.27), channel_id=1, source_target_pairs={{0,2},{2,0},{1,3},{3,1},{4,6},{6,4},{5,7},{7,5},{8,10},{10,8},{9,1... | collective-permute-start | bytes 786440 | tf_op jit(solution)/shard_map/ppermute | solution.py:493
  70.5 9.8 %collective-permute-start.9 = (bf16[2,8,16,128]{3,2,1,0:T(8,128)(2,1)S(1)}, bf16[2,8,16,128]{3,2,1,0:T(8,128)(2,1)S(1)}, u32[]{:S(2)}, u32[]{:S(2)}) collective-permute-start(bf16[2,8,16,128]{3,2,1,0:T(8,128)(2,1)S(1)} %pad_maximum_fusion.7), channel_id=1, source_target_pairs={{0,1},{1,0},{4,5},{5,4},{8,9},{9,8},{12,13},{13,12},{2,3},{3,2},{6... | collective-permute-start | bytes 196616 | tf_op jit(solution)/shard_map/ppermute | solution.py:493
  72.2 9.9 %collective-permute-start.10 = (bf16[2,8,16,128]{3,2,1,0:T(8,128)(2,1)S(1)}, bf16[2,8,16,128]{3,2,1,0:T(8,128)(2,1)S(1)}, u32[]{:S(2)}, u32[]{:S(2)}) collective-permute-start(bf16[2,8,16,128]{3,2,1,0:T(8,128)(2,1)S(1)} %pad_maximum_fusion.8), channel_id=1, source_target_pairs={{0,4},{1,5},{4,0},{5,1},{8,12},{9,13},{12,8},{13,9},{2,6},{3,7},{6... | collective-permute-start | bytes 196616 | tf_op jit(solution)/shard_map/ppermute | solution.py:493
  73.7 13.6 %collective-permute-start.11 = (bf16[2,8,16,128]{3,2,1,0:T(8,128)(2,1)S(1)}, bf16[2,8,16,128]{3,2,1,0:T(8,128)(2,1)S(1)}, u32[]{:S(2)}, u32[]{:S(2)}) collective-permute-start(bf16[2,8,16,128]{3,2,1,0:T(8,128)(2,1)S(1)} %pad_maximum_fusion.9), channel_id=1, source_target_pairs={{0,5},{1,4},{4,1},{5,0},{8,13},{9,12},{12,9},{13,8},{2,7},{3,6},{6... | collective-permute-start | bytes 196616 | tf_op jit(solution)/shard_map/ppermute | solution.py:493
  74.2 13.6 %collective-permute-start.12 = (bf16[2,8,16,128]{3,2,1,0:T(8,128)(2,1)S(1)}, bf16[2,8,16,128]{3,2,1,0:T(8,128)(2,1)S(1)}, u32[]{:S(2)}, u32[]{:S(2)}) collective-permute-start(bf16[2,8,16,128]{3,2,1,0:T(8,128)(2,1)S(1)} %pad_maximum_fusion.10), channel_id=1, source_target_pairs={{0,8},{1,9},{4,12},{5,13},{8,0},{9,1},{12,4},{13,5},{2,10},{3,11},... | collective-permute-start | bytes 196616 | tf_op jit(solution)/shard_map/ppermute | solution.py:493
  75.9 13.3 %collective-permute-start.13 = (bf16[2,8,16,128]{3,2,1,0:T(8,128)(2,1)S(1)}, bf16[2,8,16,128]{3,2,1,0:T(8,128)(2,1)S(1)}, u32[]{:S(2)}, u32[]{:S(2)}) collective-permute-start(bf16[2,8,16,128]{3,2,1,0:T(8,128)(2,1)S(1)} %pad_maximum_fusion.11), channel_id=1, source_target_pairs={{0,9},{1,8},{4,13},{5,12},{8,1},{9,0},{12,5},{13,4},{2,11},{3,10},... | collective-permute-start | bytes 196616 | tf_op jit(solution)/shard_map/ppermute | solution.py:493
  80.3 11.5 %collective-permute-start.14 = (bf16[2,8,16,128]{3,2,1,0:T(8,128)(2,1)S(1)}, bf16[2,8,16,128]{3,2,1,0:T(8,128)(2,1)S(1)}, u32[]{:S(2)}, u32[]{:S(2)}) collective-permute-start(bf16[2,8,16,128]{3,2,1,0:T(8,128)(2,1)S(1)} %pad_maximum_fusion.12), channel_id=1, source_target_pairs={{0,12},{1,13},{4,8},{5,9},{8,4},{9,5},{12,0},{13,1},{2,14},{3,15},... | collective-permute-start | bytes 196616 | tf_op jit(solution)/shard_map/ppermute | solution.py:493
  82.1 12.6 %collective-permute-start.15 = (bf16[2,8,16,128]{3,2,1,0:T(8,128)(2,1)S(1)}, bf16[2,8,16,128]{3,2,1,0:T(8,128)(2,1)S(1)}, u32[]{:S(2)}, u32[]{:S(2)}) collective-permute-start(bf16[2,8,16,128]{3,2,1,0:T(8,128)(2,1)S(1)} %pad_maximum_fusion.13), channel_id=1, source_target_pairs={{0,13},{1,12},{4,9},{5,8},{8,5},{9,4},{12,1},{13,0},{2,15},{3,14},... | collective-permute-start | bytes 196616 | tf_op jit(solution)/shard_map/ppermute | solution.py:493

commit v16 on v13

--- a/solution.py
+++ b/solution.py
@@ -66,8 +66,8 @@
         copy.wait()
 
 
-def groups_of(rows):
-    size = math.gcd(rows, 4)
+def groups_of(rows, most=2):
+    size = math.gcd(rows, most)
     return [(at, size) for at in range(0, rows, size)]
 
 
@@ -134,11 +134,13 @@
         zbar[:, at * cols : (at + size) * cols] = (zhat * gain_b + bias_b).astype(BF16)
 
     def channels(first, count):
+        block = jnp.concatenate(
+            [weight[first : first + count], weight[hidden + first : hidden + first + count]], axis=0
+        )
         for at, size in groups:
-            z = zbar[:, at * cols : (at + size) * cols]
-            p = dot(weight[first : first + count], z)
-            q = dot(weight[hidden + first : hidden + first + count], z)
-            values = sigmoid(p) * q * pair_mask(mask_s, mask_v, at, size, rows, cols)
+            proj = dot(block, zbar[:, at * cols : (at + size) * cols])
+            pm = pair_mask(mask_s, mask_v, at, size, rows, cols)
+            values = sigmoid(proj[:count]) * proj[count:] * pm
             for r in range(size):
                 plane[pl.ds(first * rows + at + r, count, stride=rows), :] = values[
                     :, r * cols : (r + 1) * cols
@@ -150,7 +152,7 @@
         return
     (out_h,), (ready, out_sems) = outs, more
     n_place, share = ready.shape[:2]
-    size = n_place // math.gcd(n_place, 4)
+    size = n_place // math.gcd(n_place, 2)
     leaving = []
     for n, at in enumerate(range(0, n_place, size)):
         channels(at * share, size * share)
@@ -368,7 +370,7 @@
     ) = refs[-14:]
     rows, cols, width = out.shape
     hidden = left.shape[0] // rows
-    groups = groups_of(rows)
+    groups, parts = groups_of(rows), groups_of(rows, 4)
     small = start(sems, [(gain_h, gain), (proj_h, proj_weight), (inv_h, inv)])
     ahead = rows // math.gcd(rows, 2)
     blocks = [
@@ -380,7 +382,7 @@
                 (coef_h, coef, coef_sems), (zhat_h, zhat, zhat_sems), (dzg_h, dzg, dzg_sems)
             )
         ]
-        for n, (at, size) in enumerate(groups)
+        for n, (at, size) in enumerate(parts)
     ]
     for copy in sum(blocks[:2], []):
         copy.start()
@@ -398,8 +400,9 @@
     leaving = []
     for copy in sum(blocks[2:], []):
         copy.start()
-    for n, (at, size) in enumerate(groups):
-        wait(blocks[n])
+    arriving = {at: copies for (at, _), copies in zip(parts, blocks)}
+    for at, size in groups:
+        wait(arriving.get(at, []))
         columns = []
         for r in range(size):
             gl = left[pl.ds(at + r, hidden, stride=rows), :].astype(BF16)
@@ -468,6 +471,7 @@
     share = hidden // n_place
     cells = rows * cols
     n_groups = len(groups_of(rows))
+    n_parts = len(groups_of(rows, 4))
     mask_row = mask.reshape(1, -1)
     gain_in, bias_in = gain_in.reshape(1, -1), bias_in.reshape(1, -1)
     norm_gain, norm_bias = product_norm_gain.reshape(1, -1), product_norm_bias.reshape(1, -1)
@@ -532,7 +536,7 @@
     (right,) = front(
         2,
         (shape(n_half, n_place, share, rows, cols),),
-        [everywhere, pltpu.SemaphoreType.DMA((n_half, math.gcd(n_place, 4)))],
+        [everywhere, pltpu.SemaphoreType.DMA((n_half, math.gcd(n_place, 2)))],
         (),
     )
     right = exchange_all(right).reshape(n_half, n_line, n_col, share, rows, cols)
@@ -625,7 +629,7 @@
         [
             vmem(rows, 4, hidden, cols), short, vmem(rows, cols, dtype=F32), short,
             vector, proj_v, block, plane, plane,
-            sems(3), sems(n_groups), sems(n_groups), sems(n_groups), sems(2),
+            sems(3), sems(n_parts), sems(n_parts), sems(n_parts), sems(2),
         ],
         (grad_right, coef, short_zhat, inv, dzg, gain_in, proj_weight, *grad_left),
         near=(0, *range(7, 7 + n_pieces)),

time: 100 us -> 100 us (level)
  transfers between devices with their start and end apart: 18 -> 18, of which waited for: 12 -> 11; matrix products, arithmetic and copies ran while one was open for 0% -> 0% of each run, Pallas kernels for 15% -> 15%
where the time goes in v16:
time: 100 us; the launch traced here: 99.6 us
  starting transfers between devices  29.1 us (29%)
  Pallas kernels  25.1 us (25%)
  blocking collectives  24.9 us (25%)
  waiting for transfers between devices  19.3 us (19%)
    pallas_call x10, Pallas kernels, call(): pl.pallas_call(kernel, out_shape=[out if at in outs_near else pltpu.HBM(o...  25.1 us
    all_to_all x2, blocking collectives, exchange(): lax.all_to_all(values, within, split_axis=0, concat_axis=0, tiled=True)  24.9 us
    ppermute x16, waiting for transfers between devices, permute(): lax.ppermute(values, axes, [(at, at ^ distance) for at in range(size)])  19.3 us
    ppermute x16, starting transfers between devices, permute(): lax.ppermute(values, axes, [(at, at ^ distance) for at in range(size)])  18.2 us
    all_to_all x2, starting transfers between devices, exchange_all(): lax.all_to_all(flat, ('half', *within), split_axis=0, concat_axis=0, tile...  10.9 us
  transfers between devices with their start and end apart: 18, of which 11 were waited for; matrix products, arithmetic and copies ran while one was open for 0% of the time, Pallas kernels for 15%

profile of v16, /device:TPU:0, one launch (start us, length us, event | category | flops | bytes accessed | tf_op | source)
XLA Modules:
  0.0 99.6 jit_solution(7835463733728199817)
XLA Ops:
  0.6 3.1 %shard_map.113 = bf16[2,16,8,16,128]{4,3,2,1,0:T(8,128)(2,1)} custom-call(bf16[16,128,128]{2,1,0:T(8,128)(2,1)} %pair_h.5, s32[256]{0:T(256)} %mask_h.5, s32[1,256]{1,0:T(1,128)} %bitcast.26, f32[1,128]{1,0:T(1,128)} %bitcast.29, f32[1,128]{1,0:T(1,128)} %bitcast.34, bf16[128,512]{1,0:T(8,128)(2,1)} %proj_h.7), custom_call_target="tpu_custom_call" | custom-call | flops 201326592 | bytes 1310720 | tf_op jit(solution)/shard_map/pallas_call | solution.py:438
  3.7 7.3 %all-to-all-start = ((bf16[32,8,16,128]{3,2,1,0:T(8,128)(2,1)}), bf16[32,8,16,128]{3,2,1,0:T(8,128)(2,1)S(1)}, u32[]{:S(2)}, u32[]{:S(2)}) async-start(bf16[32,8,16,128]{3,2,1,0:T(8,128)(2,1)} %bitcast.25), calls=%async_computation | async-start | bytes 2097152 | tf_op jit(solution)/shard_map/all_to_all | solution.py:493
  11.0 2.2 %shard_map.116 = (bf16[8,8,16,128]{3,2,1,0:T(8,128)(2,1)S(1)}, bf16[8,8,16,128]{3,2,1,0:T(8,128)(2,1)S(1)}) custom-call(bf16[16,128,128]{2,1,0:T(8,128)(2,1)} %pair_h.5, s32[256]{0:T(256)} %mask_h.5, s32[1,256]{1,0:T(1,128)} %bitcast.27, f32[1,128]{1,0:T(1,128)} %bitcast.30, f32[1,128]{1,0:T(1,128)} %bitcast.35, bf16[128,512]{1,0:T(8,128)(2,1)} %proj_h.7), custom_call_target="tpu_custom_call" | custom-call | flops 201326592 | bytes 1310720 | tf_op jit(solution)/shard_map/pallas_call | solution.py:438
  14.9 1.8 %collective-permute-start.1 = (bf16[2,8,16,128]{3,2,1,0:T(8,128)(2,1)S(1)}, bf16[2,8,16,128]{3,2,1,0:T(8,128)(2,1)S(1)}, u32[]{:S(2)}, u32[]{:S(2)}) collective-permute-start(bf16[2,8,16,128]{3,2,1,0:T(8,128)(2,1)S(1)} %pad_maximum_fusion), channel_id=1, source_target_pairs={{0,1},{1,0},{4,5},{5,4},{8,9},{9,8},{12,13},{13,12},{2,3},{3,2},{6... | collective-permute-start | bytes 196616 | tf_op jit(solution)/shard_map/ppermute | solution.py:498
  16.8 1.5 %collective-permute-start.2 = (bf16[2,8,16,128]{3,2,1,0:T(8,128)(2,1)S(1)}, bf16[2,8,16,128]{3,2,1,0:T(8,128)(2,1)S(1)}, u32[]{:S(2)}, u32[]{:S(2)}) collective-permute-start(bf16[2,8,16,128]{3,2,1,0:T(8,128)(2,1)S(1)} %pad_maximum_fusion.1), channel_id=1, source_target_pairs={{0,4},{1,5},{4,0},{5,1},{8,12},{9,13},{12,8},{13,9},{2,6},{3,7},{6... | collective-permute-start | bytes 196616 | tf_op jit(solution)/shard_map/ppermute | solution.py:498
  18.6 1.8 %collective-permute-start.4 = (bf16[2,8,16,128]{3,2,1,0:T(8,128)(2,1)S(1)}, bf16[2,8,16,128]{3,2,1,0:T(8,128)(2,1)S(1)}, u32[]{:S(2)}, u32[]{:S(2)}) collective-permute-start(bf16[2,8,16,128]{3,2,1,0:T(8,128)(2,1)S(1)} %pad_maximum_fusion.3), channel_id=1, source_target_pairs={{0,8},{1,9},{4,12},{5,13},{8,0},{9,1},{12,4},{13,5},{2,10},{3,11},... | collective-permute-start | bytes 196616 | tf_op jit(solution)/shard_map/ppermute | solution.py:498
  20.5 1.5 %collective-permute-start.5 = (bf16[2,8,16,128]{3,2,1,0:T(8,128)(2,1)S(1)}, bf16[2,8,16,128]{3,2,1,0:T(8,128)(2,1)S(1)}, u32[]{:S(2)}, u32[]{:S(2)}) collective-permute-start(bf16[2,8,16,128]{3,2,1,0:T(8,128)(2,1)S(1)} %pad_maximum_fusion.4), channel_id=1, source_target_pairs={{0,9},{1,8},{4,13},{5,12},{8,1},{9,0},{12,5},{13,4},{2,11},{3,10},... | collective-permute-start | bytes 196616 | tf_op jit(solution)/shard_map/ppermute | solution.py:498
  22.8 1.6 %collective-permute-start.6 = (bf16[2,8,16,128]{3,2,1,0:T(8,128)(2,1)S(1)}, bf16[2,8,16,128]{3,2,1,0:T(8,128)(2,1)S(1)}, u32[]{:S(2)}, u32[]{:S(2)}) collective-permute-start(bf16[2,8,16,128]{3,2,1,0:T(8,128)(2,1)S(1)} %pad_maximum_fusion.5), channel_id=1, source_target_pairs={{0,12},{1,13},{4,8},{5,9},{8,4},{9,5},{12,0},{13,1},{2,14},{3,15},... | collective-permute-start | bytes 196616 | tf_op jit(solution)/shard_map/ppermute | solution.py:498
  25.6 4.5 %shard_map.114 = (f32[16,128,128]{2,1,0:T(8,128)}, bf16[16,128,128]{2,1,0:T(8,128)(2,1)}, f32[16,128]{1,0:T(8,128)}, f32[16,128,128]{2,1,0:T(8,128)}, f32[2048,128]{1,0:T(8,128)S(1)}) custom-call(bf16[16,128,128]{2,1,0:T(8,128)(2,1)} %pair_h.5, bf16[16,128,128]{2,1,0:T(8,128)(2,1)} %cot_h.3, f32[1,128]{1,0:T(1,128)} %bitcast.31, f32[1,128]{1,0:T(1,128)} %bitcast.36, ...), custom_call_target="tpu_custom_call" | custom-call | flops 268435456 | bytes 4194304 | tf_op jit(solution)/shard_map/pallas_call | solution.py:438
  30.1 3.1 %shard_map.115.after.coef_h = bf16[16,4,128,128]{3,2,1,0:T(8,128)(2,1)} custom-call(f32[16,128,128]{2,1,0:T(8,128)} %get-tuple-element.15.zhat_h, s32[256]{0:T(256)} %mask_h.5, s32[1,256]{1,0:T(1,128)} %bitcast.28, f32[1,128]{1,0:T(1,128)} %bitcast.32, f32[1,128]{1,0:T(1,128)} %bitcast.37, bf16[128,512]{1,0:T(8,128)(2,1)} %proj_h.7), custom_call_target="tpu_custom_call" | custom-call | flops 335544320 | bytes 4194304 | tf_op jit(solution)/shard_map/pallas_call | solution.py:438
  34.6 2.9 %collective-permute-done.7.refs_8_ = bf16[2,8,16,128]{3,2,1,0:T(8,128)(2,1)S(1)} collective-permute-done((bf16[2,8,16,128]{3,2,1,0:T(8,128)(2,1)S(1)}, bf16[2,8,16,128]{3,2,1,0:T(8,128)(2,1)S(1)}, u32[]{:S(2)}, u32[]{:S(2)}) %collective-permute-start.7) | collective-permute-done | bytes 65568 | tf_op jit(solution)/shard_map/ppermute | solution.py:498
  38.0 12.9 %all_to_all.20 = bf16[16,8,16,128]{3,2,1,0:T(8,128)(2,1)S(1)} all-to-all(bf16[16,8,16,128]{3,2,1,0:T(8,128)(2,1)S(1)} %bitcast.23), channel_id=1, replica_groups=mesh['grp'=1,'half'=2,'row'=4,'core'=2,'col'=2] {'row','core','col'}, dimensions={0} | all-to-all | bytes 1048576 | tf_op jit(solution)/shard_map/all_to_all | solution.py:489
  51.5 12.0 %all_to_all.21 = bf16[16,8,16,128]{3,2,1,0:T(8,128)(2,1)S(1)} all-to-all(bf16[16,8,16,128]{3,2,1,0:T(8,128)(2,1)S(1)} %bitcast.21), channel_id=1, replica_groups=mesh['grp'=1,'half'=2,'row'=4,'core'=2,'col'=2] {'row','core','col'}, dimensions={0} | all-to-all | bytes 1048576 | tf_op jit(solution)/shard_map/all_to_all | solution.py:489
  64.8 3.6 %all-to-all-start.3 = ((bf16[32,8,16,128]{3,2,1,0:T(8,128)(2,1)}), bf16[32,8,16,128]{3,2,1,0:T(8,128)(2,1)S(1)}, u32[]{:S(2)}, u32[]{:S(2)}) async-start(bf16[32,8,16,128]{3,2,1,0:T(8,128)(2,1)} %bitcast.24), calls=%async_computation.3 | async-start | bytes 2097152 | tf_op jit(solution)/shard_map/all_to_all | solution.py:493
  69.0 1.4 %collective-permute-done.8.refs_1_ = bf16[8,8,16,128]{3,2,1,0:T(8,128)(2,1)S(1)} collective-permute-done((bf16[8,8,16,128]{3,2,1,0:T(8,128)(2,1)S(1)}, bf16[8,8,16,128]{3,2,1,0:T(8,128)(2,1)S(1)}, u32[]{:S(2)}, u32[]{:S(2)}) %collective-permute-start.8) | collective-permute-done | bytes 262176 | tf_op jit(solution)/shard_map/ppermute | solution.py:498
  70.5 1.7 %collective-permute-start.9 = (bf16[2,8,16,128]{3,2,1,0:T(8,128)(2,1)S(1)}, bf16[2,8,16,128]{3,2,1,0:T(8,128)(2,1)S(1)}, u32[]{:S(2)}, u32[]{:S(2)}) collective-permute-start(bf16[2,8,16,128]{3,2,1,0:T(8,128)(2,1)S(1)} %pad_maximum_fusion.7), channel_id=1, source_target_pairs={{0,1},{1,0},{4,5},{5,4},{8,9},{9,8},{12,13},{13,12},{2,3},{3,2},{6... | collective-permute-start | bytes 196616 | tf_op jit(solution)/shard_map/ppermute | solution.py:498
  72.2 1.5 %collective-permute-start.10 = (bf16[2,8,16,128]{3,2,1,0:T(8,128)(2,1)S(1)}, bf16[2,8,16,128]{3,2,1,0:T(8,128)(2,1)S(1)}, u32[]{:S(2)}, u32[]{:S(2)}) collective-permute-start(bf16[2,8,16,128]{3,2,1,0:T(8,128)(2,1)S(1)} %pad_maximum_fusion.8), channel_id=1, source_target_pairs={{0,4},{1,5},{4,0},{5,1},{8,12},{9,13},{12,8},{13,9},{2,6},{3,7},{6... | collective-permute-start | bytes 196616 | tf_op jit(solution)/shard_map/ppermute | solution.py:498
  74.2 1.7 %collective-permute-start.12 = (bf16[2,8,16,128]{3,2,1,0:T(8,128)(2,1)S(1)}, bf16[2,8,16,128]{3,2,1,0:T(8,128)(2,1)S(1)}, u32[]{:S(2)}, u32[]{:S(2)}) collective-permute-start(bf16[2,8,16,128]{3,2,1,0:T(8,128)(2,1)S(1)} %pad_maximum_fusion.10), channel_id=1, source_target_pairs={{0,8},{1,9},{4,12},{5,13},{8,0},{9,1},{12,4},{13,5},{2,10},{3,11},... | collective-permute-start | bytes 196616 | tf_op jit(solution)/shard_map/ppermute | solution.py:498
  75.9 1.5 %collective-permute-start.13 = (bf16[2,8,16,128]{3,2,1,0:T(8,128)(2,1)S(1)}, bf16[2,8,16,128]{3,2,1,0:T(8,128)(2,1)S(1)}, u32[]{:S(2)}, u32[]{:S(2)}) collective-permute-start(bf16[2,8,16,128]{3,2,1,0:T(8,128)(2,1)S(1)} %pad_maximum_fusion.11), channel_id=1, source_target_pairs={{0,9},{1,8},{4,13},{5,12},{8,1},{9,0},{12,5},{13,4},{2,11},{3,10},... | collective-permute-start | bytes 196616 | tf_op jit(solution)/shard_map/ppermute | solution.py:498
  77.4 2.9 %collective-permute-done.9.refs_2_ = bf16[2,8,16,128]{3,2,1,0:T(8,128)(2,1)S(1)} collective-permute-done((bf16[2,8,16,128]{3,2,1,0:T(8,128)(2,1)S(1)}, bf16[2,8,16,128]{3,2,1,0:T(8,128)(2,1)S(1)}, u32[]{:S(2)}, u32[]{:S(2)}) %collective-permute-start.9) | collective-permute-done | bytes 65568 | tf_op jit(solution)/shard_map/ppermute | solution.py:498
  83.3 4.5 %shard_map.120 = (bf16[16,128,128]{2,1,0:T(8,128)(2,1)}, bf16[16,128,128]{2,1,0:T(8,128)(2,1)}) custom-call(bf16[128,16,128]{2,1,0:T(8,128)(2,1)S(1)} %bitcast.19, f32[16,128,128]{2,1,0:T(8,128)} %get-tuple-element.19.gate_h, bf16[16,128,128]{2,1,0:T(8,128)(2,1)} %cot_h.3, f32[1,128]{1,0:T(1,128)} %bitcast.39, f32[1,128]{1,0:T(1,128)} %bitcast.40, ...), custom_call_target="tpu_custom_call" | custom-call | flops 201326592 | bytes 3670016 | tf_op jit(solution)/shard_map/pallas_call | solution.py:438
  89.2 2.7 %collective-permute-done.14.refs_7_ = bf16[2,8,16,128]{3,2,1,0:T(8,128)(2,1)S(1)} collective-permute-done((bf16[2,8,16,128]{3,2,1,0:T(8,128)(2,1)S(1)}, bf16[2,8,16,128]{3,2,1,0:T(8,128)(2,1)S(1)}, u32[]{:S(2)}, u32[]{:S(2)}) %collective-permute-start.14) | collective-permute-done | bytes 65568 | tf_op jit(solution)/shard_map/ppermute | solution.py:498
  91.8 2.9 %collective-permute-done.15.refs_8_ = bf16[2,8,16,128]{3,2,1,0:T(8,128)(2,1)S(1)} collective-permute-done((bf16[2,8,16,128]{3,2,1,0:T(8,128)(2,1)S(1)}, bf16[2,8,16,128]{3,2,1,0:T(8,128)(2,1)S(1)}, u32[]{:S(2)}, u32[]{:S(2)}) %collective-permute-start.15) | collective-permute-done | bytes 65568 | tf_op jit(solution)/shard_map/ppermute | solution.py:498
  94.7 4.7 %shard_map.122 = bf16[16,128,128]{2,1,0:T(8,128)(2,1)} custom-call(bf16[2,16,8,16,128]{4,3,2,1,0:T(8,128)(2,1)S(1)} %bitcast.20, bf16[16,4,128,128]{3,2,1,0:T(8,128)(2,1)} %shard_map.115.after.coef_h, bf16[16,128,128]{2,1,0:T(8,128)(2,1)} %get-tuple-element.23.zhat_h, f32[16,128]{1,0:T(8,128)} %get-tuple-element.24.inv_h, ...), custom_call_target="tpu_custom_call" | custom-call | flops 335544320 | bytes 7864320 | tf_op jit(solution)/shard_map/pallas_call | solution.py:438
  (42 shorter events, 13.1 us)
Async XLA Ops:
  3.7 33.7 %all-to-all-start = ((bf16[32,8,16,128]{3,2,1,0:T(8,128)(2,1)}), bf16[32,8,16,128]{3,2,1,0:T(8,128)(2,1)S(1)}, u32[]{:S(2)}, u32[]{:S(2)}) async-start(bf16[32,8,16,128]{3,2,1,0:T(8,128)(2,1)} %bitcast.25), calls=%async_computation | async-start | bytes 2097152 | tf_op jit(solution)/shard_map/all_to_all | solution.py:493
  13.3 1.6 %collective-permute-start = (bf16[8,8,16,128]{3,2,1,0:T(8,128)(2,1)S(1)}, bf16[8,8,16,128]{3,2,1,0:T(8,128)(2,1)S(1)}, u32[]{:S(2)}, u32[]{:S(2)}) collective-permute-start(bf16[8,8,16,128]{3,2,1,0:T(8,128)(2,1)S(1)} %get-tuple-element.17), channel_id=1, source_target_pairs={{0,2},{2,0},{1,3},{3,1},{4,6},{6,4},{5,7},{7,5},{8,10},{10,8},{9,1... | collective-permute-start | bytes 786440 | tf_op jit(solution)/shard_map/ppermute | solution.py:498
  14.9 7.9 %collective-permute-start.1 = (bf16[2,8,16,128]{3,2,1,0:T(8,128)(2,1)S(1)}, bf16[2,8,16,128]{3,2,1,0:T(8,128)(2,1)S(1)}, u32[]{:S(2)}, u32[]{:S(2)}) collective-permute-start(bf16[2,8,16,128]{3,2,1,0:T(8,128)(2,1)S(1)} %pad_maximum_fusion), channel_id=1, source_target_pairs={{0,1},{1,0},{4,5},{5,4},{8,9},{9,8},{12,13},{13,12},{2,3},{3,2},{6... | collective-permute-start | bytes 196616 | tf_op jit(solution)/shard_map/ppermute | solution.py:498
  16.8 8.3 %collective-permute-start.2 = (bf16[2,8,16,128]{3,2,1,0:T(8,128)(2,1)S(1)}, bf16[2,8,16,128]{3,2,1,0:T(8,128)(2,1)S(1)}, u32[]{:S(2)}, u32[]{:S(2)}) collective-permute-start(bf16[2,8,16,128]{3,2,1,0:T(8,128)(2,1)S(1)} %pad_maximum_fusion.1), channel_id=1, source_target_pairs={{0,4},{1,5},{4,0},{5,1},{8,12},{9,13},{12,8},{13,9},{2,6},{3,7},{6... | collective-permute-start | bytes 196616 | tf_op jit(solution)/shard_map/ppermute | solution.py:498
  18.3 15.0 %collective-permute-start.3 = (bf16[2,8,16,128]{3,2,1,0:T(8,128)(2,1)S(1)}, bf16[2,8,16,128]{3,2,1,0:T(8,128)(2,1)S(1)}, u32[]{:S(2)}, u32[]{:S(2)}) collective-permute-start(bf16[2,8,16,128]{3,2,1,0:T(8,128)(2,1)S(1)} %pad_maximum_fusion.2), channel_id=1, source_target_pairs={{0,5},{1,4},{4,1},{5,0},{8,13},{9,12},{12,9},{13,8},{2,7},{3,6},{6... | collective-permute-start | bytes 196616 | tf_op jit(solution)/shard_map/ppermute | solution.py:498
  18.6 14.7 %collective-permute-start.4 = (bf16[2,8,16,128]{3,2,1,0:T(8,128)(2,1)S(1)}, bf16[2,8,16,128]{3,2,1,0:T(8,128)(2,1)S(1)}, u32[]{:S(2)}, u32[]{:S(2)}) collective-permute-start(bf16[2,8,16,128]{3,2,1,0:T(8,128)(2,1)S(1)} %pad_maximum_fusion.3), channel_id=1, source_target_pairs={{0,8},{1,9},{4,12},{5,13},{8,0},{9,1},{12,4},{13,5},{2,10},{3,11},... | collective-permute-start | bytes 196616 | tf_op jit(solution)/shard_map/ppermute | solution.py:498
  20.5 12.9 %collective-permute-start.5 = (bf16[2,8,16,128]{3,2,1,0:T(8,128)(2,1)S(1)}, bf16[2,8,16,128]{3,2,1,0:T(8,128)(2,1)S(1)}, u32[]{:S(2)}, u32[]{:S(2)}) collective-permute-start(bf16[2,8,16,128]{3,2,1,0:T(8,128)(2,1)S(1)} %pad_maximum_fusion.4), channel_id=1, source_target_pairs={{0,9},{1,8},{4,13},{5,12},{8,1},{9,0},{12,5},{13,4},{2,11},{3,10},... | collective-permute-start | bytes 196616 | tf_op jit(solution)/shard_map/ppermute | solution.py:498
  22.8 11.8 %collective-permute-start.6 = (bf16[2,8,16,128]{3,2,1,0:T(8,128)(2,1)S(1)}, bf16[2,8,16,128]{3,2,1,0:T(8,128)(2,1)S(1)}, u32[]{:S(2)}, u32[]{:S(2)}) collective-permute-start(bf16[2,8,16,128]{3,2,1,0:T(8,128)(2,1)S(1)} %pad_maximum_fusion.5), channel_id=1, source_target_pairs={{0,12},{1,13},{4,8},{5,9},{8,4},{9,5},{12,0},{13,1},{2,14},{3,15},... | collective-permute-start | bytes 196616 | tf_op jit(solution)/shard_map/ppermute | solution.py:498
  25.0 12.5 %collective-permute-start.7 = (bf16[2,8,16,128]{3,2,1,0:T(8,128)(2,1)S(1)}, bf16[2,8,16,128]{3,2,1,0:T(8,128)(2,1)S(1)}, u32[]{:S(2)}, u32[]{:S(2)}) collective-permute-start(bf16[2,8,16,128]{3,2,1,0:T(8,128)(2,1)S(1)} %pad_maximum_fusion.6), channel_id=1, source_target_pairs={{0,13},{1,12},{4,9},{5,8},{8,5},{9,4},{12,1},{13,0},{2,15},{3,14},... | collective-permute-start | bytes 196616 | tf_op jit(solution)/shard_map/ppermute | solution.py:498
  64.8 29.9 %all-to-all-start.3 = ((bf16[32,8,16,128]{3,2,1,0:T(8,128)(2,1)}), bf16[32,8,16,128]{3,2,1,0:T(8,128)(2,1)S(1)}, u32[]{:S(2)}, u32[]{:S(2)}) async-start(bf16[32,8,16,128]{3,2,1,0:T(8,128)(2,1)} %bitcast.24), calls=%async_computation.3 | async-start | bytes 2097152 | tf_op jit(solution)/shard_map/all_to_all | solution.py:493
  68.9 1.6 %collective-permute-start.8 = (bf16[8,8,16,128]{3,2,1,0:T(8,128)(2,1)S(1)}, bf16[8,8,16,128]{3,2,1,0:T(8,128)(2,1)S(1)}, u32[]{:S(2)}, u32[]{:S(2)}) collective-permute-start(bf16[8,8,16,128]{3,2,1,0:T(8,128)(2,1)S(1)} %get-tuple-element.27), channel_id=1, source_target_pairs={{0,2},{2,0},{1,3},{3,1},{4,6},{6,4},{5,7},{7,5},{8,10},{10,8},{9,1... | collective-permute-start | bytes 786440 | tf_op jit(solution)/shard_map/ppermute | solution.py:498
  70.5 9.8 %collective-permute-start.9 = (bf16[2,8,16,128]{3,2,1,0:T(8,128)(2,1)S(1)}, bf16[2,8,16,128]{3,2,1,0:T(8,128)(2,1)S(1)}, u32[]{:S(2)}, u32[]{:S(2)}) collective-permute-start(bf16[2,8,16,128]{3,2,1,0:T(8,128)(2,1)S(1)} %pad_maximum_fusion.7), channel_id=1, source_target_pairs={{0,1},{1,0},{4,5},{5,4},{8,9},{9,8},{12,13},{13,12},{2,3},{3,2},{6... | collective-permute-start | bytes 196616 | tf_op jit(solution)/shard_map/ppermute | solution.py:498
  72.2 9.9 %collective-permute-start.10 = (bf16[2,8,16,128]{3,2,1,0:T(8,128)(2,1)S(1)}, bf16[2,8,16,128]{3,2,1,0:T(8,128)(2,1)S(1)}, u32[]{:S(2)}, u32[]{:S(2)}) collective-permute-start(bf16[2,8,16,128]{3,2,1,0:T(8,128)(2,1)S(1)} %pad_maximum_fusion.8), channel_id=1, source_target_pairs={{0,4},{1,5},{4,0},{5,1},{8,12},{9,13},{12,8},{13,9},{2,6},{3,7},{6... | collective-permute-start | bytes 196616 | tf_op jit(solution)/shard_map/ppermute | solution.py:498
  73.7 14.2 %collective-permute-start.11 = (bf16[2,8,16,128]{3,2,1,0:T(8,128)(2,1)S(1)}, bf16[2,8,16,128]{3,2,1,0:T(8,128)(2,1)S(1)}, u32[]{:S(2)}, u32[]{:S(2)}) collective-permute-start(bf16[2,8,16,128]{3,2,1,0:T(8,128)(2,1)S(1)} %pad_maximum_fusion.9), channel_id=1, source_target_pairs={{0,5},{1,4},{4,1},{5,0},{8,13},{9,12},{12,9},{13,8},{2,7},{3,6},{6... | collective-permute-start | bytes 196616 | tf_op jit(solution)/shard_map/ppermute | solution.py:498
  74.2 13.7 %collective-permute-start.12 = (bf16[2,8,16,128]{3,2,1,0:T(8,128)(2,1)S(1)}, bf16[2,8,16,128]{3,2,1,0:T(8,128)(2,1)S(1)}, u32[]{:S(2)}, u32[]{:S(2)}) collective-permute-start(bf16[2,8,16,128]{3,2,1,0:T(8,128)(2,1)S(1)} %pad_maximum_fusion.10), channel_id=1, source_target_pairs={{0,8},{1,9},{4,12},{5,13},{8,0},{9,1},{12,4},{13,5},{2,10},{3,11},... | collective-permute-start | bytes 196616 | tf_op jit(solution)/shard_map/ppermute | solution.py:498
  75.9 13.3 %collective-permute-start.13 = (bf16[2,8,16,128]{3,2,1,0:T(8,128)(2,1)S(1)}, bf16[2,8,16,128]{3,2,1,0:T(8,128)(2,1)S(1)}, u32[]{:S(2)}, u32[]{:S(2)}) collective-permute-start(bf16[2,8,16,128]{3,2,1,0:T(8,128)(2,1)S(1)} %pad_maximum_fusion.11), channel_id=1, source_target_pairs={{0,9},{1,8},{4,13},{5,12},{8,1},{9,0},{12,5},{13,4},{2,11},{3,10},... | collective-permute-start | bytes 196616 | tf_op jit(solution)/shard_map/ppermute | solution.py:498
  80.3 11.5 %collective-permute-start.14 = (bf16[2,8,16,128]{3,2,1,0:T(8,128)(2,1)S(1)}, bf16[2,8,16,128]{3,2,1,0:T(8,128)(2,1)S(1)}, u32[]{:S(2)}, u32[]{:S(2)}) collective-permute-start(bf16[2,8,16,128]{3,2,1,0:T(8,128)(2,1)S(1)} %pad_maximum_fusion.12), channel_id=1, source_target_pairs={{0,12},{1,13},{4,8},{5,9},{8,4},{9,5},{12,0},{13,1},{2,14},{3,15},... | collective-permute-start | bytes 196616 | tf_op jit(solution)/shard_map/ppermute | solution.py:498
  82.1 12.6 %collective-permute-start.15 = (bf16[2,8,16,128]{3,2,1,0:T(8,128)(2,1)S(1)}, bf16[2,8,16,128]{3,2,1,0:T(8,128)(2,1)S(1)}, u32[]{:S(2)}, u32[]{:S(2)}) collective-permute-start(bf16[2,8,16,128]{3,2,1,0:T(8,128)(2,1)S(1)} %pad_maximum_fusion.13), channel_id=1, source_target_pairs={{0,13},{1,12},{4,9},{5,8},{8,5},{9,4},{12,1},{13,0},{2,15},{3,14},... | collective-permute-start | bytes 196616 | tf_op jit(solution)/shard_map/ppermute | solution.py:498

commit v17 on v16

--- a/solution.py
+++ b/solution.py
@@ -371,7 +371,6 @@
     rows, cols, width = out.shape
     hidden = left.shape[0] // rows
     groups, parts = groups_of(rows), groups_of(rows, 4)
-    small = start(sems, [(gain_h, gain), (proj_h, proj_weight), (inv_h, inv)])
     ahead = rows // math.gcd(rows, 2)
     blocks = [
         [
@@ -384,8 +383,9 @@
         ]
         for n, (at, size) in enumerate(parts)
     ]
-    for copy in sum(blocks[:2], []):
+    for copy in sum(blocks, []):
         copy.start()
+    small = start(sems, [(gain_h, gain), (proj_h, proj_weight), (inv_h, inv)])
     arrived = received(pieces, n_chip)
     length = left.shape[0] // len(arrived)
     for number, piece in arrived:
@@ -398,8 +398,6 @@
     wait(small)
     gain_b = jnp.concatenate([down_lanes(gain[...], cols)] * groups[0][1], axis=1)
     leaving = []
-    for copy in sum(blocks[2:], []):
-        copy.start()
     arriving = {at: copies for (at, _), copies in zip(parts, blocks)}
     for at, size in groups:
         wait(arriving.get(at, []))

time: 100 us -> 100 us (level)
  no operation moved by 1% of the time
where the time goes in v17:
time: 100 us; the launch traced here: 99.9 us
  starting transfers between devices  29.1 us (29%)
  Pallas kernels  25.4 us (25%)
  blocking collectives  24.9 us (25%)
  waiting for transfers between devices  19.3 us (19%)
    pallas_call x10, Pallas kernels, call(): pl.pallas_call(kernel, out_shape=[out if at in outs_near else pltpu.HBM(o...  25.4 us
    all_to_all x2, blocking collectives, exchange(): lax.all_to_all(values, within, split_axis=0, concat_axis=0, tiled=True)  24.9 us
    ppermute x16, waiting for transfers between devices, permute(): lax.ppermute(values, axes, [(at, at ^ distance) for at in range(size)])  19.3 us
    ppermute x16, starting transfers between devices, permute(): lax.ppermute(values, axes, [(at, at ^ distance) for at in range(size)])  18.2 us
    all_to_all x2, starting transfers between devices, exchange_all(): lax.all_to_all(flat, ('half', *within), split_axis=0, concat_axis=0, tile...  10.9 us
  transfers between devices with their start and end apart: 18, of which 11 were waited for; matrix products, arithmetic and copies ran while one was open for 0% of the time, Pallas kernels for 15%

profile of v17, /device:TPU:0, one launch (start us, length us, event | category | flops | bytes accessed | tf_op | source)
XLA Modules:
  0.0 99.9 jit_solution(3410384678226347184)
XLA Ops:
  0.6 3.1 %shard_map.113 = bf16[2,16,8,16,128]{4,3,2,1,0:T(8,128)(2,1)} custom-call(bf16[16,128,128]{2,1,0:T(8,128)(2,1)} %pair_h.5, s32[256]{0:T(256)} %mask_h.5, s32[1,256]{1,0:T(1,128)} %bitcast.26, f32[1,128]{1,0:T(1,128)} %bitcast.29, f32[1,128]{1,0:T(1,128)} %bitcast.34, bf16[128,512]{1,0:T(8,128)(2,1)} %proj_h.7), custom_call_target="tpu_custom_call" | custom-call | flops 201326592 | bytes 1310720 | tf_op jit(solution)/shard_map/pallas_call | solution.py:436
  3.7 7.3 %all-to-all-start = ((bf16[32,8,16,128]{3,2,1,0:T(8,128)(2,1)}), bf16[32,8,16,128]{3,2,1,0:T(8,128)(2,1)S(1)}, u32[]{:S(2)}, u32[]{:S(2)}) async-start(bf16[32,8,16,128]{3,2,1,0:T(8,128)(2,1)} %bitcast.25), calls=%async_computation | async-start | bytes 2097152 | tf_op jit(solution)/shard_map/all_to_all | solution.py:491
  11.0 2.2 %shard_map.116 = (bf16[8,8,16,128]{3,2,1,0:T(8,128)(2,1)S(1)}, bf16[8,8,16,128]{3,2,1,0:T(8,128)(2,1)S(1)}) custom-call(bf16[16,128,128]{2,1,0:T(8,128)(2,1)} %pair_h.5, s32[256]{0:T(256)} %mask_h.5, s32[1,256]{1,0:T(1,128)} %bitcast.27, f32[1,128]{1,0:T(1,128)} %bitcast.30, f32[1,128]{1,0:T(1,128)} %bitcast.35, bf16[128,512]{1,0:T(8,128)(2,1)} %proj_h.7), custom_call_target="tpu_custom_call" | custom-call | flops 201326592 | bytes 1310720 | tf_op jit(solution)/shard_map/pallas_call | solution.py:436
  14.9 1.8 %collective-permute-start.1 = (bf16[2,8,16,128]{3,2,1,0:T(8,128)(2,1)S(1)}, bf16[2,8,16,128]{3,2,1,0:T(8,128)(2,1)S(1)}, u32[]{:S(2)}, u32[]{:S(2)}) collective-permute-start(bf16[2,8,16,128]{3,2,1,0:T(8,128)(2,1)S(1)} %pad_maximum_fusion), channel_id=1, source_target_pairs={{0,1},{1,0},{4,5},{5,4},{8,9},{9,8},{12,13},{13,12},{2,3},{3,2},{6... | collective-permute-start | bytes 196616 | tf_op jit(solution)/shard_map/ppermute | solution.py:496
  16.8 1.5 %collective-permute-start.2 = (bf16[2,8,16,128]{3,2,1,0:T(8,128)(2,1)S(1)}, bf16[2,8,16,128]{3,2,1,0:T(8,128)(2,1)S(1)}, u32[]{:S(2)}, u32[]{:S(2)}) collective-permute-start(bf16[2,8,16,128]{3,2,1,0:T(8,128)(2,1)S(1)} %pad_maximum_fusion.1), channel_id=1, source_target_pairs={{0,4},{1,5},{4,0},{5,1},{8,12},{9,13},{12,8},{13,9},{2,6},{3,7},{6... | collective-permute-start | bytes 196616 | tf_op jit(solution)/shard_map/ppermute | solution.py:496
  18.6 1.8 %collective-permute-start.4 = (bf16[2,8,16,128]{3,2,1,0:T(8,128)(2,1)S(1)}, bf16[2,8,16,128]{3,2,1,0:T(8,128)(2,1)S(1)}, u32[]{:S(2)}, u32[]{:S(2)}) collective-permute-start(bf16[2,8,16,128]{3,2,1,0:T(8,128)(2,1)S(1)} %pad_maximum_fusion.3), channel_id=1, source_target_pairs={{0,8},{1,9},{4,12},{5,13},{8,0},{9,1},{12,4},{13,5},{2,10},{3,11},... | collective-permute-start | bytes 196616 | tf_op jit(solution)/shard_map/ppermute | solution.py:496
  20.5 1.5 %collective-permute-start.5 = (bf16[2,8,16,128]{3,2,1,0:T(8,128)(2,1)S(1)}, bf16[2,8,16,128]{3,2,1,0:T(8,128)(2,1)S(1)}, u32[]{:S(2)}, u32[]{:S(2)}) collective-permute-start(bf16[2,8,16,128]{3,2,1,0:T(8,128)(2,1)S(1)} %pad_maximum_fusion.4), channel_id=1, source_target_pairs={{0,9},{1,8},{4,13},{5,12},{8,1},{9,0},{12,5},{13,4},{2,11},{3,10},... | collective-permute-start | bytes 196616 | tf_op jit(solution)/shard_map/ppermute | solution.py:496
  22.8 1.6 %collective-permute-start.6 = (bf16[2,8,16,128]{3,2,1,0:T(8,128)(2,1)S(1)}, bf16[2,8,16,128]{3,2,1,0:T(8,128)(2,1)S(1)}, u32[]{:S(2)}, u32[]{:S(2)}) collective-permute-start(bf16[2,8,16,128]{3,2,1,0:T(8,128)(2,1)S(1)} %pad_maximum_fusion.5), channel_id=1, source_target_pairs={{0,12},{1,13},{4,8},{5,9},{8,4},{9,5},{12,0},{13,1},{2,14},{3,15},... | collective-permute-start | bytes 196616 | tf_op jit(solution)/shard_map/ppermute | solution.py:496
  25.6 4.5 %shard_map.114 = (f32[16,128,128]{2,1,0:T(8,128)}, bf16[16,128,128]{2,1,0:T(8,128)(2,1)}, f32[16,128]{1,0:T(8,128)}, f32[16,128,128]{2,1,0:T(8,128)}, f32[2048,128]{1,0:T(8,128)S(1)}) custom-call(bf16[16,128,128]{2,1,0:T(8,128)(2,1)} %pair_h.5, bf16[16,128,128]{2,1,0:T(8,128)(2,1)} %cot_h.3, f32[1,128]{1,0:T(1,128)} %bitcast.31, f32[1,128]{1,0:T(1,128)} %bitcast.36, ...), custom_call_target="tpu_custom_call" | custom-call | flops 268435456 | bytes 4194304 | tf_op jit(solution)/shard_map/pallas_call | solution.py:436
  30.1 3.1 %shard_map.115.after.coef_h = bf16[16,4,128,128]{3,2,1,0:T(8,128)(2,1)} custom-call(f32[16,128,128]{2,1,0:T(8,128)} %get-tuple-element.15.zhat_h, s32[256]{0:T(256)} %mask_h.5, s32[1,256]{1,0:T(1,128)} %bitcast.28, f32[1,128]{1,0:T(1,128)} %bitcast.32, f32[1,128]{1,0:T(1,128)} %bitcast.37, bf16[128,512]{1,0:T(8,128)(2,1)} %proj_h.7), custom_call_target="tpu_custom_call" | custom-call | flops 335544320 | bytes 4194304 | tf_op jit(solution)/shard_map/pallas_call | solution.py:436
  34.6 2.9 %collective-permute-done.7.refs_8_ = bf16[2,8,16,128]{3,2,1,0:T(8,128)(2,1)S(1)} collective-permute-done((bf16[2,8,16,128]{3,2,1,0:T(8,128)(2,1)S(1)}, bf16[2,8,16,128]{3,2,1,0:T(8,128)(2,1)S(1)}, u32[]{:S(2)}, u32[]{:S(2)}) %collective-permute-start.7) | collective-permute-done | bytes 65568 | tf_op jit(solution)/shard_map/ppermute | solution.py:496
  38.0 12.9 %all_to_all.20 = bf16[16,8,16,128]{3,2,1,0:T(8,128)(2,1)S(1)} all-to-all(bf16[16,8,16,128]{3,2,1,0:T(8,128)(2,1)S(1)} %bitcast.23), channel_id=1, replica_groups=mesh['grp'=1,'half'=2,'row'=4,'core'=2,'col'=2] {'row','core','col'}, dimensions={0} | all-to-all | bytes 1048576 | tf_op jit(solution)/shard_map/all_to_all | solution.py:487
  51.5 12.0 %all_to_all.21 = bf16[16,8,16,128]{3,2,1,0:T(8,128)(2,1)S(1)} all-to-all(bf16[16,8,16,128]{3,2,1,0:T(8,128)(2,1)S(1)} %bitcast.21), channel_id=1, replica_groups=mesh['grp'=1,'half'=2,'row'=4,'core'=2,'col'=2] {'row','core','col'}, dimensions={0} | all-to-all | bytes 1048576 | tf_op jit(solution)/shard_map/all_to_all | solution.py:487
  64.8 3.6 %all-to-all-start.3 = ((bf16[32,8,16,128]{3,2,1,0:T(8,128)(2,1)}), bf16[32,8,16,128]{3,2,1,0:T(8,128)(2,1)S(1)}, u32[]{:S(2)}, u32[]{:S(2)}) async-start(bf16[32,8,16,128]{3,2,1,0:T(8,128)(2,1)} %bitcast.24), calls=%async_computation.3 | async-start | bytes 2097152 | tf_op jit(solution)/shard_map/all_to_all | solution.py:491
  69.0 1.4 %collective-permute-done.8.refs_1_ = bf16[8,8,16,128]{3,2,1,0:T(8,128)(2,1)S(1)} collective-permute-done((bf16[8,8,16,128]{3,2,1,0:T(8,128)(2,1)S(1)}, bf16[8,8,16,128]{3,2,1,0:T(8,128)(2,1)S(1)}, u32[]{:S(2)}, u32[]{:S(2)}) %collective-permute-start.8) | collective-permute-done | bytes 262176 | tf_op jit(solution)/shard_map/ppermute | solution.py:496
  70.5 1.7 %collective-permute-start.9 = (bf16[2,8,16,128]{3,2,1,0:T(8,128)(2,1)S(1)}, bf16[2,8,16,128]{3,2,1,0:T(8,128)(2,1)S(1)}, u32[]{:S(2)}, u32[]{:S(2)}) collective-permute-start(bf16[2,8,16,128]{3,2,1,0:T(8,128)(2,1)S(1)} %pad_maximum_fusion.7), channel_id=1, source_target_pairs={{0,1},{1,0},{4,5},{5,4},{8,9},{9,8},{12,13},{13,12},{2,3},{3,2},{6... | collective-permute-start | bytes 196616 | tf_op jit(solution)/shard_map/ppermute | solution.py:496
  72.2 1.5 %collective-permute-start.10 = (bf16[2,8,16,128]{3,2,1,0:T(8,128)(2,1)S(1)}, bf16[2,8,16,128]{3,2,1,0:T(8,128)(2,1)S(1)}, u32[]{:S(2)}, u32[]{:S(2)}) collective-permute-start(bf16[2,8,16,128]{3,2,1,0:T(8,128)(2,1)S(1)} %pad_maximum_fusion.8), channel_id=1, source_target_pairs={{0,4},{1,5},{4,0},{5,1},{8,12},{9,13},{12,8},{13,9},{2,6},{3,7},{6... | collective-permute-start | bytes 196616 | tf_op jit(solution)/shard_map/ppermute | solution.py:496
  74.2 1.7 %collective-permute-start.12 = (bf16[2,8,16,128]{3,2,1,0:T(8,128)(2,1)S(1)}, bf16[2,8,16,128]{3,2,1,0:T(8,128)(2,1)S(1)}, u32[]{:S(2)}, u32[]{:S(2)}) collective-permute-start(bf16[2,8,16,128]{3,2,1,0:T(8,128)(2,1)S(1)} %pad_maximum_fusion.10), channel_id=1, source_target_pairs={{0,8},{1,9},{4,12},{5,13},{8,0},{9,1},{12,4},{13,5},{2,10},{3,11},... | collective-permute-start | bytes 196616 | tf_op jit(solution)/shard_map/ppermute | solution.py:496
  75.9 1.5 %collective-permute-start.13 = (bf16[2,8,16,128]{3,2,1,0:T(8,128)(2,1)S(1)}, bf16[2,8,16,128]{3,2,1,0:T(8,128)(2,1)S(1)}, u32[]{:S(2)}, u32[]{:S(2)}) collective-permute-start(bf16[2,8,16,128]{3,2,1,0:T(8,128)(2,1)S(1)} %pad_maximum_fusion.11), channel_id=1, source_target_pairs={{0,9},{1,8},{4,13},{5,12},{8,1},{9,0},{12,5},{13,4},{2,11},{3,10},... | collective-permute-start | bytes 196616 | tf_op jit(solution)/shard_map/ppermute | solution.py:496
  77.4 2.9 %collective-permute-done.9.refs_2_ = bf16[2,8,16,128]{3,2,1,0:T(8,128)(2,1)S(1)} collective-permute-done((bf16[2,8,16,128]{3,2,1,0:T(8,128)(2,1)S(1)}, bf16[2,8,16,128]{3,2,1,0:T(8,128)(2,1)S(1)}, u32[]{:S(2)}, u32[]{:S(2)}) %collective-permute-start.9) | collective-permute-done | bytes 65568 | tf_op jit(solution)/shard_map/ppermute | solution.py:496
  83.3 4.5 %shard_map.120 = (bf16[16,128,128]{2,1,0:T(8,128)(2,1)}, bf16[16,128,128]{2,1,0:T(8,128)(2,1)}) custom-call(bf16[128,16,128]{2,1,0:T(8,128)(2,1)S(1)} %bitcast.19, f32[16,128,128]{2,1,0:T(8,128)} %get-tuple-element.19.gate_h, bf16[16,128,128]{2,1,0:T(8,128)(2,1)} %cot_h.3, f32[1,128]{1,0:T(1,128)} %bitcast.39, f32[1,128]{1,0:T(1,128)} %bitcast.40, ...), custom_call_target="tpu_custom_call" | custom-call | flops 201326592 | bytes 3670016 | tf_op jit(solution)/shard_map/pallas_call | solution.py:436
  89.2 2.7 %collective-permute-done.14.refs_7_ = bf16[2,8,16,128]{3,2,1,0:T(8,128)(2,1)S(1)} collective-permute-done((bf16[2,8,16,128]{3,2,1,0:T(8,128)(2,1)S(1)}, bf16[2,8,16,128]{3,2,1,0:T(8,128)(2,1)S(1)}, u32[]{:S(2)}, u32[]{:S(2)}) %collective-permute-start.14) | collective-permute-done | bytes 65568 | tf_op jit(solution)/shard_map/ppermute | solution.py:496
  91.8 2.9 %collective-permute-done.15.refs_8_ = bf16[2,8,16,128]{3,2,1,0:T(8,128)(2,1)S(1)} collective-permute-done((bf16[2,8,16,128]{3,2,1,0:T(8,128)(2,1)S(1)}, bf16[2,8,16,128]{3,2,1,0:T(8,128)(2,1)S(1)}, u32[]{:S(2)}, u32[]{:S(2)}) %collective-permute-start.15) | collective-permute-done | bytes 65568 | tf_op jit(solution)/shard_map/ppermute | solution.py:496
  94.7 5.1 %shard_map.122 = bf16[16,128,128]{2,1,0:T(8,128)(2,1)} custom-call(bf16[2,16,8,16,128]{4,3,2,1,0:T(8,128)(2,1)S(1)} %bitcast.20, bf16[16,4,128,128]{3,2,1,0:T(8,128)(2,1)} %shard_map.115.after.coef_h, bf16[16,128,128]{2,1,0:T(8,128)(2,1)} %get-tuple-element.23.zhat_h, f32[16,128]{1,0:T(8,128)} %get-tuple-element.24.inv_h, ...), custom_call_target="tpu_custom_call" | custom-call | flops 335544320 | bytes 7864320 | tf_op jit(solution)/shard_map/pallas_call | solution.py:436
  (42 shorter events, 13.1 us)
Async XLA Ops:
  3.7 33.7 %all-to-all-start = ((bf16[32,8,16,128]{3,2,1,0:T(8,128)(2,1)}), bf16[32,8,16,128]{3,2,1,0:T(8,128)(2,1)S(1)}, u32[]{:S(2)}, u32[]{:S(2)}) async-start(bf16[32,8,16,128]{3,2,1,0:T(8,128)(2,1)} %bitcast.25), calls=%async_computation | async-start | bytes 2097152 | tf_op jit(solution)/shard_map/all_to_all | solution.py:491
  13.3 1.6 %collective-permute-start = (bf16[8,8,16,128]{3,2,1,0:T(8,128)(2,1)S(1)}, bf16[8,8,16,128]{3,2,1,0:T(8,128)(2,1)S(1)}, u32[]{:S(2)}, u32[]{:S(2)}) collective-permute-start(bf16[8,8,16,128]{3,2,1,0:T(8,128)(2,1)S(1)} %get-tuple-element.17), channel_id=1, source_target_pairs={{0,2},{2,0},{1,3},{3,1},{4,6},{6,4},{5,7},{7,5},{8,10},{10,8},{9,1... | collective-permute-start | bytes 786440 | tf_op jit(solution)/shard_map/ppermute | solution.py:496
  14.9 7.9 %collective-permute-start.1 = (bf16[2,8,16,128]{3,2,1,0:T(8,128)(2,1)S(1)}, bf16[2,8,16,128]{3,2,1,0:T(8,128)(2,1)S(1)}, u32[]{:S(2)}, u32[]{:S(2)}) collective-permute-start(bf16[2,8,16,128]{3,2,1,0:T(8,128)(2,1)S(1)} %pad_maximum_fusion), channel_id=1, source_target_pairs={{0,1},{1,0},{4,5},{5,4},{8,9},{9,8},{12,13},{13,12},{2,3},{3,2},{6... | collective-permute-start | bytes 196616 | tf_op jit(solution)/shard_map/ppermute | solution.py:496
  16.8 8.3 %collective-permute-start.2 = (bf16[2,8,16,128]{3,2,1,0:T(8,128)(2,1)S(1)}, bf16[2,8,16,128]{3,2,1,0:T(8,128)(2,1)S(1)}, u32[]{:S(2)}, u32[]{:S(2)}) collective-permute-start(bf16[2,8,16,128]{3,2,1,0:T(8,128)(2,1)S(1)} %pad_maximum_fusion.1), channel_id=1, source_target_pairs={{0,4},{1,5},{4,0},{5,1},{8,12},{9,13},{12,8},{13,9},{2,6},{3,7},{6... | collective-permute-start | bytes 196616 | tf_op jit(solution)/shard_map/ppermute | solution.py:496
  18.3 15.0 %collective-permute-start.3 = (bf16[2,8,16,128]{3,2,1,0:T(8,128)(2,1)S(1)}, bf16[2,8,16,128]{3,2,1,0:T(8,128)(2,1)S(1)}, u32[]{:S(2)}, u32[]{:S(2)}) collective-permute-start(bf16[2,8,16,128]{3,2,1,0:T(8,128)(2,1)S(1)} %pad_maximum_fusion.2), channel_id=1, source_target_pairs={{0,5},{1,4},{4,1},{5,0},{8,13},{9,12},{12,9},{13,8},{2,7},{3,6},{6... | collective-permute-start | bytes 196616 | tf_op jit(solution)/shard_map/ppermute | solution.py:496
  18.6 14.7 %collective-permute-start.4 = (bf16[2,8,16,128]{3,2,1,0:T(8,128)(2,1)S(1)}, bf16[2,8,16,128]{3,2,1,0:T(8,128)(2,1)S(1)}, u32[]{:S(2)}, u32[]{:S(2)}) collective-permute-start(bf16[2,8,16,128]{3,2,1,0:T(8,128)(2,1)S(1)} %pad_maximum_fusion.3), channel_id=1, source_target_pairs={{0,8},{1,9},{4,12},{5,13},{8,0},{9,1},{12,4},{13,5},{2,10},{3,11},... | collective-permute-start | bytes 196616 | tf_op jit(solution)/shard_map/ppermute | solution.py:496
  20.5 12.9 %collective-permute-start.5 = (bf16[2,8,16,128]{3,2,1,0:T(8,128)(2,1)S(1)}, bf16[2,8,16,128]{3,2,1,0:T(8,128)(2,1)S(1)}, u32[]{:S(2)}, u32[]{:S(2)}) collective-permute-start(bf16[2,8,16,128]{3,2,1,0:T(8,128)(2,1)S(1)} %pad_maximum_fusion.4), channel_id=1, source_target_pairs={{0,9},{1,8},{4,13},{5,12},{8,1},{9,0},{12,5},{13,4},{2,11},{3,10},... | collective-permute-start | bytes 196616 | tf_op jit(solution)/shard_map/ppermute | solution.py:496
  22.8 11.8 %collective-permute-start.6 = (bf16[2,8,16,128]{3,2,1,0:T(8,128)(2,1)S(1)}, bf16[2,8,16,128]{3,2,1,0:T(8,128)(2,1)S(1)}, u32[]{:S(2)}, u32[]{:S(2)}) collective-permute-start(bf16[2,8,16,128]{3,2,1,0:T(8,128)(2,1)S(1)} %pad_maximum_fusion.5), channel_id=1, source_target_pairs={{0,12},{1,13},{4,8},{5,9},{8,4},{9,5},{12,0},{13,1},{2,14},{3,15},... | collective-permute-start | bytes 196616 | tf_op jit(solution)/shard_map/ppermute | solution.py:496
  25.0 12.5 %collective-permute-start.7 = (bf16[2,8,16,128]{3,2,1,0:T(8,128)(2,1)S(1)}, bf16[2,8,16,128]{3,2,1,0:T(8,128)(2,1)S(1)}, u32[]{:S(2)}, u32[]{:S(2)}) collective-permute-start(bf16[2,8,16,128]{3,2,1,0:T(8,128)(2,1)S(1)} %pad_maximum_fusion.6), channel_id=1, source_target_pairs={{0,13},{1,12},{4,9},{5,8},{8,5},{9,4},{12,1},{13,0},{2,15},{3,14},... | collective-permute-start | bytes 196616 | tf_op jit(solution)/shard_map/ppermute | solution.py:496
  64.8 29.9 %all-to-all-start.3 = ((bf16[32,8,16,128]{3,2,1,0:T(8,128)(2,1)}), bf16[32,8,16,128]{3,2,1,0:T(8,128)(2,1)S(1)}, u32[]{:S(2)}, u32[]{:S(2)}) async-start(bf16[32,8,16,128]{3,2,1,0:T(8,128)(2,1)} %bitcast.24), calls=%async_computation.3 | async-start | bytes 2097152 | tf_op jit(solution)/shard_map/all_to_all | solution.py:491
  68.9 1.6 %collective-permute-start.8 = (bf16[8,8,16,128]{3,2,1,0:T(8,128)(2,1)S(1)}, bf16[8,8,16,128]{3,2,1,0:T(8,128)(2,1)S(1)}, u32[]{:S(2)}, u32[]{:S(2)}) collective-permute-start(bf16[8,8,16,128]{3,2,1,0:T(8,128)(2,1)S(1)} %get-tuple-element.27), channel_id=1, source_target_pairs={{0,2},{2,0},{1,3},{3,1},{4,6},{6,4},{5,7},{7,5},{8,10},{10,8},{9,1... | collective-permute-start | bytes 786440 | tf_op jit(solution)/shard_map/ppermute | solution.py:496
  70.5 9.8 %collective-permute-start.9 = (bf16[2,8,16,128]{3,2,1,0:T(8,128)(2,1)S(1)}, bf16[2,8,16,128]{3,2,1,0:T(8,128)(2,1)S(1)}, u32[]{:S(2)}, u32[]{:S(2)}) collective-permute-start(bf16[2,8,16,128]{3,2,1,0:T(8,128)(2,1)S(1)} %pad_maximum_fusion.7), channel_id=1, source_target_pairs={{0,1},{1,0},{4,5},{5,4},{8,9},{9,8},{12,13},{13,12},{2,3},{3,2},{6... | collective-permute-start | bytes 196616 | tf_op jit(solution)/shard_map/ppermute | solution.py:496
  72.2 9.9 %collective-permute-start.10 = (bf16[2,8,16,128]{3,2,1,0:T(8,128)(2,1)S(1)}, bf16[2,8,16,128]{3,2,1,0:T(8,128)(2,1)S(1)}, u32[]{:S(2)}, u32[]{:S(2)}) collective-permute-start(bf16[2,8,16,128]{3,2,1,0:T(8,128)(2,1)S(1)} %pad_maximum_fusion.8), channel_id=1, source_target_pairs={{0,4},{1,5},{4,0},{5,1},{8,12},{9,13},{12,8},{13,9},{2,6},{3,7},{6... | collective-permute-start | bytes 196616 | tf_op jit(solution)/shard_map/ppermute | solution.py:496
  73.7 14.2 %collective-permute-start.11 = (bf16[2,8,16,128]{3,2,1,0:T(8,128)(2,1)S(1)}, bf16[2,8,16,128]{3,2,1,0:T(8,128)(2,1)S(1)}, u32[]{:S(2)}, u32[]{:S(2)}) collective-permute-start(bf16[2,8,16,128]{3,2,1,0:T(8,128)(2,1)S(1)} %pad_maximum_fusion.9), channel_id=1, source_target_pairs={{0,5},{1,4},{4,1},{5,0},{8,13},{9,12},{12,9},{13,8},{2,7},{3,6},{6... | collective-permute-start | bytes 196616 | tf_op jit(solution)/shard_map/ppermute | solution.py:496
  74.2 13.7 %collective-permute-start.12 = (bf16[2,8,16,128]{3,2,1,0:T(8,128)(2,1)S(1)}, bf16[2,8,16,128]{3,2,1,0:T(8,128)(2,1)S(1)}, u32[]{:S(2)}, u32[]{:S(2)}) collective-permute-start(bf16[2,8,16,128]{3,2,1,0:T(8,128)(2,1)S(1)} %pad_maximum_fusion.10), channel_id=1, source_target_pairs={{0,8},{1,9},{4,12},{5,13},{8,0},{9,1},{12,4},{13,5},{2,10},{3,11},... | collective-permute-start | bytes 196616 | tf_op jit(solution)/shard_map/ppermute | solution.py:496
  75.9 13.3 %collective-permute-start.13 = (bf16[2,8,16,128]{3,2,1,0:T(8,128)(2,1)S(1)}, bf16[2,8,16,128]{3,2,1,0:T(8,128)(2,1)S(1)}, u32[]{:S(2)}, u32[]{:S(2)}) collective-permute-start(bf16[2,8,16,128]{3,2,1,0:T(8,128)(2,1)S(1)} %pad_maximum_fusion.11), channel_id=1, source_target_pairs={{0,9},{1,8},{4,13},{5,12},{8,1},{9,0},{12,5},{13,4},{2,11},{3,10},... | collective-permute-start | bytes 196616 | tf_op jit(solution)/shard_map/ppermute | solution.py:496
  80.3 11.5 %collective-permute-start.14 = (bf16[2,8,16,128]{3,2,1,0:T(8,128)(2,1)S(1)}, bf16[2,8,16,128]{3,2,1,0:T(8,128)(2,1)S(1)}, u32[]{:S(2)}, u32[]{:S(2)}) collective-permute-start(bf16[2,8,16,128]{3,2,1,0:T(8,128)(2,1)S(1)} %pad_maximum_fusion.12), channel_id=1, source_target_pairs={{0,12},{1,13},{4,8},{5,9},{8,4},{9,5},{12,0},{13,1},{2,14},{3,15},... | collective-permute-start | bytes 196616 | tf_op jit(solution)/shard_map/ppermute | solution.py:496
  82.1 12.6 %collective-permute-start.15 = (bf16[2,8,16,128]{3,2,1,0:T(8,128)(2,1)S(1)}, bf16[2,8,16,128]{3,2,1,0:T(8,128)(2,1)S(1)}, u32[]{:S(2)}, u32[]{:S(2)}) collective-permute-start(bf16[2,8,16,128]{3,2,1,0:T(8,128)(2,1)S(1)} %pad_maximum_fusion.13), channel_id=1, source_target_pairs={{0,13},{1,12},{4,9},{5,8},{8,5},{9,4},{12,1},{13,0},{2,15},{3,14},... | collective-permute-start | bytes 196616 | tf_op jit(solution)/shard_map/ppermute | solution.py:496

commit v18 on v16

--- a/solution.py
+++ b/solution.py
@@ -372,7 +372,7 @@
     hidden = left.shape[0] // rows
     groups, parts = groups_of(rows), groups_of(rows, 4)
     small = start(sems, [(gain_h, gain), (proj_h, proj_weight), (inv_h, inv)])
-    ahead = rows // math.gcd(rows, 2)
+    ahead = rows // math.gcd(rows, 4)
     blocks = [
         [
             pltpu.make_async_copy(
@@ -629,7 +629,7 @@
         [
             vmem(rows, 4, hidden, cols), short, vmem(rows, cols, dtype=F32), short,
             vector, proj_v, block, plane, plane,
-            sems(3), sems(n_parts), sems(n_parts), sems(n_parts), sems(2),
+            sems(3), sems(n_parts), sems(n_parts), sems(n_parts), sems(n_parts),
         ],
         (grad_right, coef, short_zhat, inv, dzg, gain_in, proj_weight, *grad_left),
         near=(0, *range(7, 7 + n_pieces)),

time: 100 us -> 100 us (level)
  no operation moved by 1% of the time
where the time goes in v18:
time: 100 us; the launch traced here: 99.6 us
  starting transfers between devices  29.1 us (29%)
  Pallas kernels  25.1 us (25%)
  blocking collectives  24.9 us (25%)
  waiting for transfers between devices  19.3 us (19%)
    pallas_call x10, Pallas kernels, call(): pl.pallas_call(kernel, out_shape=[out if at in outs_near else pltpu.HBM(o...  25.1 us
    all_to_all x2, blocking collectives, exchange(): lax.all_to_all(values, within, split_axis=0, concat_axis=0, tiled=True)  24.9 us
    ppermute x16, waiting for transfers between devices, permute(): lax.ppermute(values, axes, [(at, at ^ distance) for at in range(size)])  19.3 us
    ppermute x16, starting transfers between devices, permute(): lax.ppermute(values, axes, [(at, at ^ distance) for at in range(size)])  18.2 us
    all_to_all x2, starting transfers between devices, exchange_all(): lax.all_to_all(flat, ('half', *within), split_axis=0, concat_axis=0, tile...  10.9 us
  transfers between devices with their start and end apart: 18, of which 11 were waited for; matrix products, arithmetic and copies ran while one was open for 0% of the time, Pallas kernels for 15%

profile of v18, /device:TPU:0, one launch (start us, length us, event | category | flops | bytes accessed | tf_op | source)
XLA Modules:
  0.0 99.6 jit_solution(12801653612322353554)
XLA Ops:
  0.6 3.1 %shard_map.113 = bf16[2,16,8,16,128]{4,3,2,1,0:T(8,128)(2,1)} custom-call(bf16[16,128,128]{2,1,0:T(8,128)(2,1)} %pair_h.5, s32[256]{0:T(256)} %mask_h.5, s32[1,256]{1,0:T(1,128)} %bitcast.26, f32[1,128]{1,0:T(1,128)} %bitcast.29, f32[1,128]{1,0:T(1,128)} %bitcast.34, bf16[128,512]{1,0:T(8,128)(2,1)} %proj_h.7), custom_call_target="tpu_custom_call" | custom-call | flops 201326592 | bytes 1310720 | tf_op jit(solution)/shard_map/pallas_call | solution.py:438
  3.7 7.3 %all-to-all-start = ((bf16[32,8,16,128]{3,2,1,0:T(8,128)(2,1)}), bf16[32,8,16,128]{3,2,1,0:T(8,128)(2,1)S(1)}, u32[]{:S(2)}, u32[]{:S(2)}) async-start(bf16[32,8,16,128]{3,2,1,0:T(8,128)(2,1)} %bitcast.25), calls=%async_computation | async-start | bytes 2097152 | tf_op jit(solution)/shard_map/all_to_all | solution.py:493
  11.0 2.2 %shard_map.116 = (bf16[8,8,16,128]{3,2,1,0:T(8,128)(2,1)S(1)}, bf16[8,8,16,128]{3,2,1,0:T(8,128)(2,1)S(1)}) custom-call(bf16[16,128,128]{2,1,0:T(8,128)(2,1)} %pair_h.5, s32[256]{0:T(256)} %mask_h.5, s32[1,256]{1,0:T(1,128)} %bitcast.27, f32[1,128]{1,0:T(1,128)} %bitcast.30, f32[1,128]{1,0:T(1,128)} %bitcast.35, bf16[128,512]{1,0:T(8,128)(2,1)} %proj_h.7), custom_call_target="tpu_custom_call" | custom-call | flops 201326592 | bytes 1310720 | tf_op jit(solution)/shard_map/pallas_call | solution.py:438
  14.9 1.8 %collective-permute-start.1 = (bf16[2,8,16,128]{3,2,1,0:T(8,128)(2,1)S(1)}, bf16[2,8,16,128]{3,2,1,0:T(8,128)(2,1)S(1)}, u32[]{:S(2)}, u32[]{:S(2)}) collective-permute-start(bf16[2,8,16,128]{3,2,1,0:T(8,128)(2,1)S(1)} %pad_maximum_fusion), channel_id=1, source_target_pairs={{0,1},{1,0},{4,5},{5,4},{8,9},{9,8},{12,13},{13,12},{2,3},{3,2},{6... | collective-permute-start | bytes 196616 | tf_op jit(solution)/shard_map/ppermute | solution.py:498
  16.8 1.5 %collective-permute-start.2 = (bf16[2,8,16,128]{3,2,1,0:T(8,128)(2,1)S(1)}, bf16[2,8,16,128]{3,2,1,0:T(8,128)(2,1)S(1)}, u32[]{:S(2)}, u32[]{:S(2)}) collective-permute-start(bf16[2,8,16,128]{3,2,1,0:T(8,128)(2,1)S(1)} %pad_maximum_fusion.1), channel_id=1, source_target_pairs={{0,4},{1,5},{4,0},{5,1},{8,12},{9,13},{12,8},{13,9},{2,6},{3,7},{6... | collective-permute-start | bytes 196616 | tf_op jit(solution)/shard_map/ppermute | solution.py:498
  18.6 1.8 %collective-permute-start.4 = (bf16[2,8,16,128]{3,2,1,0:T(8,128)(2,1)S(1)}, bf16[2,8,16,128]{3,2,1,0:T(8,128)(2,1)S(1)}, u32[]{:S(2)}, u32[]{:S(2)}) collective-permute-start(bf16[2,8,16,128]{3,2,1,0:T(8,128)(2,1)S(1)} %pad_maximum_fusion.3), channel_id=1, source_target_pairs={{0,8},{1,9},{4,12},{5,13},{8,0},{9,1},{12,4},{13,5},{2,10},{3,11},... | collective-permute-start | bytes 196616 | tf_op jit(solution)/shard_map/ppermute | solution.py:498
  20.5 1.5 %collective-permute-start.5 = (bf16[2,8,16,128]{3,2,1,0:T(8,128)(2,1)S(1)}, bf16[2,8,16,128]{3,2,1,0:T(8,128)(2,1)S(1)}, u32[]{:S(2)}, u32[]{:S(2)}) collective-permute-start(bf16[2,8,16,128]{3,2,1,0:T(8,128)(2,1)S(1)} %pad_maximum_fusion.4), channel_id=1, source_target_pairs={{0,9},{1,8},{4,13},{5,12},{8,1},{9,0},{12,5},{13,4},{2,11},{3,10},... | collective-permute-start | bytes 196616 | tf_op jit(solution)/shard_map/ppermute | solution.py:498
  22.8 1.6 %collective-permute-start.6 = (bf16[2,8,16,128]{3,2,1,0:T(8,128)(2,1)S(1)}, bf16[2,8,16,128]{3,2,1,0:T(8,128)(2,1)S(1)}, u32[]{:S(2)}, u32[]{:S(2)}) collective-permute-start(bf16[2,8,16,128]{3,2,1,0:T(8,128)(2,1)S(1)} %pad_maximum_fusion.5), channel_id=1, source_target_pairs={{0,12},{1,13},{4,8},{5,9},{8,4},{9,5},{12,0},{13,1},{2,14},{3,15},... | collective-permute-start | bytes 196616 | tf_op jit(solution)/shard_map/ppermute | solution.py:498
  25.6 4.5 %shard_map.114 = (f32[16,128,128]{2,1,0:T(8,128)}, bf16[16,128,128]{2,1,0:T(8,128)(2,1)}, f32[16,128]{1,0:T(8,128)}, f32[16,128,128]{2,1,0:T(8,128)}, f32[2048,128]{1,0:T(8,128)S(1)}) custom-call(bf16[16,128,128]{2,1,0:T(8,128)(2,1)} %pair_h.5, bf16[16,128,128]{2,1,0:T(8,128)(2,1)} %cot_h.3, f32[1,128]{1,0:T(1,128)} %bitcast.31, f32[1,128]{1,0:T(1,128)} %bitcast.36, ...), custom_call_target="tpu_custom_call" | custom-call | flops 268435456 | bytes 4194304 | tf_op jit(solution)/shard_map/pallas_call | solution.py:438
  30.1 3.1 %shard_map.115.after.coef_h = bf16[16,4,128,128]{3,2,1,0:T(8,128)(2,1)} custom-call(f32[16,128,128]{2,1,0:T(8,128)} %get-tuple-element.15.zhat_h, s32[256]{0:T(256)} %mask_h.5, s32[1,256]{1,0:T(1,128)} %bitcast.28, f32[1,128]{1,0:T(1,128)} %bitcast.32, f32[1,128]{1,0:T(1,128)} %bitcast.37, bf16[128,512]{1,0:T(8,128)(2,1)} %proj_h.7), custom_call_target="tpu_custom_call" | custom-call | flops 335544320 | bytes 4194304 | tf_op jit(solution)/shard_map/pallas_call | solution.py:438
  34.6 2.9 %collective-permute-done.7.refs_8_ = bf16[2,8,16,128]{3,2,1,0:T(8,128)(2,1)S(1)} collective-permute-done((bf16[2,8,16,128]{3,2,1,0:T(8,128)(2,1)S(1)}, bf16[2,8,16,128]{3,2,1,0:T(8,128)(2,1)S(1)}, u32[]{:S(2)}, u32[]{:S(2)}) %collective-permute-start.7) | collective-permute-done | bytes 65568 | tf_op jit(solution)/shard_map/ppermute | solution.py:498
  38.0 12.9 %all_to_all.20 = bf16[16,8,16,128]{3,2,1,0:T(8,128)(2,1)S(1)} all-to-all(bf16[16,8,16,128]{3,2,1,0:T(8,128)(2,1)S(1)} %bitcast.23), channel_id=1, replica_groups=mesh['grp'=1,'half'=2,'row'=4,'core'=2,'col'=2] {'row','core','col'}, dimensions={0} | all-to-all | bytes 1048576 | tf_op jit(solution)/shard_map/all_to_all | solution.py:489
  51.5 12.0 %all_to_all.21 = bf16[16,8,16,128]{3,2,1,0:T(8,128)(2,1)S(1)} all-to-all(bf16[16,8,16,128]{3,2,1,0:T(8,128)(2,1)S(1)} %bitcast.21), channel_id=1, replica_groups=mesh['grp'=1,'half'=2,'row'=4,'core'=2,'col'=2] {'row','core','col'}, dimensions={0} | all-to-all | bytes 1048576 | tf_op jit(solution)/shard_map/all_to_all | solution.py:489
  64.8 3.6 %all-to-all-start.3 = ((bf16[32,8,16,128]{3,2,1,0:T(8,128)(2,1)}), bf16[32,8,16,128]{3,2,1,0:T(8,128)(2,1)S(1)}, u32[]{:S(2)}, u32[]{:S(2)}) async-start(bf16[32,8,16,128]{3,2,1,0:T(8,128)(2,1)} %bitcast.24), calls=%async_computation.3 | async-start | bytes 2097152 | tf_op jit(solution)/shard_map/all_to_all | solution.py:493
  69.0 1.4 %collective-permute-done.8.refs_1_ = bf16[8,8,16,128]{3,2,1,0:T(8,128)(2,1)S(1)} collective-permute-done((bf16[8,8,16,128]{3,2,1,0:T(8,128)(2,1)S(1)}, bf16[8,8,16,128]{3,2,1,0:T(8,128)(2,1)S(1)}, u32[]{:S(2)}, u32[]{:S(2)}) %collective-permute-start.8) | collective-permute-done | bytes 262176 | tf_op jit(solution)/shard_map/ppermute | solution.py:498
  70.5 1.7 %collective-permute-start.9 = (bf16[2,8,16,128]{3,2,1,0:T(8,128)(2,1)S(1)}, bf16[2,8,16,128]{3,2,1,0:T(8,128)(2,1)S(1)}, u32[]{:S(2)}, u32[]{:S(2)}) collective-permute-start(bf16[2,8,16,128]{3,2,1,0:T(8,128)(2,1)S(1)} %pad_maximum_fusion.7), channel_id=1, source_target_pairs={{0,1},{1,0},{4,5},{5,4},{8,9},{9,8},{12,13},{13,12},{2,3},{3,2},{6... | collective-permute-start | bytes 196616 | tf_op jit(solution)/shard_map/ppermute | solution.py:498
  72.2 1.5 %collective-permute-start.10 = (bf16[2,8,16,128]{3,2,1,0:T(8,128)(2,1)S(1)}, bf16[2,8,16,128]{3,2,1,0:T(8,128)(2,1)S(1)}, u32[]{:S(2)}, u32[]{:S(2)}) collective-permute-start(bf16[2,8,16,128]{3,2,1,0:T(8,128)(2,1)S(1)} %pad_maximum_fusion.8), channel_id=1, source_target_pairs={{0,4},{1,5},{4,0},{5,1},{8,12},{9,13},{12,8},{13,9},{2,6},{3,7},{6... | collective-permute-start | bytes 196616 | tf_op jit(solution)/shard_map/ppermute | solution.py:498
  74.2 1.7 %collective-permute-start.12 = (bf16[2,8,16,128]{3,2,1,0:T(8,128)(2,1)S(1)}, bf16[2,8,16,128]{3,2,1,0:T(8,128)(2,1)S(1)}, u32[]{:S(2)}, u32[]{:S(2)}) collective-permute-start(bf16[2,8,16,128]{3,2,1,0:T(8,128)(2,1)S(1)} %pad_maximum_fusion.10), channel_id=1, source_target_pairs={{0,8},{1,9},{4,12},{5,13},{8,0},{9,1},{12,4},{13,5},{2,10},{3,11},... | collective-permute-start | bytes 196616 | tf_op jit(solution)/shard_map/ppermute | solution.py:498
  75.9 1.5 %collective-permute-start.13 = (bf16[2,8,16,128]{3,2,1,0:T(8,128)(2,1)S(1)}, bf16[2,8,16,128]{3,2,1,0:T(8,128)(2,1)S(1)}, u32[]{:S(2)}, u32[]{:S(2)}) collective-permute-start(bf16[2,8,16,128]{3,2,1,0:T(8,128)(2,1)S(1)} %pad_maximum_fusion.11), channel_id=1, source_target_pairs={{0,9},{1,8},{4,13},{5,12},{8,1},{9,0},{12,5},{13,4},{2,11},{3,10},... | collective-permute-start | bytes 196616 | tf_op jit(solution)/shard_map/ppermute | solution.py:498
  77.4 2.9 %collective-permute-done.9.refs_2_ = bf16[2,8,16,128]{3,2,1,0:T(8,128)(2,1)S(1)} collective-permute-done((bf16[2,8,16,128]{3,2,1,0:T(8,128)(2,1)S(1)}, bf16[2,8,16,128]{3,2,1,0:T(8,128)(2,1)S(1)}, u32[]{:S(2)}, u32[]{:S(2)}) %collective-permute-start.9) | collective-permute-done | bytes 65568 | tf_op jit(solution)/shard_map/ppermute | solution.py:498
  83.3 4.5 %shard_map.120 = (bf16[16,128,128]{2,1,0:T(8,128)(2,1)}, bf16[16,128,128]{2,1,0:T(8,128)(2,1)}) custom-call(bf16[128,16,128]{2,1,0:T(8,128)(2,1)S(1)} %bitcast.19, f32[16,128,128]{2,1,0:T(8,128)} %get-tuple-element.19.gate_h, bf16[16,128,128]{2,1,0:T(8,128)(2,1)} %cot_h.3, f32[1,128]{1,0:T(1,128)} %bitcast.39, f32[1,128]{1,0:T(1,128)} %bitcast.40, ...), custom_call_target="tpu_custom_call" | custom-call | flops 201326592 | bytes 3670016 | tf_op jit(solution)/shard_map/pallas_call | solution.py:438
  89.2 2.7 %collective-permute-done.14.refs_7_ = bf16[2,8,16,128]{3,2,1,0:T(8,128)(2,1)S(1)} collective-permute-done((bf16[2,8,16,128]{3,2,1,0:T(8,128)(2,1)S(1)}, bf16[2,8,16,128]{3,2,1,0:T(8,128)(2,1)S(1)}, u32[]{:S(2)}, u32[]{:S(2)}) %collective-permute-start.14) | collective-permute-done | bytes 65568 | tf_op jit(solution)/shard_map/ppermute | solution.py:498
  91.8 2.9 %collective-permute-done.15.refs_8_ = bf16[2,8,16,128]{3,2,1,0:T(8,128)(2,1)S(1)} collective-permute-done((bf16[2,8,16,128]{3,2,1,0:T(8,128)(2,1)S(1)}, bf16[2,8,16,128]{3,2,1,0:T(8,128)(2,1)S(1)}, u32[]{:S(2)}, u32[]{:S(2)}) %collective-permute-start.15) | collective-permute-done | bytes 65568 | tf_op jit(solution)/shard_map/ppermute | solution.py:498
  94.7 4.7 %shard_map.122 = bf16[16,128,128]{2,1,0:T(8,128)(2,1)} custom-call(bf16[2,16,8,16,128]{4,3,2,1,0:T(8,128)(2,1)S(1)} %bitcast.20, bf16[16,4,128,128]{3,2,1,0:T(8,128)(2,1)} %shard_map.115.after.coef_h, bf16[16,128,128]{2,1,0:T(8,128)(2,1)} %get-tuple-element.23.zhat_h, f32[16,128]{1,0:T(8,128)} %get-tuple-element.24.inv_h, ...), custom_call_target="tpu_custom_call" | custom-call | flops 335544320 | bytes 7864320 | tf_op jit(solution)/shard_map/pallas_call | solution.py:438
  (42 shorter events, 13.1 us)
Async XLA Ops:
  3.7 33.7 %all-to-all-start = ((bf16[32,8,16,128]{3,2,1,0:T(8,128)(2,1)}), bf16[32,8,16,128]{3,2,1,0:T(8,128)(2,1)S(1)}, u32[]{:S(2)}, u32[]{:S(2)}) async-start(bf16[32,8,16,128]{3,2,1,0:T(8,128)(2,1)} %bitcast.25), calls=%async_computation | async-start | bytes 2097152 | tf_op jit(solution)/shard_map/all_to_all | solution.py:493
  13.3 1.6 %collective-permute-start = (bf16[8,8,16,128]{3,2,1,0:T(8,128)(2,1)S(1)}, bf16[8,8,16,128]{3,2,1,0:T(8,128)(2,1)S(1)}, u32[]{:S(2)}, u32[]{:S(2)}) collective-permute-start(bf16[8,8,16,128]{3,2,1,0:T(8,128)(2,1)S(1)} %get-tuple-element.17), channel_id=1, source_target_pairs={{0,2},{2,0},{1,3},{3,1},{4,6},{6,4},{5,7},{7,5},{8,10},{10,8},{9,1... | collective-permute-start | bytes 786440 | tf_op jit(solution)/shard_map/ppermute | solution.py:498
  14.9 7.9 %collective-permute-start.1 = (bf16[2,8,16,128]{3,2,1,0:T(8,128)(2,1)S(1)}, bf16[2,8,16,128]{3,2,1,0:T(8,128)(2,1)S(1)}, u32[]{:S(2)}, u32[]{:S(2)}) collective-permute-start(bf16[2,8,16,128]{3,2,1,0:T(8,128)(2,1)S(1)} %pad_maximum_fusion), channel_id=1, source_target_pairs={{0,1},{1,0},{4,5},{5,4},{8,9},{9,8},{12,13},{13,12},{2,3},{3,2},{6... | collective-permute-start | bytes 196616 | tf_op jit(solution)/shard_map/ppermute | solution.py:498
  16.8 8.3 %collective-permute-start.2 = (bf16[2,8,16,128]{3,2,1,0:T(8,128)(2,1)S(1)}, bf16[2,8,16,128]{3,2,1,0:T(8,128)(2,1)S(1)}, u32[]{:S(2)}, u32[]{:S(2)}) collective-permute-start(bf16[2,8,16,128]{3,2,1,0:T(8,128)(2,1)S(1)} %pad_maximum_fusion.1), channel_id=1, source_target_pairs={{0,4},{1,5},{4,0},{5,1},{8,12},{9,13},{12,8},{13,9},{2,6},{3,7},{6... | collective-permute-start | bytes 196616 | tf_op jit(solution)/shard_map/ppermute | solution.py:498
  18.3 15.0 %collective-permute-start.3 = (bf16[2,8,16,128]{3,2,1,0:T(8,128)(2,1)S(1)}, bf16[2,8,16,128]{3,2,1,0:T(8,128)(2,1)S(1)}, u32[]{:S(2)}, u32[]{:S(2)}) collective-permute-start(bf16[2,8,16,128]{3,2,1,0:T(8,128)(2,1)S(1)} %pad_maximum_fusion.2), channel_id=1, source_target_pairs={{0,5},{1,4},{4,1},{5,0},{8,13},{9,12},{12,9},{13,8},{2,7},{3,6},{6... | collective-permute-start | bytes 196616 | tf_op jit(solution)/shard_map/ppermute | solution.py:498
  18.6 14.7 %collective-permute-start.4 = (bf16[2,8,16,128]{3,2,1,0:T(8,128)(2,1)S(1)}, bf16[2,8,16,128]{3,2,1,0:T(8,128)(2,1)S(1)}, u32[]{:S(2)}, u32[]{:S(2)}) collective-permute-start(bf16[2,8,16,128]{3,2,1,0:T(8,128)(2,1)S(1)} %pad_maximum_fusion.3), channel_id=1, source_target_pairs={{0,8},{1,9},{4,12},{5,13},{8,0},{9,1},{12,4},{13,5},{2,10},{3,11},... | collective-permute-start | bytes 196616 | tf_op jit(solution)/shard_map/ppermute | solution.py:498
  20.5 12.9 %collective-permute-start.5 = (bf16[2,8,16,128]{3,2,1,0:T(8,128)(2,1)S(1)}, bf16[2,8,16,128]{3,2,1,0:T(8,128)(2,1)S(1)}, u32[]{:S(2)}, u32[]{:S(2)}) collective-permute-start(bf16[2,8,16,128]{3,2,1,0:T(8,128)(2,1)S(1)} %pad_maximum_fusion.4), channel_id=1, source_target_pairs={{0,9},{1,8},{4,13},{5,12},{8,1},{9,0},{12,5},{13,4},{2,11},{3,10},... | collective-permute-start | bytes 196616 | tf_op jit(solution)/shard_map/ppermute | solution.py:498
  22.8 11.8 %collective-permute-start.6 = (bf16[2,8,16,128]{3,2,1,0:T(8,128)(2,1)S(1)}, bf16[2,8,16,128]{3,2,1,0:T(8,128)(2,1)S(1)}, u32[]{:S(2)}, u32[]{:S(2)}) collective-permute-start(bf16[2,8,16,128]{3,2,1,0:T(8,128)(2,1)S(1)} %pad_maximum_fusion.5), channel_id=1, source_target_pairs={{0,12},{1,13},{4,8},{5,9},{8,4},{9,5},{12,0},{13,1},{2,14},{3,15},... | collective-permute-start | bytes 196616 | tf_op jit(solution)/shard_map/ppermute | solution.py:498
  25.0 12.5 %collective-permute-start.7 = (bf16[2,8,16,128]{3,2,1,0:T(8,128)(2,1)S(1)}, bf16[2,8,16,128]{3,2,1,0:T(8,128)(2,1)S(1)}, u32[]{:S(2)}, u32[]{:S(2)}) collective-permute-start(bf16[2,8,16,128]{3,2,1,0:T(8,128)(2,1)S(1)} %pad_maximum_fusion.6), channel_id=1, source_target_pairs={{0,13},{1,12},{4,9},{5,8},{8,5},{9,4},{12,1},{13,0},{2,15},{3,14},... | collective-permute-start | bytes 196616 | tf_op jit(solution)/shard_map/ppermute | solution.py:498
  64.8 29.9 %all-to-all-start.3 = ((bf16[32,8,16,128]{3,2,1,0:T(8,128)(2,1)}), bf16[32,8,16,128]{3,2,1,0:T(8,128)(2,1)S(1)}, u32[]{:S(2)}, u32[]{:S(2)}) async-start(bf16[32,8,16,128]{3,2,1,0:T(8,128)(2,1)} %bitcast.24), calls=%async_computation.3 | async-start | bytes 2097152 | tf_op jit(solution)/shard_map/all_to_all | solution.py:493
  68.9 1.6 %collective-permute-start.8 = (bf16[8,8,16,128]{3,2,1,0:T(8,128)(2,1)S(1)}, bf16[8,8,16,128]{3,2,1,0:T(8,128)(2,1)S(1)}, u32[]{:S(2)}, u32[]{:S(2)}) collective-permute-start(bf16[8,8,16,128]{3,2,1,0:T(8,128)(2,1)S(1)} %get-tuple-element.27), channel_id=1, source_target_pairs={{0,2},{2,0},{1,3},{3,1},{4,6},{6,4},{5,7},{7,5},{8,10},{10,8},{9,1... | collective-permute-start | bytes 786440 | tf_op jit(solution)/shard_map/ppermute | solution.py:498
  70.5 9.8 %collective-permute-start.9 = (bf16[2,8,16,128]{3,2,1,0:T(8,128)(2,1)S(1)}, bf16[2,8,16,128]{3,2,1,0:T(8,128)(2,1)S(1)}, u32[]{:S(2)}, u32[]{:S(2)}) collective-permute-start(bf16[2,8,16,128]{3,2,1,0:T(8,128)(2,1)S(1)} %pad_maximum_fusion.7), channel_id=1, source_target_pairs={{0,1},{1,0},{4,5},{5,4},{8,9},{9,8},{12,13},{13,12},{2,3},{3,2},{6... | collective-permute-start | bytes 196616 | tf_op jit(solution)/shard_map/ppermute | solution.py:498
  72.2 9.9 %collective-permute-start.10 = (bf16[2,8,16,128]{3,2,1,0:T(8,128)(2,1)S(1)}, bf16[2,8,16,128]{3,2,1,0:T(8,128)(2,1)S(1)}, u32[]{:S(2)}, u32[]{:S(2)}) collective-permute-start(bf16[2,8,16,128]{3,2,1,0:T(8,128)(2,1)S(1)} %pad_maximum_fusion.8), channel_id=1, source_target_pairs={{0,4},{1,5},{4,0},{5,1},{8,12},{9,13},{12,8},{13,9},{2,6},{3,7},{6... | collective-permute-start | bytes 196616 | tf_op jit(solution)/shard_map/ppermute | solution.py:498
  73.7 14.2 %collective-permute-start.11 = (bf16[2,8,16,128]{3,2,1,0:T(8,128)(2,1)S(1)}, bf16[2,8,16,128]{3,2,1,0:T(8,128)(2,1)S(1)}, u32[]{:S(2)}, u32[]{:S(2)}) collective-permute-start(bf16[2,8,16,128]{3,2,1,0:T(8,128)(2,1)S(1)} %pad_maximum_fusion.9), channel_id=1, source_target_pairs={{0,5},{1,4},{4,1},{5,0},{8,13},{9,12},{12,9},{13,8},{2,7},{3,6},{6... | collective-permute-start | bytes 196616 | tf_op jit(solution)/shard_map/ppermute | solution.py:498
  74.2 13.7 %collective-permute-start.12 = (bf16[2,8,16,128]{3,2,1,0:T(8,128)(2,1)S(1)}, bf16[2,8,16,128]{3,2,1,0:T(8,128)(2,1)S(1)}, u32[]{:S(2)}, u32[]{:S(2)}) collective-permute-start(bf16[2,8,16,128]{3,2,1,0:T(8,128)(2,1)S(1)} %pad_maximum_fusion.10), channel_id=1, source_target_pairs={{0,8},{1,9},{4,12},{5,13},{8,0},{9,1},{12,4},{13,5},{2,10},{3,11},... | collective-permute-start | bytes 196616 | tf_op jit(solution)/shard_map/ppermute | solution.py:498
  75.9 13.3 %collective-permute-start.13 = (bf16[2,8,16,128]{3,2,1,0:T(8,128)(2,1)S(1)}, bf16[2,8,16,128]{3,2,1,0:T(8,128)(2,1)S(1)}, u32[]{:S(2)}, u32[]{:S(2)}) collective-permute-start(bf16[2,8,16,128]{3,2,1,0:T(8,128)(2,1)S(1)} %pad_maximum_fusion.11), channel_id=1, source_target_pairs={{0,9},{1,8},{4,13},{5,12},{8,1},{9,0},{12,5},{13,4},{2,11},{3,10},... | collective-permute-start | bytes 196616 | tf_op jit(solution)/shard_map/ppermute | solution.py:498
  80.3 11.5 %collective-permute-start.14 = (bf16[2,8,16,128]{3,2,1,0:T(8,128)(2,1)S(1)}, bf16[2,8,16,128]{3,2,1,0:T(8,128)(2,1)S(1)}, u32[]{:S(2)}, u32[]{:S(2)}) collective-permute-start(bf16[2,8,16,128]{3,2,1,0:T(8,128)(2,1)S(1)} %pad_maximum_fusion.12), channel_id=1, source_target_pairs={{0,12},{1,13},{4,8},{5,9},{8,4},{9,5},{12,0},{13,1},{2,14},{3,15},... | collective-permute-start | bytes 196616 | tf_op jit(solution)/shard_map/ppermute | solution.py:498
  82.1 12.6 %collective-permute-start.15 = (bf16[2,8,16,128]{3,2,1,0:T(8,128)(2,1)S(1)}, bf16[2,8,16,128]{3,2,1,0:T(8,128)(2,1)S(1)}, u32[]{:S(2)}, u32[]{:S(2)}) collective-permute-start(bf16[2,8,16,128]{3,2,1,0:T(8,128)(2,1)S(1)} %pad_maximum_fusion.13), channel_id=1, source_target_pairs={{0,13},{1,12},{4,9},{5,8},{8,5},{9,4},{12,1},{13,0},{2,15},{3,14},... | collective-permute-start | bytes 196616 | tf_op jit(solution)/shard_map/ppermute | solution.py:498
